TPU v7x, 32 devices: a whole 2x2x4 slice. The times are simulated.
32 devices in a mesh: dp: 4 (over y, x), fsdp: 8 (over z, core).
Axes of the slice: x: 2, y: 2, z: 4, core: 2. Of those that a mesh axis runs over, the one named last changes fastest.
Arguments:
- images: bfloat16 [768, 197, 384], P(('dp', 'fsdp')), may hold values from -6 to 6
- cotangent: bfloat16 [768, 197, 384], P(('dp', 'fsdp')), may hold values from -6 to 6
- counts: int32 [32], P(('dp', 'fsdp')), may hold values from 1 to 24, as said below
- w_qkv: float32 [384, 1152], P('fsdp'), may hold values from -0.3125 to 0.3125
- w_proj: float32 [384, 384], P('fsdp'), may hold values from -1.25 to 1.25
- w_fc1: float32 [384, 1152], P('fsdp'), may hold values from -0.3125 to 0.3125
- w_fc2: float32 [1152, 384], P(None, 'fsdp'), may hold values from -0.1875 to 0.1875
- b_fc1: float32 [1152], P('fsdp'), may hold values from -3 to 3
- vectors: float32 [6, 384], P(None, 'fsdp'), may hold values from 0.1 to 1.9
- m_qkv: float32 [384, 1152], P('fsdp'), may hold values from -0.125 to 0.125
- m_proj: float32 [384, 384], P('fsdp'), may hold values from -0.125 to 0.125
- m_fc1: float32 [384, 1152], P('fsdp'), may hold values from -0.125 to 0.125
- m_fc2: float32 [1152, 384], P(None, 'fsdp'), may hold values from -0.125 to 0.125
- m_bias1: float32 [1152], P('fsdp'), may hold values from -0.125 to 0.125
- m_vectors: float32 [6, 384], P(None, 'fsdp'), may hold values from -0.125 to 0.125
- v_qkv: float32 [384, 1152], P('fsdp'), may hold values from 1e-05 to 0.001
- v_proj: float32 [384, 384], P('fsdp'), may hold values from 1e-05 to 0.001
- v_fc1: float32 [384, 1152], P('fsdp'), may hold values from 1e-05 to 0.001
- v_fc2: float32 [1152, 384], P(None, 'fsdp'), may hold values from 1e-05 to 0.001
- v_bias1: float32 [1152], P('fsdp'), may hold values from 1e-05 to 0.001
- v_vectors: float32 [6, 384], P(None, 'fsdp'), may hold values from 1e-05 to 0.001
- decay_flags: int32 [6], replicated, may hold values from 0 to 1
- group_ids: int32 [6], replicated, may hold values from 0 to 2
- group_scales: float32 [3], replicated, may hold values from 0.5 to 4
Outputs:
- out_block: bfloat16 [768, 197, 384], P(('dp', 'fsdp'))
- grad_input: bfloat16 [768, 197, 384], P(('dp', 'fsdp'))
- g_qkv: float32 [384, 1152], P('fsdp')
- g_proj: float32 [384, 384], P('fsdp')
- g_fc1: float32 [384, 1152], P('fsdp')
- g_fc2: float32 [1152, 384], P(None, 'fsdp')
- g_bias1: float32 [1152], P('fsdp')
- g_vectors: float32 [6, 384], P(None, 'fsdp')
- new_qkv: float32 [384, 1152], P('fsdp')
- new_proj: float32 [384, 384], P('fsdp')
- new_fc1: float32 [384, 1152], P('fsdp')
- new_fc2: float32 [1152, 384], P(None, 'fsdp')
- new_bias1: float32 [1152], P('fsdp')
- new_vectors: float32 [6, 384], P(None, 'fsdp')
- first_qkv: float32 [384, 1152], P('fsdp')
- first_proj: float32 [384, 384], P('fsdp')
- first_fc1: float32 [384, 1152], P('fsdp')
- first_fc2: float32 [1152, 384], P(None, 'fsdp')
- first_bias1: float32 [1152], P('fsdp')
- first_vectors: float32 [6, 384], P(None, 'fsdp')
- second_qkv: float32 [384, 1152], P('fsdp')
- second_proj: float32 [384, 384], P('fsdp')
- second_fc1: float32 [384, 1152], P('fsdp')
- second_fc2: float32 [1152, 384], P(None, 'fsdp')
- second_bias1: float32 [1152], P('fsdp')
- second_vectors: float32 [6, 384], P(None, 'fsdp')
Inputs may be any that keep to these rules, and one draw needn't show every extreme that they name: `counts`: number of real images among a device's 24 slots, the first ones; some device has all slots real.
All inputs are finite; a program needn't handle non-finite values.
Results may differ from a plain program's by a relative error of at most 0.022.
The roundings to bfloat16 on the way count: a program that leaves them out, or rounds other values in their place, can miss the bound.
Values may be sent and summed in bfloat16 or wider, within the bound.
No kernel may reach another device: no remote copies, remote signals or barrier semaphores. Data moves between devices by JAX's collectives and lax.ppermute only.
A program may use at most 256 MiB of HBM per device.

v0:
```python
from functools import partial

import jax
import jax.numpy as jnp
from jax import lax
from jax.sharding import PartitionSpec as P

HEAD_DIM = 64
ATT_IMG = 4


EPS_LN = 1e-06
LEARN_RATE = 0.2
BETA_ONE = 0.9
BETA_TWO = 0.999
ADAM_EPS = 1e-08
DECAY_RATE = 0.5
adam_steps = 10.0


def norm_affine(inputs, gain, shift):
    centre = inputs - jnp.mean(inputs, axis=-1, keepdims=True)
    spread = jnp.mean(centre * centre, axis=-1, keepdims=True)
    return centre * lax.rsqrt(spread + EPS_LN) * gain + shift


def attend_block(inputs):
    queries, keys_in, values_in = inputs
    factor = queries.shape[-1] ** (-0.5)
    scores = (
        jnp.einsum("bqhd,bkhd->bhqk", queries, keys_in, preferred_element_type=jnp.float32) * factor
    )
    row_max = jnp.max(scores, axis=-1, keepdims=True)
    expo = jnp.exp(scores - row_max)
    row_sum = jnp.sum(expo, axis=-1, keepdims=True)
    probs = (expo / row_sum).astype(jnp.bfloat16)
    mixed = jnp.einsum("bhqk,bkhd->bqhd", probs, values_in, preferred_element_type=jnp.float32)
    return (mixed.astype(jnp.bfloat16), row_max + jnp.log(row_sum))


def attend_back(inputs):
    queries, keys_in, values_in, log_sums, grad_mixed = inputs
    factor = queries.shape[-1] ** (-0.5)
    scores = (
        jnp.einsum("bqhd,bkhd->bhqk", queries, keys_in, preferred_element_type=jnp.float32) * factor
    )
    probs = jnp.exp(scores - log_sums)
    grad_values = jnp.einsum(
        "bhqk,bqhd->bkhd",
        probs.astype(jnp.bfloat16),
        grad_mixed,
        preferred_element_type=jnp.float32,
    )
    grad_probs = jnp.einsum(
        "bqhd,bkhd->bhqk", grad_mixed, values_in, preferred_element_type=jnp.float32
    )
    inner = jnp.sum(grad_probs * probs, axis=-1, keepdims=True)
    grad_scores = (probs * (grad_probs - inner) * factor).astype(jnp.bfloat16)
    grad_queries = jnp.einsum(
        "bhqk,bkhd->bqhd", grad_scores, keys_in, preferred_element_type=jnp.float32
    )
    grad_keys = jnp.einsum(
        "bhqk,bqhd->bkhd", grad_scores, queries, preferred_element_type=jnp.float32
    )
    return (grad_queries, grad_keys, grad_values)


def adam_update(weight, grad, first, second, flag, lr_scale):
    first_new = BETA_ONE * first + (1.0 - BETA_ONE) * grad
    second_new = BETA_TWO * second + (1.0 - BETA_TWO) * grad * grad
    corr_one = 1.0 - BETA_ONE**adam_steps
    corr_two = 1.0 - BETA_TWO**adam_steps
    direction = first_new / corr_one / (jnp.sqrt(second_new / corr_two) + ADAM_EPS)
    weight_new = weight - LEARN_RATE * lr_scale * (direction + DECAY_RATE * flag * weight)
    return (weight_new, first_new, second_new)


def local(
    images,
    cotangent,
    counts,
    w_qkv,
    w_proj,
    w_fc1,
    w_fc2,
    b_fc1,
    vectors,
    m_qkv,
    m_proj,
    m_fc1,
    m_fc2,
    m_bias1,
    m_vectors,
    v_qkv,
    v_proj,
    v_fc1,
    v_fc2,
    v_bias1,
    v_vectors,
    decay_flags,
    group_ids,
    group_scales,
):
    masters = (w_qkv, w_proj, w_fc1, w_fc2, b_fc1, vectors)
    lowered = [weight.astype(jnp.bfloat16) for weight in masters]
    gathered = (
        lax.all_gather(lowered[0], "fsdp", axis=0, tiled=True),
        lax.all_gather(lowered[1], "fsdp", axis=0, tiled=True),
        lax.all_gather(lowered[2], "fsdp", axis=0, tiled=True),
        lax.all_gather(lowered[3], "fsdp", axis=1, tiled=True),
        lax.all_gather(lowered[4], "fsdp", axis=0, tiled=True),
        lax.all_gather(lowered[5], "fsdp", axis=1, tiled=True),
    )
    qkv_weight, proj_weight, fc1_weight, fc2_weight = (
        gathered[0],
        gathered[1],
        gathered[2],
        gathered[3],
    )
    fc1_bias = gathered[4].astype(jnp.float32)
    vector_rows = gathered[5].astype(jnp.float32)
    count_img, seq_len, model_width = images.shape
    total_rows = count_img * seq_len
    head_size = HEAD_DIM
    head_count = model_width // head_size
    blocks_count = count_img // ATT_IMG

    def to_blocks(array):
        return array.reshape((blocks_count, ATT_IMG) + array.shape[1:])

    def from_blocks(array):
        return array.reshape((count_img,) + array.shape[2:])

    valid_img = (jnp.arange(count_img) < counts[0]).astype(jnp.float32)
    valid_rows = jnp.broadcast_to(valid_img[:, None], (count_img, seq_len)).reshape(total_rows, 1)
    tokens_f = images.astype(jnp.float32).reshape(total_rows, model_width)
    normed_a = norm_affine(tokens_f, vector_rows[0], vector_rows[1]).astype(jnp.bfloat16)
    packed = jnp.dot(normed_a, qkv_weight, preferred_element_type=jnp.float32).astype(jnp.bfloat16)
    packed = packed.reshape(count_img, seq_len, 3, head_count, head_size)
    queries = to_blocks(packed[:, :, 0])
    keys_in = to_blocks(packed[:, :, 1])
    values_in = to_blocks(packed[:, :, 2])
    attended, log_sums = lax.map(attend_block, (queries, keys_in, values_in))
    mixed = from_blocks(attended).reshape(total_rows, model_width)
    middle = (
        tokens_f + jnp.dot(mixed, proj_weight, preferred_element_type=jnp.float32) + vector_rows[2]
    )
    normed_b = norm_affine(middle, vector_rows[3], vector_rows[4]).astype(jnp.bfloat16)
    hidden = jnp.dot(normed_b, fc1_weight, preferred_element_type=jnp.float32) + fc1_bias
    active = jax.nn.gelu(hidden, approximate=False).astype(jnp.bfloat16)
    output = (
        middle + jnp.dot(active, fc2_weight, preferred_element_type=jnp.float32) + vector_rows[5]
    )
    out_block = (output * valid_rows).astype(jnp.bfloat16).reshape(images.shape)
    regathered = (
        lax.all_gather(lowered[0], "fsdp", axis=0, tiled=True),
        lax.all_gather(lowered[1], "fsdp", axis=0, tiled=True),
        lax.all_gather(lowered[2], "fsdp", axis=0, tiled=True),
        lax.all_gather(lowered[3], "fsdp", axis=1, tiled=True),
        lax.all_gather(lowered[4], "fsdp", axis=0, tiled=True),
        lax.all_gather(lowered[5], "fsdp", axis=1, tiled=True),
    )
    qkv_back, proj_back, fc1_back, fc2_back = (
        regathered[0],
        regathered[1],
        regathered[2],
        regathered[3],
    )
    vector_back = regathered[5].astype(jnp.float32)
    grad_out = cotangent.astype(jnp.float32).reshape(total_rows, model_width) * valid_rows
    grad_low = grad_out.astype(jnp.bfloat16)
    grad_fc2 = jnp.einsum("rf,rd->fd", active, grad_low, preferred_element_type=jnp.float32)
    grad_active = jnp.einsum("rd,fd->rf", grad_low, fc2_back, preferred_element_type=jnp.float32)
    _, gelu_pull = jax.vjp(partial(jax.nn.gelu, approximate=False), hidden)
    grad_hidden = gelu_pull(grad_active)[0]
    grad_hidden_low = grad_hidden.astype(jnp.bfloat16)
    grad_bias1 = jnp.sum(grad_hidden, axis=0)
    grad_fc1 = jnp.einsum(
        "rd,rf->df", normed_b, grad_hidden_low, preferred_element_type=jnp.float32
    )
    grad_normed_b = jnp.einsum(
        "rf,df->rd", grad_hidden_low, fc1_back, preferred_element_type=jnp.float32
    )
    _, norm_pull_b = jax.vjp(norm_affine, middle, vector_back[3], vector_back[4])
    grad_mid_norm, grad_gain_b, grad_shift_b = norm_pull_b(grad_normed_b)
    grad_middle = grad_out + grad_mid_norm
    grad_middle_low = grad_middle.astype(jnp.bfloat16)
    grad_pbias = jnp.sum(grad_middle, axis=0)
    grad_proj = jnp.einsum("rd,re->de", mixed, grad_middle_low, preferred_element_type=jnp.float32)
    grad_mixed = jnp.einsum(
        "re,de->rd", grad_middle_low, proj_back, preferred_element_type=jnp.float32
    ).astype(jnp.bfloat16)
    grad_mixed = to_blocks(grad_mixed.reshape(count_img, seq_len, head_count, head_size))
    grad_queries, grad_keys, grad_values = lax.map(
        attend_back, (queries, keys_in, values_in, log_sums, grad_mixed)
    )
    grad_packed = jnp.stack(
        [from_blocks(grad_queries), from_blocks(grad_keys), from_blocks(grad_values)], axis=2
    )
    grad_packed = grad_packed.reshape(total_rows, 3 * model_width).astype(jnp.bfloat16)
    grad_qkv = jnp.einsum("rd,rf->df", normed_a, grad_packed, preferred_element_type=jnp.float32)
    grad_normed_a = jnp.einsum(
        "rf,df->rd", grad_packed, qkv_back, preferred_element_type=jnp.float32
    )
    _, norm_pull_a = jax.vjp(norm_affine, tokens_f, vector_back[0], vector_back[1])
    grad_in_norm, grad_gain_a, grad_shift_a = norm_pull_a(grad_normed_a)
    grad_input = (grad_middle + grad_in_norm).astype(jnp.bfloat16).reshape(images.shape)
    grad_vectors = jnp.stack(
        [
            grad_gain_a,
            grad_shift_a,
            grad_pbias,
            grad_gain_b,
            grad_shift_b,
            jnp.sum(grad_out, axis=0),
        ]
    )
    shares = (
        lax.psum_scatter(grad_qkv, "fsdp", scatter_dimension=0, tiled=True),
        lax.psum_scatter(grad_proj, "fsdp", scatter_dimension=0, tiled=True),
        lax.psum_scatter(grad_fc1, "fsdp", scatter_dimension=0, tiled=True),
        lax.psum_scatter(grad_fc2, "fsdp", scatter_dimension=1, tiled=True),
        lax.psum_scatter(grad_bias1, "fsdp", scatter_dimension=0, tiled=True),
        lax.psum_scatter(grad_vectors, "fsdp", scatter_dimension=1, tiled=True),
    )
    totals = (
        lax.psum(shares[0].astype(jnp.bfloat16), "dp").astype(jnp.float32),
        lax.psum(shares[1].astype(jnp.bfloat16), "dp").astype(jnp.float32),
        lax.psum(shares[2].astype(jnp.bfloat16), "dp").astype(jnp.float32),
        lax.psum(shares[3].astype(jnp.bfloat16), "dp").astype(jnp.float32),
        lax.psum(shares[4].astype(jnp.bfloat16), "dp").astype(jnp.float32),
        lax.psum(shares[5].astype(jnp.bfloat16), "dp").astype(jnp.float32),
    )
    slot_total = count_img * lax.axis_size("dp") * lax.axis_size("fsdp")
    grads = [total / slot_total for total in totals]
    firsts = (m_qkv, m_proj, m_fc1, m_fc2, m_bias1, m_vectors)
    seconds = (v_qkv, v_proj, v_fc1, v_fc2, v_bias1, v_vectors)
    group_range = jnp.arange(group_scales.shape[0])
    new_weights, new_firsts, new_seconds = ([], [], [])
    for place in range(6):
        flag = decay_flags[place].astype(jnp.float32)
        lr_scale = jnp.sum(jnp.where(group_range == group_ids[place], group_scales, 0.0))
        weight_n, first_n, second_n = adam_update(
            masters[place], grads[place], firsts[place], seconds[place], flag, lr_scale
        )
        new_weights.append(weight_n)
        new_firsts.append(first_n)
        new_seconds.append(second_n)
    return (
        out_block,
        grad_input,
        grads[0],
        grads[1],
        grads[2],
        grads[3],
        grads[4],
        grads[5],
        new_weights[0],
        new_weights[1],
        new_weights[2],
        new_weights[3],
        new_weights[4],
        new_weights[5],
        new_firsts[0],
        new_firsts[1],
        new_firsts[2],
        new_firsts[3],
        new_firsts[4],
        new_firsts[5],
        new_seconds[0],
        new_seconds[1],
        new_seconds[2],
        new_seconds[3],
        new_seconds[4],
        new_seconds[5],
    )


def solution(mesh):
    return jax.shard_map(
        local,
        mesh=mesh,
        in_specs=(
            P(("dp", "fsdp"), None, None),
            P(("dp", "fsdp"), None, None),
            P(("dp", "fsdp")),
            P("fsdp", None),
            P("fsdp", None),
            P("fsdp", None),
            P(None, "fsdp"),
            P("fsdp"),
            P(None, "fsdp"),
            P("fsdp", None),
            P("fsdp", None),
            P("fsdp", None),
            P(None, "fsdp"),
            P("fsdp"),
            P(None, "fsdp"),
            P("fsdp", None),
            P("fsdp", None),
            P("fsdp", None),
            P(None, "fsdp"),
            P("fsdp"),
            P(None, "fsdp"),
            P(),
            P(),
            P(),
        ),
        out_specs=(
            P(("dp", "fsdp"), None, None),
            P(("dp", "fsdp"), None, None),
            P("fsdp", None),
            P("fsdp", None),
            P("fsdp", None),
            P(None, "fsdp"),
            P("fsdp"),
            P(None, "fsdp"),
            P("fsdp", None),
            P("fsdp", None),
            P("fsdp", None),
            P(None, "fsdp"),
            P("fsdp"),
            P(None, "fsdp"),
            P("fsdp", None),
            P("fsdp", None),
            P("fsdp", None),
            P(None, "fsdp"),
            P("fsdp"),
            P(None, "fsdp"),
            P("fsdp", None),
            P("fsdp", None),
            P("fsdp", None),
            P(None, "fsdp"),
            P("fsdp"),
            P(None, "fsdp"),
        ),
        check_vma=False,
    )
```

profile of v0, /device:TPU:0, one launch (start us, length us, event | category | flops | bytes accessed | tf_op | source)
XLA Modules:
  0.0 921.4 jit_solution(10194459360705201848)
XLA Ops:
  15.9 14.4 %all-gather = bf16[8,48,6]{1,2,0:T(8,128)(2,1)S(1)} all-gather(bf16[1,48,6]{1,2,0:T(8,128)(2,1)S(1)} %convert_bitcast_fusion), channel_id=1, replica_groups=mesh['dp'=4,'fsdp'=8] {'fsdp'}, dimensions={0}, use_global_device_ids=true | all-gather | bytes 5184 | tf_op jit(solution)/shard_map/all_gather | solution.py:112
  31.0 7.5 multiply_reduce_fusion.8
  39.9 7.4 reshape.239
  47.3 16.1 %all_gather.24 = bf16[384,1152]{1,0:T(8,128)(2,1)S(1)} all-gather(bf16[48,1152]{1,0:T(8,128)(2,1)S(1)} %convert_element_type.165), channel_id=1, replica_groups=mesh['dp'=4,'fsdp'=8] {'fsdp'}, dimensions={0}, use_global_device_ids=true | all-gather | bytes 995328 | tf_op jit(solution)/shard_map/all_gather | solution.py:107
  64.3 12.3 %convolution_convert_fusion = bf16[4728,1152]{1,0:T(8,128)(2,1)} fusion(bf16[384,1152]{1,0:T(8,128)(2,1)S(1)} %all_gather.24, f32[4728,384]{1,0:T(8,128)} %reshape.239, f32[384]{0:T(512)S(1)} %get-tuple-element.281, f32[384]{0:T(512)S(1)} %get-tuple-element.282, f32[4728]{0:T(1024)S(1)} %rsqrt.25, f32[4728]{0:T(1024)S(1)} %div.159), kind=kOutput, calls=%fused_computation.83 | convolution fusion | flops 4197556224 | bytes 19081152 | tf_op jit(solution)/shard_map/dot_general | solution.py:138
  76.7 14.6 %copy.121 = bf16[4728,1152]{0,1:T(8,128)(2,1)} copy(bf16[4728,1152]{1,0:T(8,128)(2,1)} %convolution_convert_fusion) | data formatting | bytes 21786624 | tf_op jit(solution)/shard_map/convert_element_type | solution.py:138
  91.2 27.4 %reshape.240 = bf16[24,197,3,6,64]{1,0,4,3,2:T(8,128)(2,1)} reshape(bf16[4728,1152]{0,1:T(8,128)(2,1)} %copy.121) | data formatting | bytes 21786624 | tf_op jit(solution)/shard_map/reshape | solution.py:139
  134.0 46.9 %while.26 = (s32[]{:T(128)}, bf16[6,4,197,6,64]{2,1,0,4,3:T(4,128)(2,1)}, f32[6,4,6,197,1]{3,2,1,4,0:T(8,128)}, bf16[6,4,197,6,64]{2,4,3,1,0:T(8,128)(2,1)}, bf1...) while((s32[]{:T(128)}, bf16[6,4,197,6,64]{2,1,0,4,3:T(4,128)(2,1)}, ...), condition=%wide.region_5.6_spmd, body=%wide.region_2.5_spmd.sunk | while | flops 247123104 | bytes 15700877 | solution.py:143
  180.9 9.3 %reshape_reshape.6 = bf16[4728,384]{0,1:T(8,128)(2,1)} reshape(bf16[6,4,197,6,64]{2,1,0,4,3:T(4,128)(2,1)} %get-tuple-element.108) | data formatting | bytes 7262208 | tf_op jit(solution)/shard_map/reshape;reshape | solution.py:144
  190.2 14.3 %all_gather.25 = bf16[384,384]{1,0:T(8,128)(2,1)S(1)} all-gather(bf16[48,384]{1,0:T(8,128)(2,1)S(1)} %convert_element_type.167), channel_id=1, replica_groups=mesh['dp'=4,'fsdp'=8] {'fsdp'}, dimensions={0}, use_global_device_ids=true | all-gather | bytes 331776 | tf_op jit(solution)/shard_map/all_gather | solution.py:108
  204.4 7.2 fusion.136
  216.9 15.8 %all_gather.26 = bf16[384,1152]{1,0:T(8,128)(2,1)S(1)} all-gather(bf16[48,1152]{1,0:T(8,128)(2,1)S(1)} %convert_element_type.169), channel_id=1, replica_groups=mesh['dp'=4,'fsdp'=8] {'fsdp'}, dimensions={0}, use_global_device_ids=true | all-gather | bytes 995328 | tf_op jit(solution)/shard_map/all_gather | solution.py:109
  234.3 17.2 %all-reduce = bf16[1152]{0:T(1024)(128)(2,1)S(1)} all-reduce(bf16[1152]{0:T(1024)(128)(2,1)S(1)} %dynamic-update-slice), channel_id=1, replica_groups=mesh['dp'=4,'fsdp'=8] {'fsdp'}, use_global_device_ids=true, to_apply=%add | all-reduce | flops 1152 | bytes 4608
  260.7 7.3 reshape.242
  268.1 16.7 %all_gather.28 = bf16[1152,384]{0,1:T(8,128)(2,1)} all-gather(bf16[1152,48]{0,1:T(8,128)(2,1)S(1)} %convert_element_type.173), channel_id=1, replica_groups=mesh['dp'=4,'fsdp'=8] {'fsdp'}, dimensions={1}, use_global_device_ids=true | all-gather | bytes 995328 | tf_op jit(solution)/shard_map/all_gather | solution.py:110
  284.8 56.5 %multiply_convert_fusion.1 = (bf16[4728,1152]{1,0:T(8,128)(2,1)}, f32[4728,1152]{1,0:T(8,128)}, f32[4728,1152]{1,0:T(8,128)}) fusion(f32[1152]{0:T(1024)S(1)} %convert_element_type.171, bf16[384,1152]{1,0:T(8,128)(2,1)S(1)} %all_gather.26, f32[4728,384]{1,0:T(8,128)} %copy-done.1, f32[384]{0:T(512)S(1)} %get-tuple-element.278, ...), kind=kOutput, calls=%fused_computation.69 | convolution fusion | flops 4551588864 | bytes 62659008 | tf_op jit(solution)/shard_map/dot_general | solution.py:149
  341.3 27.4 %fusion.137 = (f32[1152]{0:T(1024)}, bf16[4728,1152]{1,0:T(8,128)(2,1)}) fusion(f32[4728,1152]{1,0:T(8,128)} %get-tuple-element.356, f32[4728,1152]{1,0:T(8,128)} %get-tuple-element.380, bf16[1152,384]{0,1:T(8,128)(2,1)S(1)} %copy-done.11, f32[4728,384]{1,0:T(8,128)} %reshape.242, f32[4728]{0:T(1024)S(1)} %copy-done.34), kind=kOutput, calls=%fused_computation.198 | convolution fusion | flops 4268361728 | bytes 62637024 | tf_op jit(solution)/shard_map/rd,fd->rf/dot_general | solution.py:173
  368.7 14.8 %multiply_reduce_fusion.3 = (f32[384]{0:T(512)S(1)}, f32[4728]{0:T(1024)S(1)}, f32[384]{0:T(512)S(1)}, f32[4728,384]{1,0:T(8,128)}) fusion(f32[4728,384]{1,0:T(8,128)} %copy-done.1, f32[4728]{0:T(1024)S(1)} %fusion.101, f32[4728]{0:T(1024)S(1)} %broadcast_multiply_fusion.1, f32[384]{0:T(512)S(1)} %get-tuple-element.279, ...), kind=kOutput, calls=%fused_computation.89 | convolution fusion | flops 4197550592 | bytes 26363808 | tf_op jit(solution)/shard_map/rf,df->rd/dot_general | solution.py:181
  383.5 10.1 %fusion.130 = (f32[4728]{0:T(1024)S(1)}, f32[4728,384]{1,0:T(8,128)}) fusion(f32[4728]{0:T(1024)S(1)} %multiply_multiply_fusion.6, f32[4728,384]{1,0:T(8,128)} %copy-done.1, f32[4728]{0:T(1024)S(1)} %broadcast_multiply_fusion.1, f32[4728]{0:T(1024)S(1)} %fusion.101, f32[4728,384]{1,0:T(8,128)} %get-tuple-element.381, f32[384]{0:T(512)S(1)} %get-tuple-element.279), kind=kLoop, calls=%fused_computation.192 | loop fusion | flops 12704136 | bytes 21863808 | tf_op jit(solution)/shard_map/transpose(jvp())/reduce_sum | solution.py:22
  407.1 12.0 %reshape.256 = bf16[6,4,197,6,64]{4,3,2,1,0:T(8,128)(2,1)} reshape(bf16[4728,384]{1,0:T(8,128)(2,1)} %convolution_convert_fusion.1) | data formatting | bytes 7262208 | tf_op jit(solution)/shard_map/reshape;reshape | solution.py:129
  419.1 11.5 %copy.130 = bf16[6,4,197,6,64]{2,4,3,1,0:T(8,128)(2,1)} copy(bf16[6,4,197,6,64]{4,3,2,1,0:T(8,128)(2,1)} %reshape.256) | data formatting | bytes 7262208 | tf_op jit(solution)/shard_map/while | solution.py:194
  430.5 207.5 %while.27 = (s32[]{:T(128)}, bf16[6,4,197,6,64]{2,4,3,1,0:T(8,128)(2,1)}, bf16[6,4,197,6,64]{2,4,3,1,0:T(8,128)(2,1)}, bf16[6,4,197,6,64]{2,4,3,1,0:T(8,128)(2,1...) while((s32[]{:T(128)}, ...), condition=%wide.region_12.13_spmd, body=%wide.region_10.12_spmd.sunk | while | flops 615675776 | bytes 62104776 | solution.py:194
  440.3 10.2 %bitcast_dynamic-update-slice_fusion.10 = bf16[6,4,197,6,64]{2,4,3,1,0:T(8,128)(2,1)} fusion(bf16[6,4,197,6,64]{2,4,3,1,0:T(8,128)(2,1)} %get-tuple-element.520, s32[]{:T(128)} %get-tuple-element.518, f32[4,6,197,197]{2,3,1,0:T(8,128)} %fusion.185, f32[4,6,197,197]{2,3,1,0:T(8,128)} %fusion.186, f32[4,6,197]{2,1,0:T(8,128)S(1)} %dynamic-slice_bitcast_fusion.2, ...), kind=kOutput, calls=%fused_computation.35.clone.1 | convolution fusion | flops 127608912 | bytes 22086656 | tf_op jit(solution)/shard_map/while/body/eval_jaxpr/bhqk,bqhd->bkhd/dot_general | solution.py:62
  450.5 10.2 %bitcast_dynamic-update-slice_fusion.9 = bf16[6,4,197,6,64]{2,4,3,1,0:T(8,128)(2,1)} fusion(bf16[6,4,197,6,64]{2,4,3,1,0:T(8,128)(2,1)} %get-tuple-element.519, s32[]{:T(128)} %get-tuple-element.518, f32[4,6,197,197]{2,3,1,0:T(8,128)} %fusion.185, f32[4,6,197,197]{2,3,1,0:T(8,128)} %fusion.186, f32[4,6,197]{2,1,0:T(8,128)S(1)} %dynamic-slice_bitcast_fusion.2, ...), kind=kOutput, calls=%fused_computation.36.clone.1 | convolution fusion | flops 127608912 | bytes 22086656 | tf_op jit(solution)/shard_map/while/body/eval_jaxpr/bhqk,bkhd->bqhd/dot_general | solution.py:59
  474.8 10.2 %bitcast_dynamic-update-slice_fusion.10 = bf16[6,4,197,6,64]{2,4,3,1,0:T(8,128)(2,1)} fusion(bf16[6,4,197,6,64]{2,4,3,1,0:T(8,128)(2,1)} %get-tuple-element.520, s32[]{:T(128)} %get-tuple-element.518, f32[4,6,197,197]{2,3,1,0:T(8,128)} %fusion.185, f32[4,6,197,197]{2,3,1,0:T(8,128)} %fusion.186, f32[4,6,197]{2,1,0:T(8,128)S(1)} %dynamic-slice_bitcast_fusion.2, ...), kind=kOutput, calls=%fused_computation.35.clone.1 | convolution fusion | flops 127608912 | bytes 22086656 | tf_op jit(solution)/shard_map/while/body/eval_jaxpr/bhqk,bqhd->bkhd/dot_general | solution.py:62
  485.0 10.1 %bitcast_dynamic-update-slice_fusion.9 = bf16[6,4,197,6,64]{2,4,3,1,0:T(8,128)(2,1)} fusion(bf16[6,4,197,6,64]{2,4,3,1,0:T(8,128)(2,1)} %get-tuple-element.519, s32[]{:T(128)} %get-tuple-element.518, f32[4,6,197,197]{2,3,1,0:T(8,128)} %fusion.185, f32[4,6,197,197]{2,3,1,0:T(8,128)} %fusion.186, f32[4,6,197]{2,1,0:T(8,128)S(1)} %dynamic-slice_bitcast_fusion.2, ...), kind=kOutput, calls=%fused_computation.36.clone.1 | convolution fusion | flops 127608912 | bytes 22086656 | tf_op jit(solution)/shard_map/while/body/eval_jaxpr/bhqk,bkhd->bqhd/dot_general | solution.py:59
  509.3 10.1 %bitcast_dynamic-update-slice_fusion.10 = bf16[6,4,197,6,64]{2,4,3,1,0:T(8,128)(2,1)} fusion(bf16[6,4,197,6,64]{2,4,3,1,0:T(8,128)(2,1)} %get-tuple-element.520, s32[]{:T(128)} %get-tuple-element.518, f32[4,6,197,197]{2,3,1,0:T(8,128)} %fusion.185, f32[4,6,197,197]{2,3,1,0:T(8,128)} %fusion.186, f32[4,6,197]{2,1,0:T(8,128)S(1)} %dynamic-slice_bitcast_fusion.2, ...), kind=kOutput, calls=%fused_computation.35.clone.1 | convolution fusion | flops 127608912 | bytes 22086656 | tf_op jit(solution)/shard_map/while/body/eval_jaxpr/bhqk,bqhd->bkhd/dot_general | solution.py:62
  519.4 10.2 %bitcast_dynamic-update-slice_fusion.9 = bf16[6,4,197,6,64]{2,4,3,1,0:T(8,128)(2,1)} fusion(bf16[6,4,197,6,64]{2,4,3,1,0:T(8,128)(2,1)} %get-tuple-element.519, s32[]{:T(128)} %get-tuple-element.518, f32[4,6,197,197]{2,3,1,0:T(8,128)} %fusion.185, f32[4,6,197,197]{2,3,1,0:T(8,128)} %fusion.186, f32[4,6,197]{2,1,0:T(8,128)S(1)} %dynamic-slice_bitcast_fusion.2, ...), kind=kOutput, calls=%fused_computation.36.clone.1 | convolution fusion | flops 127608912 | bytes 22086656 | tf_op jit(solution)/shard_map/while/body/eval_jaxpr/bhqk,bkhd->bqhd/dot_general | solution.py:59
  543.8 10.2 %bitcast_dynamic-update-slice_fusion.10 = bf16[6,4,197,6,64]{2,4,3,1,0:T(8,128)(2,1)} fusion(bf16[6,4,197,6,64]{2,4,3,1,0:T(8,128)(2,1)} %get-tuple-element.520, s32[]{:T(128)} %get-tuple-element.518, f32[4,6,197,197]{2,3,1,0:T(8,128)} %fusion.185, f32[4,6,197,197]{2,3,1,0:T(8,128)} %fusion.186, f32[4,6,197]{2,1,0:T(8,128)S(1)} %dynamic-slice_bitcast_fusion.2, ...), kind=kOutput, calls=%fused_computation.35.clone.1 | convolution fusion | flops 127608912 | bytes 22086656 | tf_op jit(solution)/shard_map/while/body/eval_jaxpr/bhqk,bqhd->bkhd/dot_general | solution.py:62
  554.0 10.2 %bitcast_dynamic-update-slice_fusion.9 = bf16[6,4,197,6,64]{2,4,3,1,0:T(8,128)(2,1)} fusion(bf16[6,4,197,6,64]{2,4,3,1,0:T(8,128)(2,1)} %get-tuple-element.519, s32[]{:T(128)} %get-tuple-element.518, f32[4,6,197,197]{2,3,1,0:T(8,128)} %fusion.185, f32[4,6,197,197]{2,3,1,0:T(8,128)} %fusion.186, f32[4,6,197]{2,1,0:T(8,128)S(1)} %dynamic-slice_bitcast_fusion.2, ...), kind=kOutput, calls=%fused_computation.36.clone.1 | convolution fusion | flops 127608912 | bytes 22086656 | tf_op jit(solution)/shard_map/while/body/eval_jaxpr/bhqk,bkhd->bqhd/dot_general | solution.py:59
  578.3 10.1 %bitcast_dynamic-update-slice_fusion.10 = bf16[6,4,197,6,64]{2,4,3,1,0:T(8,128)(2,1)} fusion(bf16[6,4,197,6,64]{2,4,3,1,0:T(8,128)(2,1)} %get-tuple-element.520, s32[]{:T(128)} %get-tuple-element.518, f32[4,6,197,197]{2,3,1,0:T(8,128)} %fusion.185, f32[4,6,197,197]{2,3,1,0:T(8,128)} %fusion.186, f32[4,6,197]{2,1,0:T(8,128)S(1)} %dynamic-slice_bitcast_fusion.2, ...), kind=kOutput, calls=%fused_computation.35.clone.1 | convolution fusion | flops 127608912 | bytes 22086656 | tf_op jit(solution)/shard_map/while/body/eval_jaxpr/bhqk,bqhd->bkhd/dot_general | solution.py:62
  588.4 10.2 %bitcast_dynamic-update-slice_fusion.9 = bf16[6,4,197,6,64]{2,4,3,1,0:T(8,128)(2,1)} fusion(bf16[6,4,197,6,64]{2,4,3,1,0:T(8,128)(2,1)} %get-tuple-element.519, s32[]{:T(128)} %get-tuple-element.518, f32[4,6,197,197]{2,3,1,0:T(8,128)} %fusion.185, f32[4,6,197,197]{2,3,1,0:T(8,128)} %fusion.186, f32[4,6,197]{2,1,0:T(8,128)S(1)} %dynamic-slice_bitcast_fusion.2, ...), kind=kOutput, calls=%fused_computation.36.clone.1 | convolution fusion | flops 127608912 | bytes 22086656 | tf_op jit(solution)/shard_map/while/body/eval_jaxpr/bhqk,bkhd->bqhd/dot_general | solution.py:59
  612.7 10.2 %bitcast_dynamic-update-slice_fusion.10 = bf16[6,4,197,6,64]{2,4,3,1,0:T(8,128)(2,1)} fusion(bf16[6,4,197,6,64]{2,4,3,1,0:T(8,128)(2,1)} %get-tuple-element.520, s32[]{:T(128)} %get-tuple-element.518, f32[4,6,197,197]{2,3,1,0:T(8,128)} %fusion.185, f32[4,6,197,197]{2,3,1,0:T(8,128)} %fusion.186, f32[4,6,197]{2,1,0:T(8,128)S(1)} %dynamic-slice_bitcast_fusion.2, ...), kind=kOutput, calls=%fused_computation.35.clone.1 | convolution fusion | flops 127608912 | bytes 22086656 | tf_op jit(solution)/shard_map/while/body/eval_jaxpr/bhqk,bqhd->bkhd/dot_general | solution.py:62
  622.9 10.2 %bitcast_dynamic-update-slice_fusion.9 = bf16[6,4,197,6,64]{2,4,3,1,0:T(8,128)(2,1)} fusion(bf16[6,4,197,6,64]{2,4,3,1,0:T(8,128)(2,1)} %get-tuple-element.519, s32[]{:T(128)} %get-tuple-element.518, f32[4,6,197,197]{2,3,1,0:T(8,128)} %fusion.185, f32[4,6,197,197]{2,3,1,0:T(8,128)} %fusion.186, f32[4,6,197]{2,1,0:T(8,128)S(1)} %dynamic-slice_bitcast_fusion.2, ...), kind=kOutput, calls=%fused_computation.36.clone.1 | convolution fusion | flops 127608912 | bytes 22086656 | tf_op jit(solution)/shard_map/while/body/eval_jaxpr/bhqk,bkhd->bqhd/dot_general | solution.py:59
  649.2 6.7 maximum_convert_fusion
  655.9 22.0 %convert_element_type.182 = bf16[4728,1152]{0,1:T(8,128)(2,1)} reshape(bf16[24,197,3,6,64]{1,0,4,3,2:T(8,128)(2,1)} %maximum_convert_fusion) | data formatting | bytes 21786624 | tf_op jit(solution)/shard_map/convert_element_type | solution.py:200
  678.0 16.4 %multiply_reduce_fusion.4 = (f32[384]{0:T(512)S(1)}, f32[4728]{0:T(1024)S(1)}, f32[384]{0:T(512)S(1)}, f32[4728,384]{1,0:T(8,128)}) fusion(f32[4728,384]{1,0:T(8,128)} %reshape.239, f32[4728]{0:T(1024)S(1)} %copy-done.33, f32[4728]{0:T(1024)S(1)} %copy-done.31, f32[384]{0:T(512)S(1)} %copy-done.38, bf16[4728,1152]{0,1:T(8,128)(2,1)} %convert_element_type.182, ...), kind=kOutput, calls=%fused_computation.90 | convolution fusion | flops 4197550592 | bytes 26363808 | tf_op jit(solution)/shard_map/rf,df->rd/dot_general | solution.py:202
  695.4 7.1 fusion.86
  702.6 12.8 %fusion.78 = f32[384,1152]{1,0:T(8,128)} fusion(bf16[4728,1152]{1,0:T(8,128)(2,1)} %get-tuple-element.384, f32[4728,384]{1,0:T(8,128)} %copy-done.1, f32[384]{0:T(512)S(1)} %copy-done.52, f32[384]{0:T(512)S(1)} %get-tuple-element.279, f32[4728]{0:T(1024)S(1)} %fusion.101, f32[4728]{0:T(1024)S(1)} %broadcast_multiply_fusion.1), kind=kOutput, calls=%fused_computation.103 | convolution fusion | flops 4192109568 | bytes 19965888 | tf_op jit(solution)/shard_map/rd,rf->df/dot_general | solution.py:178
  727.0 11.5 %fusion.138 = f32[384,1152]{1,0:T(8,128)} fusion(bf16[4728,384]{1,0:T(8,128)(2,1)} %convert_element_type.185, bf16[4728,1152]{0,1:T(8,128)(2,1)} %convert_element_type.182), kind=kOutput, calls=%fused_computation.199 | convolution fusion | flops 4183031808 | bytes 16293888 | tf_op jit(solution)/shard_map/rd,rf->df/dot_general | solution.py:201
  738.6 12.6 %fusion.115 = f32[1152,384]{0,1:T(8,128)} fusion(bf16[4728,1152]{1,0:T(8,128)(2,1)} %get-tuple-element.355, f32[4728,384]{1,0:T(8,128)} %reshape.242, f32[4728]{0:T(1024)S(1)} %copy-done.34), kind=kOutput, calls=%fused_computation.189 | convolution fusion | flops 4186662912 | bytes 19943904 | tf_op jit(solution)/shard_map/rf,rd->fd/dot_general | solution.py:172
  765.1 10.1 %fusion.129 = (f32[4728]{0:T(1024)S(1)}, f32[4728,384]{1,0:T(8,128)}) fusion(f32[4728]{0:T(1024)S(1)} %multiply_multiply_fusion.5, f32[4728,384]{1,0:T(8,128)} %reshape.239, f32[4728]{0:T(1024)S(1)} %copy-done.31, f32[4728]{0:T(1024)S(1)} %copy-done.33, f32[4728,384]{1,0:T(8,128)} %get-tuple-element.382, f32[384]{0:T(512)S(1)} %copy-done.38), kind=kLoop, calls=%fused_computation.191 | loop fusion | flops 12704136 | bytes 21863808 | tf_op jit(solution)/shard_map/transpose(jvp())/reduce_sum | solution.py:22
  775.2 7.9 add_convert_fusion.1
  792.8 12.3 %multiply_convert_fusion.2 = bf16[4728,384]{1,0:T(8,128)(2,1)} fusion(f32[4728,384]{1,0:T(8,128)} %copy-done.1, bf16[4728,1152]{1,0:T(8,128)(2,1)} %get-tuple-element.355, bf16[1152,384]{0,1:T(8,128)(2,1)S(1)} %copy-done.12, f32[4728]{0:T(1024)S(1)} %copy-done.34, f32[384]{0:T(512)S(1)} %copy-done.50), kind=kOutput, calls=%fused_computation.96 | convolution fusion | flops 4190294016 | bytes 22691808 | tf_op jit(solution)/shard_map/dot_general | solution.py:152
  815.7 14.8 %all-reduce.1 = bf16[1152]{0:T(1024)(128)(2,1)S(1)} all-reduce(f32[1152]{0:T(1024)S(1)} %copy-done.46), channel_id=6, replica_groups=mesh['dp'=4,'fsdp'=8] {'fsdp'}, use_global_device_ids=true, to_apply=%region_24.25.clone | all-reduce | flops 1152 | bytes 6912
  832.3 16.6 %all-reduce.2 = (bf16[48,384]{1,0:T(8,128)(2,1)S(1)}, bf16[144]{0:T(256)(128)(2,1)S(1)}, bf16[6,48]{1,0:T(8,128)(2,1)S(1)}) all-reduce(bf16[48,384]{1,0:T(8,128)(2,1)S(1)} %convert_element_type.188, bf16[144]{0:T(256)(128)(2,1)S(1)} %dynamic-slice.4, bf16[6,48]{1,0:T(8,128)(2,1)S(1)} %copy.146), channel_id=1, replica_groups=mesh['dp'=4,'fsdp'=8] {'dp'}, use_global_device_ids=true, to_apply=%region_18.19 | all-reduce | flops 18864 | bytes 75456 | tf_op jit(solution)/shard_map/psum | solution.py:228
  852.8 9.8 %reduce-scatter.14.cloned.1.call-done = f32[1152,48]{0,1:T(8,128)} async-done(((f32[1152,384]{0,1:T(8,128)}), f32[1152,48]{0,1:T(8,128)}) %reduce-scatter.14.cloned.1.call-update) | async-done | bytes 221200 | tf_op jit(solution)/shard_map/reduce_scatter | solution.py:222
  865.6 44.3 %all-reduce.6.cloned.1.call-done = (bf16[48,1152]{1,0:T(8,128)(2,1)}, bf16[48,1152]{1,0:T(8,128)(2,1)}, bf16[1152,48]{0,1:T(8,128)(2,1)}) async-done(((bf16[48,1152]{1,0:T(8,128)(2,1)}, bf16[48,1152]{1,0:T(8,128)(2,1)}, bf16[1152,48]{0,1:T(8,128)(2,1)}), (bf16[48,1152]{1,0:T(8,128)(2,1)}, bf16[48,1152]{1,0:T(8,128)(2,1)}, bf16[1152,48]{0,1:T(8,128)(2,1)})) %all-reduce.6.cloned.1.call-update) | async-done | bytes 331792 | tf_op jit(solution)/shard_map/psum | solution.py:227
  (275 shorter events, 248.7 us)
Async XLA Ops:
  7.2 823.4 %reduce-scatter.16.cloned.1.call-start = ((), (), s32[]{:S(2)}) async-start(), calls=%async_computation.9 | async-start | bytes 221184
  15.7 31.6 %copy-start.5 = (f32[24,197]{0,1:T(8,128)}, f32[24,197]{0,1:T(8,128)S(1)}, u32[]{:S(2)}) copy-start(f32[24,197]{0,1:T(8,128)S(1)} %copy.118) | copy-start | bytes 56740
  15.8 47.7 %copy-start.30 = (f32[4728]{0:T(1024)}, f32[4728]{0:T(1024)S(1)}, u32[]{:S(2)}) copy-start(f32[4728]{0:T(1024)S(1)} %div.159) | copy-start | bytes 56740
  31.0 32.5 %copy-start.37 = (f32[384]{0:T(512)}, f32[384]{0:T(512)S(1)}, u32[]{:S(2)}) copy-start(f32[384]{0:T(512)S(1)} %get-tuple-element.282) | copy-start | bytes 4612
  31.0 32.5 %copy-start.44 = (f32[384]{0:T(512)}, f32[384]{0:T(512)S(1)}, u32[]{:S(2)}) copy-start(f32[384]{0:T(512)S(1)} %get-tuple-element.281) | copy-start | bytes 4612
  31.0 253.8 %copy-start.51 = (f32[384]{0:T(512)}, f32[384]{0:T(512)S(1)}, u32[]{:S(2)}) copy-start(f32[384]{0:T(512)S(1)} %get-tuple-element.278) | copy-start | bytes 4612
  39.9 23.5 %copy-start.32 = (f32[4728]{0:T(1024)}, f32[4728]{0:T(1024)S(1)}, u32[]{:S(2)}) copy-start(f32[4728]{0:T(1024)S(1)} %rsqrt.25) | copy-start | bytes 56740
  211.7 21.0 %copy-start.53 = (f32[144]{0:T(256)S(1)}, f32[144]{0:T(256)}, u32[]{:S(2)}) copy-start(f32[144]{0:T(256)} %param.35) | copy-start | bytes 1732
  211.7 21.0 %copy-start.49 = (u32[32]{0:T(128)S(1)}, u32[32]{0:T(128)}, u32[]{:S(2)}) copy-start(u32[32]{0:T(128)} %constant.214) | copy-start | bytes 388
  284.8 56.5 %copy-start.11 = (bf16[1152,384]{0,1:T(8,128)(2,1)S(1)}, bf16[1152,384]{0,1:T(8,128)(2,1)}, u32[]{:S(2)}) copy-start(bf16[1152,384]{0,1:T(8,128)(2,1)} %all_gather.28) | copy-start | bytes 2654212
  284.8 56.5 %copy-start.34 = (f32[4728]{0:T(1024)S(1)}, f32[4728]{0:T(1024)}, u32[]{:S(2)}) copy-start(f32[4728]{0:T(1024)} %mul.482) | copy-start | bytes 56740
  368.7 14.8 %copy-start.26 = (f32[4728]{0:T(1024)S(1)}, f32[4728]{0:T(1024)}, u32[]{:S(2)}) copy-start(f32[4728]{0:T(1024)} %copy-done.25) | copy-start | bytes 56740
  655.9 22.0 %copy-start.14 = (bf16[384,1152]{1,0:T(8,128)(2,1)S(1)}, bf16[384,1152]{1,0:T(8,128)(2,1)}, u32[]{:S(2)}) copy-start(bf16[384,1152]{1,0:T(8,128)(2,1)} %copy-done.13) | copy-start | bytes 2654212
  655.9 22.0 %copy-start.31 = (f32[4728]{0:T(1024)S(1)}, f32[4728]{0:T(1024)}, u32[]{:S(2)}) copy-start(f32[4728]{0:T(1024)} %copy-done.30) | copy-start | bytes 56740
  655.9 22.0 %copy-start.33 = (f32[4728]{0:T(1024)S(1)}, f32[4728]{0:T(1024)}, u32[]{:S(2)}) copy-start(f32[4728]{0:T(1024)} %copy-done.32) | copy-start | bytes 56740
  655.9 22.0 %copy-start.38 = (f32[384]{0:T(512)S(1)}, f32[384]{0:T(512)}, u32[]{:S(2)}) copy-start(f32[384]{0:T(512)} %copy-done.37) | copy-start | bytes 4612
  678.0 16.5 %copy-start.43 = (f32[384]{0:T(512)S(1)}, f32[384]{0:T(512)}, u32[]{:S(2)}) copy-start(f32[384]{0:T(512)} %multiply_reduce_fusion.2) | copy-start | bytes 4612
  695.3 136.1 %reduce-scatter.10.cloned.1.call-start = ((), (), s32[]{:S(2)}) async-start(), calls=%async_computation.6 | async-start | bytes 663552 | tf_op jit(solution)/shard_map/reduce_scatter | solution.py:220
  702.5 13.2 %copy-start.29 = (f32[24,197]{1,0:T(8,128)S(1)}, f32[24,197]{1,0:T(8,128)}, u32[]{:S(2)}) copy-start(f32[24,197]{1,0:T(8,128)} %get-tuple-element.362) | copy-start | bytes 56740
  702.5 13.3 %copy-start.6 = (f32[24,197]{0,1:T(8,128)S(1)}, f32[24,197]{0,1:T(8,128)}, u32[]{:S(2)}) copy-start(f32[24,197]{0,1:T(8,128)} %copy-done.5) | copy-start | bytes 56740
  702.5 13.3 %copy-start.45 = (f32[384]{0:T(512)S(1)}, f32[384]{0:T(512)}, u32[]{:S(2)}) copy-start(f32[384]{0:T(512)} %copy-done.44) | copy-start | bytes 4612
  702.5 147.1 %reduce-scatter.12.cloned.1.call-start = ((), (), s32[]{:S(2)}) async-start(), calls=%async_computation.7 | async-start | bytes 1990656 | tf_op jit(solution)/shard_map/reduce_scatter | solution.py:221
  715.4 135.8 %reduce-scatter.8.cloned.1.call-start = ((), (), s32[]{:S(2)}) async-start(), calls=%async_computation.5 | async-start | bytes 1990656 | tf_op jit(solution)/shard_map/reduce_scatter | solution.py:219
  738.5 124.1 %reduce-scatter.14.cloned.1.call-start = ((), (), s32[]{:S(2)}) async-start(), calls=%async_computation.8 | async-start | bytes 1990656 | tf_op jit(solution)/shard_map/reduce_scatter | solution.py:222
  738.5 13.0 %copy-start.39 = (s32[6]{0:T(128)S(1)}, s32[6]{0:T(128)}, u32[]{:S(2)}) copy-start(s32[6]{0:T(128)} %param.50) | copy-start | bytes 76
  738.5 13.6 %copy-start.40 = (s32[6]{0:T(128)S(1)}, s32[6]{0:T(128)}, u32[]{:S(2)}) copy-start(s32[6]{0:T(128)} %param.49) | copy-start | bytes 76
  738.6 14.8 %copy-start.57 = (f32[3]{0:T(128)S(1)}, f32[3]{0:T(128)}, u32[]{:S(2)}) copy-start(f32[3]{0:T(128)} %param.51) | copy-start | bytes 40
  738.6 26.5 %copy-start.28 = (f32[4728]{0:T(1024)S(1)}, f32[4728]{0:T(1024)}, u32[]{:S(2)}) copy-start(f32[4728]{0:T(1024)} %copy-done.27) | copy-start | bytes 56740
  751.2 158.6 %all-reduce.6.cloned.1.call-start = ((), (), s32[]{:S(2)}) async-start(), calls=%async_computation.10 | async-start | bytes 663552 | tf_op jit(solution)/shard_map/psum | solution.py:227
  805.0 10.7 %copy-start.46 = (f32[1152]{0:T(1024)S(1)}, f32[1152]{0:T(1024)}, u32[]{:S(2)}) copy-start(f32[1152]{0:T(1024)} %get-tuple-element.383) | copy-start | bytes 13828
  805.0 43.9 %copy-start.42 = (f32[6,48]{1,0:T(8,128)S(1)}, f32[6,48]{1,0:T(8,128)}, u32[]{:S(2)}) copy-start(f32[6,48]{1,0:T(8,128)} %param.36) | copy-start | bytes 3460
  805.0 43.9 %copy-start.47 = (f32[6,48]{1,0:T(8,128)S(1)}, f32[6,48]{1,0:T(8,128)}, u32[]{:S(2)}) copy-start(f32[6,48]{1,0:T(8,128)} %param.42) | copy-start | bytes 3460
  805.0 43.9 %copy-start.48 = (f32[6,48]{1,0:T(8,128)S(1)}, f32[6,48]{1,0:T(8,128)}, u32[]{:S(2)}) copy-start(f32[6,48]{1,0:T(8,128)} %param.48) | copy-start | bytes 3460
  805.0 59.1 %copy-start.54 = (f32[144]{0:T(256)S(1)}, f32[144]{0:T(256)}, u32[]{:S(2)}) copy-start(f32[144]{0:T(256)} %param.35) | copy-start | bytes 1732
  805.1 59.1 %copy-start.55 = (f32[144]{0:T(256)S(1)}, f32[144]{0:T(256)}, u32[]{:S(2)}) copy-start(f32[144]{0:T(256)} %param.41) | copy-start | bytes 1732
  805.1 59.1 %copy-start.56 = (f32[144]{0:T(256)S(1)}, f32[144]{0:T(256)}, u32[]{:S(2)}) copy-start(f32[144]{0:T(256)} %param.47) | copy-start | bytes 1732
  805.1 59.7 %copy-start.18 = (f32[48,384]{1,0:T(8,128)S(1)}, f32[48,384]{1,0:T(8,128)}, u32[]{:S(2)}) copy-start(f32[48,384]{1,0:T(8,128)} %param.32) | copy-start | bytes 221188
  805.1 59.7 %copy-start.35 = (f32[48,384]{1,0:T(8,128)S(1)}, f32[48,384]{1,0:T(8,128)}, u32[]{:S(2)}) copy-start(f32[48,384]{1,0:T(8,128)} %param.38) | copy-start | bytes 221188
  805.1 59.7 %copy-start.36 = (f32[48,384]{1,0:T(8,128)S(1)}, f32[48,384]{1,0:T(8,128)}, u32[]{:S(2)}) copy-start(f32[48,384]{1,0:T(8,128)} %param.44) | copy-start | bytes 221188
  805.1 104.7 %copy-start.16 = (f32[1152,48]{0,1:T(8,128)S(1)}, f32[1152,48]{0,1:T(8,128)}, u32[]{:S(2)}) copy-start(f32[1152,48]{0,1:T(8,128)} %param.34) | copy-start | bytes 663556
  805.1 104.7 %copy-start.23 = (f32[1152,48]{0,1:T(8,128)S(1)}, f32[1152,48]{0,1:T(8,128)}, u32[]{:S(2)}) copy-start(f32[1152,48]{0,1:T(8,128)} %param.40) | copy-start | bytes 663556
  805.1 104.7 %copy-start.24 = (f32[1152,48]{0,1:T(8,128)S(1)}, f32[1152,48]{0,1:T(8,128)}, u32[]{:S(2)}) copy-start(f32[1152,48]{0,1:T(8,128)} %param.46) | copy-start | bytes 663556
  810.6 101.2 %copy-start.8 = (f32[48,1152]{1,0:T(8,128)S(1)}, f32[48,1152]{1,0:T(8,128)}, u32[]{:S(2)}) copy-start(f32[48,1152]{1,0:T(8,128)} %param.31) | copy-start | bytes 663556
  810.6 101.2 %copy-start.10 = (f32[48,1152]{1,0:T(8,128)S(1)}, f32[48,1152]{1,0:T(8,128)}, u32[]{:S(2)}) copy-start(f32[48,1152]{1,0:T(8,128)} %param.33) | copy-start | bytes 663556
  810.6 101.2 %copy-start.19 = (f32[48,1152]{1,0:T(8,128)S(1)}, f32[48,1152]{1,0:T(8,128)}, u32[]{:S(2)}) copy-start(f32[48,1152]{1,0:T(8,128)} %param.39) | copy-start | bytes 663556
  810.6 101.2 %copy-start.20 = (f32[48,1152]{1,0:T(8,128)S(1)}, f32[48,1152]{1,0:T(8,128)}, u32[]{:S(2)}) copy-start(f32[48,1152]{1,0:T(8,128)} %param.45) | copy-start | bytes 663556
  810.6 101.2 %copy-start.21 = (f32[48,1152]{1,0:T(8,128)S(1)}, f32[48,1152]{1,0:T(8,128)}, u32[]{:S(2)}) copy-start(f32[48,1152]{1,0:T(8,128)} %param.43) | copy-start | bytes 663556
  810.6 101.2 %copy-start.22 = (f32[48,1152]{1,0:T(8,128)S(1)}, f32[48,1152]{1,0:T(8,128)}, u32[]{:S(2)}) copy-start(f32[48,1152]{1,0:T(8,128)} %param.37) | copy-start | bytes 663556
  (20 other events, 118.7 us)
Sparse Core Ops, SparseCore 0:
  695.5 29.1 reduce-scatter.15
  727.0 29.1 reduce-scatter.9
  758.6 33.2 reduce-scatter.11
  794.2 32.9 reduce-scatter.7
  829.5 33.0 reduce-scatter.13
  867.2 42.6 all-reduce.5
where the time goes:
time: 930 us; the launch traced here: 921 us
  matrix products  425 us (46%)
  local copies, waits for them, and re-layouts  204 us (22%)
  blocking collectives  126 us (14%)
  other arithmetic  85.5 us (9%)
  waiting for transfers between devices  54.1 us (6%)
  between operations  25.3 us (3%)
    dot_general x6, matrix products, attend_back(): jnp.einsum('bhqk,bkhd->bqhd', grad_scores, keys_in, preferred_element_typ...  61 us
    dot_general x6, matrix products, attend_back(): jnp.einsum('bhqk,bqhd->bkhd', grad_scores, queries, preferred_element_typ...  61 us
    dot_general x1, matrix products, local(): jnp.dot(normed_b, fc1_weight, preferred_element_type=jnp.float32) + fc1_bias  56.5 us
    psum x1, waiting for transfers between devices, local(): lax.psum(shares[0].astype(jnp.bfloat16), 'dp').astype(jnp.float32)  44.3 us
    unnamed x2, blocking collectives  32 us
    dot_general x1, matrix products, local(): jnp.einsum('rd,fd->rf', grad_low, fc2_back, preferred_element_type=jnp.fl...  27.4 us
    reshape x1, local copies, waits for them, and re-layouts, local(): packed = packed.reshape(count_img, seq_len, 3, head_count, head_size)  27.4 us
    dot_general x6, matrix products, attend_back(): jnp.einsum('bhqk,bqhd->bkhd', probs.astype(jnp.bfloat16), grad_mixed, pre...  27.3 us
  transfers between devices with their start and end apart: 6, of which 2 were waited for; matrix products, arithmetic and copies ran while one was open for 13% of the time, Pallas kernels for 0%

commit v1 on v0

v1 whole, which is shorter than its diff:
```python
import functools
import math

import jax
import jax.numpy as jnp
from jax import lax
from jax.experimental import pallas as pl
from jax.experimental.pallas import tpu as pltpu
from jax.sharding import PartitionSpec as P

BF=jnp.bfloat16; F32=jnp.float32
EPS=1e-6
HD=64
def rup(n,m): return (n+m-1)//m*m
def dot(a,b,ca=1,cb=0):
    return lax.dot_general(a,b,(((ca,),(cb,)),((),())),preferred_element_type=F32)
def ln_hat(x):
    c=x-jnp.mean(x,axis=-1,keepdims=True)
    r=lax.rsqrt(jnp.mean(c*c,axis=-1,keepdims=True)+EPS)
    return c*r,r
VM=pltpu.CompilerParams(vmem_limit_bytes=56<<20)

def k1_body(SEQ,SP,D,IB,x_ref,w_ref,vec_ref,qkv_ref,o_ref,l_ref,a_scr):
    H=D//HD
    @pl.when(pl.program_id(0)==0)
    def _():
        a_scr[...]=jnp.zeros_like(a_scr)
    g=vec_ref[0:1,:]; e=vec_ref[1:2,:]
    for i in range(IB):
        x=x_ref[i].astype(F32)
        xh,_=ln_hat(x)
        a_scr[i*SP:i*SP+SEQ,:]=(xh*g+e).astype(BF)
    for t in range(3):
        y=dot(a_scr[...],w_ref[:,t*D:(t+1)*D])
        if t==0: y=y*(HD**-0.5)
        qkv_ref[:,:,t*D:(t+1)*D]=y.astype(BF).reshape(IB,SP,D)
    for i in range(IB):
        for h in range(0,H,2):
            outs=[]
            for j in range(2):
                lo=(h+j)*HD
                q=qkv_ref[i,:,lo:lo+HD]
                k=qkv_ref[i,0:SEQ,D+lo:D+lo+HD]
                v=qkv_ref[i,0:SEQ,2*D+lo:2*D+lo+HD]
                s=dot(k,q,1,1)
                m=jnp.max(s,axis=0,keepdims=True)
                p=jnp.exp(s-m)
                l=jnp.sum(p,axis=0,keepdims=True)
                l_ref[i,h+j:h+j+1,:]=m+jnp.log(l)
                pb=(p*(1.0/l)).astype(BF)
                outs.append(dot(pb,v,0,0))
            o_ref[i,:,h*HD:(h+2)*HD]=jnp.concatenate(outs,axis=1).astype(BF)

def k1(images,w,vec,IB=2):
    N,SEQ,D=images.shape; SP=rup(SEQ,16); W3=w.shape[1]; H=D//HD
    return pl.pallas_call(functools.partial(k1_body,SEQ,SP,D,IB),grid=(N//IB,),
      in_specs=[pl.BlockSpec((IB,SEQ,D),lambda i:(i,0,0)),pl.BlockSpec(w.shape,lambda i:(0,0)),pl.BlockSpec(vec.shape,lambda i:(0,0))],
      out_specs=[pl.BlockSpec((IB,SP,W3),lambda i:(i,0,0)),pl.BlockSpec((IB,SP,D),lambda i:(i,0,0)),pl.BlockSpec((IB,8,SP),lambda i:(i,0,0))],
      out_shape=[jax.ShapeDtypeStruct((N,SP,W3),BF),jax.ShapeDtypeStruct((N,SP,D),BF),jax.ShapeDtypeStruct((N,8,SP),F32)],
      scratch_shapes=[pltpu.VMEM((IB*SP,D),BF)],compiler_params=VM,name="k1")(images,w,vec)

RS2=math.sqrt(0.5)
def gelu_pair(u):
    a=jnp.abs(u)
    t=1.0/(1.0+(0.3275911*RS2)*a)
    e=jnp.exp(-0.5*(u*u))
    q=t*(0.127414796+t*(-0.142248368+t*(0.7107068705+t*(-0.7265760135+t*0.5307027145))))*e
    phi=jnp.where(u>=0,1.0-q,q)
    return u*phi, phi+u*e*0.3989422804014327

def k2_body(SEQ,SP,D,FF,IB,cnt_ref,x_ref,o_ref,cot_ref,wp_ref,w1_ref,w2t_ref,c1_ref,vec_ref,
            out_ref,dx1_ref,do_ref,tp_ref,t1_ref,t2_ref,tc1_ref,tv_ref,
            b_scr,dy_scr,x1_scr,xh_scr,r_scr,g_scr,du_scr,dx_scr):
    s=pl.program_id(0)
    @pl.when(s==0)
    def _():
        dy_scr[...]=jnp.zeros_like(dy_scr)
        x1_scr[...]=jnp.zeros_like(x1_scr)
        for r in (tp_ref,t1_ref,t2_ref,tc1_ref,tv_ref): r[...]=jnp.zeros_like(r)
    cp=vec_ref[2:3,:]; g2=vec_ref[3:4,:]; e2=vec_ref[4:5,:]; c2=vec_ref[5:6,:]
    R=IB*SP
    for i in range(IB):
        x1_scr[i*SP:i*SP+SEQ,:]=x_ref[i].astype(F32)
        val=(s*IB+i<cnt_ref[0])
        dy_scr[i*SP:i*SP+SEQ,:]=jnp.where(val,cot_ref[i],jnp.zeros((),BF))
    ob=o_ref[...].reshape(R,D)
    x1=x1_scr[...]+dot(ob,wp_ref[...])+cp
    x1_scr[...]=x1
    xh,r=ln_hat(x1)
    xh_scr[...]=xh
    b_scr[...]=(xh*g2+e2).astype(BF)
    r_scr[...]=jnp.broadcast_to(r,(R,128))
    C=D
    for c in range(FF//C):
        sl=slice(c*C,(c+1)*C)
        u=dot(b_scr[...],w1_ref[:,sl])+c1_ref[0:1,sl]
        ga,dg=gelu_pair(u)
        g_scr[:,sl]=ga.astype(BF)
        du=dot(dy_scr[...],w2t_ref[:,sl])*dg
        du_scr[:,sl]=du.astype(BF)
        tc1_ref[0:1,sl]+=jnp.sum(du,axis=0,keepdims=True)
    y=x1_scr[...]+dot(g_scr[...],w2t_ref[...],1,1)+c2
    for i in range(IB):
        val=(s*IB+i<cnt_ref[0])
        out_ref[i]=jnp.where(val,y[i*SP:i*SP+SEQ],0.0).astype(BF)
    db=dot(du_scr[...],w1_ref[...],1,1)
    xh=xh_scr[...]
    dyf=dy_scr[...].astype(F32)
    dxh=db*g2
    m1=jnp.mean(dxh,axis=-1,keepdims=True)
    m2=jnp.mean(dxh*xh,axis=-1,keepdims=True)
    dx=dyf+r_scr[:,0:1]*(dxh-m1-xh*m2)
    tv_ref[3:4,:]+=jnp.sum(db*xh,axis=0,keepdims=True)
    tv_ref[4:5,:]+=jnp.sum(db,axis=0,keepdims=True)
    tv_ref[5:6,:]+=jnp.sum(dyf,axis=0,keepdims=True)
    tv_ref[2:3,:]+=jnp.sum(dx,axis=0,keepdims=True)
    dx1_ref[...]=dx.reshape(IB,SP,D)
    dx_scr[...]=dx.astype(BF)
    do_ref[...]=dot(dx_scr[...],wp_ref[...],1,1).astype(BF).reshape(IB,SP,D)
    tp_ref[...]+=dot(ob,dx_scr[...],0,0)
    t1_ref[...]+=dot(b_scr[...],du_scr[...],0,0)
    t2_ref[...]+=dot(dy_scr[...],g_scr[...],0,0)

def k2(cnt,images,o,cot,wp,w1,w2t,c1,vec,IB=2):
    N,SEQ,D=images.shape; SP=o.shape[1]; FF=w1.shape[1]
    full=lambda a:pl.BlockSpec(a.shape,lambda i,*_:(0,0))
    blk=lambda r,d:pl.BlockSpec((IB,r,d),lambda i,*_:(i,0,0))
    fo=lambda r,c:pl.BlockSpec((r,c),lambda i,*_:(0,0))
    R=IB*SP
    return pl.pallas_call(functools.partial(k2_body,SEQ,SP,D,FF,IB),
      grid_spec=pltpu.PrefetchScalarGridSpec(num_scalar_prefetch=1,grid=(N//IB,),
      in_specs=[blk(SEQ,D),blk(SP,D),blk(SEQ,D),full(wp),full(w1),full(w2t),full(c1),full(vec)],
      out_specs=[blk(SEQ,D),blk(SP,D),blk(SP,D),fo(D,D),fo(D,FF),fo(D,FF),fo(8,FF),fo(8,D)],
      scratch_shapes=[pltpu.VMEM((R,D),BF),pltpu.VMEM((R,D),BF),pltpu.VMEM((R,D),F32),pltpu.VMEM((R,D),F32),pltpu.VMEM((R,128),F32),
         pltpu.VMEM((R,FF),BF),pltpu.VMEM((R,FF),BF),pltpu.VMEM((R,D),BF)]),
      out_shape=[jax.ShapeDtypeStruct((N,SEQ,D),BF),jax.ShapeDtypeStruct((N,SP,D),F32),jax.ShapeDtypeStruct((N,SP,D),BF),
        jax.ShapeDtypeStruct((D,D),F32),jax.ShapeDtypeStruct((D,FF),F32),jax.ShapeDtypeStruct((D,FF),F32),jax.ShapeDtypeStruct((8,FF),F32),jax.ShapeDtypeStruct((8,D),F32)],
      compiler_params=VM,name="k2")(cnt,images,o,cot,wp,w1,w2t,c1,vec)

def k3_body(SEQ,SP,D,IB,x_ref,qkv_ref,l_ref,do_ref,dx1_ref,w_ref,vec_ref,gi_ref,tq_ref,tv_ref,a_scr,d_scr):
    H=D//HD
    @pl.when(pl.program_id(0)==0)
    def _():
        a_scr[...]=jnp.zeros_like(a_scr); d_scr[...]=jnp.zeros_like(d_scr)
        tq_ref[...]=jnp.zeros_like(tq_ref); tv_ref[...]=jnp.zeros_like(tv_ref)
    g=vec_ref[0:1,:]; e=vec_ref[1:2,:]
    for i in range(IB):
        xh,_=ln_hat(x_ref[i].astype(F32))
        a_scr[i*SP:i*SP+SEQ,:]=(xh*g+e).astype(BF)
    for i in range(IB):
        for h in range(0,H,2):
            dq,dk,dv=[],[],[]
            for j in range(2):
                lo=(h+j)*HD
                q=qkv_ref[i,:,lo:lo+HD]
                k=qkv_ref[i,0:SEQ,D+lo:D+lo+HD]
                v=qkv_ref[i,0:SEQ,2*D+lo:2*D+lo+HD]
                do=do_ref[i,:,lo:lo+HD]
                p=jnp.exp(dot(k,q,1,1)-l_ref[i,h+j:h+j+1,:])
                dp=dot(v,do,1,1)
                t=p*dp
                inner=jnp.sum(t,axis=0,keepdims=True)
                ds=(t-p*inner).astype(BF)
                pb=p.astype(BF)
                dv.append(dot(pb,do)); dk.append(dot(ds,q)); dq.append(dot(ds,k,0,0))
            r0=i*SP
            d_scr[r0:r0+SP,h*HD:(h+2)*HD]=(jnp.concatenate(dq,axis=1)*(HD**-0.5)).astype(BF)
            d_scr[r0:r0+SEQ,D+h*HD:D+(h+2)*HD]=jnp.concatenate(dk,axis=1).astype(BF)
            d_scr[r0:r0+SEQ,2*D+h*HD:2*D+(h+2)*HD]=jnp.concatenate(dv,axis=1).astype(BF)
    da=dot(d_scr[...],w_ref[...],1,1)
    tq_ref[...]+=dot(a_scr[...],d_scr[...],0,0)
    for i in range(IB):
        xh,r=ln_hat(x_ref[i].astype(F32))
        d=da[i*SP:i*SP+SEQ]
        dxh=d*g
        m1=jnp.mean(dxh,axis=-1,keepdims=True)
        m2=jnp.mean(dxh*xh,axis=-1,keepdims=True)
        gi_ref[i]=(dx1_ref[i,0:SEQ,:]+r*(dxh-m1-xh*m2)).astype(BF)
        tv_ref[0:1,:]+=jnp.sum(d*xh,axis=0,keepdims=True)
        tv_ref[1:2,:]+=jnp.sum(d,axis=0,keepdims=True)

def k3(images,qkv,l,do,dx1,w,vec,IB=2):
    N,SEQ,D=images.shape; SP=do.shape[1]; W3=w.shape[1]
    full=lambda a:pl.BlockSpec(a.shape,lambda i,*_:(0,0))
    blk=lambda r,d:pl.BlockSpec((IB,r,d),lambda i,*_:(i,0,0))
    fo=lambda r,c:pl.BlockSpec((r,c),lambda i,*_:(0,0))
    return pl.pallas_call(functools.partial(k3_body,SEQ,SP,D,IB),grid=(N//IB,),
      in_specs=[blk(SEQ,D),blk(SP,W3),blk(8,SP),blk(SP,D),blk(SP,D),full(w),full(vec)],
      out_specs=[blk(SEQ,D),fo(D,W3),fo(8,D)],
      out_shape=[jax.ShapeDtypeStruct((N,SEQ,D),BF),jax.ShapeDtypeStruct((D,W3),F32),jax.ShapeDtypeStruct((8,D),F32)],
      scratch_shapes=[pltpu.VMEM((IB*SP,D),BF),pltpu.VMEM((IB*SP,W3),BF)],compiler_params=VM,name="k3")(images,qkv,l,do,dx1,w,vec)


LEARN_RATE = 0.2
BETA_ONE = 0.9
BETA_TWO = 0.999
ADAM_EPS = 1e-08
DECAY_RATE = 0.5
adam_steps = 10.0


def adam_update(weight, grad, first, second, flag, lr_scale):
    first_new = BETA_ONE * first + (1.0 - BETA_ONE) * grad
    second_new = BETA_TWO * second + (1.0 - BETA_TWO) * grad * grad
    corr_one = 1.0 - BETA_ONE**adam_steps
    corr_two = 1.0 - BETA_TWO**adam_steps
    direction = first_new / corr_one / (jnp.sqrt(second_new / corr_two) + ADAM_EPS)
    weight_new = weight - LEARN_RATE * lr_scale * (direction + DECAY_RATE * flag * weight)
    return (weight_new, first_new, second_new)


def pairs(n, k):
    return [(i, i ^ k) for i in range(n)]


def direct(n):
    return 2 <= n <= 8 and n & (n - 1) == 0


def gather(x):
    n = lax.axis_size("fsdp")
    if not direct(n):
        return lax.all_gather(x, "fsdp", axis=0, tiled=True)
    me = lax.axis_index("fsdp")
    pieces = [None] * n
    pieces[0] = x
    for k in range(2, n, 2):
        pieces[k] = lax.ppermute(x, "fsdp", pairs(n, k))
    for k in range(0, n, 2):
        pieces[k + 1] = lax.ppermute(pieces[k], "fsdp", pairs(n, 1))
    out = jnp.stack(pieces)
    bit = 1
    while bit < n:
        v = out.reshape((n // (2 * bit), 2, bit) + x.shape)
        out = jnp.where((me & bit) != 0, v[:, ::-1], v).reshape(out.shape)
        bit *= 2
    return out.reshape((n * x.shape[0],) + x.shape[1:])


def reduce_scatter(g):
    n = lax.axis_size("fsdp")
    d = lax.axis_size("dp")
    r = g.shape[0] // n
    if not (direct(n) and d == 4):
        share = lax.psum_scatter(g, "fsdp", scatter_dimension=0, tiled=True)
        return lax.psum(share.astype(BF), "dp").astype(F32)
    me = lax.axis_index("fsdp")
    core = me % 2
    z = me // 2
    v = g.reshape((n // 2, 2, r) + g.shape[1:])
    mine = lax.dynamic_index_in_dim(v, core, 1, keepdims=False)
    other = lax.dynamic_index_in_dim(v, 1 - core, 1, keepdims=False)
    h = mine + lax.ppermute(other.astype(BF), "fsdp", pairs(n, 1)).astype(F32)
    got = [
        lax.ppermute(
            lax.dynamic_index_in_dim(h, z ^ k, 0, keepdims=False).astype(BF), "fsdp", pairs(n, 2 * k)
        )
        for k in range(1, n // 2)
    ]
    own = lax.dynamic_index_in_dim(h, z, 0, keepdims=False)
    for piece in got:
        own = own + piece.astype(F32)
    b = own.astype(BF)
    p1, p2, p3 = [lax.ppermute(b, "dp", pairs(d, k)).astype(F32) for k in (1, 2, 3)]
    return (b.astype(F32) + p1) + (p2 + p3)


def local(
    images, cotangent, counts,
    w_qkv, w_proj, w_fc1, w_fc2, b_fc1, vectors,
    m_qkv, m_proj, m_fc1, m_fc2, m_bias1, m_vectors,
    v_qkv, v_proj, v_fc1, v_fc2, v_bias1, v_vectors,
    decay_flags, group_ids, group_scales,
):
    masters = (w_qkv, w_proj, w_fc1, w_fc2, b_fc1, vectors)
    r = w_qkv.shape[0]
    D = images.shape[2]
    FF = w_fc1.shape[1]
    nb = b_fc1.shape[0] // r
    nv = vectors.shape[0]
    small = jnp.concatenate(
        [vectors.T, b_fc1.reshape(r, nb), jnp.zeros((r, 128 - nv - nb), F32)], axis=1
    )
    pack_a = jnp.concatenate([w_qkv, small], axis=1).astype(BF)
    pack_b = jnp.concatenate([w_fc1, w_fc2.T, w_proj], axis=1).astype(BF)
    full_a = gather(pack_a)
    full_b = gather(pack_b)
    W3 = w_qkv.shape[1]
    wq = full_a[:, :W3]
    sm = full_a[:, W3:].astype(F32)
    vec = jnp.pad(sm[:, :nv].T, ((0, 8 - nv), (0, 0)))
    c1 = jnp.broadcast_to(sm[:, nv : nv + nb].reshape(1, FF), (8, FF))
    w1 = full_b[:, :FF]
    w2t = full_b[:, FF : 2 * FF]
    wp = full_b[:, 2 * FF :]
    qkv, o, logs = k1(images, wq, vec)
    out_block, dx1, do, tp, t1, t2, tc1, tv2 = k2(counts, images, o, cotangent, wp, w1, w2t, c1, vec)
    grad_input, tq, tv1 = k3(images, qkv, logs, do, dx1, wq, vec)
    gsm = jnp.concatenate([tv2[:nv].T, tc1[0].reshape(D, nb), jnp.zeros((D, 128 - nv - nb), F32)], axis=1)
    red_b = reduce_scatter(jnp.concatenate([t1, t2, tp, gsm], axis=1))
    red_a = reduce_scatter(jnp.concatenate([tq, jnp.pad(tv1[:2].T, ((0, 0), (0, 126)))], axis=1))
    g_small = red_b[:, 2 * FF + D :]
    totals = (
        red_a[:, :W3],
        red_b[:, 2 * FF : 2 * FF + D],
        red_b[:, :FF],
        red_b[:, FF : 2 * FF].T,
        g_small[:, nv : nv + nb].reshape(-1),
        jnp.concatenate([red_a[:, W3 : W3 + 2], g_small[:, 2:nv]], axis=1).T,
    )
    slot_total = images.shape[0] * lax.axis_size("dp") * lax.axis_size("fsdp")
    grads = [total / slot_total for total in totals]
    firsts = (m_qkv, m_proj, m_fc1, m_fc2, m_bias1, m_vectors)
    seconds = (v_qkv, v_proj, v_fc1, v_fc2, v_bias1, v_vectors)
    group_range = jnp.arange(group_scales.shape[0])
    new_weights, new_firsts, new_seconds = ([], [], [])
    for place in range(6):
        flag = decay_flags[place].astype(jnp.float32)
        lr_scale = jnp.sum(jnp.where(group_range == group_ids[place], group_scales, 0.0))
        weight_n, first_n, second_n = adam_update(
            masters[place], grads[place], firsts[place], seconds[place], flag, lr_scale
        )
        new_weights.append(weight_n)
        new_firsts.append(first_n)
        new_seconds.append(second_n)
    return (out_block, grad_input, *grads, *new_weights, *new_firsts, *new_seconds)


def solution(mesh):
    return jax.shard_map(
        local,
        mesh=mesh,
        in_specs=(
            P(("dp", "fsdp"), None, None),
            P(("dp", "fsdp"), None, None),
            P(("dp", "fsdp")),
            P("fsdp", None),
            P("fsdp", None),
            P("fsdp", None),
            P(None, "fsdp"),
            P("fsdp"),
            P(None, "fsdp"),
            P("fsdp", None),
            P("fsdp", None),
            P("fsdp", None),
            P(None, "fsdp"),
            P("fsdp"),
            P(None, "fsdp"),
            P("fsdp", None),
            P("fsdp", None),
            P("fsdp", None),
            P(None, "fsdp"),
            P("fsdp"),
            P(None, "fsdp"),
            P(),
            P(),
            P(),
        ),
        out_specs=(
            P(("dp", "fsdp"), None, None),
            P(("dp", "fsdp"), None, None),
            P("fsdp", None),
            P("fsdp", None),
            P("fsdp", None),
            P(None, "fsdp"),
            P("fsdp"),
            P(None, "fsdp"),
            P("fsdp", None),
            P("fsdp", None),
            P("fsdp", None),
            P(None, "fsdp"),
            P("fsdp"),
            P(None, "fsdp"),
            P("fsdp", None),
            P("fsdp", None),
            P("fsdp", None),
            P(None, "fsdp"),
            P("fsdp"),
            P(None, "fsdp"),
            P("fsdp", None),
            P("fsdp", None),
            P("fsdp", None),
            P(None, "fsdp"),
            P("fsdp"),
            P(None, "fsdp"),
        ),
        check_vma=False,
    )
```

time: 930 us -> 310 us (0.33)
  matrix products: 425 us -> 0 us
  Pallas kernels: 0 us -> 169 us
  local copies, waits for them, and re-layouts: 204 us -> 50.1 us
  blocking collectives: 126 us -> 0 us
  other arithmetic: 85.5 us -> 23.2 us
  waiting for transfers between devices: 54.1 us -> 25.7 us
  starting transfers between devices: 0.71 us -> 27.9 us
  between operations: 25.3 us -> 9.83 us
    dot_general x54 -> x0, matrix products: 425 us -> none  [the longest x6 61 us: attend_back(): jnp.einsum('bhqk,bkhd->bqhd', grad_scores, keys_in, preferred_element_typ...]
    pallas_call x0 -> x3, Pallas kernels: none -> 169 us  [the longest x1 73 us: k2(): pl.pallas_call(functools.partial(k2_body, SEQ, SP, D, FF, IB), grid_spec=...]
    all_gather x5 -> x0, blocking collectives: 77.3 us -> none  [the longest x1 16.7 us: local(): lax.all_gather(lowered[3], 'fsdp', axis=1, tiled=True)]
    reshape x9 -> x1, local copies, waits for them, and re-layouts: 52.8 us -> 0.13 us  [local(): b_fc1.reshape(r, nb)]
    convert_element_type x7 -> x4, local copies, waits for them, and re-layouts: 55.3 us -> 4.24 us  [the longest x2 2.69 us: reduce_scatter(): h = mine + lax.ppermute(other.astype(BF), 'fsdp', pairs(n, 1)).astype(F32)]
    reduce_sum x13 -> x0, other arithmetic: 46.3 us -> none  [the longest x3 22.9 us: norm_affine(): centre = inputs - jnp.mean(inputs, axis=-1, keepdims=True)]
    psum x1 -> x0, waiting for transfers between devices: 44.3 us -> none  [local(): lax.psum(shares[0].astype(jnp.bfloat16), 'dp').astype(jnp.float32)]
    another operation x8 -> x3, local copies, waits for them, and re-layouts: 32.4 us -> 0.14 us  [the longest x1 12 us: to_blocks(): return array.reshape((blocks_count, ATT_IMG) + array.shape[1:])]
  transfers between devices with their start and end apart: 6 -> 28, of which waited for: 2 -> 7; matrix products, arithmetic and copies ran while one was open for 13% -> 16% of each run, Pallas kernels for 0% -> 10%
where the time goes in v1:
time: 310 us; the launch traced here: 306 us
  Pallas kernels  169 us (55%)
  local copies, waits for them, and re-layouts  50.1 us (16%)
  starting transfers between devices  27.9 us (9%)
  waiting for transfers between devices  25.7 us (8%)
  other arithmetic  23.2 us (7%)
  between operations  9.83 us (3%)
    pallas_call x1, Pallas kernels, k2(): pl.pallas_call(functools.partial(k2_body, SEQ, SP, D, FF, IB), grid_spec=...  73 us
    pallas_call x1, Pallas kernels, k3(): pl.pallas_call(functools.partial(k3_body, SEQ, SP, D, IB), grid=(N // IB,...  66.6 us
    pallas_call x1, Pallas kernels, k1(): pl.pallas_call(functools.partial(k1_body, SEQ, SP, D, IB), grid=(N // IB,...  29.5 us
    unnamed x83, local copies, waits for them, and re-layouts  23.9 us
    ppermute x6, waiting for transfers between devices, reduce_scatter(): lax.ppermute(lax.dynamic_index_in_dim(h, z ^ k, 0, keepdims=False).astype...  18.4 us
    concatenate x8, local copies, waits for them, and re-layouts, local(): red_b = reduce_scatter(jnp.concatenate([t1, t2, tp, gsm], axis=1))  12 us
    ppermute x6, starting transfers between devices, gather(): pieces[k] = lax.ppermute(x, 'fsdp', pairs(n, k))  9.74 us
    ppermute x6, starting transfers between devices, reduce_scatter(): lax.ppermute(lax.dynamic_index_in_dim(h, z ^ k, 0, keepdims=False).astype...  8.77 us
  transfers between devices with their start and end apart: 28, of which 7 were waited for; matrix products, arithmetic and copies ran while one was open for 16% of the time, Pallas kernels for 10%

profile of v1, /device:TPU:0, one launch (start us, length us, event | category | flops | bytes accessed | tf_op | source)
XLA Modules:
  0.0 305.8 jit_solution(12398289649117693857)
XLA Ops:
  2.4 1.0 convert.35
  4.5 2.6 collective-permute-start.1
  7.1 2.6 collective-permute-start.3
  9.7 1.0 convert_bitcast_fusion.1
  10.7 1.0 convert.38
  13.2 4.6 %copy.201.x_ref = bf16[24,197,384]{2,1,0:T(8,128)(2,1)} copy(bf16[24,197,384]{2,0,1:T(8,128)(2,1)} %param.24) | data formatting | bytes 7262208 | tf_op args[0]
  17.7 2.3 copy.202.cot_ref
  21.4 0.9 collective-permute-start.8
  22.5 0.9 bitcast_dynamic-update-slice_fusion.13
  23.5 0.9 bitcast_dynamic-update-slice_fusion.12
  24.4 3.6 %collective-permute-start.10 = (bf16[48,2688]{1,0:T(8,128)(2,1)S(1)}, bf16[48,2688]{1,0:T(8,128)(2,1)}, u32[]{:S(2)}, u32[]{:S(2)}) collective-permute-start(bf16[48,2688]{1,0:T(8,128)(2,1)S(1)} %pad_maximum_fusion), channel_id=1, source_target_pairs={{0,4},{1,5},{2,6},{3,7},{4,0},{5,1},{6,2},{7,3},{8,12},{9,13},{10,... | collective-permute-start | bytes 774152 | tf_op jit(solution)/shard_map/ppermute | solution.py:228
  28.0 0.9 bitcast_dynamic-update-slice_fusion.10
  29.7 1.2 collective-permute-done.6
  31.4 1.0 slice.119.w_ref
  33.5 29.5 %k1.1 = (bf16[24,208,1152]{2,1,0:T(8,128)(2,1)}, bf16[24,208,384]{2,1,0:T(8,128)(2,1)}, f32[24,8,208]{2,1,0:T(8,128)}) custom-call(bf16[24,197,384]{2,1,0:T(8,128)(2,1)} %copy.201.x_ref, bf16[384,1152]{1,0:T(8,128)(2,1)} %slice.119.w_ref, f32[8,384]{1,0:T(8,128)} %pad.8.vec_ref), custom_call_target="tpu_custom_call" | custom-call | tf_op jit(solution)/shard_map/k1/pallas_call | solution.py:56
  63.2 1.0 bitcast_dynamic-update-slice_fusion.6
  64.2 1.0 bitcast_dynamic-update-slice_fusion.5
  65.7 1.0 bitcast_dynamic-update-slice_fusion.3
  67.0 1.0 bitcast_dynamic-update-slice_fusion.1
  69.0 1.3 fusion.24
  71.7 73.0 %k2.1 = (bf16[24,197,384]{2,1,0:T(8,128)(2,1)}, f32[24,208,384]{2,1,0:T(8,128)}, bf16[24,208,384]{2,1,0:T(8,128)(2,1)}, f32[384,384]{1,0:T(8,128)}, f32[384,1152...) custom-call(s32[1]{0:T(128)S(6)} %copy.232.cnt_ref, bf16[24,197,384]{2,1,0:T(8,128)(2,1)} %copy.201.x_ref, ...), custom_call_target="tpu_custom_call" | custom-call | tf_op jit(solution)/shard_map/k2/pallas_call | solution.py:130
  144.7 1.7 copy.206
  150.1 1.6 copy.210
  151.7 66.6 %k3.1 = (bf16[24,197,384]{2,1,0:T(8,128)(2,1)}, f32[384,1152]{1,0:T(8,128)}, f32[8,384]{1,0:T(8,128)}) custom-call(bf16[24,197,384]{2,1,0:T(8,128)(2,1)} %copy.201.x_ref, bf16[24,208,1152]{2,1,0:T(8,128)(2,1)} %get-tuple-element.42.qkv_ref, f32[24,8,208]{2,1,0:T(8,128)} %get-tuple-element.43.l_ref, bf16[24,208,384]{2,1,0:T(8,128)(2,1)} %get-tuple-element.44.do_ref, ...), custom_call_target="tpu_custom_call" | custom-call | tf_op jit(solution)/shard_map/k3/pallas_call | solution.py:187
  219.8 1.7 select_maximum_fusion
  221.6 1.3 copy-done
  224.8 1.6 copy.209
  227.0 4.5 %concatenate.76 = f32[4,2,48,2816]{3,2,0,1:T(8,128)} concatenate(f32[4,2,48,1152]{3,2,0,1:T(8,128)S(1)} %copy.206, f32[4,2,48,1152]{3,2,0,1:T(8,128)S(1)} %copy.207, f32[4,2,48,384]{3,2,0,1:T(8,128)} %copy.208, f32[4,2,48,6]{3,2,0,1:T(8,128)} %copy.209, f32[4,2,48,3]{3,2,0,1:T(8,128)} %copy.210, f32[4,2,48,119]{3,2,0,1:T(8,128)} %broadcast_in_dim.28), dimensions={3} | concatenate | bytes 8650752 | tf_op jit(solution)/shard_map/concatenate | solution.py:300
  231.6 1.9 fusion
  233.8 1.1 bitcast_add_fusion.1
  236.0 3.5 %collective-permute-start.16 = (bf16[48,1280]{1,0:T(8,128)(2,1)}, bf16[48,1280]{1,0:T(8,128)(2,1)}, u32[]{:S(2)}, u32[]{:S(2)}) collective-permute-start(bf16[48,1280]{1,0:T(8,128)(2,1)} %get-tuple-element.220), channel_id=1, source_target_pairs={{0,4},{1,5},{2,6},{3,7},{4,0},{5,1},{6,2},{7,3},{8,12},{9,13},{10,... | collective-permute-start | bytes 368648 | tf_op jit(solution)/shard_map/ppermute | solution.py:255
  241.3 4.5 %fusion.21 = (f32[]{:T(128)}, f32[]{:T(128)}, f32[]{:T(128)}, f32[]{:T(128)}, f32[]{:T(128)}, /*index=5*/f32[]{:T(128)}) fusion(f32[3]{0:T(128)S(1)} %copy-done.29, s32[]{:T(128)} %bitcast.62, s32[]{:T(128)} %bitcast.56, s32[]{:T(128)} %bitcast.54, s32[]{:T(128)} %bitcast.52, s32[]{:T(128)} %bitcast.50, s32[]{:T(128)} %bitcast.60), kind=kLoop, calls=%fused_computation.101 | loop fusion | flops 48 | bytes 60 | tf_op jit(solution)/shard_map/reduce_sum | solution.py:319
  253.0 4.5 %copy.214 = bf16[24,197,384]{2,0,1:T(8,128)(2,1)} copy(bf16[24,197,384]{2,1,0:T(8,128)(2,1)} %get-tuple-element.159) | data formatting | bytes 7262208
  257.5 2.3 copy.213
  259.8 1.3 fusion.10
  261.1 1.5 collective-permute-start.18
  262.6 1.5 collective-permute-start.19
  265.7 3.8 %collective-permute-start.23 = (bf16[48,2816]{1,0:T(8,128)(2,1)S(1)}, bf16[48,2816]{1,0:T(8,128)(2,1)}, u32[]{:S(2)}, u32[]{:S(2)}) collective-permute-start(bf16[48,2816]{1,0:T(8,128)(2,1)S(1)} %get-tuple-element.215), channel_id=1, source_target_pairs={{0,4},{1,5},{2,6},{3,7},{4,0},{5,1},{6,2},{7,3},{8,12},{9,13},{10,... | collective-permute-start | bytes 811016 | tf_op jit(solution)/shard_map/ppermute | solution.py:255
  270.3 7.2 %collective-permute-done.22 = bf16[48,2816]{1,0:T(8,128)(2,1)S(1)} collective-permute-done((bf16[48,2816]{1,0:T(8,128)(2,1)}, bf16[48,2816]{1,0:T(8,128)(2,1)S(1)}, u32[]{:S(2)}, u32[]{:S(2)}) %collective-permute-start.22) | collective-permute-done | bytes 270368 | tf_op jit(solution)/shard_map/ppermute | solution.py:255
  277.5 11.2 %collective-permute-done.23 = bf16[48,2816]{1,0:T(8,128)(2,1)} collective-permute-done((bf16[48,2816]{1,0:T(8,128)(2,1)S(1)}, bf16[48,2816]{1,0:T(8,128)(2,1)}, u32[]{:S(2)}, u32[]{:S(2)}) %collective-permute-start.23) | collective-permute-done | bytes 270368 | tf_op jit(solution)/shard_map/ppermute | solution.py:255
  288.7 1.2 fusion.3
  289.9 1.6 collective-permute-start.25
  291.4 1.5 collective-permute-start.26
  293.4 2.1 multiply_subtract_fusion.2
  295.5 1.2 collective-permute-done.25
  296.7 4.1 %collective-permute-done.26 = bf16[48,2816]{1,0:T(8,128)(2,1)S(1)} collective-permute-done((bf16[48,2816]{1,0:T(8,128)(2,1)S(1)}, bf16[48,2816]{1,0:T(8,128)(2,1)S(1)}, u32[]{:S(2)}, u32[]{:S(2)}) %collective-permute-start.26) | collective-permute-done | bytes 270368 | tf_op jit(solution)/shard_map/ppermute | solution.py:264
  301.7 1.0 multiply_subtract_fusion
  302.7 1.0 multiply_subtract_fusion.1
  (173 shorter events, 26.9 us)
Async XLA Ops:
  0.7 12.1 %copy-start.4 = (f32[48,1152]{1,0:T(8,128)S(1)}, f32[48,1152]{1,0:T(8,128)}, u32[]{:S(2)}) copy-start(f32[48,1152]{1,0:T(8,128)} %param.27) | copy-start | bytes 663556
  0.7 12.1 %copy-start.6 = (f32[48,1152]{1,0:T(8,128)S(1)}, f32[48,1152]{1,0:T(8,128)}, u32[]{:S(2)}) copy-start(f32[48,1152]{1,0:T(8,128)} %param.29) | copy-start | bytes 663556
  0.7 12.1 %copy-start.10 = (f32[48,384]{1,0:T(8,128)S(1)}, f32[48,384]{1,0:T(8,128)}, u32[]{:S(2)}) copy-start(f32[48,384]{1,0:T(8,128)} %param.28) | copy-start | bytes 221188
  4.1 17.3 %collective-permute-start = (bf16[48,1280]{1,0:T(8,128)(2,1)}, bf16[48,1280]{1,0:T(8,128)(2,1)}, u32[]{:S(2)}, u32[]{:S(2)}) collective-permute-start(bf16[48,1280]{1,0:T(8,128)(2,1)} %concatenate.64), channel_id=1, source_target_pairs={{0,1},{1,0},{2,3},{3,2},{4,5},{5,4},{6,7},{7,6},{8,9},{9,8},{10,11... | collective-permute-start | bytes 368648 | tf_op jit(solution)/shard_map/ppermute | solution.py:230
  4.5 17.8 %collective-permute-start.1 = (bf16[48,1280]{1,0:T(8,128)(2,1)}, bf16[48,1280]{1,0:T(8,128)(2,1)}, u32[]{:S(2)}, u32[]{:S(2)}) collective-permute-start(bf16[48,1280]{1,0:T(8,128)(2,1)} %concatenate.64), channel_id=1, source_target_pairs={{0,2},{1,3},{2,0},{3,1},{4,6},{5,7},{6,4},{7,5},{8,10},{9,11},{10,... | collective-permute-start | bytes 368648 | tf_op jit(solution)/shard_map/ppermute | solution.py:228
  7.1 17.2 %collective-permute-start.3 = (bf16[48,1280]{1,0:T(8,128)(2,1)}, bf16[48,1280]{1,0:T(8,128)(2,1)}, u32[]{:S(2)}, u32[]{:S(2)}) collective-permute-start(bf16[48,1280]{1,0:T(8,128)(2,1)} %concatenate.64), channel_id=1, source_target_pairs={{0,4},{1,5},{2,6},{3,7},{4,0},{5,1},{6,2},{7,3},{8,12},{9,13},{10,... | collective-permute-start | bytes 368648 | tf_op jit(solution)/shard_map/ppermute | solution.py:228
  9.7 19.2 %collective-permute-start.5 = (bf16[48,1280]{1,0:T(8,128)(2,1)}, bf16[48,1280]{1,0:T(8,128)(2,1)S(1)}, u32[]{:S(2)}, u32[]{:S(2)}) collective-permute-start(bf16[48,1280]{1,0:T(8,128)(2,1)} %concatenate.64), channel_id=1, source_target_pairs={{0,6},{1,7},{2,4},{3,5},{4,2},{5,3},{6,0},{7,1},{8,14},{9,15},{10,... | collective-permute-start | bytes 368648 | tf_op jit(solution)/shard_map/ppermute | solution.py:228
  12.5 50.6 %collective-permute-start.7 = (bf16[48,2688]{1,0:T(8,128)(2,1)S(1)}, bf16[48,2688]{1,0:T(8,128)(2,1)}, u32[]{:S(2)}, u32[]{:S(2)}) collective-permute-start(bf16[48,2688]{1,0:T(8,128)(2,1)S(1)} %pad_maximum_fusion), channel_id=1, source_target_pairs={{0,1},{1,0},{2,3},{3,2},{4,5},{5,4},{6,7},{7,6},{8,9},{9,8},{10,11... | collective-permute-start | bytes 774152 | tf_op jit(solution)/shard_map/ppermute | solution.py:230
  13.1 4.6 %copy-start.3 = (bf16[24,197,384]{2,0,1:T(8,128)(2,1)S(1)}, bf16[24,197,384]{2,0,1:T(8,128)(2,1)}, u32[]{:S(2)}) copy-start(bf16[24,197,384]{2,0,1:T(8,128)(2,1)} %param.25) | copy-start | bytes 10893316
  21.4 41.6 %collective-permute-start.8 = (bf16[48,2688]{1,0:T(8,128)(2,1)S(1)}, bf16[48,2688]{1,0:T(8,128)(2,1)}, u32[]{:S(2)}, u32[]{:S(2)}) collective-permute-start(bf16[48,2688]{1,0:T(8,128)(2,1)S(1)} %pad_maximum_fusion), channel_id=1, source_target_pairs={{0,2},{1,3},{2,0},{3,1},{4,6},{5,7},{6,4},{7,5},{8,10},{9,11},{10,... | collective-permute-start | bytes 774152 | tf_op jit(solution)/shard_map/ppermute | solution.py:228
  22.3 5.6 %collective-permute-start.2 = (bf16[48,1280]{1,0:T(8,128)(2,1)}, bf16[48,1280]{1,0:T(8,128)(2,1)S(1)}, u32[]{:S(2)}, u32[]{:S(2)}) collective-permute-start(bf16[48,1280]{1,0:T(8,128)(2,1)} %collective-permute-done.1), channel_id=1, source_target_pairs={{0,1},{1,0},{2,3},{3,2},{4,5},{5,4},{6,7},{7,6},{8,9},{9,8},{10,11... | collective-permute-start | bytes 368648 | tf_op jit(solution)/shard_map/ppermute | solution.py:230
  24.4 40.8 %collective-permute-start.10 = (bf16[48,2688]{1,0:T(8,128)(2,1)S(1)}, bf16[48,2688]{1,0:T(8,128)(2,1)}, u32[]{:S(2)}, u32[]{:S(2)}) collective-permute-start(bf16[48,2688]{1,0:T(8,128)(2,1)S(1)} %pad_maximum_fusion), channel_id=1, source_target_pairs={{0,4},{1,5},{2,6},{3,7},{4,0},{5,1},{6,2},{7,3},{8,12},{9,13},{10,... | collective-permute-start | bytes 774152 | tf_op jit(solution)/shard_map/ppermute | solution.py:228
  27.9 1.5 collective-permute-start.4
  28.9 36.7 %collective-permute-start.12 = (bf16[48,2688]{1,0:T(8,128)(2,1)S(1)}, bf16[48,2688]{1,0:T(8,128)(2,1)}, u32[]{:S(2)}, u32[]{:S(2)}) collective-permute-start(bf16[48,2688]{1,0:T(8,128)(2,1)S(1)} %pad_maximum_fusion), channel_id=1, source_target_pairs={{0,6},{1,7},{2,4},{3,5},{4,2},{5,3},{6,0},{7,1},{8,14},{9,15},{10,... | collective-permute-start | bytes 774152 | tf_op jit(solution)/shard_map/ppermute | solution.py:228
  29.5 1.3 collective-permute-start.6
  63.0 2.8 collective-permute-start.9
  65.1 1.8 collective-permute-start.11
  65.6 2.4 collective-permute-start.13
  219.8 4.2 %copy-start.22 = (f32[8,384]{1,0:T(8,128)S(1)}, f32[8,384]{1,0:T(8,128)}, u32[]{:S(2)}) copy-start(f32[8,384]{1,0:T(8,128)} %get-tuple-element.52) | copy-start | bytes 36868
  223.7 10.0 %collective-permute-start.14 = (bf16[4,48,1280]{2,1,0:T(8,128)(2,1)}, bf16[4,48,1280]{2,1,0:T(8,128)(2,1)}, u32[]{:S(2)}, u32[]{:S(2)}) collective-permute-start(bf16[4,48,1280]{2,1,0:T(8,128)(2,1)} %fusion.4), channel_id=1, source_target_pairs={{0,1},{1,0},{2,3},{3,2},{4,5},{5,4},{6,7},{7,6},{8,9},{9,8},{10,11... | collective-permute-start | bytes 1474568 | tf_op jit(solution)/shard_map/ppermute | solution.py:253
  233.4 6.6 %copy-start.20 = (s32[6]{0:T(128)S(1)}, s32[6]{0:T(128)}, u32[]{:S(2)}) copy-start(s32[6]{0:T(128)} %param.45) | copy-start | bytes 76
  233.5 7.8 %copy-start.29 = (f32[3]{0:T(128)S(1)}, f32[3]{0:T(128)}, u32[]{:S(2)}) copy-start(f32[3]{0:T(128)} %param.47) | copy-start | bytes 40
  233.5 31.2 %collective-permute-start.21 = (bf16[4,48,2816]{2,1,0:T(8,128)(2,1)S(1)}, bf16[4,48,2816]{2,1,0:T(8,128)(2,1)S(1)}, u32[]{:S(2)}, u32[]{:S(2)}) collective-permute-start(bf16[4,48,2816]{2,1,0:T(8,128)(2,1)S(1)} %fusion), channel_id=1, source_target_pairs={{0,1},{1,0},{2,3},{3,2},{4,5},{5,4},{6,7},{7,6},{8,9},{9,8},{10,11... | collective-permute-start | bytes 3244040 | tf_op jit(solution)/shard_map/ppermute | solution.py:253
  235.7 24.1 %collective-permute-start.15 = (bf16[48,1280]{1,0:T(8,128)(2,1)}, bf16[48,1280]{1,0:T(8,128)(2,1)S(1)}, u32[]{:S(2)}, u32[]{:S(2)}) collective-permute-start(bf16[48,1280]{1,0:T(8,128)(2,1)} %get-tuple-element.218), channel_id=1, source_target_pairs={{0,2},{1,3},{2,0},{3,1},{4,6},{5,7},{6,4},{7,5},{8,10},{9,11},{10,... | collective-permute-start | bytes 368648 | tf_op jit(solution)/shard_map/ppermute | solution.py:255
  236.0 23.7 %collective-permute-start.16 = (bf16[48,1280]{1,0:T(8,128)(2,1)}, bf16[48,1280]{1,0:T(8,128)(2,1)}, u32[]{:S(2)}, u32[]{:S(2)}) collective-permute-start(bf16[48,1280]{1,0:T(8,128)(2,1)} %get-tuple-element.220), channel_id=1, source_target_pairs={{0,4},{1,5},{2,6},{3,7},{4,0},{5,1},{6,2},{7,3},{8,12},{9,13},{10,... | collective-permute-start | bytes 368648 | tf_op jit(solution)/shard_map/ppermute | solution.py:255
  239.5 20.3 %collective-permute-start.17 = (bf16[48,1280]{1,0:T(8,128)(2,1)S(1)}, bf16[48,1280]{1,0:T(8,128)(2,1)}, u32[]{:S(2)}, u32[]{:S(2)}) collective-permute-start(bf16[48,1280]{1,0:T(8,128)(2,1)S(1)} %get-tuple-element.219), channel_id=1, source_target_pairs={{0,6},{1,7},{2,4},{3,5},{4,2},{5,3},{6,0},{7,1},{8,14},{9,15},{10,... | collective-permute-start | bytes 368648 | tf_op jit(solution)/shard_map/ppermute | solution.py:255
  253.0 4.5 %copy-start.2 = (bf16[24,197,384]{2,1,0:T(8,128)(2,1)S(1)}, bf16[24,197,384]{2,1,0:T(8,128)(2,1)}, u32[]{:S(2)}) copy-start(bf16[24,197,384]{2,1,0:T(8,128)(2,1)} %get-tuple-element.158) | copy-start | bytes 10893316
  257.4 7.2 %slice-start = ((s8[4325376]{0:T(1024)(128)(4,1)}), s8[4194304]{0:T(1024)(128)(4,1)S(1)}, s32[]{:S(2)}) async-start(s8[4325376]{0:T(1024)(128)(4,1)} %bitcast.138), calls=%async_computation | async-start | bytes 8388608
  257.4 7.2 %slice-start.1 = ((s8[4325376]{0:T(1024)(128)(4,1)}), s8[131072]{0:T(1024)(128)(4,1)S(1)}, s32[]{:S(2)}) async-start(s8[4325376]{0:T(1024)(128)(4,1)} %bitcast.138), calls=%async_computation.1 | async-start | bytes 262144
  261.1 8.5 %collective-permute-start.18 = (bf16[48,1280]{1,0:T(8,128)(2,1)S(1)}, bf16[48,1280]{1,0:T(8,128)(2,1)S(1)}, u32[]{:S(2)}, u32[]{:S(2)}) collective-permute-start(bf16[48,1280]{1,0:T(8,128)(2,1)S(1)} %fusion.10), channel_id=1, source_target_pairs={{0,8},{8,0},{16,24},{24,16},{1,9},{9,1},{17,25},{25,17},{2,10},{10... | collective-permute-start | bytes 368648 | tf_op jit(solution)/shard_map/ppermute | solution.py:264
  262.6 7.5 %collective-permute-start.19 = (bf16[48,1280]{1,0:T(8,128)(2,1)S(1)}, bf16[48,1280]{1,0:T(8,128)(2,1)S(1)}, u32[]{:S(2)}, u32[]{:S(2)}) collective-permute-start(bf16[48,1280]{1,0:T(8,128)(2,1)S(1)} %fusion.10), channel_id=1, source_target_pairs={{0,16},{8,24},{16,0},{24,8},{1,17},{9,25},{17,1},{25,9},{2,18},{10... | collective-permute-start | bytes 368648 | tf_op jit(solution)/shard_map/ppermute | solution.py:264
  264.2 6.0 %collective-permute-start.20 = (bf16[48,1280]{1,0:T(8,128)(2,1)S(1)}, bf16[48,1280]{1,0:T(8,128)(2,1)S(1)}, u32[]{:S(2)}, u32[]{:S(2)}) collective-permute-start(bf16[48,1280]{1,0:T(8,128)(2,1)S(1)} %fusion.10), channel_id=1, source_target_pairs={{0,24},{8,16},{16,8},{24,0},{1,25},{9,17},{17,9},{25,1},{2,26},{10... | collective-permute-start | bytes 368648 | tf_op jit(solution)/shard_map/ppermute | solution.py:264
  264.9 28.5 %copy-start.5 = (f32[48,1152]{1,0:T(8,128)S(1)}, f32[48,1152]{1,0:T(8,128)}, u32[]{:S(2)}) copy-start(f32[48,1152]{1,0:T(8,128)} %param.27) | copy-start | bytes 663556
  265.7 11.8 %collective-permute-start.22 = (bf16[48,2816]{1,0:T(8,128)(2,1)}, bf16[48,2816]{1,0:T(8,128)(2,1)S(1)}, u32[]{:S(2)}, u32[]{:S(2)}) collective-permute-start(bf16[48,2816]{1,0:T(8,128)(2,1)} %get-tuple-element.213), channel_id=1, source_target_pairs={{0,2},{1,3},{2,0},{3,1},{4,6},{5,7},{6,4},{7,5},{8,10},{9,11},{10,... | collective-permute-start | bytes 811016 | tf_op jit(solution)/shard_map/ppermute | solution.py:255
  265.7 22.9 %collective-permute-start.23 = (bf16[48,2816]{1,0:T(8,128)(2,1)S(1)}, bf16[48,2816]{1,0:T(8,128)(2,1)}, u32[]{:S(2)}, u32[]{:S(2)}) collective-permute-start(bf16[48,2816]{1,0:T(8,128)(2,1)S(1)} %get-tuple-element.215), channel_id=1, source_target_pairs={{0,4},{1,5},{2,6},{3,7},{4,0},{5,1},{6,2},{7,3},{8,12},{9,13},{10,... | collective-permute-start | bytes 811016 | tf_op jit(solution)/shard_map/ppermute | solution.py:255
  269.6 19.1 %collective-permute-start.24 = (bf16[48,2816]{1,0:T(8,128)(2,1)S(1)}, bf16[48,2816]{1,0:T(8,128)(2,1)}, u32[]{:S(2)}, u32[]{:S(2)}) collective-permute-start(bf16[48,2816]{1,0:T(8,128)(2,1)S(1)} %get-tuple-element.214), channel_id=1, source_target_pairs={{0,6},{1,7},{2,4},{3,5},{4,2},{5,3},{6,0},{7,1},{8,14},{9,15},{10,... | collective-permute-start | bytes 811016 | tf_op jit(solution)/shard_map/ppermute | solution.py:255
  289.8 11.8 %copy-start.9 = (f32[1152,48]{0,1:T(8,128)S(1)}, f32[1152,48]{0,1:T(8,128)}, u32[]{:S(2)}) copy-start(f32[1152,48]{0,1:T(8,128)} %param.30) | copy-start | bytes 663556
  289.8 11.8 %copy-start.13 = (f32[1152,48]{0,1:T(8,128)S(1)}, f32[1152,48]{0,1:T(8,128)}, u32[]{:S(2)}) copy-start(f32[1152,48]{0,1:T(8,128)} %param.36) | copy-start | bytes 663556
  289.8 11.8 %copy-start.14 = (f32[1152,48]{0,1:T(8,128)S(1)}, f32[1152,48]{0,1:T(8,128)}, u32[]{:S(2)}) copy-start(f32[1152,48]{0,1:T(8,128)} %param.42) | copy-start | bytes 663556
  289.9 6.9 %collective-permute-start.25 = (bf16[48,2816]{1,0:T(8,128)(2,1)S(1)}, bf16[48,2816]{1,0:T(8,128)(2,1)S(1)}, u32[]{:S(2)}, u32[]{:S(2)}) collective-permute-start(bf16[48,2816]{1,0:T(8,128)(2,1)S(1)} %fusion.3), channel_id=1, source_target_pairs={{0,8},{8,0},{16,24},{24,16},{1,9},{9,1},{17,25},{25,17},{2,10},{10... | collective-permute-start | bytes 811016 | tf_op jit(solution)/shard_map/ppermute | solution.py:264
  291.4 9.4 %collective-permute-start.26 = (bf16[48,2816]{1,0:T(8,128)(2,1)S(1)}, bf16[48,2816]{1,0:T(8,128)(2,1)S(1)}, u32[]{:S(2)}, u32[]{:S(2)}) collective-permute-start(bf16[48,2816]{1,0:T(8,128)(2,1)S(1)} %fusion.3), channel_id=1, source_target_pairs={{0,16},{8,24},{16,0},{24,8},{1,17},{9,25},{17,1},{25,9},{2,18},{10... | collective-permute-start | bytes 811016 | tf_op jit(solution)/shard_map/ppermute | solution.py:264
  292.9 7.9 %collective-permute-start.27 = (bf16[48,2816]{1,0:T(8,128)(2,1)S(1)}, bf16[48,2816]{1,0:T(8,128)(2,1)S(1)}, u32[]{:S(2)}, u32[]{:S(2)}) collective-permute-start(bf16[48,2816]{1,0:T(8,128)(2,1)S(1)} %fusion.3), channel_id=1, source_target_pairs={{0,24},{8,16},{16,8},{24,0},{1,25},{9,17},{17,9},{25,1},{2,26},{10... | collective-permute-start | bytes 811016 | tf_op jit(solution)/shard_map/ppermute | solution.py:264
  295.5 7.2 %copy-start.7 = (f32[48,1152]{1,0:T(8,128)S(1)}, f32[48,1152]{1,0:T(8,128)}, u32[]{:S(2)}) copy-start(f32[48,1152]{1,0:T(8,128)} %param.29) | copy-start | bytes 663556
  295.5 7.2 %copy-start.15 = (f32[48,1152]{1,0:T(8,128)S(1)}, f32[48,1152]{1,0:T(8,128)}, u32[]{:S(2)}) copy-start(f32[48,1152]{1,0:T(8,128)} %param.35) | copy-start | bytes 663556
  295.5 7.2 %copy-start.16 = (f32[48,1152]{1,0:T(8,128)S(1)}, f32[48,1152]{1,0:T(8,128)}, u32[]{:S(2)}) copy-start(f32[48,1152]{1,0:T(8,128)} %param.41) | copy-start | bytes 663556
  301.3 3.9 %copy-start.23 = (f32[144]{0:T(256)}, f32[144]{0:T(256)S(1)}, u32[]{:S(2)}) copy-start(f32[144]{0:T(256)S(1)} %div.132) | copy-start | bytes 1732
  301.7 3.5 %copy-start.26 = (f32[144]{0:T(256)S(1)}, f32[144]{0:T(256)}, u32[]{:S(2)}) copy-start(f32[144]{0:T(256)} %param.31) | copy-start | bytes 1732
  301.7 3.5 %copy-start.27 = (f32[144]{0:T(256)S(1)}, f32[144]{0:T(256)}, u32[]{:S(2)}) copy-start(f32[144]{0:T(256)} %param.37) | copy-start | bytes 1732
  (12 other events, 30.3 us)

commit v2 on v0

v2 whole, which is shorter than its diff:
```python
import math
from functools import partial

import jax
import jax.numpy as jnp
from jax import lax
from jax.experimental import pallas as pl
from jax.experimental.pallas import tpu as pltpu
from jax.sharding import PartitionSpec

BF = jnp.bfloat16
F32 = jnp.float32
HEAD_DIM = 64
EPS_LN = 1e-06
LEARN_RATE = 0.2
BETA_ONE = 0.9
BETA_TWO = 0.999
ADAM_EPS = 1e-08
DECAY_RATE = 0.5
ADAM_STEPS = 10.0
GROUP = 8
PAIR = 2
EXTRA = 8
ROOT_HALF = math.sqrt(0.5)


def up(n, m):
    return (n + m - 1) // m * m


def dot(a, b, ca=1, cb=0):
    return lax.dot_general(a, b, (((ca,), (cb,)), ((), ())), preferred_element_type=F32)


def tiles(n, w):
    return [(a, min(w, n - a)) for a in range(0, n, w)]


def params(flops=0, nbytes=0):
    return dict(
        compiler_params=pltpu.CompilerParams(vmem_limit_bytes=58 << 20),
        cost_estimate=pl.CostEstimate(flops=flops, bytes_accessed=nbytes, transcendentals=0),
    )


def weave(ms, vs):
    k = 0
    for a, f in enumerate(ms):
        f()
        while k * len(ms) < len(vs) * (a + 1):
            vs[k]()
            k += 1
    for f in vs[k:]:
        f()


def norm_rows(x):
    c = x - jnp.mean(x, axis=-1, keepdims=True)
    r = lax.rsqrt(jnp.mean(c * c, axis=-1, keepdims=True) + EPS_LN)
    return c * r, r


def gelu_pair(u):
    t = 1.0 / (1.0 + (0.3275911 * ROOT_HALF) * jnp.abs(u))
    e = jnp.exp(-0.5 * (u * u))
    q = t * (0.127414796 + t * (-0.142248368 + t * (0.7107068705 + t * (-0.7265760135 + t * 0.5307027145)))) * e
    phi = jnp.where(u >= 0, 1.0 - q, q)
    return u * phi, phi + u * e * 0.3989422804014327


def full(a):
    return pl.BlockSpec(a.shape, lambda *_: (0,) * len(a.shape))


def whole(*shape):
    return pl.BlockSpec(shape, lambda *_: (0,) * len(shape))


def spread(src, dst, seq):
    for t, n in tiles(seq, 20):
        x = src[t : t + n].astype(F32).reshape(n * GROUP, src.shape[2])
        for c in range(dst.shape[0]):
            dst[c, t * GROUP : (t + n) * GROUP, :] = x[:, c * 128 : (c + 1) * 128]


def image(ref, i, t, n):
    return jnp.concatenate(
        [ref[c, pl.ds(t * GROUP + i, n, stride=GROUP), :] for c in range(ref.shape[0])], axis=1
    )


def token(ref, t, tp):
    return jnp.concatenate(
        [ref[c, pl.ds(t, GROUP, stride=tp), :] for c in range(ref.shape[0])], axis=1
    )


def tokens(ref, t, tp):
    return jnp.stack([token(ref, t, tp), token(ref, t + 1, tp)])


def pack_body(r, wq_ref, vec_ref, b_ref, w1_ref, w2_ref, wp_ref, a_ref, b_out, sm):
    FF = w1_ref.shape[1]
    a_ref[0:r, :] = wq_ref[...].astype(BF)
    sm[...] = jnp.zeros_like(sm)
    sm[0 : vec_ref.shape[0], 0 : vec_ref.shape[1]] = vec_ref[...]
    sm[6:7, 0 : b_ref.shape[1]] = b_ref[...]
    a_ref[r : r + EXTRA, :] = sm[...].astype(BF)
    b_out[:, 0:FF] = w1_ref[...].astype(BF)
    b_out[:, FF : 2 * FF] = w2_ref[...].astype(BF)
    b_out[:, 2 * FF :] = wp_ref[...].astype(BF)


def pack(wq, vec, b, w1, w2t, wp):
    r, W3 = wq.shape
    FF = w1.shape[1]
    C = 2 * FF + wp.shape[1]
    return pl.pallas_call(
        partial(pack_body, r),
        out_shape=[jax.ShapeDtypeStruct((r + EXTRA, W3), BF), jax.ShapeDtypeStruct((r, C), BF)],
        scratch_shapes=[pltpu.VMEM((EXTRA, W3), F32)],
        name="pack",
        **params(),
    )(wq, vec, b, w1, w2t, wp)


def attend_body(SEQ, SP, TP, D, np_, me_ref, x_ref, *refs):
    H = D // HEAD_DIM
    g = pl.program_id(0)
    j = pl.program_id(1)
    if np_:
        pieces, refs = refs[:np_], refs[np_:]
        qkv_ref, o_ref, l_ref, xi_ref, w_ref, vec_ref, c1_ref, sm = refs[:8]
        refs = refs[8:]
    else:
        w_ref, vec_ref, qkv_ref, o_ref, l_ref, xi_ref = refs[:6]
        refs = refs[6:]
    xs, os_, a_scr, s0, s1, p0, p1 = refs

    @pl.when((g == 0) & (j == 0))
    def _():
        for ref in (a_scr, p0, p1, os_):
            ref[...] = jnp.zeros_like(ref)
        if np_:
            r = pieces[0].shape[0] - EXTRA
            for k in range(np_):
                s = me_ref[0] ^ k
                w_ref[pl.ds(pl.multiple_of(s * r, 16), r), :] = pieces[k][0:r, :]
                sm[s] = pieces[k][r : r + EXTRA, 0 : sm.shape[2]].astype(F32)
            nb = c1_ref.shape[1] // np_
            vec_ref[...] = jnp.concatenate([sm[s, :, 0:r] for s in range(np_)], axis=1)
            c1_ref[...] = jnp.broadcast_to(
                jnp.concatenate([sm[s, 6:7, 0:nb] for s in range(np_)], axis=1), c1_ref.shape
            )

    @pl.when(j == 0)
    def _():
        spread(x_ref, xs, SEQ)

    gain = vec_ref[0:1, :]
    shift = vec_ref[1:2, :]
    ss = (s0, s1)
    pp = (p0, p1)
    st = {}
    S8 = SEQ // 8 * 8

    def ln(i, t, n):
        x = image(xs, j * PAIR + i, t, n)
        xi_ref[i, t : t + n, :] = x.astype(BF)
        xh, _ = norm_rows(x)
        a_scr[i * SP + t : i * SP + t + n, :] = (xh * gain + shift).astype(BF)

    def qkv(i, t, c, w):
        y = dot(a_scr[i * SP : (i + 1) * SP, :], w_ref[:, t * D + c : t * D + c + w])
        if t == 0:
            y = y * (HEAD_DIM**-0.5)
        qkv_ref[i, :, t * D + c : t * D + c + w] = y.astype(BF)

    def score(u):
        i, h = divmod(u, H)
        lo = h * HEAD_DIM
        ss[u % 2][...] = dot(
            qkv_ref[i, :, D + lo : D + lo + HEAD_DIM], qkv_ref[i, :, lo : lo + HEAD_DIM], 1, 1
        )

    def tile(ref, t, n):
        x = ref[t : t + n, :]
        if t + n > SEQ:
            x = jnp.where(lax.broadcasted_iota(jnp.int32, (n, 1), 0) < SEQ - t, x, -1e30)
        return x

    def vmax(u, t, n):
        m = jnp.max(tile(ss[u % 2], t, n).reshape(n // 8, 8, SP), axis=0)
        st[u] = m if t == 0 else jnp.maximum(st[u], m)
        if t + n >= SEQ:
            st[u] = jnp.max(st[u], axis=0, keepdims=True)

    def vexp(u, t, n):
        i, h = divmod(u, H)
        p = jnp.exp(tile(ss[u % 2], t, n) - st[u])
        ss[u % 2][t : t + n, :] = p
        total = jnp.sum(p.reshape(n // 8, 8, SP), axis=0)
        k = ("l", u)
        st[k] = total if t == 0 else st[k] + total
        if t + n >= SEQ:
            total = jnp.sum(st[k], axis=0, keepdims=True)
            l_ref[i, h : h + 1, :] = st[u] + jnp.log(total)
            st[k] = 1.0 / total

    def vnorm(u, t, n):
        pp[u % 2][t : t + n, :] = (ss[u % 2][t : t + n, :] * st[("l", u)]).astype(BF)

    def mix(u):
        i, h = divmod(u, H)
        lo = 2 * D + h * HEAD_DIM
        y = dot(pp[u % 2][...], qkv_ref[i, :, lo : lo + HEAD_DIM], 0, 0)
        if h % 2 == 0:
            st["o"] = y
        else:
            y = jnp.concatenate([st["o"], y], axis=1)
            os_[h // 2, pl.ds(pl.multiple_of((j * PAIR + i) * TP, 8), SEQ), :] = y[:SEQ]

    rows = tiles(SEQ, 48)
    for t, n in rows:
        ln(0, t, n)
    c0 = min(256, D)
    cs = tiles(D, 256)
    weave([partial(qkv, 0, t, 0, c0) for t in range(3)], [partial(ln, 1, t, n) for t, n in rows])
    rest = [partial(qkv, 0, t, c, w) for c, w in cs[1:] for t in range(3)]
    rest += [partial(qkv, 1, t, c, w) for c, w in cs for t in range(3)]
    srows = tiles(S8, 64) + ([(S8, 8)] if S8 < SEQ else [])
    nu = PAIR * H
    score(0)
    done = 0
    for k in range(nu):
        ms = []
        need = 3 if k < 2 else 2
        ms += rest[done : done + need]
        done += need
        if k + 1 < nu:
            ms.append(partial(score, k + 1))
        if k >= 1:
            ms.append(partial(mix, k - 1))
        vs = [partial(f, k, t, n) for f in (vmax, vexp, vnorm) for t, n in srows]
        weave(ms, vs)
    assert done >= len(rest)
    mix(nu - 1)
    for i in range(PAIR):
        xi_ref[i, SEQ:SP, :] = jnp.zeros((SP - SEQ, D), BF)

    @pl.when(j == pl.num_programs(1) - 1)
    def _():
        for t in range(0, TP, 2):
            o_ref[t : t + 2] = tokens(os_, t, TP).astype(BF)


def attend(me, x, pieces, w, vec, FF, TP):
    SEQ, N, D = x.shape
    SP = up(SEQ, 16)
    W3 = 3 * D
    np_ = len(pieces)
    tok = lambda t: pl.BlockSpec((t, GROUP, D), lambda g, j, *_: (0, g, 0))
    img = lambda r, d: pl.BlockSpec((PAIR, r, d), lambda g, j, *_: (g * (GROUP // PAIR) + j, 0, 0))
    v = pltpu.VMEM
    s = jax.ShapeDtypeStruct
    ins = list(pieces) if np_ else [w, vec]
    out_specs = [img(SP, W3), tok(TP), img(8, SP), img(SP, D)]
    out_shape = [s((N, SP, W3), BF), s((TP, N, D), BF), s((N, 8, SP), F32), s((N, SP, D), BF)]
    scratch = [v((D // 128, TP * GROUP, 128), F32)] * 2 + [v((PAIR * SP, D), BF)]
    scratch += [v((SP, SP), F32)] * 2 + [v((SP, SP), BF)] * 2
    if np_:
        out_specs += [whole(D, W3), whole(8, D), whole(8, FF)]
        out_shape += [s((D, W3), BF), s((8, D), F32), s((8, FF), F32)]
        scratch = [v((np_, EXTRA, up(max(FF, D) // np_, 128)), F32)] + scratch
    return pl.pallas_call(
        partial(attend_body, SEQ, SP, TP, D, np_),
        grid_spec=pltpu.PrefetchScalarGridSpec(
            num_scalar_prefetch=1,
            grid=(N // GROUP, GROUP // PAIR),
            in_specs=[tok(SEQ)] + [full(a) for a in ins],
            out_specs=out_specs,
            scratch_shapes=scratch,
        ),
        out_shape=out_shape,
        name="attend",
        **params(20 * 10**9, 25 * 10**6),
    )(me, x, *ins)


def feed_body(SEQ, D, FF, T, N, np_, me_ref, cnt_ref, x_ref, o_ref, cot_ref, c1_ref, vec_ref, *refs):
    s = pl.program_id(0)
    R = T * N
    RT = 2 * N
    HR = R // 2
    if np_:
        pieces, refs = refs[:np_], refs[np_:]
        out_ref, dx1_ref, do_ref, tc1_ref, tv_ref, snd_ref, keep_ref = refs[:7]
        wp_ref, w1_ref, w2t_ref, tp_ref, t1_ref, t2_ref = refs[7:13]
        refs = refs[13:]
    else:
        wp_ref, w1_ref, w2t_ref, out_ref, dx1_ref, do_ref, tc1_ref, tv_ref, tp_ref, t1_ref, t2_ref = refs[:11]
        refs = refs[11:]
    b_scr, bt_scr, dy_scr, dyt_scr, xh_scr, r_scr, x1_scr, u0, u1, d0, d1, g_scr, du_scr, y_scr, db_scr, dx_scr = refs

    @pl.when(s == 0)
    def _():
        for ref in (tp_ref, t1_ref, t2_ref, tc1_ref, tv_ref):
            ref[...] = jnp.zeros_like(ref)
        if np_:
            r = pieces[0].shape[0]
            for k in range(np_):
                at = pl.ds(pl.multiple_of((me_ref[0] ^ k) * r, 16), r)
                w1_ref[at, :] = pieces[k][:, 0:FF]
                w2t_ref[at, :] = pieces[k][:, FF : 2 * FF]
                wp_ref[at, :] = pieces[k][:, 2 * FF :]

    cp = vec_ref[2:3, :]
    g2 = vec_ref[3:4, :]
    e2 = vec_ref[4:5, :]
    c2 = vec_ref[5:6, :]
    io = lax.broadcasted_iota(jnp.int32, (RT, 1), 0)
    real = lax.rem(io, N) < cnt_ref[0]
    lim = SEQ * N - s * R
    acc = {}

    def rows(ref, r):
        return ref[r // N : r // N + 2].reshape(RT, D)

    def add(key, v):
        v = jnp.sum(v.reshape(v.shape[0] // 8, 8, v.shape[1]), axis=0)
        acc[key] = v if key not in acc else acc[key] + v

    def m_proj(h):
        x1_scr[h : h + HR, :] = dot(o_ref[h // N : (h + HR) // N].reshape(HR, D), wp_ref[...])

    def v_norm(r):
        inside = (io + r) < lim
        x = jnp.where(inside, rows(x_ref, r).astype(F32), 0.0)
        dy_scr[r : r + RT, :] = jnp.where(real & inside, rows(cot_ref, r), jnp.zeros((), BF))
        x1 = x + x1_scr[r : r + RT, :] + cp
        x1_scr[r : r + RT, :] = x1 + c2
        xh, rr = norm_rows(x1)
        xh_scr[r : r + RT, :] = xh
        r_scr[r : r + RT, :] = jnp.broadcast_to(rr, (RT, 128))
        b_scr[r : r + RT, :] = (xh * g2 + e2).astype(BF)

    cols = tiles(FF, 256)
    us = (u0, u1)
    ds = (d0, d1)

    def m_u(i, h):
        c, w = cols[i]
        us[i % 2][h : h + HR, :w] = dot(b_scr[h : h + HR, :], w1_ref[:, c : c + w]) + c1_ref[0:1, c : c + w]

    def m_d(i, h):
        c, w = cols[i]
        ds[i % 2][h : h + HR, :w] = dot(dy_scr[h : h + HR, :], w2t_ref[:, c : c + w])

    def v_gelu(i, r):
        c, w = cols[i]
        ga, dg = gelu_pair(us[i % 2][r : r + 16, :w])
        g_scr[r : r + 16, c : c + w] = ga.astype(BF)
        du = ds[i % 2][r : r + 16, :w] * dg
        du_scr[r : r + 16, c : c + w] = du.astype(BF)
        add(("c1", i), du)

    def m_t1(i):
        c, w = cols[i]
        t1_ref[:, c : c + w] += dot(bt_scr[...], du_scr[:, c : c + w])

    def m_t2(i):
        c, w = cols[i]
        t2_ref[:, c : c + w] += dot(dyt_scr[...], g_scr[:, c : c + w])

    def m_y(h):
        y_scr[h : h + HR, :] = dot(g_scr[h : h + HR, :], w2t_ref[...], 1, 1)

    def m_db(h):
        db_scr[h : h + HR, :] = dot(du_scr[h : h + HR, :], w1_ref[...], 1, 1)

    def v_out(r):
        y = x1_scr[r : r + RT, :] + y_scr[r : r + RT, :]
        out_ref[r // N : r // N + 2] = jnp.where(real, y, 0.0).astype(BF).reshape(2, N, D)

    def v_back(r):
        db = db_scr[r : r + RT, :]
        xh = xh_scr[r : r + RT, :]
        dyf = dy_scr[r : r + RT, :].astype(F32)
        dxh = db * g2
        mean1 = jnp.mean(dxh, axis=-1, keepdims=True)
        mean2 = jnp.mean(dxh * xh, axis=-1, keepdims=True)
        dx = dyf + r_scr[r : r + RT, 0:1] * (dxh - mean1 - xh * mean2)
        add("g2", db * xh)
        add("e2", db)
        add("c2", dyf)
        add("cp", dx)
        dx1_ref[r // N : r // N + 2] = dx.reshape(2, N, D)
        dx_scr[r : r + RT, :] = dx.astype(BF)

    def m_do(h):
        y = dot(dx_scr[h : h + HR, :], wp_ref[...], 1, 1)
        do_ref[h // N : (h + HR) // N] = y.astype(BF).reshape(HR // N, N, D)

    def m_tp():
        tp_ref[...] += dot(o_ref[...].reshape(R, D), dx_scr[...], 0, 0)

    first = list(range(0, HR, RT))
    second = list(range(HR, R, RT))
    last = len(cols) - 1
    m_proj(0)
    weave([partial(m_proj, HR)], [partial(v_norm, r) for r in first])
    weave([partial(m_u, 0, 0), partial(m_d, 0, 0)], [partial(v_norm, r) for r in second])
    bt_scr[...] = b_scr[...].T
    dyt_scr[...] = dy_scr[...].T
    m_u(0, HR)
    m_d(0, HR)
    for i in range(len(cols)):
        ms = []
        if i < last:
            ms += [partial(f, i + 1, h) for f in (m_u, m_d) for h in (0, HR)]
        if i >= 1:
            ms += [partial(m_t1, i - 1), partial(m_t2, i - 1)]
        weave(ms, [partial(v_gelu, i, r) for r in range(0, R, 16)])
        c, w = cols[i]
        tc1_ref[:, c : c + w] += acc[("c1", i)]
    m_db(0)
    weave([partial(m_db, HR)], [partial(v_back, r) for r in first])
    weave([partial(m_y, 0), partial(m_do, 0)], [partial(v_back, r) for r in second])
    weave([partial(m_y, HR), partial(m_do, HR)], [partial(v_out, r) for r in first])
    weave([partial(m_t1, last), partial(m_t2, last), m_tp], [partial(v_out, r) for r in second])
    for i, k in ((2, "cp"), (3, "g2"), (4, "e2"), (5, "c2")):
        tv_ref[i * 8 : i * 8 + 8, :] += acc[k]

    if np_:

        @pl.when(s == pl.num_programs(0) - 1)
        def _():
            r = D // np_
            for k in range(0, np_, 2):
                for ref, flip in ((keep_ref, 0), (snd_ref, 1)):
                    at = pl.ds(pl.multiple_of((me_ref[0] ^ (k + flip)) * r, 16), r)
                    ref[k // 2, :, 0:FF] = t1_ref[at, :].astype(ref.dtype)
                    ref[k // 2, :, FF : 2 * FF] = t2_ref[at, :].astype(ref.dtype)
                    ref[k // 2, :, 2 * FF :] = tp_ref[at, :].astype(ref.dtype)


def feed(me, cnt, x, o, cot, c1, vec, pieces, weights, T):
    SEQ, N, D = x.shape
    TP = o.shape[0]
    FF = c1.shape[1]
    np_ = len(pieces)
    R = T * N
    v = pltpu.VMEM
    s = jax.ShapeDtypeStruct
    blk = pl.BlockSpec((T, N, D), lambda i, *_: (i, 0, 0))
    ins = list(pieces) if np_ else list(weights)
    out_specs = [blk, blk, blk, whole(8, FF), whole(64, D)]
    out_shape = [s((SEQ, N, D), BF), s((TP, N, D), F32), s((TP, N, D), BF), s((8, FF), F32), s((64, D), F32)]
    scratch = []
    if np_:
        shape = (np_ // 2, D // np_, 2 * FF + D)
        out_specs += [whole(*shape)] * 2
        out_shape += [s(shape, BF), s(shape, F32)]
        scratch += [v((D, D), BF), v((D, FF), BF), v((D, FF), BF), v((D, D), F32), v((D, FF), F32), v((D, FF), F32)]
    else:
        out_specs += [whole(D, D), whole(D, FF), whole(D, FF)]
        out_shape += [s((D, D), F32), s((D, FF), F32), s((D, FF), F32)]
    scratch += [v((R, D), BF), v((D, R), BF), v((R, D), BF), v((D, R), BF), v((R, D), F32), v((R, 128), F32), v((R, D), F32)]
    scratch += [v((R, 256), F32)] * 4 + [v((R, FF), BF)] * 2 + [v((R, D), F32)] * 2 + [v((R, D), BF)]
    return pl.pallas_call(
        partial(feed_body, SEQ, D, FF, T, N, np_),
        grid_spec=pltpu.PrefetchScalarGridSpec(
            num_scalar_prefetch=2,
            grid=(TP // T,),
            in_specs=[blk, blk, blk, full(c1), full(vec)] + [full(a) for a in ins],
            out_specs=out_specs,
            scratch_shapes=scratch,
        ),
        out_shape=out_shape,
        name="feed",
        **params(45 * 10**9, 30 * 10**6),
    )(me, cnt, x, o, cot, c1, vec, *ins)


def back_body(SEQ, SP, TP, D, FF, np_, me_ref, xi_ref, qkv_ref, l_ref, do_ref, dx1_ref, w_ref, vec_ref, tc1_ref, tv2_ref, gi_ref, *refs):
    if np_:
        snd_ref, keep_ref, tq_ref, sm = refs[:4]
        gv_ref, refs = refs[4], refs[5:]
    else:
        tq_ref, gv_ref, refs = refs[0], refs[1], refs[2:]
    dos, gs, dob, a_scr, at_scr, xh_scr, r_scr, d_scr, da_scr, tv_ref, s0, s1, e0, e1, p0, p1, q0, q1 = refs
    H = D // HEAD_DIM
    W3 = 3 * D
    g = pl.program_id(0)
    j = pl.program_id(1)

    @pl.when((g == 0) & (j == 0))
    def _():
        for ref in (d_scr, p0, p1, q0, q1, dob, tq_ref, tv_ref):
            ref[...] = jnp.zeros_like(ref)

    @pl.when(j == 0)
    def _():
        spread(do_ref, dos, SEQ)

    gain = vec_ref[0:1, :]
    shift = vec_ref[1:2, :]
    ss = (s0, s1)
    es = (e0, e1)
    pp = (p0, p1)
    qq = (q0, q1)
    st = {}
    S8 = SEQ // 8 * 8

    def load(i, t, n):
        dob[i * SP + t : i * SP + t + n, :] = image(dos, j * PAIR + i, t, n).astype(BF)

    def ln(i, t, n):
        xh, r = norm_rows(xi_ref[i, t : t + n, :].astype(F32))
        at = slice(i * SP + t, i * SP + t + n)
        xh_scr[at, :] = xh
        r_scr[at, :] = jnp.broadcast_to(r, (n, 128))
        a_scr[at, :] = (xh * gain + shift).astype(BF)

    def part(i, h, t):
        lo = t * D + h * HEAD_DIM
        return qkv_ref[i, :, lo : lo + HEAD_DIM]

    def dpart(i, h):
        return dob[i * SP : (i + 1) * SP, h * HEAD_DIM : (h + 1) * HEAD_DIM]

    def score(u):
        i, h = divmod(u, H)
        ss[u % 2][...] = dot(part(i, h, 1), part(i, h, 0), 1, 1)

    def dprob(u):
        i, h = divmod(u, H)
        es[u % 2][...] = dot(part(i, h, 2), dpart(i, h), 1, 1)

    def v_prob(u, t, n):
        i, h = divmod(u, H)
        p = jnp.exp(ss[u % 2][t : t + n, :] - l_ref[i, h : h + 1, :])
        if t + n > SEQ:
            p = jnp.where(lax.broadcasted_iota(jnp.int32, (n, 1), 0) < SEQ - t, p, 0.0)
        ss[u % 2][t : t + n, :] = p
        pp[u % 2][t : t + n, :] = p.astype(BF)
        x = jnp.sum((p * es[u % 2][t : t + n, :]).reshape(n // 8, 8, SP), axis=0)
        st[u] = x if t == 0 else st[u] + x
        if t + n >= SEQ:
            st[u] = jnp.sum(st[u], axis=0, keepdims=True)

    def v_ds(u, t, n):
        qq[u % 2][t : t + n, :] = (ss[u % 2][t : t + n, :] * (es[u % 2][t : t + n, :] - st[u])).astype(BF)

    def put(u, t, y):
        i, h = divmod(u, H)
        if h % 2 == 0:
            st[("d", t)] = y
        else:
            y = jnp.concatenate([st[("d", t)], y], axis=1).astype(BF)
            lo = t * D + (h - 1) * HEAD_DIM
            d_scr[i * SP : i * SP + SEQ, lo : lo + 2 * HEAD_DIM] = y[:SEQ]

    def m_dv(u):
        put(u, 2, dot(pp[u % 2][...], dpart(*divmod(u, H))))

    def m_dk(u):
        i, h = divmod(u, H)
        put(u, 1, dot(qq[u % 2][...], part(i, h, 0)))

    def m_dq(u):
        i, h = divmod(u, H)
        put(u, 0, dot(qq[u % 2][...], part(i, h, 1), 0, 0) * (HEAD_DIM**-0.5))

    rows = tiles(SEQ, 48)
    srows = tiles(S8, 64) + ([(S8, 8)] if S8 < SEQ else [])
    for t, n in rows:
        load(0, t, n)
    pre = [partial(load, 1, t, n) for t, n in rows] + [partial(ln, i, t, n) for i in range(PAIR) for t, n in rows]
    nu = PAIR * H
    score(0)
    dprob(0)
    for k in range(nu):
        ms = []
        if k + 1 < nu:
            ms += [partial(score, k + 1), partial(dprob, k + 1)]
        if k >= 1:
            ms += [partial(m_dv, k - 1), partial(m_dk, k - 1), partial(m_dq, k - 1)]
        vs = [partial(f, k, t, n) for f in (v_prob, v_ds) for t, n in srows]
        vs += pre[3 * k : 3 * k + 3]
        weave(ms, vs)
    assert 3 * nu >= len(pre)
    m_dv(nu - 1)
    m_dk(nu - 1)
    m_dq(nu - 1)
    acc = {}

    def m_da(i):
        da_scr[i * SP : (i + 1) * SP, :] = dot(d_scr[i * SP : (i + 1) * SP, :], w_ref[...], 1, 1)

    def m_tq(c, w):
        tq_ref[:, c : c + w] += dot(at_scr[...], d_scr[:, c : c + w])

    def add(key, v):
        f = v.shape[0] // 8 * 8
        if f:
            x = jnp.sum(v[:f].reshape(f // 8, 8, D), axis=0)
            acc[key] = x if key not in acc else acc[key] + x
        if f < v.shape[0]:
            x = jnp.sum(v[f:], axis=0, keepdims=True)
            key = key + "tail"
            acc[key] = x if key not in acc else acc[key] + x

    def v_back(i, t, n):
        at = slice(i * SP + t, i * SP + t + n)
        d = da_scr[at, :]
        xh = xh_scr[at, :]
        dxh = d * gain
        mean1 = jnp.mean(dxh, axis=-1, keepdims=True)
        mean2 = jnp.mean(dxh * xh, axis=-1, keepdims=True)
        y = r_scr[at, 0:1] * (dxh - mean1 - xh * mean2)
        for c in range(gs.shape[0]):
            gs[c, pl.ds(pl.multiple_of((j * PAIR + i) * TP + t, 8), n), :] = y[:, c * 128 : (c + 1) * 128]
        add("g", d * xh)
        add("e", d)

    at_scr[...] = a_scr[...].T
    cols = tiles(W3, 256)
    m_da(0)
    weave([partial(m_da, 1)] + [partial(m_tq, c, w) for c, w in cols[:2]], [partial(v_back, 0, t, n) for t, n in rows])
    weave([partial(m_tq, c, w) for c, w in cols[2:]], [partial(v_back, 1, t, n) for t, n in rows])
    tv_ref[0:8, :] += acc["g"]
    tv_ref[8:16, :] += acc["e"]
    if "gtail" in acc:
        tv_ref[0:1, :] += acc["gtail"]
        tv_ref[8:9, :] += acc["etail"]

    @pl.when(j == pl.num_programs(1) - 1)
    def _():
        for t in range(0, SEQ - 1, 2):
            gi_ref[t : t + 2] = (tokens(gs, t, TP) + dx1_ref[t : t + 2]).astype(BF)
        if SEQ % 2:
            gi_ref[SEQ - 1] = (token(gs, SEQ - 1, TP) + dx1_ref[SEQ - 1]).astype(BF)

    @pl.when((j == pl.num_programs(1) - 1) & (g == pl.num_programs(0) - 1))
    def _():
        for i in range(2):
            gv_ref[i : i + 1, :] = jnp.sum(tv_ref[8 * i : 8 * i + 8, :], axis=0, keepdims=True)
        for i in range(2, 6):
            gv_ref[i : i + 1, :] = jnp.sum(tv2_ref[8 * i : 8 * i + 8, :], axis=0, keepdims=True)
        if np_:
            r = D // np_
            nb = FF // np_
            sm[...] = jnp.zeros_like(sm)
            bias = jnp.sum(tc1_ref[...], axis=0, keepdims=True)
            for s in range(np_):
                sm[s, 0:6, 0:r] = gv_ref[0:6, s * r : (s + 1) * r]
                sm[s, 6:7, 0:nb] = bias[:, s * nb : (s + 1) * nb]
            wide = sm.shape[2]
            for k in range(0, np_, 2):
                for ref, flip in ((keep_ref, 0), (snd_ref, 1)):
                    s = me_ref[0] ^ (k + flip)
                    ref[k // 2, 0:r, :] = tq_ref[pl.ds(pl.multiple_of(s * r, 16), r), :].astype(ref.dtype)
                    ref[k // 2, r : r + EXTRA, 0:wide] = sm[s].astype(ref.dtype)
                    ref[k // 2, r : r + EXTRA, wide:] = jnp.zeros((EXTRA, W3 - wide), ref.dtype)


def back(me, xi, qkv, l, do, dx1, w, vec, tc1, tv2, SEQ, np_):
    N, SP, D = xi.shape
    TP = do.shape[0]
    W3 = 3 * D
    FF = tc1.shape[1]
    R = PAIR * SP
    tok = lambda t: pl.BlockSpec((t, GROUP, D), lambda g, j, *_: (0, g, 0))
    img = lambda r, d: pl.BlockSpec((PAIR, r, d), lambda g, j, *_: (g * (GROUP // PAIR) + j, 0, 0))
    v = pltpu.VMEM
    s = jax.ShapeDtypeStruct
    out_specs = [tok(SEQ)]
    out_shape = [s((SEQ, N, D), BF)]
    if np_:
        shape = (np_ // 2, D // np_ + EXTRA, W3)
        out_specs += [whole(*shape)] * 2
        out_shape += [s(shape, BF), s(shape, F32)]
        scratch = [v((D, W3), F32), v((np_, EXTRA, up(max(FF, D) // np_, 128)), F32), v((8, D), F32)]
    else:
        out_specs += [whole(D, W3), whole(8, D)]
        out_shape += [s((D, W3), F32), s((8, D), F32)]
        scratch = []
    scratch += [v((D // 128, TP * GROUP, 128), F32)] * 2
    scratch += [v((R, D), BF), v((R, D), BF), v((D, R), BF), v((R, D), F32), v((R, 128), F32), v((R, W3), BF), v((R, D), F32)]
    scratch += [v((16, D), F32)] + [v((SP, SP), F32)] * 4 + [v((SP, SP), BF)] * 4
    return pl.pallas_call(
        partial(back_body, SEQ, SP, TP, D, FF, np_),
        grid_spec=pltpu.PrefetchScalarGridSpec(
            num_scalar_prefetch=1,
            grid=(N // GROUP, GROUP // PAIR),
            in_specs=[img(SP, D), img(SP, W3), img(8, SP), tok(TP), tok(TP), full(w), full(vec), full(tc1), full(tv2)],
            out_specs=out_specs,
            scratch_shapes=scratch,
        ),
        out_shape=out_shape,
        name="back",
        **params(40 * 10**9, 30 * 10**6),
    )(me, xi, qkv, l, do, dx1, w, vec, tc1, tv2)


def adam_body(na, nb_, slots, FF, flag_ref, gid_ref, scale_ref, *refs):
    pa, refs = refs[:na], refs[na:]
    pb, refs = refs[:nb_], refs[nb_:]
    weights, firsts, seconds = refs[:6], refs[6:12], refs[12:18]
    outs = refs[18:]

    def total(ps, rows, cols):
        xs = [p[rows, cols].astype(F32) for p in ps]
        return xs[0] if len(xs) == 1 else (xs[0] + xs[1]) + (xs[2] + xs[3])

    r = weights[0].shape[0]
    D = weights[1].shape[1]
    every = slice(0, r)
    where = (
        (pa, every, slice(0, 3 * D)),
        (pb, every, slice(2 * FF, 2 * FF + D)),
        (pb, every, slice(0, FF)),
        (pb, every, slice(FF, 2 * FF)),
        (pa, slice(r + 6, r + 7), slice(0, weights[4].shape[1])),
        (pa, slice(r, r + 6), slice(0, weights[5].shape[1])),
    )
    for p, (ps, rows, cols) in enumerate(where):
        grad = total(ps, rows, cols) / slots
        flag = flag_ref[p].astype(F32)
        lr = scale_ref[gid_ref[p]]
        first = BETA_ONE * firsts[p][...] + (1.0 - BETA_ONE) * grad
        second = BETA_TWO * seconds[p][...] + (1.0 - BETA_TWO) * grad * grad
        direction = first / (1.0 - BETA_ONE**ADAM_STEPS) / (jnp.sqrt(second / (1.0 - BETA_TWO**ADAM_STEPS)) + ADAM_EPS)
        weight = weights[p][...]
        outs[p][...] = grad
        outs[6 + p][...] = weight - LEARN_RATE * lr * (direction + DECAY_RATE * flag * weight)
        outs[12 + p][...] = first
        outs[18 + p][...] = second


def adam(flags, gids, scales, pa, pb, weights, firsts, seconds, slots, FF):
    smem = pl.BlockSpec(memory_space=pltpu.SMEM)
    vmem = pl.BlockSpec(memory_space=pltpu.VMEM)
    shapes = [jax.ShapeDtypeStruct(w.shape, F32) for w in weights]
    count = len(pa) + len(pb) + 18
    return pl.pallas_call(
        partial(adam_body, len(pa), len(pb), slots, FF),
        in_specs=[smem] * 3 + [vmem] * count,
        out_specs=[vmem] * 24,
        out_shape=shapes * 4,
        name="adam",
        **params(),
    )(flags, gids, scales, *pa, *pb, *weights, *firsts, *seconds)


def pairs(n, k):
    return [(i, i ^ k) for i in range(n)]


def fetch(x, n):
    pieces = [None] * n
    pieces[0] = x
    for k in range(2, n, 2):
        pieces[k] = lax.ppermute(x, "fsdp", pairs(n, k))
    for k in range(0, n, 2):
        pieces[k + 1] = lax.ppermute(pieces[k], "fsdp", pairs(n, 1))
    return pieces


def halve(snd, keep, n):
    h = keep + lax.ppermute(snd, "fsdp", pairs(n, 1)).astype(F32)
    got = [lax.ppermute(h[k].astype(BF), "fsdp", pairs(n, 2 * k)) for k in range(1, n // 2)]
    return h[0], got


def finish(own, got, d):
    for piece in got:
        own = own + piece.astype(F32)
    b = own.astype(BF)
    return [b] + [lax.ppermute(b, "dp", pairs(d, k)) for k in range(1, d)]


def local(
    images, cotangent, counts,
    w_qkv, w_proj, w_fc1, w_fc2, b_fc1, vectors,
    m_qkv, m_proj, m_fc1, m_fc2, m_bias1, m_vectors,
    v_qkv, v_proj, v_fc1, v_fc2, v_bias1, v_vectors,
    decay_flags, group_ids, group_scales,
):
    n = lax.axis_size("fsdp")
    d = lax.axis_size("dp")
    N, SEQ, D = images.shape
    r = w_qkv.shape[0]
    FF = w_fc1.shape[1]
    T = 20
    TP = up(SEQ, T)
    direct = n in (2, 4, 8) and d == 4 and r % 16 == 0
    x = jnp.transpose(images, (1, 0, 2))
    cot = jnp.transpose(cotangent, (1, 0, 2))
    me = lax.axis_index("fsdp").astype(jnp.int32).reshape(1)
    rows = lambda b: b.reshape(1, -1)
    weights = [w_qkv, w_proj, w_fc1, w_fc2.T, rows(b_fc1), vectors]
    firsts = [m_qkv, m_proj, m_fc1, m_fc2.T, rows(m_bias1), m_vectors]
    seconds = [v_qkv, v_proj, v_fc1, v_fc2.T, rows(v_bias1), v_vectors]
    pack_a, pack_b = pack(weights[0], weights[5], weights[4], weights[2], weights[3], weights[1])
    if direct:
        pieces_a = fetch(pack_a, n)
        pack_b = lax.optimization_barrier((pack_b, pieces_a))[0]
        pieces_b = fetch(pack_b, n)
        qkv, o, logs, xi, wq, vec, c1 = attend(me, x, pieces_a, None, None, FF, TP)
        out, dx1, do, tc1, tv2, snd, keep = feed(me, counts, x, o, cot, c1, vec, pieces_b, (), T)
        own_b, got_b = halve(snd, keep, n)
        do, got0 = lax.optimization_barrier((do, own_b))
        gi, snd, keep = back(me, xi, qkv, logs, do, dx1, wq, vec, tc1, tv2, SEQ, n)
        pb = finish(own_b, got_b, d)
        own_a, got_a = halve(snd, keep, n)
        pa = finish(own_a, got_a, d)
    else:
        all_a = lax.all_gather(pack_a, "fsdp", axis=0, tiled=False)
        all_b = lax.all_gather(pack_b, "fsdp", axis=0, tiled=True)
        wq = all_a[:, :r].reshape(D, 3 * D)
        nb = FF // n
        vec = jnp.transpose(all_a[:, r : r + 8, :r], (1, 0, 2)).reshape(8, D).astype(F32)
        c1 = jnp.broadcast_to(all_a[:, r + 6, :nb].reshape(1, FF), (8, FF)).astype(F32)
        ws = (all_b[:, 2 * FF :], all_b[:, :FF], all_b[:, FF : 2 * FF])
        qkv, o, logs, xi = attend(me, x, (), wq, vec, FF, TP)
        out, dx1, do, tc1, tv2, tp, t1, t2 = feed(me, counts, x, o, cot, c1, vec, (), ws, T)
        gi, tq, gv = back(me, xi, qkv, logs, do, dx1, wq, vec, tc1, tv2, SEQ, 0)
        share = lambda g, axis: lax.psum(
            lax.psum_scatter(g, "fsdp", scatter_dimension=axis, tiled=True).astype(BF), "dp"
        ).astype(F32)
        pb = [share(jnp.concatenate([t1, t2, tp], axis=1), 0)]
        small = jnp.zeros((8, 3 * D), F32).at[:6, :r].set(share(gv[:6], 1))
        small = small.at[6, :nb].set(share(jnp.sum(tc1, axis=0), 0))
        pa = [jnp.concatenate([share(tq, 0), small], axis=0)]
    res = adam(decay_flags, group_ids, group_scales, pa, pb, weights, firsts, seconds, float(N * n * d), FF)
    res = list(res)
    for k in range(4):
        res[6 * k + 3] = res[6 * k + 3].T
        res[6 * k + 4] = res[6 * k + 4].reshape(-1)
    return (jnp.transpose(out, (1, 0, 2)), jnp.transpose(gi, (1, 0, 2)), *res)


def solution(mesh):
    P = PartitionSpec
    both = ("dp", "fsdp")
    six = (P("fsdp", None), P("fsdp", None), P("fsdp", None), P(None, "fsdp"), P("fsdp"), P(None, "fsdp"))
    data = (P(both, None, None), P(both, None, None))
    return jax.shard_map(
        local,
        mesh=mesh,
        in_specs=(*data, P(both), *six, *six, *six, P(), P(), P()),
        out_specs=(*data, *six, *six, *six, *six),
        check_vma=False,
    )
```

time: 930 us -> 259 us (0.28)
  matrix products: 425 us -> 0 us
  local copies, waits for them, and re-layouts: 204 us -> 1.95 us
  Pallas kernels: 0 us -> 156 us
  blocking collectives: 126 us -> 0 us
  other arithmetic: 85.5 us -> 1.75 us
  starting transfers between devices: 0.71 us -> 27.8 us
  between operations: 25.3 us -> 1.8 us
  waiting for transfers between devices: 54.1 us -> 69.6 us
    dot_general x54 -> x0, matrix products: 425 us -> none  [the longest x6 61 us: attend_back(): jnp.einsum('bhqk,bkhd->bqhd', grad_scores, keys_in, preferred_element_typ...]
    pallas_call x0 -> x5, Pallas kernels: none -> 156 us  [the longest x1 63.4 us: feed(): pl.pallas_call(partial(feed_body, SEQ, D, FF, T, N, np_), grid_spec=pltpu...]
    all_gather x5 -> x0, blocking collectives: 77.3 us -> none  [the longest x1 16.7 us: local(): lax.all_gather(lowered[3], 'fsdp', axis=1, tiled=True)]
    ppermute x0 -> x28, waiting for transfers between devices: none -> 69.6 us  [the longest x6 29.9 us: fetch(): pieces[k] = lax.ppermute(x, 'fsdp', pairs(n, k))]
    convert_element_type x7 -> x2, local copies, waits for them, and re-layouts: 55.3 us -> 0.09 us  [halve(): h[k].astype(BF)]
    reshape x9 -> x0, local copies, waits for them, and re-layouts: 52.8 us -> none  [the longest x1 27.4 us: local(): packed = packed.reshape(count_img, seq_len, 3, head_count, head_size)]
    reduce_sum x14 -> x0, other arithmetic: 50.8 us -> none  [the longest x3 22.9 us: norm_affine(): centre = inputs - jnp.mean(inputs, axis=-1, keepdims=True)]
    psum x1 -> x0, waiting for transfers between devices: 44.3 us -> none  [local(): lax.psum(shares[0].astype(jnp.bfloat16), 'dp').astype(jnp.float32)]
  transfers between devices with their start and end apart: 6 -> 28, of which waited for: 2 -> 13; matrix products, arithmetic and copies ran while one was open for 13% -> 1% of each run, Pallas kernels for 0% -> 13%
where the time goes in v2:
time: 259 us
  Pallas kernels  156 us (60%)
  waiting for transfers between devices  69.6 us (27%)
  starting transfers between devices  27.8 us (11%)
    pallas_call x1, Pallas kernels, feed(): pl.pallas_call(partial(feed_body, SEQ, D, FF, T, N, np_), grid_spec=pltpu...  63.4 us
    pallas_call x1, Pallas kernels, back(): pl.pallas_call(partial(back_body, SEQ, SP, TP, D, FF, np_), grid_spec=plt...  52.3 us
    pallas_call x1, Pallas kernels, attend(): pl.pallas_call(partial(attend_body, SEQ, SP, TP, D, np_), grid_spec=pltpu...  34.6 us
    ppermute x6, waiting for transfers between devices, fetch(): pieces[k] = lax.ppermute(x, 'fsdp', pairs(n, k))  29.9 us
    ppermute x6, waiting for transfers between devices, halve(): lax.ppermute(h[k].astype(BF), 'fsdp', pairs(n, 2 * k))  27.2 us
    ppermute x6, starting transfers between devices, fetch(): pieces[k] = lax.ppermute(x, 'fsdp', pairs(n, k))  10 us
    ppermute x6, waiting for transfers between devices, finish(): return [b] + [lax.ppermute(b, 'dp', pairs(d, k)) for k in range(1, d)]  9.91 us
    ppermute x6, starting transfers between devices, finish(): return [b] + [lax.ppermute(b, 'dp', pairs(d, k)) for k in range(1, d)]  9.07 us
  transfers between devices with their start and end apart: 28, of which 13 were waited for; matrix products, arithmetic and copies ran while one was open for 1% of the time, Pallas kernels for 13%

profile of v2, /device:TPU:0, one launch (start us, length us, event | category | flops | bytes accessed | tf_op | source)
XLA Modules:
  0.0 259.2 jit_solution(13889048504827902176)
XLA Ops:
  0.7 2.0 pack.1
  2.7 5.0 %collective-permute-start.5 = (bf16[56,1152]{1,0:T(8,128)(2,1)}, bf16[56,1152]{1,0:T(8,128)(2,1)S(1)}, u32[]{:S(2)}, u32[]{:S(2)}) collective-permute-start(bf16[56,1152]{1,0:T(8,128)(2,1)} %get-tuple-element.71.refs_0_), channel_id=1, source_target_pairs={{0,6},{1,7},{2,4},{3,5},{4,2},{5,3},{6,0},{7,1},{8,14},{9,15},{10,... | collective-permute-start | bytes 387080 | tf_op jit(solution)/shard_map/ppermute | solution.py:765
  7.7 0.6 collective-permute-start.1
  8.3 4.0 %collective-permute-done.5.refs_6_ = bf16[56,1152]{1,0:T(8,128)(2,1)S(1)} collective-permute-done((bf16[56,1152]{1,0:T(8,128)(2,1)}, bf16[56,1152]{1,0:T(8,128)(2,1)S(1)}, u32[]{:S(2)}, u32[]{:S(2)}) %collective-permute-start.5) | collective-permute-done | bytes 129056 | tf_op jit(solution)/shard_map/ppermute | solution.py:765
  12.3 6.5 %collective-permute-done.3.refs_4_ = bf16[56,1152]{1,0:T(8,128)(2,1)S(1)} collective-permute-done((bf16[56,1152]{1,0:T(8,128)(2,1)}, bf16[56,1152]{1,0:T(8,128)(2,1)S(1)}, u32[]{:S(2)}, u32[]{:S(2)}) %collective-permute-start.3) | collective-permute-done | bytes 129056 | tf_op jit(solution)/shard_map/ppermute | solution.py:765
  18.9 0.5 collective-permute-start.2
  19.4 0.8 collective-permute-done.4.refs_5_
  20.2 0.2 collective-permute-done.2.refs_3_
  20.4 2.5 collective-permute-start.12
  22.8 1.9 collective-permute-start.8
  25.5 6.1 %collective-permute-done.12.refs_6_ = bf16[48,2688]{1,0:T(8,128)(2,1)S(1)} collective-permute-done((bf16[48,2688]{1,0:T(8,128)(2,1)}, bf16[48,2688]{1,0:T(8,128)(2,1)S(1)}, u32[]{:S(2)}, u32[]{:S(2)}) %collective-permute-start.12) | collective-permute-done | bytes 258080 | tf_op jit(solution)/shard_map/ppermute | solution.py:765
  31.6 13.3 %collective-permute-done.10.refs_4_ = bf16[48,2688]{1,0:T(8,128)(2,1)S(1)} collective-permute-done((bf16[48,2688]{1,0:T(8,128)(2,1)}, bf16[48,2688]{1,0:T(8,128)(2,1)S(1)}, u32[]{:S(2)}, u32[]{:S(2)}) %collective-permute-start.10) | collective-permute-done | bytes 258080 | tf_op jit(solution)/shard_map/ppermute | solution.py:765
  44.8 0.5 collective-permute-start.9
  45.4 34.6 %attend.1 = (bf16[24,208,1152]{2,1,0:T(8,128)(2,1)}, bf16[200,24,384]{2,1,0:T(8,128)(2,1)}, f32[24,8,208]{2,1,0:T(8,128)}, bf16[24,208,384]{2,1,0:T(8,128)(2,1)}...) custom-call(s32[1]{0:T(128)} %bitcast.me_ref, bf16[197,24,384]{2,1,0:T(8,128)(2,1)} %bitcast.53, ...), custom_call_target="tpu_custom_call" | custom-call | flops 20000000000 | bytes 25000000 | tf_op jit(solution)/shard_map/attend/pallas_call | solution.py:275
  80.1 0.6 copy-done.13
  80.7 0.1 copy-done.14
  80.8 0.1 copy-done.15
  80.9 0.1 copy-done.16
  81.0 63.4 %feed.1 = (bf16[197,24,384]{2,1,0:T(8,128)(2,1)}, f32[200,24,384]{2,1,0:T(8,128)}, bf16[200,24,384]{2,1,0:T(8,128)(2,1)}, f32[8,1152]{1,0:T(8,128)}, f32[64,384]...) custom-call(s32[1]{0:T(128)} %bitcast.me_ref, s32[1]{0:T(128)S(6)} %copy.50.cnt_ref, ...), custom_call_target="tpu_custom_call" | custom-call | flops 44999999488 | bytes 30000000 | tf_op jit(solution)/shard_map/feed/pallas_call | solution.py:470
  144.4 52.3 %back.1 = (bf16[197,24,384]{2,1,0:T(8,128)(2,1)}, bf16[4,56,1152]{2,1,0:T(8,128)(2,1)}, f32[4,56,1152]{2,1,0:T(8,128)}) custom-call(s32[1]{0:T(128)} %bitcast.me_ref, bf16[24,208,384]{2,1,0:T(8,128)(2,1)} %get-tuple-element.78.xi_ref, bf16[24,208,1152]{2,1,0:T(8,128)(2,1)} %get-tuple-element.79.qkv_ref, f32[24,8,208]{2,1,0:T(8,128)} %get-tuple-element.80.l_ref, ...), custom_call_target="tpu_custom_call" | custom-call | flops 40000000000 | bytes 30000000 | tf_op jit(solution)/shard_map/back/pallas_call | solution.py:692
  196.7 0.1 collective-permute-start.15
  196.8 0.4 collective-permute-start.14
  197.2 1.6 collective-permute-done.15
  198.8 1.3 fusion.5
  200.3 1.9 collective-permute-start.18
  202.2 1.6 collective-permute-start.17
  203.8 0.2 fusion.4
  204.1 1.0 collective-permute-start.22
  205.1 1.8 collective-permute-start.24
  207.0 0.7 collective-permute-start.23
  207.6 1.6 collective-permute-done.18
  209.2 7.2 %collective-permute-done.17 = bf16[56,1152]{1,0:T(8,128)(2,1)S(1)} collective-permute-done((bf16[56,1152]{1,0:T(8,128)(2,1)S(1)}, bf16[56,1152]{1,0:T(8,128)(2,1)S(1)}, u32[]{:S(2)}, u32[]{:S(2)}) %collective-permute-start.17) | collective-permute-done | bytes 129056 | tf_op jit(solution)/shard_map/ppermute | solution.py:773
  216.5 2.5 collective-permute-start.21
  219.0 4.1 %collective-permute-done.24 = bf16[48,2688]{1,0:T(8,128)(2,1)S(1)} collective-permute-done((bf16[48,2688]{1,0:T(8,128)(2,1)S(1)}, bf16[48,2688]{1,0:T(8,128)(2,1)S(1)}, u32[]{:S(2)}, u32[]{:S(2)}) %collective-permute-start.24) | collective-permute-done | bytes 258080 | tf_op jit(solution)/shard_map/ppermute | solution.py:773
  223.1 14.3 %collective-permute-done.23 = bf16[48,2688]{1,0:T(8,128)(2,1)S(1)} collective-permute-done((bf16[48,2688]{1,0:T(8,128)(2,1)S(1)}, bf16[48,2688]{1,0:T(8,128)(2,1)S(1)}, u32[]{:S(2)}, u32[]{:S(2)}) %collective-permute-start.23) | collective-permute-done | bytes 258080 | tf_op jit(solution)/shard_map/ppermute | solution.py:773
  237.4 0.1 add_convert_fusion.refs_4_
  237.5 2.5 collective-permute-start.27
  240.0 0.5 collective-permute-start.26
  240.6 0.5 collective-permute-start.25
  241.1 1.5 collective-permute-start.20
  242.6 1.5 collective-permute-start.19
  244.1 9.8 %collective-permute-done.20.refs_2_ = bf16[56,1152]{1,0:T(8,128)(2,1)S(1)} collective-permute-done((bf16[56,1152]{1,0:T(8,128)(2,1)S(1)}, bf16[56,1152]{1,0:T(8,128)(2,1)S(1)}, u32[]{:S(2)}, u32[]{:S(2)}) %collective-permute-start.20) | collective-permute-done | bytes 129056 | tf_op jit(solution)/shard_map/ppermute | solution.py:781
  253.9 0.1 collective-permute-done.19.refs_1_
  254.1 0.5 copy-done.7
  254.6 0.1 copy-done.8
  254.7 0.1 copy-done.3
  254.8 0.1 copy-done.5
  255.0 4.0 %adam.1 = (f32[48,1152]{1,0:T(8,128)}, f32[48,384]{1,0:T(8,128)}, f32[48,1152]{1,0:T(8,128)}, f32[48,1152]{1,0:T(8,128)}, f32[1,144]{1,0:T(1,128)}, /*index=5*/f...) custom-call(s32[6]{0:T(128)} %flag_ref.1, ...), custom_call_target="tpu_custom_call" | custom-call | tf_op jit(solution)/shard_map/adam/pallas_call | solution.py:747
  (67 shorter events, 0.5 us)
Async XLA Ops:
  2.7 9.6 %collective-permute-start.5 = (bf16[56,1152]{1,0:T(8,128)(2,1)}, bf16[56,1152]{1,0:T(8,128)(2,1)S(1)}, u32[]{:S(2)}, u32[]{:S(2)}) collective-permute-start(bf16[56,1152]{1,0:T(8,128)(2,1)} %get-tuple-element.71.refs_0_), channel_id=1, source_target_pairs={{0,6},{1,7},{2,4},{3,5},{4,2},{5,3},{6,0},{7,1},{8,14},{9,15},{10,... | collective-permute-start | bytes 387080 | tf_op jit(solution)/shard_map/ppermute | solution.py:765
  7.7 11.1 %collective-permute-start.3 = (bf16[56,1152]{1,0:T(8,128)(2,1)}, bf16[56,1152]{1,0:T(8,128)(2,1)S(1)}, u32[]{:S(2)}, u32[]{:S(2)}) collective-permute-start(bf16[56,1152]{1,0:T(8,128)(2,1)} %get-tuple-element.71.refs_0_), channel_id=1, source_target_pairs={{0,4},{1,5},{2,6},{3,7},{4,0},{5,1},{6,2},{7,3},{8,12},{9,13},{10,... | collective-permute-start | bytes 387080 | tf_op jit(solution)/shard_map/ppermute | solution.py:765
  7.7 11.1 %collective-permute-start.1 = (bf16[56,1152]{1,0:T(8,128)(2,1)}, bf16[56,1152]{1,0:T(8,128)(2,1)S(1)}, u32[]{:S(2)}, u32[]{:S(2)}) collective-permute-start(bf16[56,1152]{1,0:T(8,128)(2,1)} %get-tuple-element.71.refs_0_), channel_id=1, source_target_pairs={{0,2},{1,3},{2,0},{3,1},{4,6},{5,7},{6,4},{7,5},{8,10},{9,11},{10,... | collective-permute-start | bytes 387080 | tf_op jit(solution)/shard_map/ppermute | solution.py:765
  8.3 11.1 %collective-permute-start = (bf16[56,1152]{1,0:T(8,128)(2,1)}, bf16[56,1152]{1,0:T(8,128)(2,1)S(1)}, u32[]{:S(2)}, u32[]{:S(2)}) collective-permute-start(bf16[56,1152]{1,0:T(8,128)(2,1)} %get-tuple-element.71.refs_0_), channel_id=1, source_target_pairs={{0,1},{1,0},{2,3},{3,2},{4,5},{5,4},{6,7},{7,6},{8,9},{9,8},{10,11... | collective-permute-start | bytes 387080 | tf_op jit(solution)/shard_map/ppermute | solution.py:767
  12.3 33.0 %copy-start.17 = (bf16[56,1152]{1,0:T(8,128)(2,1)}, bf16[56,1152]{1,0:T(8,128)(2,1)S(1)}, u32[]{:S(2)}) copy-start(bf16[56,1152]{1,0:T(8,128)(2,1)S(1)} %collective-permute-done.5.refs_6_) | copy-start | bytes 387076
  12.3 7.0 %collective-permute-start.6 = (bf16[56,1152]{1,0:T(8,128)(2,1)S(1)}, bf16[56,1152]{1,0:T(8,128)(2,1)S(1)}, u32[]{:S(2)}, u32[]{:S(2)}) collective-permute-start(bf16[56,1152]{1,0:T(8,128)(2,1)S(1)} %collective-permute-done.5.refs_6_), channel_id=1, source_target_pairs={{0,1},{1,0},{2,3},{3,2},{4,5},{5,4},{6,7},{7,6},{8,9},{9,8},{10,11... | collective-permute-start | bytes 387080 | tf_op jit(solution)/shard_map/ppermute | solution.py:767
  18.8 26.5 %copy-start.18 = (bf16[56,1152]{1,0:T(8,128)(2,1)}, bf16[56,1152]{1,0:T(8,128)(2,1)S(1)}, u32[]{:S(2)}) copy-start(bf16[56,1152]{1,0:T(8,128)(2,1)S(1)} %collective-permute-done.3.refs_4_) | copy-start | bytes 387076
  18.8 1.3 collective-permute-start.4
  18.8 26.5 %copy-start.19 = (bf16[56,1152]{1,0:T(8,128)(2,1)}, bf16[56,1152]{1,0:T(8,128)(2,1)S(1)}, u32[]{:S(2)}) copy-start(bf16[56,1152]{1,0:T(8,128)(2,1)S(1)} %collective-permute-done.1.refs_2_) | copy-start | bytes 387076
  18.9 1.5 collective-permute-start.2
  19.4 26.0 %copy-start.20 = (bf16[56,1152]{1,0:T(8,128)(2,1)}, bf16[56,1152]{1,0:T(8,128)(2,1)S(1)}, u32[]{:S(2)}) copy-start(bf16[56,1152]{1,0:T(8,128)(2,1)S(1)} %collective-permute-done.refs_1_) | copy-start | bytes 387076
  19.4 26.0 %copy-start.21 = (bf16[56,1152]{1,0:T(8,128)(2,1)}, bf16[56,1152]{1,0:T(8,128)(2,1)S(1)}, u32[]{:S(2)}) copy-start(bf16[56,1152]{1,0:T(8,128)(2,1)S(1)} %collective-permute-done.6.refs_7_) | copy-start | bytes 387076
  20.2 25.2 %copy-start.22 = (bf16[56,1152]{1,0:T(8,128)(2,1)}, bf16[56,1152]{1,0:T(8,128)(2,1)S(1)}, u32[]{:S(2)}) copy-start(bf16[56,1152]{1,0:T(8,128)(2,1)S(1)} %collective-permute-done.4.refs_5_) | copy-start | bytes 387076
  20.4 25.0 %copy-start.23 = (bf16[56,1152]{1,0:T(8,128)(2,1)}, bf16[56,1152]{1,0:T(8,128)(2,1)S(1)}, u32[]{:S(2)}) copy-start(bf16[56,1152]{1,0:T(8,128)(2,1)S(1)} %collective-permute-done.2.refs_3_) | copy-start | bytes 387076
  20.4 11.2 %collective-permute-start.12 = (bf16[48,2688]{1,0:T(8,128)(2,1)}, bf16[48,2688]{1,0:T(8,128)(2,1)S(1)}, u32[]{:S(2)}, u32[]{:S(2)}) collective-permute-start(bf16[48,2688]{1,0:T(8,128)(2,1)} %get-tuple-element.76.refs_0_), channel_id=1, source_target_pairs={{0,6},{1,7},{2,4},{3,5},{4,2},{5,3},{6,0},{7,1},{8,14},{9,15},{10,... | collective-permute-start | bytes 774152 | tf_op jit(solution)/shard_map/ppermute | solution.py:765
  22.8 22.0 %collective-permute-start.10 = (bf16[48,2688]{1,0:T(8,128)(2,1)}, bf16[48,2688]{1,0:T(8,128)(2,1)S(1)}, u32[]{:S(2)}, u32[]{:S(2)}) collective-permute-start(bf16[48,2688]{1,0:T(8,128)(2,1)} %get-tuple-element.76.refs_0_), channel_id=1, source_target_pairs={{0,4},{1,5},{2,6},{3,7},{4,0},{5,1},{6,2},{7,3},{8,12},{9,13},{10,... | collective-permute-start | bytes 774152 | tf_op jit(solution)/shard_map/ppermute | solution.py:765
  22.8 22.0 %collective-permute-start.8 = (bf16[48,2688]{1,0:T(8,128)(2,1)}, bf16[48,2688]{1,0:T(8,128)(2,1)S(1)}, u32[]{:S(2)}, u32[]{:S(2)}) collective-permute-start(bf16[48,2688]{1,0:T(8,128)(2,1)} %get-tuple-element.76.refs_0_), channel_id=1, source_target_pairs={{0,2},{1,3},{2,0},{3,1},{4,6},{5,7},{6,4},{7,5},{8,10},{9,11},{10,... | collective-permute-start | bytes 774152 | tf_op jit(solution)/shard_map/ppermute | solution.py:765
  25.4 54.6 %collective-permute-start.7 = (bf16[48,2688]{1,0:T(8,128)(2,1)}, bf16[48,2688]{1,0:T(8,128)(2,1)S(1)}, u32[]{:S(2)}, u32[]{:S(2)}) collective-permute-start(bf16[48,2688]{1,0:T(8,128)(2,1)} %get-tuple-element.76.refs_0_), channel_id=1, source_target_pairs={{0,1},{1,0},{2,3},{3,2},{4,5},{5,4},{6,7},{7,6},{8,9},{9,8},{10,11... | collective-permute-start | bytes 774152 | tf_op jit(solution)/shard_map/ppermute | solution.py:767
  31.6 48.4 %copy-start.10 = (bf16[48,2688]{1,0:T(8,128)(2,1)}, bf16[48,2688]{1,0:T(8,128)(2,1)S(1)}, u32[]{:S(2)}) copy-start(bf16[48,2688]{1,0:T(8,128)(2,1)S(1)} %collective-permute-done.12.refs_6_) | copy-start | bytes 774148
  31.6 48.4 %collective-permute-start.13 = (bf16[48,2688]{1,0:T(8,128)(2,1)S(1)}, bf16[48,2688]{1,0:T(8,128)(2,1)S(1)}, u32[]{:S(2)}, u32[]{:S(2)}) collective-permute-start(bf16[48,2688]{1,0:T(8,128)(2,1)S(1)} %collective-permute-done.12.refs_6_), channel_id=1, source_target_pairs={{0,1},{1,0},{2,3},{3,2},{4,5},{5,4},{6,7},{7,6},{8,9},{9,8},{10,11... | collective-permute-start | bytes 774152 | tf_op jit(solution)/shard_map/ppermute | solution.py:767
  44.8 35.1 %copy-start.11 = (bf16[48,2688]{1,0:T(8,128)(2,1)}, bf16[48,2688]{1,0:T(8,128)(2,1)S(1)}, u32[]{:S(2)}) copy-start(bf16[48,2688]{1,0:T(8,128)(2,1)S(1)} %collective-permute-done.10.refs_4_) | copy-start | bytes 774148
  44.8 35.2 %collective-permute-start.11 = (bf16[48,2688]{1,0:T(8,128)(2,1)S(1)}, bf16[48,2688]{1,0:T(8,128)(2,1)S(1)}, u32[]{:S(2)}, u32[]{:S(2)}) collective-permute-start(bf16[48,2688]{1,0:T(8,128)(2,1)S(1)} %collective-permute-done.10.refs_4_), channel_id=1, source_target_pairs={{0,1},{1,0},{2,3},{3,2},{4,5},{5,4},{6,7},{7,6},{8,9},{9,8},{10,11... | collective-permute-start | bytes 774152 | tf_op jit(solution)/shard_map/ppermute | solution.py:767
  44.8 35.1 %copy-start.12 = (bf16[48,2688]{1,0:T(8,128)(2,1)}, bf16[48,2688]{1,0:T(8,128)(2,1)S(1)}, u32[]{:S(2)}) copy-start(bf16[48,2688]{1,0:T(8,128)(2,1)S(1)} %collective-permute-done.8.refs_2_) | copy-start | bytes 774148
  44.8 35.2 %collective-permute-start.9 = (bf16[48,2688]{1,0:T(8,128)(2,1)S(1)}, bf16[48,2688]{1,0:T(8,128)(2,1)S(1)}, u32[]{:S(2)}, u32[]{:S(2)}) collective-permute-start(bf16[48,2688]{1,0:T(8,128)(2,1)S(1)} %collective-permute-done.8.refs_2_), channel_id=1, source_target_pairs={{0,1},{1,0},{2,3},{3,2},{4,5},{5,4},{6,7},{7,6},{8,9},{9,8},{10,11... | collective-permute-start | bytes 774152 | tf_op jit(solution)/shard_map/ppermute | solution.py:767
  80.0 0.8 copy-start.14
  80.0 0.8 copy-start.15
  80.1 0.9 copy-start.16
  144.4 52.4 %copy-start.9 = (bf16[4,48,2688]{2,1,0:T(8,128)(2,1)S(1)}, bf16[4,48,2688]{2,1,0:T(8,128)(2,1)}, u32[]{:S(2)}) copy-start(bf16[4,48,2688]{2,1,0:T(8,128)(2,1)} %get-tuple-element.83) | copy-start | bytes 3096580
  196.7 7.1 %copy-start = (f32[4,48,2688]{2,1,0:T(8,128)S(1)}, f32[4,48,2688]{2,1,0:T(8,128)}, u32[]{:S(2)}) copy-start(f32[4,48,2688]{2,1,0:T(8,128)} %get-tuple-element.82) | copy-start | bytes 6193156
  196.7 2.2 collective-permute-start.15
  196.8 7.0 %collective-permute-start.14 = (bf16[4,48,2688]{2,1,0:T(8,128)(2,1)S(1)}, bf16[4,48,2688]{2,1,0:T(8,128)(2,1)S(1)}, u32[]{:S(2)}, u32[]{:S(2)}) collective-permute-start(bf16[4,48,2688]{2,1,0:T(8,128)(2,1)S(1)} %copy-done.9), channel_id=1, source_target_pairs={{0,1},{1,0},{2,3},{3,2},{4,5},{5,4},{6,7},{7,6},{8,9},{9,8},{10,11... | collective-permute-start | bytes 3096584 | tf_op jit(solution)/shard_map/ppermute | solution.py:772
  200.2 6.7 %collective-permute-start.16 = (bf16[56,1152]{1,0:T(8,128)(2,1)S(1)}, bf16[56,1152]{1,0:T(8,128)(2,1)S(1)}, u32[]{:S(2)}, u32[]{:S(2)}) collective-permute-start(bf16[56,1152]{1,0:T(8,128)(2,1)S(1)} %get-tuple-element.123), channel_id=1, source_target_pairs={{0,2},{1,3},{2,0},{3,1},{4,6},{5,7},{6,4},{7,5},{8,10},{9,11},{10,... | collective-permute-start | bytes 387080 | tf_op jit(solution)/shard_map/ppermute | solution.py:773
  200.3 8.9 %collective-permute-start.18 = (bf16[56,1152]{1,0:T(8,128)(2,1)S(1)}, bf16[56,1152]{1,0:T(8,128)(2,1)S(1)}, u32[]{:S(2)}, u32[]{:S(2)}) collective-permute-start(bf16[56,1152]{1,0:T(8,128)(2,1)S(1)} %get-tuple-element.124), channel_id=1, source_target_pairs={{0,6},{1,7},{2,4},{3,5},{4,2},{5,3},{6,0},{7,1},{8,14},{9,15},{10,... | collective-permute-start | bytes 387080 | tf_op jit(solution)/shard_map/ppermute | solution.py:773
  202.2 14.2 %collective-permute-start.17 = (bf16[56,1152]{1,0:T(8,128)(2,1)S(1)}, bf16[56,1152]{1,0:T(8,128)(2,1)S(1)}, u32[]{:S(2)}, u32[]{:S(2)}) collective-permute-start(bf16[56,1152]{1,0:T(8,128)(2,1)S(1)} %get-tuple-element.125), channel_id=1, source_target_pairs={{0,4},{1,5},{2,6},{3,7},{4,0},{5,1},{6,2},{7,3},{8,12},{9,13},{10,... | collective-permute-start | bytes 387080 | tf_op jit(solution)/shard_map/ppermute | solution.py:773
  204.1 14.9 %collective-permute-start.22 = (bf16[48,2688]{1,0:T(8,128)(2,1)S(1)}, bf16[48,2688]{1,0:T(8,128)(2,1)S(1)}, u32[]{:S(2)}, u32[]{:S(2)}) collective-permute-start(bf16[48,2688]{1,0:T(8,128)(2,1)S(1)} %get-tuple-element.120), channel_id=1, source_target_pairs={{0,2},{1,3},{2,0},{3,1},{4,6},{5,7},{6,4},{7,5},{8,10},{9,11},{10,... | collective-permute-start | bytes 774152 | tf_op jit(solution)/shard_map/ppermute | solution.py:773
  205.1 18.0 %collective-permute-start.24 = (bf16[48,2688]{1,0:T(8,128)(2,1)S(1)}, bf16[48,2688]{1,0:T(8,128)(2,1)S(1)}, u32[]{:S(2)}, u32[]{:S(2)}) collective-permute-start(bf16[48,2688]{1,0:T(8,128)(2,1)S(1)} %get-tuple-element.121), channel_id=1, source_target_pairs={{0,6},{1,7},{2,4},{3,5},{4,2},{5,3},{6,0},{7,1},{8,14},{9,15},{10,... | collective-permute-start | bytes 774152 | tf_op jit(solution)/shard_map/ppermute | solution.py:773
  207.0 30.4 %collective-permute-start.23 = (bf16[48,2688]{1,0:T(8,128)(2,1)S(1)}, bf16[48,2688]{1,0:T(8,128)(2,1)S(1)}, u32[]{:S(2)}, u32[]{:S(2)}) collective-permute-start(bf16[48,2688]{1,0:T(8,128)(2,1)S(1)} %get-tuple-element.122), channel_id=1, source_target_pairs={{0,4},{1,5},{2,6},{3,7},{4,0},{5,1},{6,2},{7,3},{8,12},{9,13},{10,... | collective-permute-start | bytes 774152 | tf_op jit(solution)/shard_map/ppermute | solution.py:773
  216.5 37.6 %copy-start.2 = (bf16[56,1152]{1,0:T(8,128)(2,1)}, bf16[56,1152]{1,0:T(8,128)(2,1)S(1)}, u32[]{:S(2)}) copy-start(bf16[56,1152]{1,0:T(8,128)(2,1)S(1)} %fusion.3.refs_0_) | copy-start | bytes 387076
  216.5 26.1 %collective-permute-start.21 = (bf16[56,1152]{1,0:T(8,128)(2,1)S(1)}, bf16[56,1152]{1,0:T(8,128)(2,1)S(1)}, u32[]{:S(2)}, u32[]{:S(2)}) collective-permute-start(bf16[56,1152]{1,0:T(8,128)(2,1)S(1)} %fusion.3.refs_0_), channel_id=1, source_target_pairs={{0,24},{8,16},{16,8},{24,0},{1,25},{9,17},{17,9},{25,1},{2,26},{10... | collective-permute-start | bytes 387080 | tf_op jit(solution)/shard_map/ppermute | solution.py:781
  237.5 16.5 %copy-start.1 = (bf16[48,2688]{1,0:T(8,128)(2,1)}, bf16[48,2688]{1,0:T(8,128)(2,1)S(1)}, u32[]{:S(2)}) copy-start(bf16[48,2688]{1,0:T(8,128)(2,1)S(1)} %add_convert_fusion.refs_4_) | copy-start | bytes 774148
  237.5 16.5 %collective-permute-start.27 = (bf16[48,2688]{1,0:T(8,128)(2,1)S(1)}, bf16[48,2688]{1,0:T(8,128)(2,1)S(1)}, u32[]{:S(2)}, u32[]{:S(2)}) collective-permute-start(bf16[48,2688]{1,0:T(8,128)(2,1)S(1)} %add_convert_fusion.refs_4_), channel_id=1, source_target_pairs={{0,24},{8,16},{16,8},{24,0},{1,25},{9,17},{17,9},{25,1},{2,26},{10... | collective-permute-start | bytes 774152 | tf_op jit(solution)/shard_map/ppermute | solution.py:781
  240.0 14.0 %collective-permute-start.26 = (bf16[48,2688]{1,0:T(8,128)(2,1)S(1)}, bf16[48,2688]{1,0:T(8,128)(2,1)S(1)}, u32[]{:S(2)}, u32[]{:S(2)}) collective-permute-start(bf16[48,2688]{1,0:T(8,128)(2,1)S(1)} %add_convert_fusion.refs_4_), channel_id=1, source_target_pairs={{0,16},{8,24},{16,0},{24,8},{1,17},{9,25},{17,1},{25,9},{2,18},{10... | collective-permute-start | bytes 774152 | tf_op jit(solution)/shard_map/ppermute | solution.py:781
  240.6 13.5 %collective-permute-start.25 = (bf16[48,2688]{1,0:T(8,128)(2,1)S(1)}, bf16[48,2688]{1,0:T(8,128)(2,1)S(1)}, u32[]{:S(2)}, u32[]{:S(2)}) collective-permute-start(bf16[48,2688]{1,0:T(8,128)(2,1)S(1)} %add_convert_fusion.refs_4_), channel_id=1, source_target_pairs={{0,8},{8,0},{16,24},{24,16},{1,9},{9,1},{17,25},{25,17},{2,10},{10... | collective-permute-start | bytes 774152 | tf_op jit(solution)/shard_map/ppermute | solution.py:781
  241.1 12.8 %collective-permute-start.20 = (bf16[56,1152]{1,0:T(8,128)(2,1)S(1)}, bf16[56,1152]{1,0:T(8,128)(2,1)S(1)}, u32[]{:S(2)}, u32[]{:S(2)}) collective-permute-start(bf16[56,1152]{1,0:T(8,128)(2,1)S(1)} %fusion.3.refs_0_), channel_id=1, source_target_pairs={{0,16},{8,24},{16,0},{24,8},{1,17},{9,25},{17,1},{25,9},{2,18},{10... | collective-permute-start | bytes 387080 | tf_op jit(solution)/shard_map/ppermute | solution.py:781
  242.6 11.5 %copy-start.6 = (bf16[56,1152]{1,0:T(8,128)(2,1)}, bf16[56,1152]{1,0:T(8,128)(2,1)S(1)}, u32[]{:S(2)}) copy-start(bf16[56,1152]{1,0:T(8,128)(2,1)S(1)} %collective-permute-done.21.refs_3_) | copy-start | bytes 387076
  242.6 11.4 %collective-permute-start.19 = (bf16[56,1152]{1,0:T(8,128)(2,1)S(1)}, bf16[56,1152]{1,0:T(8,128)(2,1)S(1)}, u32[]{:S(2)}, u32[]{:S(2)}) collective-permute-start(bf16[56,1152]{1,0:T(8,128)(2,1)S(1)} %fusion.3.refs_0_), channel_id=1, source_target_pairs={{0,8},{8,0},{16,24},{24,16},{1,9},{9,1},{17,25},{25,17},{2,10},{10... | collective-permute-start | bytes 387080 | tf_op jit(solution)/shard_map/ppermute | solution.py:781
  254.0 0.8 copy-start.4
  254.0 0.9 copy-start.5
  (4 other events, 2.7 us)

commit v3 on v2

--- a/solution.py
+++ b/solution.py
@@ -124,18 +124,49 @@
     )(wq, vec, b, w1, w2t, wp)
 
 
-def attend_body(SEQ, SP, TP, D, np_, me_ref, x_ref, *refs):
+def norm_body(SEQ, D, x_ref, xh_ref, r_ref, xs):
+    j = pl.program_id(1)
+
+    @pl.when(j == 0)
+    def _():
+        spread(x_ref, xs, SEQ)
+
+    for i in range(PAIR):
+        for t, n in tiles(SEQ, 48):
+            xh, r = norm_rows(image(xs, j * PAIR + i, t, n))
+            xh_ref[i, t : t + n, :] = xh
+            r_ref[i, t : t + n, :] = jnp.broadcast_to(r, (n, 128))
+
+
+def norm(x):
+    SEQ, N, D = x.shape
+    SP = up(SEQ, 16)
+    tok = pl.BlockSpec((SEQ, GROUP, D), lambda g, j: (0, g, 0))
+    img = lambda d: pl.BlockSpec((PAIR, SP, d), lambda g, j: (g * (GROUP // PAIR) + j, 0, 0))
+    return pl.pallas_call(
+        partial(norm_body, SEQ, D),
+        grid=(N // GROUP, GROUP // PAIR),
+        in_specs=[tok],
+        out_specs=[img(D), img(128)],
+        out_shape=[jax.ShapeDtypeStruct((N, SP, d), F32) for d in (D, 128)],
+        scratch_shapes=[pltpu.VMEM((D // 128, SEQ * GROUP, 128), F32)],
+        name="norm",
+        **params(8 * 10**9, 15 * 10**6),
+    )(x)
+
+
+def attend_body(SEQ, SP, TP, D, np_, me_ref, xh_ref, *refs):
     H = D // HEAD_DIM
     g = pl.program_id(0)
     j = pl.program_id(1)
     if np_:
         pieces, refs = refs[:np_], refs[np_:]
-        qkv_ref, o_ref, l_ref, xi_ref, w_ref, vec_ref, c1_ref, sm = refs[:8]
+        qkv_ref, o_ref, l_ref, a_ref, w_ref, vec_ref, c1_ref, sm = refs[:8]
         refs = refs[8:]
     else:
-        w_ref, vec_ref, qkv_ref, o_ref, l_ref, xi_ref = refs[:6]
+        w_ref, vec_ref, qkv_ref, o_ref, l_ref, a_ref = refs[:6]
         refs = refs[6:]
-    xs, os_, a_scr, s0, s1, p0, p1 = refs
+    os_, a_scr, s0, s1, p0, p1 = refs
 
     @pl.when((g == 0) & (j == 0))
     def _():
@@ -153,10 +184,6 @@
                 jnp.concatenate([sm[s, 6:7, 0:nb] for s in range(np_)], axis=1), c1_ref.shape
             )
 
-    @pl.when(j == 0)
-    def _():
-        spread(x_ref, xs, SEQ)
-
     gain = vec_ref[0:1, :]
     shift = vec_ref[1:2, :]
     ss = (s0, s1)
@@ -165,10 +192,9 @@
     S8 = SEQ // 8 * 8
 
     def ln(i, t, n):
-        x = image(xs, j * PAIR + i, t, n)
-        xi_ref[i, t : t + n, :] = x.astype(BF)
-        xh, _ = norm_rows(x)
-        a_scr[i * SP + t : i * SP + t + n, :] = (xh * gain + shift).astype(BF)
+        y = (xh_ref[i, t : t + n, :] * gain + shift).astype(BF)
+        a_scr[i * SP + t : i * SP + t + n, :] = y
+        a_ref[i, t : t + n, :] = y
 
     def qkv(i, t, c, w):
         y = dot(a_scr[i * SP : (i + 1) * SP, :], w_ref[:, t * D + c : t * D + c + w])
@@ -246,7 +272,7 @@
     assert done >= len(rest)
     mix(nu - 1)
     for i in range(PAIR):
-        xi_ref[i, SEQ:SP, :] = jnp.zeros((SP - SEQ, D), BF)
+        a_ref[i, SEQ:SP, :] = jnp.zeros((SP - SEQ, D), BF)
 
     @pl.when(j == pl.num_programs(1) - 1)
     def _():
@@ -254,9 +280,8 @@
             o_ref[t : t + 2] = tokens(os_, t, TP).astype(BF)
 
 
-def attend(me, x, pieces, w, vec, FF, TP):
-    SEQ, N, D = x.shape
-    SP = up(SEQ, 16)
+def attend(me, xh, pieces, w, vec, FF, SEQ, TP):
+    N, SP, D = xh.shape
     W3 = 3 * D
     np_ = len(pieces)
     tok = lambda t: pl.BlockSpec((t, GROUP, D), lambda g, j, *_: (0, g, 0))
@@ -266,7 +291,7 @@
     ins = list(pieces) if np_ else [w, vec]
     out_specs = [img(SP, W3), tok(TP), img(8, SP), img(SP, D)]
     out_shape = [s((N, SP, W3), BF), s((TP, N, D), BF), s((N, 8, SP), F32), s((N, SP, D), BF)]
-    scratch = [v((D // 128, TP * GROUP, 128), F32)] * 2 + [v((PAIR * SP, D), BF)]
+    scratch = [v((D // 128, TP * GROUP, 128), F32), v((PAIR * SP, D), BF)]
     scratch += [v((SP, SP), F32)] * 2 + [v((SP, SP), BF)] * 2
     if np_:
         out_specs += [whole(D, W3), whole(8, D), whole(8, FF)]
@@ -277,14 +302,14 @@
         grid_spec=pltpu.PrefetchScalarGridSpec(
             num_scalar_prefetch=1,
             grid=(N // GROUP, GROUP // PAIR),
-            in_specs=[tok(SEQ)] + [full(a) for a in ins],
+            in_specs=[img(SP, D)] + [full(a) for a in ins],
             out_specs=out_specs,
             scratch_shapes=scratch,
         ),
         out_shape=out_shape,
         name="attend",
         **params(20 * 10**9, 25 * 10**6),
-    )(me, x, *ins)
+    )(me, xh, *ins)
 
 
 def feed_body(SEQ, D, FF, T, N, np_, me_ref, cnt_ref, x_ref, o_ref, cot_ref, c1_ref, vec_ref, *refs):
@@ -482,13 +507,14 @@
     )(me, cnt, x, o, cot, c1, vec, *ins)
 
 
-def back_body(SEQ, SP, TP, D, FF, np_, me_ref, xi_ref, qkv_ref, l_ref, do_ref, dx1_ref, w_ref, vec_ref, tc1_ref, tv2_ref, gi_ref, *refs):
+def back_body(SEQ, SP, TP, D, FF, np_, DEPS, me_ref, a_ref, xh_ref, r_ref, qkv_ref, l_ref, do_ref, dx1_ref, w_ref, vec_ref, tc1_ref, tv2_ref, *refs):
+    gi_ref, refs = refs[DEPS], refs[DEPS + 1 :]
     if np_:
         snd_ref, keep_ref, tq_ref, sm = refs[:4]
         gv_ref, refs = refs[4], refs[5:]
     else:
         tq_ref, gv_ref, refs = refs[0], refs[1], refs[2:]
-    dos, gs, dob, a_scr, at_scr, xh_scr, r_scr, d_scr, da_scr, tv_ref, s0, s1, e0, e1, p0, p1, q0, q1 = refs
+    dos, gs, dob, at_scr, d_scr, da_scr, tv_ref, s0, s1, e0, e1, p0, p1, q0, q1 = refs
     H = D // HEAD_DIM
     W3 = 3 * D
     g = pl.program_id(0)
@@ -504,7 +530,6 @@
         spread(do_ref, dos, SEQ)
 
     gain = vec_ref[0:1, :]
-    shift = vec_ref[1:2, :]
     ss = (s0, s1)
     es = (e0, e1)
     pp = (p0, p1)
@@ -514,13 +539,6 @@
 
     def load(i, t, n):
         dob[i * SP + t : i * SP + t + n, :] = image(dos, j * PAIR + i, t, n).astype(BF)
-
-    def ln(i, t, n):
-        xh, r = norm_rows(xi_ref[i, t : t + n, :].astype(F32))
-        at = slice(i * SP + t, i * SP + t + n)
-        xh_scr[at, :] = xh
-        r_scr[at, :] = jnp.broadcast_to(r, (n, 128))
-        a_scr[at, :] = (xh * gain + shift).astype(BF)
 
     def part(i, h, t):
         lo = t * D + h * HEAD_DIM
@@ -576,7 +594,8 @@
     srows = tiles(S8, 64) + ([(S8, 8)] if S8 < SEQ else [])
     for t, n in rows:
         load(0, t, n)
-    pre = [partial(load, 1, t, n) for t, n in rows] + [partial(ln, i, t, n) for i in range(PAIR) for t, n in rows]
+    at_scr[...] = a_ref[...].reshape(PAIR * SP, D).T
+    pre = [partial(load, 1, t, n) for t, n in rows]
     nu = PAIR * H
     score(0)
     dprob(0)
@@ -614,17 +633,16 @@
     def v_back(i, t, n):
         at = slice(i * SP + t, i * SP + t + n)
         d = da_scr[at, :]
-        xh = xh_scr[at, :]
+        xh = xh_ref[i, t : t + n, :]
         dxh = d * gain
         mean1 = jnp.mean(dxh, axis=-1, keepdims=True)
         mean2 = jnp.mean(dxh * xh, axis=-1, keepdims=True)
-        y = r_scr[at, 0:1] * (dxh - mean1 - xh * mean2)
+        y = r_ref[i, t : t + n, 0:1] * (dxh - mean1 - xh * mean2)
         for c in range(gs.shape[0]):
             gs[c, pl.ds(pl.multiple_of((j * PAIR + i) * TP + t, 8), n), :] = y[:, c * 128 : (c + 1) * 128]
         add("g", d * xh)
         add("e", d)
 
-    at_scr[...] = a_scr[...].T
     cols = tiles(W3, 256)
     m_da(0)
     weave([partial(m_da, 1)] + [partial(m_tq, c, w) for c, w in cols[:2]], [partial(v_back, 0, t, n) for t, n in rows])
@@ -665,8 +683,8 @@
                     ref[k // 2, r : r + EXTRA, wide:] = jnp.zeros((EXTRA, W3 - wide), ref.dtype)
 
 
-def back(me, xi, qkv, l, do, dx1, w, vec, tc1, tv2, SEQ, np_):
-    N, SP, D = xi.shape
+def back(me, a, xh, r, qkv, l, do, dx1, w, vec, tc1, tv2, deps, SEQ, np_):
+    N, SP, D = a.shape
     TP = do.shape[0]
     W3 = 3 * D
     FF = tc1.shape[1]
@@ -687,91 +705,95 @@
         out_shape += [s((D, W3), F32), s((8, D), F32)]
         scratch = []
     scratch += [v((D // 128, TP * GROUP, 128), F32)] * 2
-    scratch += [v((R, D), BF), v((R, D), BF), v((D, R), BF), v((R, D), F32), v((R, 128), F32), v((R, W3), BF), v((R, D), F32)]
+    scratch += [v((R, D), BF), v((D, R), BF), v((R, W3), BF), v((R, D), F32)]
     scratch += [v((16, D), F32)] + [v((SP, SP), F32)] * 4 + [v((SP, SP), BF)] * 4
     return pl.pallas_call(
-        partial(back_body, SEQ, SP, TP, D, FF, np_),
+        partial(back_body, SEQ, SP, TP, D, FF, np_, len(deps)),
         grid_spec=pltpu.PrefetchScalarGridSpec(
             num_scalar_prefetch=1,
             grid=(N // GROUP, GROUP // PAIR),
-            in_specs=[img(SP, D), img(SP, W3), img(8, SP), tok(TP), tok(TP), full(w), full(vec), full(tc1), full(tv2)],
+            in_specs=[img(SP, D), img(SP, D), img(SP, 128), img(SP, W3), img(8, SP), tok(TP), tok(TP)]
+            + [full(w), full(vec), full(tc1), full(tv2)]
+            + [pl.BlockSpec(memory_space=pl.ANY)] * len(deps),
             out_specs=out_specs,
             scratch_shapes=scratch,
         ),
         out_shape=out_shape,
         name="back",
         **params(40 * 10**9, 30 * 10**6),
-    )(me, xi, qkv, l, do, dx1, w, vec, tc1, tv2)
-
-
-def adam_body(na, nb_, slots, FF, flag_ref, gid_ref, scale_ref, *refs):
-    pa, refs = refs[:na], refs[na:]
-    pb, refs = refs[:nb_], refs[nb_:]
-    weights, firsts, seconds = refs[:6], refs[6:12], refs[12:18]
-    outs = refs[18:]
-
-    def total(ps, rows, cols):
-        xs = [p[rows, cols].astype(F32) for p in ps]
-        return xs[0] if len(xs) == 1 else (xs[0] + xs[1]) + (xs[2] + xs[3])
-
-    r = weights[0].shape[0]
-    D = weights[1].shape[1]
-    every = slice(0, r)
-    where = (
-        (pa, every, slice(0, 3 * D)),
-        (pb, every, slice(2 * FF, 2 * FF + D)),
-        (pb, every, slice(0, FF)),
-        (pb, every, slice(FF, 2 * FF)),
-        (pa, slice(r + 6, r + 7), slice(0, weights[4].shape[1])),
-        (pa, slice(r, r + 6), slice(0, weights[5].shape[1])),
-    )
-    for p, (ps, rows, cols) in enumerate(where):
-        grad = total(ps, rows, cols) / slots
+    )(me, a, xh, r, qkv, l, do, dx1, w, vec, tc1, tv2, *deps)
+
+
+def adam_body(np_, count, slots, where, flag_ref, gid_ref, scale_ref, *refs):
+    pieces, refs = refs[:np_], refs[np_:]
+    weights, firsts, seconds, outs = refs[:count], refs[count : 2 * count], refs[2 * count : 3 * count], refs[3 * count :]
+    for k, (p, row, col) in enumerate(where):
+        r, c = weights[k].shape
+        xs = [x[row : row + r, col : col + c].astype(F32) for x in pieces]
+        grad = (xs[0] if len(xs) == 1 else (xs[0] + xs[1]) + (xs[2] + xs[3])) / slots
         flag = flag_ref[p].astype(F32)
         lr = scale_ref[gid_ref[p]]
-        first = BETA_ONE * firsts[p][...] + (1.0 - BETA_ONE) * grad
-        second = BETA_TWO * seconds[p][...] + (1.0 - BETA_TWO) * grad * grad
+        first = BETA_ONE * firsts[k][...] + (1.0 - BETA_ONE) * grad
+        second = BETA_TWO * seconds[k][...] + (1.0 - BETA_TWO) * grad * grad
         direction = first / (1.0 - BETA_ONE**ADAM_STEPS) / (jnp.sqrt(second / (1.0 - BETA_TWO**ADAM_STEPS)) + ADAM_EPS)
-        weight = weights[p][...]
-        outs[p][...] = grad
-        outs[6 + p][...] = weight - LEARN_RATE * lr * (direction + DECAY_RATE * flag * weight)
-        outs[12 + p][...] = first
-        outs[18 + p][...] = second
-
-
-def adam(flags, gids, scales, pa, pb, weights, firsts, seconds, slots, FF):
+        weight = weights[k][...]
+        outs[k][...] = grad
+        outs[count + k][...] = weight - LEARN_RATE * lr * (direction + DECAY_RATE * flag * weight)
+        outs[2 * count + k][...] = first
+        outs[3 * count + k][...] = second
+
+
+def adam(flags, gids, scales, pieces, arrays, slots, where):
     smem = pl.BlockSpec(memory_space=pltpu.SMEM)
     vmem = pl.BlockSpec(memory_space=pltpu.VMEM)
-    shapes = [jax.ShapeDtypeStruct(w.shape, F32) for w in weights]
-    count = len(pa) + len(pb) + 18
+    mine = [[xs[p] for p, _, _ in where] for xs in arrays]
+    shapes = [jax.ShapeDtypeStruct(w.shape, F32) for w in mine[0]]
     return pl.pallas_call(
-        partial(adam_body, len(pa), len(pb), slots, FF),
-        in_specs=[smem] * 3 + [vmem] * count,
-        out_specs=[vmem] * 24,
+        partial(adam_body, len(pieces), len(where), slots, where),
+        in_specs=[smem] * 3 + [vmem] * (len(pieces) + 3 * len(where)),
+        out_specs=[vmem] * (4 * len(where)),
         out_shape=shapes * 4,
         name="adam",
-        **params(),
-    )(flags, gids, scales, *pa, *pb, *weights, *firsts, *seconds)
+        **params(10**9, 5 * 10**6),
+    )(flags, gids, scales, *pieces, *mine[0], *mine[1], *mine[2])
 
 
 def pairs(n, k):
     return [(i, i ^ k) for i in range(n)]
 
 
+def touch_body(*refs):
+    pass
+
+
+def touch(dep, xs):
+    spec = pl.BlockSpec(memory_space=pl.ANY)
+    return pl.pallas_call(
+        touch_body,
+        in_specs=[spec] * (len(xs) + 1),
+        out_specs=[spec] * len(xs),
+        out_shape=[jax.ShapeDtypeStruct(x.shape, x.dtype) for x in xs],
+        input_output_aliases={k: k for k in range(len(xs))},
+        name="touch",
+    )(*xs, dep)
+
+
 def fetch(x, n):
-    pieces = [None] * n
-    pieces[0] = x
-    for k in range(2, n, 2):
-        pieces[k] = lax.ppermute(x, "fsdp", pairs(n, k))
-    for k in range(0, n, 2):
-        pieces[k + 1] = lax.ppermute(pieces[k], "fsdp", pairs(n, 1))
-    return pieces
+    return [x] + [lax.ppermute(x, "fsdp", pairs(n, k)) for k in range(2, n, 2)]
+
+
+def fetch_core(own, n):
+    other = [lax.ppermute(x, "fsdp", pairs(n, 1)) for x in own]
+    return [x for both in zip(own, other) for x in both]
 
 
 def halve(snd, keep, n):
     h = keep + lax.ppermute(snd, "fsdp", pairs(n, 1)).astype(F32)
-    got = [lax.ppermute(h[k].astype(BF), "fsdp", pairs(n, 2 * k)) for k in range(1, n // 2)]
-    return h[0], got
+    return h[0], [h[k].astype(BF) for k in range(1, n // 2)]
+
+
+def along_z(xs, n):
+    return [lax.ppermute(x, "fsdp", pairs(n, 2 * k + 2)) for k, x in enumerate(xs)]
 
 
 def finish(own, got, d):
@@ -804,17 +826,21 @@
     firsts = [m_qkv, m_proj, m_fc1, m_fc2.T, rows(m_bias1), m_vectors]
     seconds = [v_qkv, v_proj, v_fc1, v_fc2.T, rows(v_bias1), v_vectors]
     pack_a, pack_b = pack(weights[0], weights[5], weights[4], weights[2], weights[3], weights[1])
+    xh, rf = norm(x)
     if direct:
-        pieces_a = fetch(pack_a, n)
-        pack_b = lax.optimization_barrier((pack_b, pieces_a))[0]
-        pieces_b = fetch(pack_b, n)
-        qkv, o, logs, xi, wq, vec, c1 = attend(me, x, pieces_a, None, None, FF, TP)
+        half_a = touch(rf, fetch(pack_a, n))
+        pieces_a = fetch_core(half_a, n)
+        half_b = fetch(touch(half_a[-1], [pack_b])[0], n)
+        qkv, o, logs, a, wq, vec, c1 = attend(me, xh, pieces_a, None, None, FF, SEQ, TP)
+        pieces_b = fetch_core(touch(vec, half_b), n)
         out, dx1, do, tc1, tv2, snd, keep = feed(me, counts, x, o, cot, c1, vec, pieces_b, (), T)
-        own_b, got_b = halve(snd, keep, n)
-        do, got0 = lax.optimization_barrier((do, own_b))
-        gi, snd, keep = back(me, xi, qkv, logs, do, dx1, wq, vec, tc1, tv2, SEQ, n)
+        own_b, sends = halve(snd, keep, n)
+        got_b = along_z(sends, n)
+        gi, snd, keep = back(me, a, xh, rf, qkv, logs, do, dx1, wq, vec, tc1, tv2, sends, SEQ, n)
+        snd, *got_b = touch(vec, [snd, *got_b])
+        own_a, sends = halve(snd, keep, n)
+        got_a = along_z(sends, n)
         pb = finish(own_b, got_b, d)
-        own_a, got_a = halve(snd, keep, n)
         pa = finish(own_a, got_a, d)
     else:
         all_a = lax.all_gather(pack_a, "fsdp", axis=0, tiled=False)
@@ -824,9 +850,9 @@
         vec = jnp.transpose(all_a[:, r : r + 8, :r], (1, 0, 2)).reshape(8, D).astype(F32)
         c1 = jnp.broadcast_to(all_a[:, r + 6, :nb].reshape(1, FF), (8, FF)).astype(F32)
         ws = (all_b[:, 2 * FF :], all_b[:, :FF], all_b[:, FF : 2 * FF])
-        qkv, o, logs, xi = attend(me, x, (), wq, vec, FF, TP)
+        qkv, o, logs, a = attend(me, xh, (), wq, vec, FF, SEQ, TP)
         out, dx1, do, tc1, tv2, tp, t1, t2 = feed(me, counts, x, o, cot, c1, vec, (), ws, T)
-        gi, tq, gv = back(me, xi, qkv, logs, do, dx1, wq, vec, tc1, tv2, SEQ, 0)
+        gi, tq, gv = back(me, a, xh, rf, qkv, logs, do, dx1, wq, vec, tc1, tv2, (), SEQ, 0)
         share = lambda g, axis: lax.psum(
             lax.psum_scatter(g, "fsdp", scatter_dimension=axis, tiled=True).astype(BF), "dp"
         ).astype(F32)
@@ -834,8 +860,16 @@
         small = jnp.zeros((8, 3 * D), F32).at[:6, :r].set(share(gv[:6], 1))
         small = small.at[6, :nb].set(share(jnp.sum(tc1, axis=0), 0))
         pa = [jnp.concatenate([share(tq, 0), small], axis=0)]
-    res = adam(decay_flags, group_ids, group_scales, pa, pb, weights, firsts, seconds, float(N * n * d), FF)
-    res = list(res)
+    arrays = (weights, firsts, seconds)
+    slots = float(N * n * d)
+    where_a = ((0, 0, 0), (4, r + 6, 0), (5, r, 0))
+    where_b = ((1, 0, 2 * FF), (2, 0, 0), (3, 0, FF))
+    res = [None] * 24
+    for pieces, where in ((pb, where_b), (pa, where_a)):
+        got = adam(decay_flags, group_ids, group_scales, pieces, arrays, slots, where)
+        for j in range(4):
+            for k, (p, _, _) in enumerate(where):
+                res[6 * j + p] = got[3 * j + k]
     for k in range(4):
         res[6 * k + 3] = res[6 * k + 3].T
         res[6 * k + 4] = res[6 * k + 4].reshape(-1)

time: 259 us -> 220 us (0.85)
  waiting for transfers between devices: 69.6 us -> 15 us
  Pallas kernels: 156 us -> 165 us
  local copies, waits for them, and re-layouts: 1.95 us -> 5.27 us
    ppermute x20, waiting for transfers between devices: 58.1 us -> 9.25 us  [the longest x6 8.06 us: along_z(): lax.ppermute(x, 'fsdp', pairs(n, 2 * k + 2))]
    pallas_call x2 -> x8, Pallas kernels: 56.3 us -> 69.4 us  [the longest x1 51.9 us: back(): pl.pallas_call(partial(back_body, SEQ, SP, TP, D, FF, np_, len(deps)), gr...]
    ppermute x6, waiting for transfers between devices: 9.91 us -> 0.94 us  [finish(): return [b] + [lax.ppermute(b, 'dp', pairs(d, k)) for k in range(1, d)]]
    pallas_call x1, Pallas kernels: 34.6 us -> 30.7 us  [attend(): pl.pallas_call(partial(attend_body, SEQ, SP, TP, D, np_), grid_spec=pltpu...]
    unnamed x48 -> x62, local copies, waits for them, and re-layouts: 1.87 us -> 5.18 us
    ppermute x2, waiting for transfers between devices: 1.6 us -> 4.81 us  [halve(): h = keep + lax.ppermute(snd, 'fsdp', pairs(n, 1)).astype(F32)]
    ppermute x20, starting transfers between devices: 18.2 us -> 20.9 us  [the longest x6 10.5 us: fetch(): return [x] + [lax.ppermute(x, 'fsdp', pairs(n, k)) for k in range(2, n, 2)]]
  transfers between devices with their start and end apart: 28 -> 28, of which waited for: 13 -> 10; matrix products, arithmetic and copies ran while one was open for 1% -> 0% of each run, Pallas kernels for 13% -> 44%
where the time goes in v3:
time: 220 us; the launch traced here: 219 us
  Pallas kernels  165 us (75%)
  starting transfers between devices  28.3 us (13%)
  waiting for transfers between devices  15 us (7%)
  local copies, waits for them, and re-layouts  5.27 us (2%)
  other arithmetic  3.38 us (2%)
    pallas_call x1, Pallas kernels, feed(): pl.pallas_call(partial(feed_body, SEQ, D, FF, T, N, np_), grid_spec=pltpu...  63.4 us
    pallas_call x1, Pallas kernels, back(): pl.pallas_call(partial(back_body, SEQ, SP, TP, D, FF, np_, len(deps)), gr...  51.9 us
    pallas_call x1, Pallas kernels, attend(): pl.pallas_call(partial(attend_body, SEQ, SP, TP, D, np_), grid_spec=pltpu...  30.7 us
    pallas_call x1, Pallas kernels, norm(): pl.pallas_call(partial(norm_body, SEQ, D), grid=(N // GROUP, GROUP // PAI...  11.5 us
    ppermute x6, starting transfers between devices, fetch(): return [x] + [lax.ppermute(x, 'fsdp', pairs(n, k)) for k in range(2, n, 2)]  10.5 us
    ppermute x6, starting transfers between devices, along_z(): lax.ppermute(x, 'fsdp', pairs(n, 2 * k + 2))  8.38 us
    ppermute x6, waiting for transfers between devices, along_z(): lax.ppermute(x, 'fsdp', pairs(n, 2 * k + 2))  8.06 us
    ppermute x6, starting transfers between devices, finish(): return [b] + [lax.ppermute(b, 'dp', pairs(d, k)) for k in range(1, d)]  7.11 us
  transfers between devices with their start and end apart: 28, of which 10 were waited for; matrix products, arithmetic and copies ran while one was open for 0% of the time, Pallas kernels for 44%

profile of v3, /device:TPU:0, one launch (start us, length us, event | category | flops | bytes accessed | tf_op | source)
XLA Modules:
  0.0 219.2 jit_solution(17221932157557571374)
XLA Ops:
  0.7 2.0 pack.1
  2.7 5.0 %collective-permute-start.2 = (bf16[56,1152]{1,0:T(8,128)(2,1)}, bf16[56,1152]{1,0:T(8,128)(2,1)S(1)}, u32[]{:S(2)}, u32[]{:S(2)}) collective-permute-start(bf16[56,1152]{1,0:T(8,128)(2,1)} %get-tuple-element.84.refs_0_), channel_id=1, source_target_pairs={{0,6},{1,7},{2,4},{3,5},{4,2},{5,3},{6,0},{7,1},{8,14},{9,15},{10,... | collective-permute-start | bytes 387080 | tf_op jit(solution)/shard_map/ppermute | solution.py:782
  7.7 0.6 collective-permute-start
  8.3 11.5 %norm.1 = (f32[24,208,384]{2,1,0:T(8,128)}, f32[24,208,128]{2,1,0:T(8,128)}) custom-call(bf16[197,24,384]{2,1,0:T(8,128)(2,1)} %bitcast.55), custom_call_target="tpu_custom_call" | custom-call | flops 8000000000 | bytes 15000000 | tf_op jit(solution)/shard_map/norm/pallas_call | solution.py:146
  19.9 0.6 copy-done.6
  20.6 0.5 collective-permute-start.4
  21.1 0.5 collective-permute-start.6
  21.6 3.8 %collective-permute-start.9 = (bf16[48,2688]{1,0:T(8,128)(2,1)}, bf16[48,2688]{1,0:T(8,128)(2,1)S(1)}, u32[]{:S(2)}, u32[]{:S(2)}) collective-permute-start(bf16[48,2688]{1,0:T(8,128)(2,1)} %touch.5.refs_0_), channel_id=1, source_target_pairs={{0,6},{1,7},{2,4},{3,5},{4,2},{5,3},{6,0},{7,1},{8,14},{9,15},{10,... | collective-permute-start | bytes 774152 | tf_op jit(solution)/shard_map/ppermute | solution.py:782
  25.4 1.1 collective-permute-start.7
  26.6 0.6 copy-done.28
  27.2 30.7 %attend.1 = (bf16[24,208,1152]{2,1,0:T(8,128)(2,1)}, bf16[200,24,384]{2,1,0:T(8,128)(2,1)}, f32[24,8,208]{2,1,0:T(8,128)}, bf16[24,208,384]{2,1,0:T(8,128)(2,1)}...) custom-call(s32[1]{0:T(128)} %bitcast.me_ref, f32[24,208,384]{2,1,0:T(8,128)} %get-tuple-element.83.xh_ref, ...), custom_call_target="tpu_custom_call" | custom-call | flops 20000000000 | bytes 25000000 | tf_op jit(solution)/shard_map/attend/pallas_call | solution.py:300
  58.0 0.6 copy-done.7
  58.8 0.5 collective-permute-start.11
  59.3 0.5 collective-permute-start.13
  60.5 0.4 collective-permute-done.11.refs_3_
  60.9 0.4 collective-permute-done.12.refs_5_
  61.2 0.4 collective-permute-done.13.refs_7_
  61.6 0.3 copy-done.22
  61.9 0.4 copy-done.23
  62.3 63.4 %feed.1 = (bf16[197,24,384]{2,1,0:T(8,128)(2,1)}, f32[200,24,384]{2,1,0:T(8,128)}, bf16[200,24,384]{2,1,0:T(8,128)(2,1)}, f32[8,1152]{1,0:T(8,128)}, f32[64,384]...) custom-call(s32[1]{0:T(128)} %bitcast.me_ref, s32[1]{0:T(128)S(6)} %copy.76.cnt_ref, ...), custom_call_target="tpu_custom_call" | custom-call | flops 44999999488 | bytes 30000000 | tf_op jit(solution)/shard_map/feed/pallas_call | solution.py:495
  125.7 0.2 collective-permute-start.14
  125.9 2.7 %collective-permute-done.14 = bf16[4,48,2688]{2,1,0:T(8,128)(2,1)S(1)} collective-permute-done((bf16[4,48,2688]{2,1,0:T(8,128)(2,1)}, bf16[4,48,2688]{2,1,0:T(8,128)(2,1)S(1)}, u32[]{:S(2)}, u32[]{:S(2)}) %collective-permute-start.14) | collective-permute-done | bytes 1032224 | tf_op jit(solution)/shard_map/ppermute | solution.py:791
  128.6 1.8 fusion.9
  130.6 3.4 %collective-permute-start.17 = (bf16[48,2688]{1,0:T(8,128)(2,1)S(1)}, bf16[48,2688]{1,0:T(8,128)(2,1)S(1)}, u32[]{:S(2)}, u32[]{:S(2)}) collective-permute-start(bf16[48,2688]{1,0:T(8,128)(2,1)S(1)} %get-tuple-element.144.refs_2_), channel_id=1, source_target_pairs={{0,6},{1,7},{2,4},{3,5},{4,2},{5,3},{6,0},{7,1},{8,14},{9,15},{10,... | collective-permute-start | bytes 774152 | tf_op jit(solution)/shard_map/ppermute | solution.py:796
  133.9 1.1 collective-permute-start.15
  135.0 51.9 %back.1 = (bf16[197,24,384]{2,1,0:T(8,128)(2,1)}, bf16[4,56,1152]{2,1,0:T(8,128)(2,1)}, f32[4,56,1152]{2,1,0:T(8,128)}) custom-call(s32[1]{0:T(128)} %bitcast.me_ref, bf16[24,208,384]{2,1,0:T(8,128)(2,1)} %get-tuple-element.99.a_ref, f32[24,208,384]{2,1,0:T(8,128)} %get-tuple-element.83.xh_ref, f32[24,208,128]{2,1,0:T(8,128)} %get-tuple-element.85.refs_4_.r_ref, ...), custom_call_target="tpu_custom_call" | custom-call | flops 40000000000 | bytes 30000000 | tf_op jit(solution)/shard_map/back/pallas_call | solution.py:710
  187.0 0.6 copy-done
  187.9 2.1 collective-permute-done.18
  190.0 1.3 fusion.8
  191.4 1.0 collective-permute-start.19
  192.4 2.4 %collective-permute-start.21 = (bf16[56,1152]{1,0:T(8,128)(2,1)S(1)}, bf16[56,1152]{1,0:T(8,128)(2,1)S(1)}, u32[]{:S(2)}, u32[]{:S(2)}) collective-permute-start(bf16[56,1152]{1,0:T(8,128)(2,1)S(1)} %get-tuple-element.148), channel_id=1, source_target_pairs={{0,6},{1,7},{2,4},{3,5},{4,2},{5,3},{6,0},{7,1},{8,14},{9,15},{10,... | collective-permute-start | bytes 387080 | tf_op jit(solution)/shard_map/ppermute | solution.py:796
  194.9 0.5 collective-permute-start.20
  195.3 0.1 fusion.3.refs_0_
  195.5 2.5 %collective-permute-start.27 = (bf16[48,2688]{1,0:T(8,128)(2,1)S(1)}, bf16[48,2688]{1,0:T(8,128)(2,1)S(1)}, u32[]{:S(2)}, u32[]{:S(2)}) collective-permute-start(bf16[48,2688]{1,0:T(8,128)(2,1)S(1)} %fusion.3.refs_0_), channel_id=1, source_target_pairs={{0,24},{8,16},{16,8},{24,0},{1,25},{9,17},{17,9},{25,1},{2,26},{10... | collective-permute-start | bytes 774152 | tf_op jit(solution)/shard_map/ppermute | solution.py:803
  198.0 0.5 collective-permute-start.26
  198.5 0.5 collective-permute-start.25
  199.1 2.8 %collective-permute-done.21 = bf16[56,1152]{1,0:T(8,128)(2,1)S(1)} collective-permute-done((bf16[56,1152]{1,0:T(8,128)(2,1)S(1)}, bf16[56,1152]{1,0:T(8,128)(2,1)S(1)}, u32[]{:S(2)}, u32[]{:S(2)}) %collective-permute-start.21) | collective-permute-done | bytes 129056 | tf_op jit(solution)/shard_map/ppermute | solution.py:796
  201.9 5.2 %collective-permute-done.20 = bf16[56,1152]{1,0:T(8,128)(2,1)S(1)} collective-permute-done((bf16[56,1152]{1,0:T(8,128)(2,1)S(1)}, bf16[56,1152]{1,0:T(8,128)(2,1)S(1)}, u32[]{:S(2)}, u32[]{:S(2)}) %collective-permute-start.20) | collective-permute-done | bytes 129056 | tf_op jit(solution)/shard_map/ppermute | solution.py:796
  207.2 2.5 %collective-permute-start.24 = (bf16[56,1152]{1,0:T(8,128)(2,1)S(1)}, bf16[56,1152]{1,0:T(8,128)(2,1)S(1)}, u32[]{:S(2)}, u32[]{:S(2)}) collective-permute-start(bf16[56,1152]{1,0:T(8,128)(2,1)S(1)} %fusion.7.refs_0_), channel_id=1, source_target_pairs={{0,24},{8,16},{16,8},{24,0},{1,25},{9,17},{17,9},{25,1},{2,26},{10... | collective-permute-start | bytes 387080 | tf_op jit(solution)/shard_map/ppermute | solution.py:803
  209.7 0.5 collective-permute-start.23
  210.2 0.5 collective-permute-start.22
  210.8 0.1 copy-done.17
  210.9 0.5 copy-done.18
  211.5 3.3 %adam.3 = (f32[48,384]{1,0:T(8,128)}, f32[48,1152]{1,0:T(8,128)}, f32[48,1152]{1,0:T(8,128)}, f32[48,384]{1,0:T(8,128)}, f32[48,1152]{1,0:T(8,128)}, /*index=5*/...) custom-call(s32[6]{0:T(128)} %flag_ref.3, ...), custom_call_target="tpu_custom_call" | custom-call | flops 1000000000 | bytes 5000000 | tf_op jit(solution)/shard_map/adam/pallas_call | solution.py:751
  214.9 0.8 collective-permute-done.23.refs_2_
  215.8 0.5 copy-done.27
  216.4 0.1 copy-done.30
  216.5 2.6 %adam.2 = (f32[48,1152]{1,0:T(8,128)}, f32[1,144]{1,0:T(1,128)}, f32[6,48]{1,0:T(8,128)}, f32[48,1152]{1,0:T(8,128)}, f32[1,144]{1,0:T(1,128)}, /*index=5*/f32[6...) custom-call(s32[6]{0:T(128)} %flag_ref.3, ...), custom_call_target="tpu_custom_call" | custom-call | flops 1000000000 | bytes 5000000 | tf_op jit(solution)/shard_map/adam/pallas_call | solution.py:751
  (87 shorter events, 1.1 us)
Async XLA Ops:
  2.7 17.1 %collective-permute-start.2 = (bf16[56,1152]{1,0:T(8,128)(2,1)}, bf16[56,1152]{1,0:T(8,128)(2,1)S(1)}, u32[]{:S(2)}, u32[]{:S(2)}) collective-permute-start(bf16[56,1152]{1,0:T(8,128)(2,1)} %get-tuple-element.84.refs_0_), channel_id=1, source_target_pairs={{0,6},{1,7},{2,4},{3,5},{4,2},{5,3},{6,0},{7,1},{8,14},{9,15},{10,... | collective-permute-start | bytes 387080 | tf_op jit(solution)/shard_map/ppermute | solution.py:782
  7.7 12.1 %collective-permute-start.1 = (bf16[56,1152]{1,0:T(8,128)(2,1)}, bf16[56,1152]{1,0:T(8,128)(2,1)S(1)}, u32[]{:S(2)}, u32[]{:S(2)}) collective-permute-start(bf16[56,1152]{1,0:T(8,128)(2,1)} %get-tuple-element.84.refs_0_), channel_id=1, source_target_pairs={{0,4},{1,5},{2,6},{3,7},{4,0},{5,1},{6,2},{7,3},{8,12},{9,13},{10,... | collective-permute-start | bytes 387080 | tf_op jit(solution)/shard_map/ppermute | solution.py:782
  7.7 12.1 %collective-permute-start = (bf16[56,1152]{1,0:T(8,128)(2,1)}, bf16[56,1152]{1,0:T(8,128)(2,1)S(1)}, u32[]{:S(2)}, u32[]{:S(2)}) collective-permute-start(bf16[56,1152]{1,0:T(8,128)(2,1)} %get-tuple-element.84.refs_0_), channel_id=1, source_target_pairs={{0,2},{1,3},{2,0},{3,1},{4,6},{5,7},{6,4},{7,5},{8,10},{9,11},{10,... | collective-permute-start | bytes 387080 | tf_op jit(solution)/shard_map/ppermute | solution.py:782
  20.6 4.8 %collective-permute-start.3 = (bf16[56,1152]{1,0:T(8,128)(2,1)}, bf16[56,1152]{1,0:T(8,128)(2,1)S(1)}, u32[]{:S(2)}, u32[]{:S(2)}) collective-permute-start(bf16[56,1152]{1,0:T(8,128)(2,1)} %get-tuple-element.86.refs_0_), channel_id=1, source_target_pairs={{0,1},{1,0},{2,3},{3,2},{4,5},{5,4},{6,7},{7,6},{8,9},{9,8},{10,11... | collective-permute-start | bytes 387080 | tf_op jit(solution)/shard_map/ppermute | solution.py:786
  20.6 4.9 %collective-permute-start.4 = (bf16[56,1152]{1,0:T(8,128)(2,1)}, bf16[56,1152]{1,0:T(8,128)(2,1)S(1)}, u32[]{:S(2)}, u32[]{:S(2)}) collective-permute-start(bf16[56,1152]{1,0:T(8,128)(2,1)} %get-tuple-element.87.refs_2_), channel_id=1, source_target_pairs={{0,1},{1,0},{2,3},{3,2},{4,5},{5,4},{6,7},{7,6},{8,9},{9,8},{10,11... | collective-permute-start | bytes 387080 | tf_op jit(solution)/shard_map/ppermute | solution.py:786
  21.1 5.4 %collective-permute-start.5 = (bf16[56,1152]{1,0:T(8,128)(2,1)}, bf16[56,1152]{1,0:T(8,128)(2,1)S(1)}, u32[]{:S(2)}, u32[]{:S(2)}) collective-permute-start(bf16[56,1152]{1,0:T(8,128)(2,1)} %get-tuple-element.88.refs_4_), channel_id=1, source_target_pairs={{0,1},{1,0},{2,3},{3,2},{4,5},{5,4},{6,7},{7,6},{8,9},{9,8},{10,11... | collective-permute-start | bytes 387080 | tf_op jit(solution)/shard_map/ppermute | solution.py:786
  21.1 5.4 %collective-permute-start.6 = (bf16[56,1152]{1,0:T(8,128)(2,1)}, bf16[56,1152]{1,0:T(8,128)(2,1)S(1)}, u32[]{:S(2)}, u32[]{:S(2)}) collective-permute-start(bf16[56,1152]{1,0:T(8,128)(2,1)} %get-tuple-element.89.refs_6_.refs_1_), channel_id=1, source_target_pairs={{0,1},{1,0},{2,3},{3,2},{4,5},{5,4},{6,7},{7,6},{8,9},{9,8},{10,11... | collective-permute-start | bytes 387080 | tf_op jit(solution)/shard_map/ppermute | solution.py:786
  21.6 36.3 %collective-permute-start.9 = (bf16[48,2688]{1,0:T(8,128)(2,1)}, bf16[48,2688]{1,0:T(8,128)(2,1)S(1)}, u32[]{:S(2)}, u32[]{:S(2)}) collective-permute-start(bf16[48,2688]{1,0:T(8,128)(2,1)} %touch.5.refs_0_), channel_id=1, source_target_pairs={{0,6},{1,7},{2,4},{3,5},{4,2},{5,3},{6,0},{7,1},{8,14},{9,15},{10,... | collective-permute-start | bytes 774152 | tf_op jit(solution)/shard_map/ppermute | solution.py:782
  25.4 1.1 copy-start.24
  25.4 32.5 %collective-permute-start.8 = (bf16[48,2688]{1,0:T(8,128)(2,1)}, bf16[48,2688]{1,0:T(8,128)(2,1)S(1)}, u32[]{:S(2)}, u32[]{:S(2)}) collective-permute-start(bf16[48,2688]{1,0:T(8,128)(2,1)} %touch.5.refs_0_), channel_id=1, source_target_pairs={{0,4},{1,5},{2,6},{3,7},{4,0},{5,1},{6,2},{7,3},{8,12},{9,13},{10,... | collective-permute-start | bytes 774152 | tf_op jit(solution)/shard_map/ppermute | solution.py:782
  25.4 1.1 copy-start.26
  25.4 32.5 %collective-permute-start.7 = (bf16[48,2688]{1,0:T(8,128)(2,1)}, bf16[48,2688]{1,0:T(8,128)(2,1)S(1)}, u32[]{:S(2)}, u32[]{:S(2)}) collective-permute-start(bf16[48,2688]{1,0:T(8,128)(2,1)} %touch.5.refs_0_), channel_id=1, source_target_pairs={{0,2},{1,3},{2,0},{3,1},{4,6},{5,7},{6,4},{7,5},{8,10},{9,11},{10,... | collective-permute-start | bytes 774152 | tf_op jit(solution)/shard_map/ppermute | solution.py:782
  57.9 0.8 copy-start.8
  57.9 0.8 copy-start.9
  58.8 1.7 collective-permute-start.10
  58.8 2.1 collective-permute-start.11
  59.3 2.0 collective-permute-start.12
  59.3 2.3 %collective-permute-start.13 = (bf16[48,2688]{1,0:T(8,128)(2,1)}, bf16[48,2688]{1,0:T(8,128)(2,1)S(1)}, u32[]{:S(2)}, u32[]{:S(2)}) collective-permute-start(bf16[48,2688]{1,0:T(8,128)(2,1)} %get-tuple-element.97.refs_6_), channel_id=1, source_target_pairs={{0,1},{1,0},{2,3},{3,2},{4,5},{5,4},{6,7},{7,6},{8,9},{9,8},{10,11... | collective-permute-start | bytes 774152 | tf_op jit(solution)/shard_map/ppermute | solution.py:786
  60.5 1.1 copy-start.20
  60.9 0.7 copy-start.21
  61.6 0.7 copy-start.23
  125.7 2.9 %collective-permute-start.14 = (bf16[4,48,2688]{2,1,0:T(8,128)(2,1)}, bf16[4,48,2688]{2,1,0:T(8,128)(2,1)S(1)}, u32[]{:S(2)}, u32[]{:S(2)}) collective-permute-start(bf16[4,48,2688]{2,1,0:T(8,128)(2,1)} %get-tuple-element.108), channel_id=1, source_target_pairs={{0,1},{1,0},{2,3},{3,2},{4,5},{5,4},{6,7},{7,6},{8,9},{9,8},{10,11... | collective-permute-start | bytes 3096584 | tf_op jit(solution)/shard_map/ppermute | solution.py:791
  130.5 4.5 %copy-start.11 = (bf16[48,2688]{1,0:T(8,128)(2,1)}, bf16[48,2688]{1,0:T(8,128)(2,1)S(1)}, u32[]{:S(2)}) copy-start(bf16[48,2688]{1,0:T(8,128)(2,1)S(1)} %get-tuple-element.146.refs_0_) | copy-start | bytes 774148
  130.6 4.5 %copy-start.12 = (bf16[48,2688]{1,0:T(8,128)(2,1)}, bf16[48,2688]{1,0:T(8,128)(2,1)S(1)}, u32[]{:S(2)}) copy-start(bf16[48,2688]{1,0:T(8,128)(2,1)S(1)} %get-tuple-element.145.refs_1_) | copy-start | bytes 774148
  130.6 4.5 %copy-start.13 = (bf16[48,2688]{1,0:T(8,128)(2,1)}, bf16[48,2688]{1,0:T(8,128)(2,1)S(1)}, u32[]{:S(2)}) copy-start(bf16[48,2688]{1,0:T(8,128)(2,1)S(1)} %get-tuple-element.144.refs_2_) | copy-start | bytes 774148
  130.6 56.4 %collective-permute-start.17 = (bf16[48,2688]{1,0:T(8,128)(2,1)S(1)}, bf16[48,2688]{1,0:T(8,128)(2,1)S(1)}, u32[]{:S(2)}, u32[]{:S(2)}) collective-permute-start(bf16[48,2688]{1,0:T(8,128)(2,1)S(1)} %get-tuple-element.144.refs_2_), channel_id=1, source_target_pairs={{0,6},{1,7},{2,4},{3,5},{4,2},{5,3},{6,0},{7,1},{8,14},{9,15},{10,... | collective-permute-start | bytes 774152 | tf_op jit(solution)/shard_map/ppermute | solution.py:796
  133.9 53.1 %collective-permute-start.16 = (bf16[48,2688]{1,0:T(8,128)(2,1)S(1)}, bf16[48,2688]{1,0:T(8,128)(2,1)S(1)}, u32[]{:S(2)}, u32[]{:S(2)}) collective-permute-start(bf16[48,2688]{1,0:T(8,128)(2,1)S(1)} %get-tuple-element.145.refs_1_), channel_id=1, source_target_pairs={{0,4},{1,5},{2,6},{3,7},{4,0},{5,1},{6,2},{7,3},{8,12},{9,13},{10,... | collective-permute-start | bytes 774152 | tf_op jit(solution)/shard_map/ppermute | solution.py:796
  133.9 53.1 %collective-permute-start.15 = (bf16[48,2688]{1,0:T(8,128)(2,1)S(1)}, bf16[48,2688]{1,0:T(8,128)(2,1)S(1)}, u32[]{:S(2)}, u32[]{:S(2)}) collective-permute-start(bf16[48,2688]{1,0:T(8,128)(2,1)S(1)} %get-tuple-element.146.refs_0_), channel_id=1, source_target_pairs={{0,2},{1,3},{2,0},{3,1},{4,6},{5,7},{6,4},{7,5},{8,10},{9,11},{10,... | collective-permute-start | bytes 774152 | tf_op jit(solution)/shard_map/ppermute | solution.py:796
  187.0 0.8 copy-start.2
  187.0 0.8 copy-start.4
  187.9 7.5 %copy-start.1 = (bf16[48,2688]{1,0:T(8,128)(2,1)S(1)}, bf16[48,2688]{1,0:T(8,128)(2,1)}, u32[]{:S(2)}) copy-start(bf16[48,2688]{1,0:T(8,128)(2,1)} %get-tuple-element.116) | copy-start | bytes 774148
  187.9 7.5 %copy-start.3 = (bf16[48,2688]{1,0:T(8,128)(2,1)S(1)}, bf16[48,2688]{1,0:T(8,128)(2,1)}, u32[]{:S(2)}) copy-start(bf16[48,2688]{1,0:T(8,128)(2,1)} %get-tuple-element.115) | copy-start | bytes 774148
  187.9 7.5 %copy-start.5 = (bf16[48,2688]{1,0:T(8,128)(2,1)S(1)}, bf16[48,2688]{1,0:T(8,128)(2,1)}, u32[]{:S(2)}) copy-start(bf16[48,2688]{1,0:T(8,128)(2,1)} %get-tuple-element.114) | copy-start | bytes 774148
  187.9 2.2 collective-permute-start.18
  191.4 7.1 %collective-permute-start.19 = (bf16[56,1152]{1,0:T(8,128)(2,1)S(1)}, bf16[56,1152]{1,0:T(8,128)(2,1)S(1)}, u32[]{:S(2)}, u32[]{:S(2)}) collective-permute-start(bf16[56,1152]{1,0:T(8,128)(2,1)S(1)} %get-tuple-element.147), channel_id=1, source_target_pairs={{0,2},{1,3},{2,0},{3,1},{4,6},{5,7},{6,4},{7,5},{8,10},{9,11},{10,... | collective-permute-start | bytes 387080 | tf_op jit(solution)/shard_map/ppermute | solution.py:796
  192.4 9.5 %collective-permute-start.21 = (bf16[56,1152]{1,0:T(8,128)(2,1)S(1)}, bf16[56,1152]{1,0:T(8,128)(2,1)S(1)}, u32[]{:S(2)}, u32[]{:S(2)}) collective-permute-start(bf16[56,1152]{1,0:T(8,128)(2,1)S(1)} %get-tuple-element.148), channel_id=1, source_target_pairs={{0,6},{1,7},{2,4},{3,5},{4,2},{5,3},{6,0},{7,1},{8,14},{9,15},{10,... | collective-permute-start | bytes 387080 | tf_op jit(solution)/shard_map/ppermute | solution.py:796
  194.9 12.3 %collective-permute-start.20 = (bf16[56,1152]{1,0:T(8,128)(2,1)S(1)}, bf16[56,1152]{1,0:T(8,128)(2,1)S(1)}, u32[]{:S(2)}, u32[]{:S(2)}) collective-permute-start(bf16[56,1152]{1,0:T(8,128)(2,1)S(1)} %get-tuple-element.149), channel_id=1, source_target_pairs={{0,4},{1,5},{2,6},{3,7},{4,0},{5,1},{6,2},{7,3},{8,12},{9,13},{10,... | collective-permute-start | bytes 387080 | tf_op jit(solution)/shard_map/ppermute | solution.py:796
  195.5 15.3 %copy-start.10 = (bf16[48,2688]{1,0:T(8,128)(2,1)}, bf16[48,2688]{1,0:T(8,128)(2,1)S(1)}, u32[]{:S(2)}) copy-start(bf16[48,2688]{1,0:T(8,128)(2,1)S(1)} %fusion.3.refs_0_) | copy-start | bytes 774148
  195.5 14.7 %collective-permute-start.27 = (bf16[48,2688]{1,0:T(8,128)(2,1)S(1)}, bf16[48,2688]{1,0:T(8,128)(2,1)S(1)}, u32[]{:S(2)}, u32[]{:S(2)}) collective-permute-start(bf16[48,2688]{1,0:T(8,128)(2,1)S(1)} %fusion.3.refs_0_), channel_id=1, source_target_pairs={{0,24},{8,16},{16,8},{24,0},{1,25},{9,17},{17,9},{25,1},{2,26},{10... | collective-permute-start | bytes 774152 | tf_op jit(solution)/shard_map/ppermute | solution.py:803
  198.0 12.7 %collective-permute-start.26 = (bf16[48,2688]{1,0:T(8,128)(2,1)S(1)}, bf16[48,2688]{1,0:T(8,128)(2,1)S(1)}, u32[]{:S(2)}, u32[]{:S(2)}) collective-permute-start(bf16[48,2688]{1,0:T(8,128)(2,1)S(1)} %fusion.3.refs_0_), channel_id=1, source_target_pairs={{0,16},{8,24},{16,0},{24,8},{1,17},{9,25},{17,1},{25,9},{2,18},{10... | collective-permute-start | bytes 774152 | tf_op jit(solution)/shard_map/ppermute | solution.py:803
  198.5 12.2 %collective-permute-start.25 = (bf16[48,2688]{1,0:T(8,128)(2,1)S(1)}, bf16[48,2688]{1,0:T(8,128)(2,1)S(1)}, u32[]{:S(2)}, u32[]{:S(2)}) collective-permute-start(bf16[48,2688]{1,0:T(8,128)(2,1)S(1)} %fusion.3.refs_0_), channel_id=1, source_target_pairs={{0,8},{8,0},{16,24},{24,16},{1,9},{9,1},{17,25},{25,17},{2,10},{10... | collective-permute-start | bytes 774152 | tf_op jit(solution)/shard_map/ppermute | solution.py:803
  207.2 8.7 %copy-start.16 = (bf16[56,1152]{1,0:T(8,128)(2,1)}, bf16[56,1152]{1,0:T(8,128)(2,1)S(1)}, u32[]{:S(2)}) copy-start(bf16[56,1152]{1,0:T(8,128)(2,1)S(1)} %fusion.7.refs_0_) | copy-start | bytes 387076
  207.2 7.7 %collective-permute-start.24 = (bf16[56,1152]{1,0:T(8,128)(2,1)S(1)}, bf16[56,1152]{1,0:T(8,128)(2,1)S(1)}, u32[]{:S(2)}, u32[]{:S(2)}) collective-permute-start(bf16[56,1152]{1,0:T(8,128)(2,1)S(1)} %fusion.7.refs_0_), channel_id=1, source_target_pairs={{0,24},{8,16},{16,8},{24,0},{1,25},{9,17},{17,9},{25,1},{2,26},{10... | collective-permute-start | bytes 387080 | tf_op jit(solution)/shard_map/ppermute | solution.py:803
  209.7 6.0 %collective-permute-start.23 = (bf16[56,1152]{1,0:T(8,128)(2,1)S(1)}, bf16[56,1152]{1,0:T(8,128)(2,1)S(1)}, u32[]{:S(2)}, u32[]{:S(2)}) collective-permute-start(bf16[56,1152]{1,0:T(8,128)(2,1)S(1)} %fusion.7.refs_0_), channel_id=1, source_target_pairs={{0,16},{8,24},{16,0},{24,8},{1,17},{9,25},{17,1},{25,9},{2,18},{10... | collective-permute-start | bytes 387080 | tf_op jit(solution)/shard_map/ppermute | solution.py:803
  210.2 0.7 copy-start.17
  210.2 5.6 %collective-permute-start.22 = (bf16[56,1152]{1,0:T(8,128)(2,1)S(1)}, bf16[56,1152]{1,0:T(8,128)(2,1)S(1)}, u32[]{:S(2)}, u32[]{:S(2)}) collective-permute-start(bf16[56,1152]{1,0:T(8,128)(2,1)S(1)} %fusion.7.refs_0_), channel_id=1, source_target_pairs={{0,8},{8,0},{16,24},{24,16},{1,9},{9,1},{17,25},{25,17},{2,10},{10... | collective-permute-start | bytes 387080 | tf_op jit(solution)/shard_map/ppermute | solution.py:803
  210.7 0.8 copy-start.19
  214.9 1.0 copy-start.25
  (11 other events, 7.5 us)

commit v4 on v3

--- a/solution.py
+++ b/solution.py
@@ -19,7 +19,7 @@
 DECAY_RATE = 0.5
 ADAM_STEPS = 10.0
 GROUP = 8
-PAIR = 2
+PAIR = 4
 EXTRA = 8
 ROOT_HALF = math.sqrt(0.5)
 
@@ -61,11 +61,9 @@
 
 
 def gelu_pair(u):
-    t = 1.0 / (1.0 + (0.3275911 * ROOT_HALF) * jnp.abs(u))
-    e = jnp.exp(-0.5 * (u * u))
-    q = t * (0.127414796 + t * (-0.142248368 + t * (0.7107068705 + t * (-0.7265760135 + t * 0.5307027145)))) * e
-    phi = jnp.where(u >= 0, 1.0 - q, q)
-    return u * phi, phi + u * e * 0.3989422804014327
+    phi = 0.5 + 0.5 * lax.erf(u * ROOT_HALF)
+    e = jnp.exp2((-0.5 * math.log2(math.e)) * (u * u))
+    return u * phi, phi + (u * (1.0 / math.sqrt(2.0 * math.pi))) * e
 
 
 def full(a):
@@ -149,7 +147,7 @@
         in_specs=[tok],
         out_specs=[img(D), img(128)],
         out_shape=[jax.ShapeDtypeStruct((N, SP, d), F32) for d in (D, 128)],
-        scratch_shapes=[pltpu.VMEM((D // 128, SEQ * GROUP, 128), F32)],
+        scratch_shapes=[pltpu.VMEM((D // 128, up(SEQ, 8) * GROUP, 128), F32)],
         name="norm",
         **params(8 * 10**9, 15 * 10**6),
     )(x)
@@ -196,11 +194,11 @@
         a_scr[i * SP + t : i * SP + t + n, :] = y
         a_ref[i, t : t + n, :] = y
 
-    def qkv(i, t, c, w):
-        y = dot(a_scr[i * SP : (i + 1) * SP, :], w_ref[:, t * D + c : t * D + c + w])
+    def qkv(t, c, w):
+        y = dot(a_scr[...], w_ref[:, t * D + c : t * D + c + w])
         if t == 0:
             y = y * (HEAD_DIM**-0.5)
-        qkv_ref[i, :, t * D + c : t * D + c + w] = y.astype(BF)
+        qkv_ref[:, :, t * D + c : t * D + c + w] = y.astype(BF).reshape(PAIR, SP, w)
 
     def score(u):
         i, h = divmod(u, H)
@@ -246,30 +244,28 @@
             y = jnp.concatenate([st["o"], y], axis=1)
             os_[h // 2, pl.ds(pl.multiple_of((j * PAIR + i) * TP, 8), SEQ), :] = y[:SEQ]
 
-    rows = tiles(SEQ, 48)
-    for t, n in rows:
-        ln(0, t, n)
+    for i in range(PAIR):
+        for t, n in tiles(SEQ, 48):
+            ln(i, t, n)
     c0 = min(256, D)
-    cs = tiles(D, 256)
-    weave([partial(qkv, 0, t, 0, c0) for t in range(3)], [partial(ln, 1, t, n) for t, n in rows])
-    rest = [partial(qkv, 0, t, c, w) for c, w in cs[1:] for t in range(3)]
-    rest += [partial(qkv, 1, t, c, w) for c, w in cs for t in range(3)]
+    hb = c0 // HEAD_DIM
+    for t in range(3):
+        qkv(t, 0, c0)
+    rest = [partial(qkv, t, c, w) for c, w in tiles(D, 256)[1:] for t in range(3)]
     srows = tiles(S8, 64) + ([(S8, 8)] if S8 < SEQ else [])
-    nu = PAIR * H
-    score(0)
-    done = 0
-    for k in range(nu):
-        ms = []
-        need = 3 if k < 2 else 2
-        ms += rest[done : done + need]
-        done += need
+    order = [i * H + h for i in range(PAIR) for h in range(hb)]
+    order += [i * H + h for i in range(PAIR) for h in range(hb, H)]
+    nu = len(order)
+    score(order[0])
+    for k, u in enumerate(order):
+        ms = rest[k : k + 1]
         if k + 1 < nu:
-            ms.append(partial(score, k + 1))
+            ms.append(partial(score, order[k + 1]))
         if k >= 1:
-            ms.append(partial(mix, k - 1))
-        vs = [partial(f, k, t, n) for f in (vmax, vexp, vnorm) for t, n in srows]
+            ms.append(partial(mix, order[k - 1]))
+        vs = [partial(f, u, t, n) for f in (vmax, vexp, vnorm) for t, n in srows]
         weave(ms, vs)
-    assert done >= len(rest)
+    nu = order[-1] + 1
     mix(nu - 1)
     for i in range(PAIR):
         a_ref[i, SEQ:SP, :] = jnp.zeros((SP - SEQ, D), BF)
@@ -373,11 +369,11 @@
     us = (u0, u1)
     ds = (d0, d1)
 
-    def m_u(i, h):
+    def m_u(i, h, HR=HR):
         c, w = cols[i]
         us[i % 2][h : h + HR, :w] = dot(b_scr[h : h + HR, :], w1_ref[:, c : c + w]) + c1_ref[0:1, c : c + w]
 
-    def m_d(i, h):
+    def m_d(i, h, HR=HR):
         c, w = cols[i]
         ds[i % 2][h : h + HR, :w] = dot(dy_scr[h : h + HR, :], w2t_ref[:, c : c + w])
 
@@ -397,10 +393,10 @@
         c, w = cols[i]
         t2_ref[:, c : c + w] += dot(dyt_scr[...], g_scr[:, c : c + w])
 
-    def m_y(h):
+    def m_y(h, HR=HR):
         y_scr[h : h + HR, :] = dot(g_scr[h : h + HR, :], w2t_ref[...], 1, 1)
 
-    def m_db(h):
+    def m_db(h, HR=HR):
         db_scr[h : h + HR, :] = dot(du_scr[h : h + HR, :], w1_ref[...], 1, 1)
 
     def v_out(r):
@@ -442,17 +438,15 @@
     for i in range(len(cols)):
         ms = []
         if i < last:
-            ms += [partial(f, i + 1, h) for f in (m_u, m_d) for h in (0, HR)]
+            ms += [partial(f, i + 1, 0, R) for f in (m_u, m_d)]
         if i >= 1:
             ms += [partial(m_t1, i - 1), partial(m_t2, i - 1)]
         weave(ms, [partial(v_gelu, i, r) for r in range(0, R, 16)])
         c, w = cols[i]
         tc1_ref[:, c : c + w] += acc[("c1", i)]
-    m_db(0)
-    weave([partial(m_db, HR)], [partial(v_back, r) for r in first])
-    weave([partial(m_y, 0), partial(m_do, 0)], [partial(v_back, r) for r in second])
-    weave([partial(m_y, HR), partial(m_do, HR)], [partial(v_out, r) for r in first])
-    weave([partial(m_t1, last), partial(m_t2, last), m_tp], [partial(v_out, r) for r in second])
+    m_db(0, R)
+    weave([partial(m_y, 0, R)], [partial(v_back, r) for r in first + second])
+    weave([partial(m_do, 0), partial(m_do, HR), m_tp, partial(m_t1, last), partial(m_t2, last)], [partial(v_out, r) for r in first + second])
     for i, k in ((2, "cp"), (3, "g2"), (4, "e2"), (5, "c2")):
         tv_ref[i * 8 : i * 8 + 8, :] += acc[k]
 
@@ -595,7 +589,7 @@
     for t, n in rows:
         load(0, t, n)
     at_scr[...] = a_ref[...].reshape(PAIR * SP, D).T
-    pre = [partial(load, 1, t, n) for t, n in rows]
+    pre = [partial(load, i, t, n) for i in range(1, PAIR) for t, n in rows]
     nu = PAIR * H
     score(0)
     dprob(0)
@@ -606,16 +600,15 @@
         if k >= 1:
             ms += [partial(m_dv, k - 1), partial(m_dk, k - 1), partial(m_dq, k - 1)]
         vs = [partial(f, k, t, n) for f in (v_prob, v_ds) for t, n in srows]
-        vs += pre[3 * k : 3 * k + 3]
+        vs += pre[k : k + 1]
         weave(ms, vs)
-    assert 3 * nu >= len(pre)
     m_dv(nu - 1)
     m_dk(nu - 1)
     m_dq(nu - 1)
     acc = {}
 
-    def m_da(i):
-        da_scr[i * SP : (i + 1) * SP, :] = dot(d_scr[i * SP : (i + 1) * SP, :], w_ref[...], 1, 1)
+    def m_da():
+        da_scr[...] = dot(d_scr[...], w_ref[...], 1, 1)
 
     def m_tq(c, w):
         tq_ref[:, c : c + w] += dot(at_scr[...], d_scr[:, c : c + w])
@@ -644,9 +637,8 @@
         add("e", d)
 
     cols = tiles(W3, 256)
-    m_da(0)
-    weave([partial(m_da, 1)] + [partial(m_tq, c, w) for c, w in cols[:2]], [partial(v_back, 0, t, n) for t, n in rows])
-    weave([partial(m_tq, c, w) for c, w in cols[2:]], [partial(v_back, 1, t, n) for t, n in rows])
+    m_da()
+    weave([partial(m_tq, c, w) for c, w in cols], [partial(v_back, i, t, n) for i in range(PAIR) for t, n in rows])
     tv_ref[0:8, :] += acc["g"]
     tv_ref[8:16, :] += acc["e"]
     if "gtail" in acc:

time: 220 us -> 205 us (0.932)
  Pallas kernels: 165 us -> 151 us
    pallas_call x1, Pallas kernels: 63.4 us -> 53.7 us  [feed(): pl.pallas_call(partial(feed_body, SEQ, D, FF, T, N, np_), grid_spec=pltpu...]
  transfers between devices with their start and end apart: 28 -> 28, of which waited for: 10 -> 11; matrix products, arithmetic and copies ran while one was open for 0% -> 0% of each run, Pallas kernels for 44% -> 45%
where the time goes in v4:
time: 205 us
  Pallas kernels  151 us (74%)
  starting transfers between devices  28.1 us (14%)
  waiting for transfers between devices  15.2 us (7%)
  local copies, waits for them, and re-layouts  5.26 us (3%)
  other arithmetic  3.38 us (2%)
    pallas_call x1, Pallas kernels, feed(): pl.pallas_call(partial(feed_body, SEQ, D, FF, T, N, np_), grid_spec=pltpu...  53.7 us
    pallas_call x1, Pallas kernels, back(): pl.pallas_call(partial(back_body, SEQ, SP, TP, D, FF, np_, len(deps)), gr...  50.1 us
    pallas_call x1, Pallas kernels, attend(): pl.pallas_call(partial(attend_body, SEQ, SP, TP, D, np_), grid_spec=pltpu...  28.7 us
    ppermute x6, starting transfers between devices, fetch(): return [x] + [lax.ppermute(x, 'fsdp', pairs(n, k)) for k in range(2, n, 2)]  10.3 us
    pallas_call x1, Pallas kernels, norm(): pl.pallas_call(partial(norm_body, SEQ, D), grid=(N // GROUP, GROUP // PAI...  10.3 us
    ppermute x6, starting transfers between devices, along_z(): lax.ppermute(x, 'fsdp', pairs(n, 2 * k + 2))  8.38 us
    ppermute x6, waiting for transfers between devices, along_z(): lax.ppermute(x, 'fsdp', pairs(n, 2 * k + 2))  8.06 us
    ppermute x6, starting transfers between devices, finish(): return [b] + [lax.ppermute(b, 'dp', pairs(d, k)) for k in range(1, d)]  7.11 us
  transfers between devices with their start and end apart: 28, of which 11 were waited for; matrix products, arithmetic and copies ran while one was open for 0% of the time, Pallas kernels for 45%

profile of v4, /device:TPU:0, one launch (start us, length us, event | category | flops | bytes accessed | tf_op | source)
XLA Modules:
  0.0 204.5 jit_solution(2450223525304970877)
XLA Ops:
  0.7 2.0 pack.1
  2.7 5.0 %collective-permute-start.2 = (bf16[56,1152]{1,0:T(8,128)(2,1)}, bf16[56,1152]{1,0:T(8,128)(2,1)S(1)}, u32[]{:S(2)}, u32[]{:S(2)}) collective-permute-start(bf16[56,1152]{1,0:T(8,128)(2,1)} %get-tuple-element.84.refs_0_), channel_id=1, source_target_pairs={{0,6},{1,7},{2,4},{3,5},{4,2},{5,3},{6,0},{7,1},{8,14},{9,15},{10,... | collective-permute-start | bytes 387080 | tf_op jit(solution)/shard_map/ppermute | solution.py:774
  7.7 0.6 collective-permute-start
  8.3 10.3 %norm.1 = (f32[24,208,384]{2,1,0:T(8,128)}, f32[24,208,128]{2,1,0:T(8,128)}) custom-call(bf16[197,24,384]{2,1,0:T(8,128)(2,1)} %bitcast.55), custom_call_target="tpu_custom_call" | custom-call | flops 8000000000 | bytes 15000000 | tf_op jit(solution)/shard_map/norm/pallas_call | solution.py:144
  18.6 0.2 collective-permute-done.1.refs_2_
  18.9 0.4 copy-done.6
  19.3 0.3 copy-done.14
  19.5 0.5 collective-permute-start.4
  20.1 0.5 collective-permute-start.6
  20.6 3.6 %collective-permute-start.9 = (bf16[48,2688]{1,0:T(8,128)(2,1)}, bf16[48,2688]{1,0:T(8,128)(2,1)S(1)}, u32[]{:S(2)}, u32[]{:S(2)}) collective-permute-start(bf16[48,2688]{1,0:T(8,128)(2,1)} %touch.5.refs_0_), channel_id=1, source_target_pairs={{0,6},{1,7},{2,4},{3,5},{4,2},{5,3},{6,0},{7,1},{8,14},{9,15},{10,... | collective-permute-start | bytes 774152 | tf_op jit(solution)/shard_map/ppermute | solution.py:774
  24.2 1.1 collective-permute-start.7
  25.3 0.6 copy-done.28
  26.0 28.7 %attend.1 = (bf16[24,208,1152]{2,1,0:T(8,128)(2,1)}, bf16[200,24,384]{2,1,0:T(8,128)(2,1)}, f32[24,8,208]{2,1,0:T(8,128)}, bf16[24,208,384]{2,1,0:T(8,128)(2,1)}...) custom-call(s32[1]{0:T(128)} %bitcast.me_ref, f32[24,208,384]{2,1,0:T(8,128)} %get-tuple-element.83.xh_ref, ...), custom_call_target="tpu_custom_call" | custom-call | flops 20000000000 | bytes 25000000 | tf_op jit(solution)/shard_map/attend/pallas_call | solution.py:296
  54.7 0.6 copy-done.7
  55.6 0.5 collective-permute-start.11
  56.1 0.5 collective-permute-start.13
  57.3 0.4 collective-permute-done.11.refs_3_
  57.7 0.4 collective-permute-done.12.refs_5_
  58.0 0.4 collective-permute-done.13.refs_7_
  58.4 0.3 copy-done.22
  58.7 0.4 copy-done.23
  59.1 53.7 %feed.1 = (bf16[197,24,384]{2,1,0:T(8,128)(2,1)}, f32[200,24,384]{2,1,0:T(8,128)}, bf16[200,24,384]{2,1,0:T(8,128)(2,1)}, f32[8,1152]{1,0:T(8,128)}, f32[64,384]...) custom-call(s32[1]{0:T(128)} %bitcast.me_ref, s32[1]{0:T(128)S(6)} %copy.76.cnt_ref, ...), custom_call_target="tpu_custom_call" | custom-call | flops 44999999488 | bytes 30000000 | tf_op jit(solution)/shard_map/feed/pallas_call | solution.py:489
  112.8 0.2 collective-permute-start.14
  113.0 2.7 %collective-permute-done.14 = bf16[4,48,2688]{2,1,0:T(8,128)(2,1)S(1)} collective-permute-done((bf16[4,48,2688]{2,1,0:T(8,128)(2,1)}, bf16[4,48,2688]{2,1,0:T(8,128)(2,1)S(1)}, u32[]{:S(2)}, u32[]{:S(2)}) %collective-permute-start.14) | collective-permute-done | bytes 1032224 | tf_op jit(solution)/shard_map/ppermute | solution.py:783
  115.8 1.8 fusion.9
  117.7 3.4 %collective-permute-start.17 = (bf16[48,2688]{1,0:T(8,128)(2,1)S(1)}, bf16[48,2688]{1,0:T(8,128)(2,1)S(1)}, u32[]{:S(2)}, u32[]{:S(2)}) collective-permute-start(bf16[48,2688]{1,0:T(8,128)(2,1)S(1)} %get-tuple-element.144.refs_2_), channel_id=1, source_target_pairs={{0,6},{1,7},{2,4},{3,5},{4,2},{5,3},{6,0},{7,1},{8,14},{9,15},{10,... | collective-permute-start | bytes 774152 | tf_op jit(solution)/shard_map/ppermute | solution.py:788
  121.1 1.1 collective-permute-start.15
  122.2 50.1 %back.1 = (bf16[197,24,384]{2,1,0:T(8,128)(2,1)}, bf16[4,56,1152]{2,1,0:T(8,128)(2,1)}, f32[4,56,1152]{2,1,0:T(8,128)}) custom-call(s32[1]{0:T(128)} %bitcast.me_ref, bf16[24,208,384]{2,1,0:T(8,128)(2,1)} %get-tuple-element.99.a_ref, f32[24,208,384]{2,1,0:T(8,128)} %get-tuple-element.83.xh_ref, f32[24,208,128]{2,1,0:T(8,128)} %get-tuple-element.85.refs_4_.r_ref, ...), custom_call_target="tpu_custom_call" | custom-call | flops 40000000000 | bytes 30000000 | tf_op jit(solution)/shard_map/back/pallas_call | solution.py:702
  172.3 0.6 copy-done
  173.2 2.1 %collective-permute-done.18 = bf16[4,56,1152]{2,1,0:T(8,128)(2,1)S(1)} collective-permute-done((bf16[4,56,1152]{2,1,0:T(8,128)(2,1)}, bf16[4,56,1152]{2,1,0:T(8,128)(2,1)S(1)}, u32[]{:S(2)}, u32[]{:S(2)}) %collective-permute-start.18) | collective-permute-done | bytes 516128 | tf_op jit(solution)/shard_map/ppermute | solution.py:783
  175.3 1.3 fusion.8
  176.7 1.0 collective-permute-start.19
  177.7 2.4 %collective-permute-start.21 = (bf16[56,1152]{1,0:T(8,128)(2,1)S(1)}, bf16[56,1152]{1,0:T(8,128)(2,1)S(1)}, u32[]{:S(2)}, u32[]{:S(2)}) collective-permute-start(bf16[56,1152]{1,0:T(8,128)(2,1)S(1)} %get-tuple-element.148), channel_id=1, source_target_pairs={{0,6},{1,7},{2,4},{3,5},{4,2},{5,3},{6,0},{7,1},{8,14},{9,15},{10,... | collective-permute-start | bytes 387080 | tf_op jit(solution)/shard_map/ppermute | solution.py:788
  180.1 0.5 collective-permute-start.20
  180.8 2.5 %collective-permute-start.27 = (bf16[48,2688]{1,0:T(8,128)(2,1)S(1)}, bf16[48,2688]{1,0:T(8,128)(2,1)S(1)}, u32[]{:S(2)}, u32[]{:S(2)}) collective-permute-start(bf16[48,2688]{1,0:T(8,128)(2,1)S(1)} %fusion.3.refs_0_), channel_id=1, source_target_pairs={{0,24},{8,16},{16,8},{24,0},{1,25},{9,17},{17,9},{25,1},{2,26},{10... | collective-permute-start | bytes 774152 | tf_op jit(solution)/shard_map/ppermute | solution.py:795
  183.3 0.5 collective-permute-start.26
  183.8 0.5 collective-permute-start.25
  184.3 2.8 %collective-permute-done.21 = bf16[56,1152]{1,0:T(8,128)(2,1)S(1)} collective-permute-done((bf16[56,1152]{1,0:T(8,128)(2,1)S(1)}, bf16[56,1152]{1,0:T(8,128)(2,1)S(1)}, u32[]{:S(2)}, u32[]{:S(2)}) %collective-permute-start.21) | collective-permute-done | bytes 129056 | tf_op jit(solution)/shard_map/ppermute | solution.py:788
  187.2 5.2 %collective-permute-done.20 = bf16[56,1152]{1,0:T(8,128)(2,1)S(1)} collective-permute-done((bf16[56,1152]{1,0:T(8,128)(2,1)S(1)}, bf16[56,1152]{1,0:T(8,128)(2,1)S(1)}, u32[]{:S(2)}, u32[]{:S(2)}) %collective-permute-start.20) | collective-permute-done | bytes 129056 | tf_op jit(solution)/shard_map/ppermute | solution.py:788
  192.5 2.5 %collective-permute-start.24 = (bf16[56,1152]{1,0:T(8,128)(2,1)S(1)}, bf16[56,1152]{1,0:T(8,128)(2,1)S(1)}, u32[]{:S(2)}, u32[]{:S(2)}) collective-permute-start(bf16[56,1152]{1,0:T(8,128)(2,1)S(1)} %fusion.7.refs_0_), channel_id=1, source_target_pairs={{0,24},{8,16},{16,8},{24,0},{1,25},{9,17},{17,9},{25,1},{2,26},{10... | collective-permute-start | bytes 387080 | tf_op jit(solution)/shard_map/ppermute | solution.py:795
  195.0 0.5 collective-permute-start.23
  195.5 0.5 collective-permute-start.22
  196.0 0.1 copy-done.17
  196.2 0.5 copy-done.18
  196.8 3.3 %adam.3 = (f32[48,384]{1,0:T(8,128)}, f32[48,1152]{1,0:T(8,128)}, f32[48,1152]{1,0:T(8,128)}, f32[48,384]{1,0:T(8,128)}, f32[48,1152]{1,0:T(8,128)}, /*index=5*/...) custom-call(s32[6]{0:T(128)} %flag_ref.3, ...), custom_call_target="tpu_custom_call" | custom-call | flops 1000000000 | bytes 5000000 | tf_op jit(solution)/shard_map/adam/pallas_call | solution.py:743
  200.2 0.8 collective-permute-done.23.refs_2_
  201.1 0.5 copy-done.27
  201.8 2.6 %adam.2 = (f32[48,1152]{1,0:T(8,128)}, f32[1,144]{1,0:T(1,128)}, f32[6,48]{1,0:T(8,128)}, f32[48,1152]{1,0:T(8,128)}, f32[1,144]{1,0:T(1,128)}, /*index=5*/f32[6...) custom-call(s32[6]{0:T(128)} %flag_ref.3, ...), custom_call_target="tpu_custom_call" | custom-call | flops 1000000000 | bytes 5000000 | tf_op jit(solution)/shard_map/adam/pallas_call | solution.py:743
  (87 shorter events, 1.3 us)
Async XLA Ops:
  2.7 15.9 %collective-permute-start.2 = (bf16[56,1152]{1,0:T(8,128)(2,1)}, bf16[56,1152]{1,0:T(8,128)(2,1)S(1)}, u32[]{:S(2)}, u32[]{:S(2)}) collective-permute-start(bf16[56,1152]{1,0:T(8,128)(2,1)} %get-tuple-element.84.refs_0_), channel_id=1, source_target_pairs={{0,6},{1,7},{2,4},{3,5},{4,2},{5,3},{6,0},{7,1},{8,14},{9,15},{10,... | collective-permute-start | bytes 387080 | tf_op jit(solution)/shard_map/ppermute | solution.py:774
  7.7 11.1 %collective-permute-start.1 = (bf16[56,1152]{1,0:T(8,128)(2,1)}, bf16[56,1152]{1,0:T(8,128)(2,1)S(1)}, u32[]{:S(2)}, u32[]{:S(2)}) collective-permute-start(bf16[56,1152]{1,0:T(8,128)(2,1)} %get-tuple-element.84.refs_0_), channel_id=1, source_target_pairs={{0,4},{1,5},{2,6},{3,7},{4,0},{5,1},{6,2},{7,3},{8,12},{9,13},{10,... | collective-permute-start | bytes 387080 | tf_op jit(solution)/shard_map/ppermute | solution.py:774
  7.7 11.1 %collective-permute-start = (bf16[56,1152]{1,0:T(8,128)(2,1)}, bf16[56,1152]{1,0:T(8,128)(2,1)S(1)}, u32[]{:S(2)}, u32[]{:S(2)}) collective-permute-start(bf16[56,1152]{1,0:T(8,128)(2,1)} %get-tuple-element.84.refs_0_), channel_id=1, source_target_pairs={{0,2},{1,3},{2,0},{3,1},{4,6},{5,7},{6,4},{7,5},{8,10},{9,11},{10,... | collective-permute-start | bytes 387080 | tf_op jit(solution)/shard_map/ppermute | solution.py:774
  19.5 4.6 %collective-permute-start.3 = (bf16[56,1152]{1,0:T(8,128)(2,1)}, bf16[56,1152]{1,0:T(8,128)(2,1)S(1)}, u32[]{:S(2)}, u32[]{:S(2)}) collective-permute-start(bf16[56,1152]{1,0:T(8,128)(2,1)} %get-tuple-element.86.refs_0_), channel_id=1, source_target_pairs={{0,1},{1,0},{2,3},{3,2},{4,5},{5,4},{6,7},{7,6},{8,9},{9,8},{10,11... | collective-permute-start | bytes 387080 | tf_op jit(solution)/shard_map/ppermute | solution.py:778
  19.5 4.6 %collective-permute-start.4 = (bf16[56,1152]{1,0:T(8,128)(2,1)}, bf16[56,1152]{1,0:T(8,128)(2,1)S(1)}, u32[]{:S(2)}, u32[]{:S(2)}) collective-permute-start(bf16[56,1152]{1,0:T(8,128)(2,1)} %get-tuple-element.87.refs_2_), channel_id=1, source_target_pairs={{0,1},{1,0},{2,3},{3,2},{4,5},{5,4},{6,7},{7,6},{8,9},{9,8},{10,11... | collective-permute-start | bytes 387080 | tf_op jit(solution)/shard_map/ppermute | solution.py:778
  20.1 5.2 %collective-permute-start.5 = (bf16[56,1152]{1,0:T(8,128)(2,1)}, bf16[56,1152]{1,0:T(8,128)(2,1)S(1)}, u32[]{:S(2)}, u32[]{:S(2)}) collective-permute-start(bf16[56,1152]{1,0:T(8,128)(2,1)} %get-tuple-element.88.refs_4_), channel_id=1, source_target_pairs={{0,1},{1,0},{2,3},{3,2},{4,5},{5,4},{6,7},{7,6},{8,9},{9,8},{10,11... | collective-permute-start | bytes 387080 | tf_op jit(solution)/shard_map/ppermute | solution.py:778
  20.1 5.2 %collective-permute-start.6 = (bf16[56,1152]{1,0:T(8,128)(2,1)}, bf16[56,1152]{1,0:T(8,128)(2,1)S(1)}, u32[]{:S(2)}, u32[]{:S(2)}) collective-permute-start(bf16[56,1152]{1,0:T(8,128)(2,1)} %get-tuple-element.89.refs_6_.refs_1_), channel_id=1, source_target_pairs={{0,1},{1,0},{2,3},{3,2},{4,5},{5,4},{6,7},{7,6},{8,9},{9,8},{10,11... | collective-permute-start | bytes 387080 | tf_op jit(solution)/shard_map/ppermute | solution.py:778
  20.6 34.1 %collective-permute-start.9 = (bf16[48,2688]{1,0:T(8,128)(2,1)}, bf16[48,2688]{1,0:T(8,128)(2,1)S(1)}, u32[]{:S(2)}, u32[]{:S(2)}) collective-permute-start(bf16[48,2688]{1,0:T(8,128)(2,1)} %touch.5.refs_0_), channel_id=1, source_target_pairs={{0,6},{1,7},{2,4},{3,5},{4,2},{5,3},{6,0},{7,1},{8,14},{9,15},{10,... | collective-permute-start | bytes 774152 | tf_op jit(solution)/shard_map/ppermute | solution.py:774
  24.2 1.1 copy-start.24
  24.2 30.5 %collective-permute-start.8 = (bf16[48,2688]{1,0:T(8,128)(2,1)}, bf16[48,2688]{1,0:T(8,128)(2,1)S(1)}, u32[]{:S(2)}, u32[]{:S(2)}) collective-permute-start(bf16[48,2688]{1,0:T(8,128)(2,1)} %touch.5.refs_0_), channel_id=1, source_target_pairs={{0,4},{1,5},{2,6},{3,7},{4,0},{5,1},{6,2},{7,3},{8,12},{9,13},{10,... | collective-permute-start | bytes 774152 | tf_op jit(solution)/shard_map/ppermute | solution.py:774
  24.2 1.1 copy-start.26
  24.2 30.5 %collective-permute-start.7 = (bf16[48,2688]{1,0:T(8,128)(2,1)}, bf16[48,2688]{1,0:T(8,128)(2,1)S(1)}, u32[]{:S(2)}, u32[]{:S(2)}) collective-permute-start(bf16[48,2688]{1,0:T(8,128)(2,1)} %touch.5.refs_0_), channel_id=1, source_target_pairs={{0,2},{1,3},{2,0},{3,1},{4,6},{5,7},{6,4},{7,5},{8,10},{9,11},{10,... | collective-permute-start | bytes 774152 | tf_op jit(solution)/shard_map/ppermute | solution.py:774
  54.7 0.8 copy-start.8
  54.7 0.8 copy-start.9
  55.6 1.7 collective-permute-start.10
  55.6 2.1 %collective-permute-start.11 = (bf16[48,2688]{1,0:T(8,128)(2,1)}, bf16[48,2688]{1,0:T(8,128)(2,1)S(1)}, u32[]{:S(2)}, u32[]{:S(2)}) collective-permute-start(bf16[48,2688]{1,0:T(8,128)(2,1)} %get-tuple-element.95.refs_2_), channel_id=1, source_target_pairs={{0,1},{1,0},{2,3},{3,2},{4,5},{5,4},{6,7},{7,6},{8,9},{9,8},{10,11... | collective-permute-start | bytes 774152 | tf_op jit(solution)/shard_map/ppermute | solution.py:778
  56.1 2.0 collective-permute-start.12
  56.1 2.3 %collective-permute-start.13 = (bf16[48,2688]{1,0:T(8,128)(2,1)}, bf16[48,2688]{1,0:T(8,128)(2,1)S(1)}, u32[]{:S(2)}, u32[]{:S(2)}) collective-permute-start(bf16[48,2688]{1,0:T(8,128)(2,1)} %get-tuple-element.97.refs_6_), channel_id=1, source_target_pairs={{0,1},{1,0},{2,3},{3,2},{4,5},{5,4},{6,7},{7,6},{8,9},{9,8},{10,11... | collective-permute-start | bytes 774152 | tf_op jit(solution)/shard_map/ppermute | solution.py:778
  57.3 1.1 copy-start.20
  57.7 0.7 copy-start.21
  58.4 0.7 copy-start.23
  112.8 2.9 %collective-permute-start.14 = (bf16[4,48,2688]{2,1,0:T(8,128)(2,1)}, bf16[4,48,2688]{2,1,0:T(8,128)(2,1)S(1)}, u32[]{:S(2)}, u32[]{:S(2)}) collective-permute-start(bf16[4,48,2688]{2,1,0:T(8,128)(2,1)} %get-tuple-element.108), channel_id=1, source_target_pairs={{0,1},{1,0},{2,3},{3,2},{4,5},{5,4},{6,7},{7,6},{8,9},{9,8},{10,11... | collective-permute-start | bytes 3096584 | tf_op jit(solution)/shard_map/ppermute | solution.py:783
  117.7 4.5 %copy-start.11 = (bf16[48,2688]{1,0:T(8,128)(2,1)}, bf16[48,2688]{1,0:T(8,128)(2,1)S(1)}, u32[]{:S(2)}) copy-start(bf16[48,2688]{1,0:T(8,128)(2,1)S(1)} %get-tuple-element.146.refs_0_) | copy-start | bytes 774148
  117.7 4.5 %copy-start.12 = (bf16[48,2688]{1,0:T(8,128)(2,1)}, bf16[48,2688]{1,0:T(8,128)(2,1)S(1)}, u32[]{:S(2)}) copy-start(bf16[48,2688]{1,0:T(8,128)(2,1)S(1)} %get-tuple-element.145.refs_1_) | copy-start | bytes 774148
  117.7 4.5 %copy-start.13 = (bf16[48,2688]{1,0:T(8,128)(2,1)}, bf16[48,2688]{1,0:T(8,128)(2,1)S(1)}, u32[]{:S(2)}) copy-start(bf16[48,2688]{1,0:T(8,128)(2,1)S(1)} %get-tuple-element.144.refs_2_) | copy-start | bytes 774148
  117.7 54.6 %collective-permute-start.17 = (bf16[48,2688]{1,0:T(8,128)(2,1)S(1)}, bf16[48,2688]{1,0:T(8,128)(2,1)S(1)}, u32[]{:S(2)}, u32[]{:S(2)}) collective-permute-start(bf16[48,2688]{1,0:T(8,128)(2,1)S(1)} %get-tuple-element.144.refs_2_), channel_id=1, source_target_pairs={{0,6},{1,7},{2,4},{3,5},{4,2},{5,3},{6,0},{7,1},{8,14},{9,15},{10,... | collective-permute-start | bytes 774152 | tf_op jit(solution)/shard_map/ppermute | solution.py:788
  121.1 51.2 %collective-permute-start.16 = (bf16[48,2688]{1,0:T(8,128)(2,1)S(1)}, bf16[48,2688]{1,0:T(8,128)(2,1)S(1)}, u32[]{:S(2)}, u32[]{:S(2)}) collective-permute-start(bf16[48,2688]{1,0:T(8,128)(2,1)S(1)} %get-tuple-element.145.refs_1_), channel_id=1, source_target_pairs={{0,4},{1,5},{2,6},{3,7},{4,0},{5,1},{6,2},{7,3},{8,12},{9,13},{10,... | collective-permute-start | bytes 774152 | tf_op jit(solution)/shard_map/ppermute | solution.py:788
  121.1 51.2 %collective-permute-start.15 = (bf16[48,2688]{1,0:T(8,128)(2,1)S(1)}, bf16[48,2688]{1,0:T(8,128)(2,1)S(1)}, u32[]{:S(2)}, u32[]{:S(2)}) collective-permute-start(bf16[48,2688]{1,0:T(8,128)(2,1)S(1)} %get-tuple-element.146.refs_0_), channel_id=1, source_target_pairs={{0,2},{1,3},{2,0},{3,1},{4,6},{5,7},{6,4},{7,5},{8,10},{9,11},{10,... | collective-permute-start | bytes 774152 | tf_op jit(solution)/shard_map/ppermute | solution.py:788
  172.3 0.8 copy-start.2
  172.3 0.8 copy-start.4
  173.1 7.5 %copy-start.1 = (bf16[48,2688]{1,0:T(8,128)(2,1)S(1)}, bf16[48,2688]{1,0:T(8,128)(2,1)}, u32[]{:S(2)}) copy-start(bf16[48,2688]{1,0:T(8,128)(2,1)} %get-tuple-element.116) | copy-start | bytes 774148
  173.1 7.5 %copy-start.3 = (bf16[48,2688]{1,0:T(8,128)(2,1)S(1)}, bf16[48,2688]{1,0:T(8,128)(2,1)}, u32[]{:S(2)}) copy-start(bf16[48,2688]{1,0:T(8,128)(2,1)} %get-tuple-element.115) | copy-start | bytes 774148
  173.1 7.5 %copy-start.5 = (bf16[48,2688]{1,0:T(8,128)(2,1)S(1)}, bf16[48,2688]{1,0:T(8,128)(2,1)}, u32[]{:S(2)}) copy-start(bf16[48,2688]{1,0:T(8,128)(2,1)} %get-tuple-element.114) | copy-start | bytes 774148
  173.1 2.2 %collective-permute-start.18 = (bf16[4,56,1152]{2,1,0:T(8,128)(2,1)}, bf16[4,56,1152]{2,1,0:T(8,128)(2,1)S(1)}, u32[]{:S(2)}, u32[]{:S(2)}) collective-permute-start(bf16[4,56,1152]{2,1,0:T(8,128)(2,1)} %get-tuple-element.112), channel_id=1, source_target_pairs={{0,1},{1,0},{2,3},{3,2},{4,5},{5,4},{6,7},{7,6},{8,9},{9,8},{10,11... | collective-permute-start | bytes 1548296 | tf_op jit(solution)/shard_map/ppermute | solution.py:783
  176.7 7.1 %collective-permute-start.19 = (bf16[56,1152]{1,0:T(8,128)(2,1)S(1)}, bf16[56,1152]{1,0:T(8,128)(2,1)S(1)}, u32[]{:S(2)}, u32[]{:S(2)}) collective-permute-start(bf16[56,1152]{1,0:T(8,128)(2,1)S(1)} %get-tuple-element.147), channel_id=1, source_target_pairs={{0,2},{1,3},{2,0},{3,1},{4,6},{5,7},{6,4},{7,5},{8,10},{9,11},{10,... | collective-permute-start | bytes 387080 | tf_op jit(solution)/shard_map/ppermute | solution.py:788
  177.7 9.5 %collective-permute-start.21 = (bf16[56,1152]{1,0:T(8,128)(2,1)S(1)}, bf16[56,1152]{1,0:T(8,128)(2,1)S(1)}, u32[]{:S(2)}, u32[]{:S(2)}) collective-permute-start(bf16[56,1152]{1,0:T(8,128)(2,1)S(1)} %get-tuple-element.148), channel_id=1, source_target_pairs={{0,6},{1,7},{2,4},{3,5},{4,2},{5,3},{6,0},{7,1},{8,14},{9,15},{10,... | collective-permute-start | bytes 387080 | tf_op jit(solution)/shard_map/ppermute | solution.py:788
  180.1 12.3 %collective-permute-start.20 = (bf16[56,1152]{1,0:T(8,128)(2,1)S(1)}, bf16[56,1152]{1,0:T(8,128)(2,1)S(1)}, u32[]{:S(2)}, u32[]{:S(2)}) collective-permute-start(bf16[56,1152]{1,0:T(8,128)(2,1)S(1)} %get-tuple-element.149), channel_id=1, source_target_pairs={{0,4},{1,5},{2,6},{3,7},{4,0},{5,1},{6,2},{7,3},{8,12},{9,13},{10,... | collective-permute-start | bytes 387080 | tf_op jit(solution)/shard_map/ppermute | solution.py:788
  180.8 15.3 %copy-start.10 = (bf16[48,2688]{1,0:T(8,128)(2,1)}, bf16[48,2688]{1,0:T(8,128)(2,1)S(1)}, u32[]{:S(2)}) copy-start(bf16[48,2688]{1,0:T(8,128)(2,1)S(1)} %fusion.3.refs_0_) | copy-start | bytes 774148
  180.8 14.7 %collective-permute-start.27 = (bf16[48,2688]{1,0:T(8,128)(2,1)S(1)}, bf16[48,2688]{1,0:T(8,128)(2,1)S(1)}, u32[]{:S(2)}, u32[]{:S(2)}) collective-permute-start(bf16[48,2688]{1,0:T(8,128)(2,1)S(1)} %fusion.3.refs_0_), channel_id=1, source_target_pairs={{0,24},{8,16},{16,8},{24,0},{1,25},{9,17},{17,9},{25,1},{2,26},{10... | collective-permute-start | bytes 774152 | tf_op jit(solution)/shard_map/ppermute | solution.py:795
  183.3 12.7 %collective-permute-start.26 = (bf16[48,2688]{1,0:T(8,128)(2,1)S(1)}, bf16[48,2688]{1,0:T(8,128)(2,1)S(1)}, u32[]{:S(2)}, u32[]{:S(2)}) collective-permute-start(bf16[48,2688]{1,0:T(8,128)(2,1)S(1)} %fusion.3.refs_0_), channel_id=1, source_target_pairs={{0,16},{8,24},{16,0},{24,8},{1,17},{9,25},{17,1},{25,9},{2,18},{10... | collective-permute-start | bytes 774152 | tf_op jit(solution)/shard_map/ppermute | solution.py:795
  183.8 12.2 %collective-permute-start.25 = (bf16[48,2688]{1,0:T(8,128)(2,1)S(1)}, bf16[48,2688]{1,0:T(8,128)(2,1)S(1)}, u32[]{:S(2)}, u32[]{:S(2)}) collective-permute-start(bf16[48,2688]{1,0:T(8,128)(2,1)S(1)} %fusion.3.refs_0_), channel_id=1, source_target_pairs={{0,8},{8,0},{16,24},{24,16},{1,9},{9,1},{17,25},{25,17},{2,10},{10... | collective-permute-start | bytes 774152 | tf_op jit(solution)/shard_map/ppermute | solution.py:795
  192.4 8.7 %copy-start.16 = (bf16[56,1152]{1,0:T(8,128)(2,1)}, bf16[56,1152]{1,0:T(8,128)(2,1)S(1)}, u32[]{:S(2)}) copy-start(bf16[56,1152]{1,0:T(8,128)(2,1)S(1)} %fusion.7.refs_0_) | copy-start | bytes 387076
  192.5 7.7 %collective-permute-start.24 = (bf16[56,1152]{1,0:T(8,128)(2,1)S(1)}, bf16[56,1152]{1,0:T(8,128)(2,1)S(1)}, u32[]{:S(2)}, u32[]{:S(2)}) collective-permute-start(bf16[56,1152]{1,0:T(8,128)(2,1)S(1)} %fusion.7.refs_0_), channel_id=1, source_target_pairs={{0,24},{8,16},{16,8},{24,0},{1,25},{9,17},{17,9},{25,1},{2,26},{10... | collective-permute-start | bytes 387080 | tf_op jit(solution)/shard_map/ppermute | solution.py:795
  195.0 6.0 %collective-permute-start.23 = (bf16[56,1152]{1,0:T(8,128)(2,1)S(1)}, bf16[56,1152]{1,0:T(8,128)(2,1)S(1)}, u32[]{:S(2)}, u32[]{:S(2)}) collective-permute-start(bf16[56,1152]{1,0:T(8,128)(2,1)S(1)} %fusion.7.refs_0_), channel_id=1, source_target_pairs={{0,16},{8,24},{16,0},{24,8},{1,17},{9,25},{17,1},{25,9},{2,18},{10... | collective-permute-start | bytes 387080 | tf_op jit(solution)/shard_map/ppermute | solution.py:795
  195.5 0.7 copy-start.17
  195.5 5.6 %collective-permute-start.22 = (bf16[56,1152]{1,0:T(8,128)(2,1)S(1)}, bf16[56,1152]{1,0:T(8,128)(2,1)S(1)}, u32[]{:S(2)}, u32[]{:S(2)}) collective-permute-start(bf16[56,1152]{1,0:T(8,128)(2,1)S(1)} %fusion.7.refs_0_), channel_id=1, source_target_pairs={{0,8},{8,0},{16,24},{24,16},{1,9},{9,1},{17,25},{25,17},{2,10},{10... | collective-permute-start | bytes 387080 | tf_op jit(solution)/shard_map/ppermute | solution.py:795
  196.0 0.8 copy-start.19
  200.2 1.0 copy-start.25
  (11 other events, 7.4 us)

commit v5 on v4

--- a/solution.py
+++ b/solution.py
@@ -159,16 +159,16 @@
     j = pl.program_id(1)
     if np_:
         pieces, refs = refs[:np_], refs[np_:]
-        qkv_ref, o_ref, l_ref, a_ref, w_ref, vec_ref, c1_ref, sm = refs[:8]
+        qkv_ref, o_ref, p_ref, a_ref, w_ref, vec_ref, c1_ref, sm = refs[:8]
         refs = refs[8:]
     else:
-        w_ref, vec_ref, qkv_ref, o_ref, l_ref, a_ref = refs[:6]
+        w_ref, vec_ref, qkv_ref, o_ref, p_ref, a_ref = refs[:6]
         refs = refs[6:]
-    os_, a_scr, s0, s1, p0, p1 = refs
+    os_, a_scr, s0, s1 = refs
 
     @pl.when((g == 0) & (j == 0))
     def _():
-        for ref in (a_scr, p0, p1, os_):
+        for ref in (a_scr, os_):
             ref[...] = jnp.zeros_like(ref)
         if np_:
             r = pieces[0].shape[0] - EXTRA
@@ -185,9 +185,8 @@
     gain = vec_ref[0:1, :]
     shift = vec_ref[1:2, :]
     ss = (s0, s1)
-    pp = (p0, p1)
     st = {}
-    S8 = SEQ // 8 * 8
+    S8 = SEQ // 16 * 16
 
     def ln(i, t, n):
         y = (xh_ref[i, t : t + n, :] * gain + shift).astype(BF)
@@ -220,7 +219,6 @@
             st[u] = jnp.max(st[u], axis=0, keepdims=True)
 
     def vexp(u, t, n):
-        i, h = divmod(u, H)
         p = jnp.exp(tile(ss[u % 2], t, n) - st[u])
         ss[u % 2][t : t + n, :] = p
         total = jnp.sum(p.reshape(n // 8, 8, SP), axis=0)
@@ -228,16 +226,16 @@
         st[k] = total if t == 0 else st[k] + total
         if t + n >= SEQ:
             total = jnp.sum(st[k], axis=0, keepdims=True)
-            l_ref[i, h : h + 1, :] = st[u] + jnp.log(total)
             st[k] = 1.0 / total
 
     def vnorm(u, t, n):
-        pp[u % 2][t : t + n, :] = (ss[u % 2][t : t + n, :] * st[("l", u)]).astype(BF)
+        i, h = divmod(u, H)
+        p_ref[i, h, t : t + n, :] = (ss[u % 2][t : t + n, :] * st[("l", u)]).astype(BF)
 
     def mix(u):
         i, h = divmod(u, H)
         lo = 2 * D + h * HEAD_DIM
-        y = dot(pp[u % 2][...], qkv_ref[i, :, lo : lo + HEAD_DIM], 0, 0)
+        y = dot(p_ref[i, h], qkv_ref[i, :, lo : lo + HEAD_DIM], 0, 0)
         if h % 2 == 0:
             st["o"] = y
         else:
@@ -252,7 +250,7 @@
     for t in range(3):
         qkv(t, 0, c0)
     rest = [partial(qkv, t, c, w) for c, w in tiles(D, 256)[1:] for t in range(3)]
-    srows = tiles(S8, 64) + ([(S8, 8)] if S8 < SEQ else [])
+    srows = tiles(S8, 64) + ([(S8, SP - S8)] if S8 < SEQ else [])
     order = [i * H + h for i in range(PAIR) for h in range(hb)]
     order += [i * H + h for i in range(PAIR) for h in range(hb, H)]
     nu = len(order)
@@ -282,13 +280,14 @@
     np_ = len(pieces)
     tok = lambda t: pl.BlockSpec((t, GROUP, D), lambda g, j, *_: (0, g, 0))
     img = lambda r, d: pl.BlockSpec((PAIR, r, d), lambda g, j, *_: (g * (GROUP // PAIR) + j, 0, 0))
+    probs = pl.BlockSpec((PAIR, D // HEAD_DIM, SP, SP), lambda g, j, *_: (g * (GROUP // PAIR) + j, 0, 0, 0))
     v = pltpu.VMEM
     s = jax.ShapeDtypeStruct
     ins = list(pieces) if np_ else [w, vec]
-    out_specs = [img(SP, W3), tok(TP), img(8, SP), img(SP, D)]
-    out_shape = [s((N, SP, W3), BF), s((TP, N, D), BF), s((N, 8, SP), F32), s((N, SP, D), BF)]
+    out_specs = [img(SP, W3), tok(TP), probs, img(SP, D)]
+    out_shape = [s((N, SP, W3), BF), s((TP, N, D), BF), s((N, D // HEAD_DIM, SP, SP), BF), s((N, SP, D), BF)]
     scratch = [v((D // 128, TP * GROUP, 128), F32), v((PAIR * SP, D), BF)]
-    scratch += [v((SP, SP), F32)] * 2 + [v((SP, SP), BF)] * 2
+    scratch += [v((SP, SP), F32)] * 2
     if np_:
         out_specs += [whole(D, W3), whole(8, D), whole(8, FF)]
         out_shape += [s((D, W3), BF), s((8, D), F32), s((8, FF), F32)]
@@ -501,14 +500,14 @@
     )(me, cnt, x, o, cot, c1, vec, *ins)
 
 
-def back_body(SEQ, SP, TP, D, FF, np_, DEPS, me_ref, a_ref, xh_ref, r_ref, qkv_ref, l_ref, do_ref, dx1_ref, w_ref, vec_ref, tc1_ref, tv2_ref, *refs):
+def back_body(SEQ, SP, TP, D, FF, np_, DEPS, me_ref, a_ref, xh_ref, r_ref, qkv_ref, p_ref, do_ref, dx1_ref, w_ref, vec_ref, tc1_ref, tv2_ref, *refs):
     gi_ref, refs = refs[DEPS], refs[DEPS + 1 :]
     if np_:
         snd_ref, keep_ref, tq_ref, sm = refs[:4]
         gv_ref, refs = refs[4], refs[5:]
     else:
         tq_ref, gv_ref, refs = refs[0], refs[1], refs[2:]
-    dos, gs, dob, at_scr, d_scr, da_scr, tv_ref, s0, s1, e0, e1, p0, p1, q0, q1 = refs
+    dos, gs, dob, at_scr, d_scr, da_scr, tv_ref, e0, e1, q0, q1 = refs
     H = D // HEAD_DIM
     W3 = 3 * D
     g = pl.program_id(0)
@@ -516,7 +515,7 @@
 
     @pl.when((g == 0) & (j == 0))
     def _():
-        for ref in (d_scr, p0, p1, q0, q1, dob, tq_ref, tv_ref):
+        for ref in (d_scr, dob, tq_ref, tv_ref):
             ref[...] = jnp.zeros_like(ref)
 
     @pl.when(j == 0)
@@ -524,12 +523,10 @@
         spread(do_ref, dos, SEQ)
 
     gain = vec_ref[0:1, :]
-    ss = (s0, s1)
     es = (e0, e1)
-    pp = (p0, p1)
     qq = (q0, q1)
     st = {}
-    S8 = SEQ // 8 * 8
+    S8 = SEQ // 16 * 16
 
     def load(i, t, n):
         dob[i * SP + t : i * SP + t + n, :] = image(dos, j * PAIR + i, t, n).astype(BF)
@@ -541,40 +538,33 @@
     def dpart(i, h):
         return dob[i * SP : (i + 1) * SP, h * HEAD_DIM : (h + 1) * HEAD_DIM]
 
-    def score(u):
-        i, h = divmod(u, H)
-        ss[u % 2][...] = dot(part(i, h, 1), part(i, h, 0), 1, 1)
-
     def dprob(u):
         i, h = divmod(u, H)
         es[u % 2][...] = dot(part(i, h, 2), dpart(i, h), 1, 1)
 
-    def v_prob(u, t, n):
-        i, h = divmod(u, H)
-        p = jnp.exp(ss[u % 2][t : t + n, :] - l_ref[i, h : h + 1, :])
-        if t + n > SEQ:
-            p = jnp.where(lax.broadcasted_iota(jnp.int32, (n, 1), 0) < SEQ - t, p, 0.0)
-        ss[u % 2][t : t + n, :] = p
-        pp[u % 2][t : t + n, :] = p.astype(BF)
-        x = jnp.sum((p * es[u % 2][t : t + n, :]).reshape(n // 8, 8, SP), axis=0)
+    def v_inner(u, t, n):
+        x = p_ref[divmod(u, H) + (slice(t, t + n),)].astype(F32) * es[u % 2][t : t + n, :]
+        x = jnp.sum(x.reshape(n // 8, 8, SP), axis=0)
         st[u] = x if t == 0 else st[u] + x
         if t + n >= SEQ:
             st[u] = jnp.sum(st[u], axis=0, keepdims=True)
 
     def v_ds(u, t, n):
-        qq[u % 2][t : t + n, :] = (ss[u % 2][t : t + n, :] * (es[u % 2][t : t + n, :] - st[u])).astype(BF)
+        p = p_ref[divmod(u, H) + (slice(t, t + n),)].astype(F32)
+        qq[u % 2][t : t + n, :] = (p * (es[u % 2][t : t + n, :] - st[u])).astype(BF)
 
     def put(u, t, y):
         i, h = divmod(u, H)
         if h % 2 == 0:
             st[("d", t)] = y
         else:
-            y = jnp.concatenate([st[("d", t)], y], axis=1).astype(BF)
+            y = jnp.concatenate([st[("d", t)], y], axis=0).T if t == 0 else jnp.concatenate([st[("d", t)], y], axis=1)
+            y = y.astype(BF)
             lo = t * D + (h - 1) * HEAD_DIM
             d_scr[i * SP : i * SP + SEQ, lo : lo + 2 * HEAD_DIM] = y[:SEQ]
 
     def m_dv(u):
-        put(u, 2, dot(pp[u % 2][...], dpart(*divmod(u, H))))
+        put(u, 2, dot(p_ref[divmod(u, H)], dpart(*divmod(u, H))))
 
     def m_dk(u):
         i, h = divmod(u, H)
@@ -582,24 +572,23 @@
 
     def m_dq(u):
         i, h = divmod(u, H)
-        put(u, 0, dot(qq[u % 2][...], part(i, h, 1), 0, 0) * (HEAD_DIM**-0.5))
+        put(u, 0, dot(part(i, h, 1), qq[u % 2][...], 0, 0) * (HEAD_DIM**-0.5))
 
     rows = tiles(SEQ, 48)
-    srows = tiles(S8, 64) + ([(S8, 8)] if S8 < SEQ else [])
+    srows = tiles(S8, 64) + ([(S8, SP - S8)] if S8 < SEQ else [])
     for t, n in rows:
         load(0, t, n)
     at_scr[...] = a_ref[...].reshape(PAIR * SP, D).T
     pre = [partial(load, i, t, n) for i in range(1, PAIR) for t, n in rows]
     nu = PAIR * H
-    score(0)
     dprob(0)
     for k in range(nu):
         ms = []
         if k + 1 < nu:
-            ms += [partial(score, k + 1), partial(dprob, k + 1)]
+            ms.append(partial(dprob, k + 1))
         if k >= 1:
             ms += [partial(m_dv, k - 1), partial(m_dk, k - 1), partial(m_dq, k - 1)]
-        vs = [partial(f, k, t, n) for f in (v_prob, v_ds) for t, n in srows]
+        vs = [partial(f, k, t, n) for f in (v_inner, v_ds) for t, n in srows]
         vs += pre[k : k + 1]
         weave(ms, vs)
     m_dv(nu - 1)
@@ -675,7 +664,7 @@
                     ref[k // 2, r : r + EXTRA, wide:] = jnp.zeros((EXTRA, W3 - wide), ref.dtype)
 
 
-def back(me, a, xh, r, qkv, l, do, dx1, w, vec, tc1, tv2, deps, SEQ, np_):
+def back(me, a, xh, r, qkv, probs, do, dx1, w, vec, tc1, tv2, deps, SEQ, np_):
     N, SP, D = a.shape
     TP = do.shape[0]
     W3 = 3 * D
@@ -685,6 +674,7 @@
     img = lambda r, d: pl.BlockSpec((PAIR, r, d), lambda g, j, *_: (g * (GROUP // PAIR) + j, 0, 0))
     v = pltpu.VMEM
     s = jax.ShapeDtypeStruct
+    prob = pl.BlockSpec((PAIR, D // HEAD_DIM, SP, SP), lambda g, j, *_: (g * (GROUP // PAIR) + j, 0, 0, 0))
     out_specs = [tok(SEQ)]
     out_shape = [s((SEQ, N, D), BF)]
     if np_:
@@ -698,13 +688,13 @@
         scratch = []
     scratch += [v((D // 128, TP * GROUP, 128), F32)] * 2
     scratch += [v((R, D), BF), v((D, R), BF), v((R, W3), BF), v((R, D), F32)]
-    scratch += [v((16, D), F32)] + [v((SP, SP), F32)] * 4 + [v((SP, SP), BF)] * 4
+    scratch += [v((16, D), F32)] + [v((SP, SP), F32)] * 2 + [v((SP, SP), BF)] * 2
     return pl.pallas_call(
         partial(back_body, SEQ, SP, TP, D, FF, np_, len(deps)),
         grid_spec=pltpu.PrefetchScalarGridSpec(
             num_scalar_prefetch=1,
             grid=(N // GROUP, GROUP // PAIR),
-            in_specs=[img(SP, D), img(SP, D), img(SP, 128), img(SP, W3), img(8, SP), tok(TP), tok(TP)]
+            in_specs=[img(SP, D), img(SP, D), img(SP, 128), img(SP, W3), prob, tok(TP), tok(TP)]
             + [full(w), full(vec), full(tc1), full(tv2)]
             + [pl.BlockSpec(memory_space=pl.ANY)] * len(deps),
             out_specs=out_specs,
@@ -713,7 +703,7 @@
         out_shape=out_shape,
         name="back",
         **params(40 * 10**9, 30 * 10**6),
-    )(me, a, xh, r, qkv, l, do, dx1, w, vec, tc1, tv2, *deps)
+    )(me, a, xh, r, qkv, probs, do, dx1, w, vec, tc1, tv2, *deps)
 
 
 def adam_body(np_, count, slots, where, flag_ref, gid_ref, scale_ref, *refs):
@@ -823,12 +813,12 @@
         half_a = touch(rf, fetch(pack_a, n))
         pieces_a = fetch_core(half_a, n)
         half_b = fetch(touch(half_a[-1], [pack_b])[0], n)
-        qkv, o, logs, a, wq, vec, c1 = attend(me, xh, pieces_a, None, None, FF, SEQ, TP)
+        qkv, o, probs, a, wq, vec, c1 = attend(me, xh, pieces_a, None, None, FF, SEQ, TP)
         pieces_b = fetch_core(touch(vec, half_b), n)
         out, dx1, do, tc1, tv2, snd, keep = feed(me, counts, x, o, cot, c1, vec, pieces_b, (), T)
         own_b, sends = halve(snd, keep, n)
         got_b = along_z(sends, n)
-        gi, snd, keep = back(me, a, xh, rf, qkv, logs, do, dx1, wq, vec, tc1, tv2, sends, SEQ, n)
+        gi, snd, keep = back(me, a, xh, rf, qkv, probs, do, dx1, wq, vec, tc1, tv2, sends, SEQ, n)
         snd, *got_b = touch(vec, [snd, *got_b])
         own_a, sends = halve(snd, keep, n)
         got_a = along_z(sends, n)
@@ -842,9 +832,9 @@
         vec = jnp.transpose(all_a[:, r : r + 8, :r], (1, 0, 2)).reshape(8, D).astype(F32)
         c1 = jnp.broadcast_to(all_a[:, r + 6, :nb].reshape(1, FF), (8, FF)).astype(F32)
         ws = (all_b[:, 2 * FF :], all_b[:, :FF], all_b[:, FF : 2 * FF])
-        qkv, o, logs, a = attend(me, xh, (), wq, vec, FF, SEQ, TP)
+        qkv, o, probs, a = attend(me, xh, (), wq, vec, FF, SEQ, TP)
         out, dx1, do, tc1, tv2, tp, t1, t2 = feed(me, counts, x, o, cot, c1, vec, (), ws, T)
-        gi, tq, gv = back(me, a, xh, rf, qkv, logs, do, dx1, wq, vec, tc1, tv2, (), SEQ, 0)
+        gi, tq, gv = back(me, a, xh, rf, qkv, probs, do, dx1, wq, vec, tc1, tv2, (), SEQ, 0)
         share = lambda g, axis: lax.psum(
             lax.psum_scatter(g, "fsdp", scatter_dimension=axis, tiled=True).astype(BF), "dp"
         ).astype(F32)

time: 205 us -> 199 us (0.971)
  Pallas kernels: 151 us -> 145 us
    pallas_call x1, Pallas kernels: 50.1 us -> 43.4 us  [back(): pl.pallas_call(partial(back_body, SEQ, SP, TP, D, FF, np_, len(deps)), gr...]
  transfers between devices with their start and end apart: 28 -> 28, of which waited for: 11 -> 11; matrix products, arithmetic and copies ran while one was open for 0% -> 0% of each run, Pallas kernels for 45% -> 43%
where the time goes in v5:
time: 199 us; the launch traced here: 198 us
  Pallas kernels  145 us (73%)
  starting transfers between devices  28.1 us (14%)
  waiting for transfers between devices  15.2 us (8%)
  local copies, waits for them, and re-layouts  5.31 us (3%)
  other arithmetic  3.38 us (2%)
    pallas_call x1, Pallas kernels, feed(): pl.pallas_call(partial(feed_body, SEQ, D, FF, T, N, np_), grid_spec=pltpu...  53.7 us
    pallas_call x1, Pallas kernels, back(): pl.pallas_call(partial(back_body, SEQ, SP, TP, D, FF, np_, len(deps)), gr...  43.4 us
    pallas_call x1, Pallas kernels, attend(): pl.pallas_call(partial(attend_body, SEQ, SP, TP, D, np_), grid_spec=pltpu...  29.2 us
    ppermute x6, starting transfers between devices, fetch(): return [x] + [lax.ppermute(x, 'fsdp', pairs(n, k)) for k in range(2, n, 2)]  10.3 us
    pallas_call x1, Pallas kernels, norm(): pl.pallas_call(partial(norm_body, SEQ, D), grid=(N // GROUP, GROUP // PAI...  10.3 us
    ppermute x6, starting transfers between devices, along_z(): lax.ppermute(x, 'fsdp', pairs(n, 2 * k + 2))  8.38 us
    ppermute x6, waiting for transfers between devices, along_z(): lax.ppermute(x, 'fsdp', pairs(n, 2 * k + 2))  8.06 us
    ppermute x6, starting transfers between devices, finish(): return [b] + [lax.ppermute(b, 'dp', pairs(d, k)) for k in range(1, d)]  7.11 us
  transfers between devices with their start and end apart: 28, of which 11 were waited for; matrix products, arithmetic and copies ran while one was open for 0% of the time, Pallas kernels for 43%

profile of v5, /device:TPU:0, one launch (start us, length us, event | category | flops | bytes accessed | tf_op | source)
XLA Modules:
  0.0 198.4 jit_solution(9269730637689623420)
XLA Ops:
  0.7 2.0 %pack.1 = (bf16[56,1152]{1,0:T(8,128)(2,1)}, bf16[48,2688]{1,0:T(8,128)(2,1)}) custom-call(f32[48,1152]{1,0:T(8,128)} %refs_4_.2, f32[6,48]{1,0:T(8,128)} %refs_6_.1, f32[1,144]{1,0:T(1,128)} %bitcast.53, f32[48,1152]{1,0:T(8,128)} %refs_5_.1, f32[48,1152]{1,0:T(8,128)} %bitcast.51, f32[48,384]{1,0:T(8,128)} %refs_4_.3), custom_call_target="tpu_custom_call" | custom-call | tf_op jit(solution)/shard_map/pack/pallas_call | solution.py:116
  2.7 5.0 %collective-permute-start.2 = (bf16[56,1152]{1,0:T(8,128)(2,1)}, bf16[56,1152]{1,0:T(8,128)(2,1)S(1)}, u32[]{:S(2)}, u32[]{:S(2)}) collective-permute-start(bf16[56,1152]{1,0:T(8,128)(2,1)} %get-tuple-element.84.refs_0_), channel_id=1, source_target_pairs={{0,6},{1,7},{2,4},{3,5},{4,2},{5,3},{6,0},{7,1},{8,14},{9,15},{10,... | collective-permute-start | bytes 387080 | tf_op jit(solution)/shard_map/ppermute | solution.py:764
  7.7 0.6 collective-permute-start
  8.3 10.3 %norm.1 = (f32[24,208,384]{2,1,0:T(8,128)}, f32[24,208,128]{2,1,0:T(8,128)}) custom-call(bf16[197,24,384]{2,1,0:T(8,128)(2,1)} %bitcast.55), custom_call_target="tpu_custom_call" | custom-call | flops 8000000000 | bytes 15000000 | tf_op jit(solution)/shard_map/norm/pallas_call | solution.py:144
  18.6 0.2 collective-permute-done.1.refs_2_
  18.9 0.4 copy-done.6
  19.3 0.2 copy-done.14
  19.5 0.5 collective-permute-start.4
  20.1 0.5 collective-permute-start.6
  20.6 3.6 %collective-permute-start.9 = (bf16[48,2688]{1,0:T(8,128)(2,1)}, bf16[48,2688]{1,0:T(8,128)(2,1)S(1)}, u32[]{:S(2)}, u32[]{:S(2)}) collective-permute-start(bf16[48,2688]{1,0:T(8,128)(2,1)} %touch.5.refs_0_), channel_id=1, source_target_pairs={{0,6},{1,7},{2,4},{3,5},{4,2},{5,3},{6,0},{7,1},{8,14},{9,15},{10,... | collective-permute-start | bytes 774152 | tf_op jit(solution)/shard_map/ppermute | solution.py:764
  24.2 1.1 collective-permute-start.7
  25.3 0.6 copy-done.28
  26.0 29.2 %attend.1 = (bf16[24,208,1152]{2,1,0:T(8,128)(2,1)}, bf16[200,24,384]{2,1,0:T(8,128)(2,1)}, bf16[24,6,208,208]{3,2,1,0:T(8,128)(2,1)}, bf16[24,208,384]{2,1,0:T(...) custom-call(s32[1]{0:T(128)} %bitcast.me_ref, ...), custom_call_target="tpu_custom_call" | custom-call | flops 20000000000 | bytes 25000000 | tf_op jit(solution)/shard_map/attend/pallas_call | solution.py:295
  55.3 0.7 copy-done.7
  56.1 0.5 collective-permute-start.11
  56.6 0.5 collective-permute-start.13
  57.9 0.4 collective-permute-done.11.refs_3_
  58.2 0.4 collective-permute-done.12.refs_5_
  58.6 0.4 collective-permute-done.13.refs_7_
  59.0 0.3 copy-done.22
  59.3 0.4 copy-done.23
  59.7 53.7 %feed.1 = (bf16[197,24,384]{2,1,0:T(8,128)(2,1)}, f32[200,24,384]{2,1,0:T(8,128)}, bf16[200,24,384]{2,1,0:T(8,128)(2,1)}, f32[8,1152]{1,0:T(8,128)}, f32[64,384]...) custom-call(s32[1]{0:T(128)} %bitcast.me_ref, s32[1]{0:T(128)S(6)} %copy.76.cnt_ref, ...), custom_call_target="tpu_custom_call" | custom-call | flops 44999999488 | bytes 30000000 | tf_op jit(solution)/shard_map/feed/pallas_call | solution.py:488
  113.4 0.2 collective-permute-start.14
  113.6 2.7 %collective-permute-done.14 = bf16[4,48,2688]{2,1,0:T(8,128)(2,1)S(1)} collective-permute-done((bf16[4,48,2688]{2,1,0:T(8,128)(2,1)}, bf16[4,48,2688]{2,1,0:T(8,128)(2,1)S(1)}, u32[]{:S(2)}, u32[]{:S(2)}) %collective-permute-start.14) | collective-permute-done | bytes 1032224 | tf_op jit(solution)/shard_map/ppermute | solution.py:773
  116.3 1.8 fusion.9
  118.2 3.4 %collective-permute-start.17 = (bf16[48,2688]{1,0:T(8,128)(2,1)S(1)}, bf16[48,2688]{1,0:T(8,128)(2,1)S(1)}, u32[]{:S(2)}, u32[]{:S(2)}) collective-permute-start(bf16[48,2688]{1,0:T(8,128)(2,1)S(1)} %get-tuple-element.144.refs_2_), channel_id=1, source_target_pairs={{0,6},{1,7},{2,4},{3,5},{4,2},{5,3},{6,0},{7,1},{8,14},{9,15},{10,... | collective-permute-start | bytes 774152 | tf_op jit(solution)/shard_map/ppermute | solution.py:778
  121.6 1.1 collective-permute-start.15
  122.7 43.4 %back.1 = (bf16[197,24,384]{2,1,0:T(8,128)(2,1)}, bf16[4,56,1152]{2,1,0:T(8,128)(2,1)}, f32[4,56,1152]{2,1,0:T(8,128)}) custom-call(s32[1]{0:T(128)} %bitcast.me_ref, bf16[24,208,384]{2,1,0:T(8,128)(2,1)} %get-tuple-element.99.a_ref, f32[24,208,384]{2,1,0:T(8,128)} %get-tuple-element.83.xh_ref, f32[24,208,128]{2,1,0:T(8,128)} %get-tuple-element.85.refs_4_.r_ref, ...), custom_call_target="tpu_custom_call" | custom-call | flops 40000000000 | bytes 30000000 | tf_op jit(solution)/shard_map/back/pallas_call | solution.py:692
  166.2 0.6 copy-done
  167.1 2.1 %collective-permute-done.18 = bf16[4,56,1152]{2,1,0:T(8,128)(2,1)S(1)} collective-permute-done((bf16[4,56,1152]{2,1,0:T(8,128)(2,1)}, bf16[4,56,1152]{2,1,0:T(8,128)(2,1)S(1)}, u32[]{:S(2)}, u32[]{:S(2)}) %collective-permute-start.18) | collective-permute-done | bytes 516128 | tf_op jit(solution)/shard_map/ppermute | solution.py:773
  169.2 1.3 fusion.8
  170.6 1.0 collective-permute-start.19
  171.6 2.4 %collective-permute-start.21 = (bf16[56,1152]{1,0:T(8,128)(2,1)S(1)}, bf16[56,1152]{1,0:T(8,128)(2,1)S(1)}, u32[]{:S(2)}, u32[]{:S(2)}) collective-permute-start(bf16[56,1152]{1,0:T(8,128)(2,1)S(1)} %get-tuple-element.148), channel_id=1, source_target_pairs={{0,6},{1,7},{2,4},{3,5},{4,2},{5,3},{6,0},{7,1},{8,14},{9,15},{10,... | collective-permute-start | bytes 387080 | tf_op jit(solution)/shard_map/ppermute | solution.py:778
  174.0 0.5 collective-permute-start.20
  174.7 2.5 %collective-permute-start.27 = (bf16[48,2688]{1,0:T(8,128)(2,1)S(1)}, bf16[48,2688]{1,0:T(8,128)(2,1)S(1)}, u32[]{:S(2)}, u32[]{:S(2)}) collective-permute-start(bf16[48,2688]{1,0:T(8,128)(2,1)S(1)} %fusion.3.refs_0_), channel_id=1, source_target_pairs={{0,24},{8,16},{16,8},{24,0},{1,25},{9,17},{17,9},{25,1},{2,26},{10... | collective-permute-start | bytes 774152 | tf_op jit(solution)/shard_map/ppermute | solution.py:785
  177.2 0.5 collective-permute-start.26
  177.7 0.5 collective-permute-start.25
  178.2 2.8 %collective-permute-done.21 = bf16[56,1152]{1,0:T(8,128)(2,1)S(1)} collective-permute-done((bf16[56,1152]{1,0:T(8,128)(2,1)S(1)}, bf16[56,1152]{1,0:T(8,128)(2,1)S(1)}, u32[]{:S(2)}, u32[]{:S(2)}) %collective-permute-start.21) | collective-permute-done | bytes 129056 | tf_op jit(solution)/shard_map/ppermute | solution.py:778
  181.1 5.2 %collective-permute-done.20 = bf16[56,1152]{1,0:T(8,128)(2,1)S(1)} collective-permute-done((bf16[56,1152]{1,0:T(8,128)(2,1)S(1)}, bf16[56,1152]{1,0:T(8,128)(2,1)S(1)}, u32[]{:S(2)}, u32[]{:S(2)}) %collective-permute-start.20) | collective-permute-done | bytes 129056 | tf_op jit(solution)/shard_map/ppermute | solution.py:778
  186.4 2.5 %collective-permute-start.24 = (bf16[56,1152]{1,0:T(8,128)(2,1)S(1)}, bf16[56,1152]{1,0:T(8,128)(2,1)S(1)}, u32[]{:S(2)}, u32[]{:S(2)}) collective-permute-start(bf16[56,1152]{1,0:T(8,128)(2,1)S(1)} %fusion.7.refs_0_), channel_id=1, source_target_pairs={{0,24},{8,16},{16,8},{24,0},{1,25},{9,17},{17,9},{25,1},{2,26},{10... | collective-permute-start | bytes 387080 | tf_op jit(solution)/shard_map/ppermute | solution.py:785
  188.9 0.5 collective-permute-start.23
  189.4 0.5 collective-permute-start.22
  189.9 0.1 copy-done.17
  190.1 0.5 copy-done.18
  190.7 3.3 %adam.3 = (f32[48,384]{1,0:T(8,128)}, f32[48,1152]{1,0:T(8,128)}, f32[48,1152]{1,0:T(8,128)}, f32[48,384]{1,0:T(8,128)}, f32[48,1152]{1,0:T(8,128)}, /*index=5*/...) custom-call(s32[6]{0:T(128)} %flag_ref.3, ...), custom_call_target="tpu_custom_call" | custom-call | flops 1000000000 | bytes 5000000 | tf_op jit(solution)/shard_map/adam/pallas_call | solution.py:733
  194.1 0.8 collective-permute-done.23.refs_2_
  195.0 0.5 copy-done.27
  195.7 2.6 %adam.2 = (f32[48,1152]{1,0:T(8,128)}, f32[1,144]{1,0:T(1,128)}, f32[6,48]{1,0:T(8,128)}, f32[48,1152]{1,0:T(8,128)}, f32[1,144]{1,0:T(1,128)}, /*index=5*/f32[6...) custom-call(s32[6]{0:T(128)} %flag_ref.3, ...), custom_call_target="tpu_custom_call" | custom-call | flops 1000000000 | bytes 5000000 | tf_op jit(solution)/shard_map/adam/pallas_call | solution.py:733
  (87 shorter events, 1.3 us)
Async XLA Ops:
  2.7 15.9 %collective-permute-start.2 = (bf16[56,1152]{1,0:T(8,128)(2,1)}, bf16[56,1152]{1,0:T(8,128)(2,1)S(1)}, u32[]{:S(2)}, u32[]{:S(2)}) collective-permute-start(bf16[56,1152]{1,0:T(8,128)(2,1)} %get-tuple-element.84.refs_0_), channel_id=1, source_target_pairs={{0,6},{1,7},{2,4},{3,5},{4,2},{5,3},{6,0},{7,1},{8,14},{9,15},{10,... | collective-permute-start | bytes 387080 | tf_op jit(solution)/shard_map/ppermute | solution.py:764
  7.7 11.1 %collective-permute-start.1 = (bf16[56,1152]{1,0:T(8,128)(2,1)}, bf16[56,1152]{1,0:T(8,128)(2,1)S(1)}, u32[]{:S(2)}, u32[]{:S(2)}) collective-permute-start(bf16[56,1152]{1,0:T(8,128)(2,1)} %get-tuple-element.84.refs_0_), channel_id=1, source_target_pairs={{0,4},{1,5},{2,6},{3,7},{4,0},{5,1},{6,2},{7,3},{8,12},{9,13},{10,... | collective-permute-start | bytes 387080 | tf_op jit(solution)/shard_map/ppermute | solution.py:764
  7.7 11.1 %collective-permute-start = (bf16[56,1152]{1,0:T(8,128)(2,1)}, bf16[56,1152]{1,0:T(8,128)(2,1)S(1)}, u32[]{:S(2)}, u32[]{:S(2)}) collective-permute-start(bf16[56,1152]{1,0:T(8,128)(2,1)} %get-tuple-element.84.refs_0_), channel_id=1, source_target_pairs={{0,2},{1,3},{2,0},{3,1},{4,6},{5,7},{6,4},{7,5},{8,10},{9,11},{10,... | collective-permute-start | bytes 387080 | tf_op jit(solution)/shard_map/ppermute | solution.py:764
  19.5 4.7 %collective-permute-start.3 = (bf16[56,1152]{1,0:T(8,128)(2,1)}, bf16[56,1152]{1,0:T(8,128)(2,1)S(1)}, u32[]{:S(2)}, u32[]{:S(2)}) collective-permute-start(bf16[56,1152]{1,0:T(8,128)(2,1)} %get-tuple-element.86.refs_0_), channel_id=1, source_target_pairs={{0,1},{1,0},{2,3},{3,2},{4,5},{5,4},{6,7},{7,6},{8,9},{9,8},{10,11... | collective-permute-start | bytes 387080 | tf_op jit(solution)/shard_map/ppermute | solution.py:768
  19.5 4.7 %collective-permute-start.4 = (bf16[56,1152]{1,0:T(8,128)(2,1)}, bf16[56,1152]{1,0:T(8,128)(2,1)S(1)}, u32[]{:S(2)}, u32[]{:S(2)}) collective-permute-start(bf16[56,1152]{1,0:T(8,128)(2,1)} %get-tuple-element.87.refs_2_), channel_id=1, source_target_pairs={{0,1},{1,0},{2,3},{3,2},{4,5},{5,4},{6,7},{7,6},{8,9},{9,8},{10,11... | collective-permute-start | bytes 387080 | tf_op jit(solution)/shard_map/ppermute | solution.py:768
  20.1 5.2 %collective-permute-start.5 = (bf16[56,1152]{1,0:T(8,128)(2,1)}, bf16[56,1152]{1,0:T(8,128)(2,1)S(1)}, u32[]{:S(2)}, u32[]{:S(2)}) collective-permute-start(bf16[56,1152]{1,0:T(8,128)(2,1)} %get-tuple-element.88.refs_4_), channel_id=1, source_target_pairs={{0,1},{1,0},{2,3},{3,2},{4,5},{5,4},{6,7},{7,6},{8,9},{9,8},{10,11... | collective-permute-start | bytes 387080 | tf_op jit(solution)/shard_map/ppermute | solution.py:768
  20.1 5.2 %collective-permute-start.6 = (bf16[56,1152]{1,0:T(8,128)(2,1)}, bf16[56,1152]{1,0:T(8,128)(2,1)S(1)}, u32[]{:S(2)}, u32[]{:S(2)}) collective-permute-start(bf16[56,1152]{1,0:T(8,128)(2,1)} %get-tuple-element.89.refs_6_.refs_1_), channel_id=1, source_target_pairs={{0,1},{1,0},{2,3},{3,2},{4,5},{5,4},{6,7},{7,6},{8,9},{9,8},{10,11... | collective-permute-start | bytes 387080 | tf_op jit(solution)/shard_map/ppermute | solution.py:768
  20.6 34.6 %collective-permute-start.9 = (bf16[48,2688]{1,0:T(8,128)(2,1)}, bf16[48,2688]{1,0:T(8,128)(2,1)S(1)}, u32[]{:S(2)}, u32[]{:S(2)}) collective-permute-start(bf16[48,2688]{1,0:T(8,128)(2,1)} %touch.5.refs_0_), channel_id=1, source_target_pairs={{0,6},{1,7},{2,4},{3,5},{4,2},{5,3},{6,0},{7,1},{8,14},{9,15},{10,... | collective-permute-start | bytes 774152 | tf_op jit(solution)/shard_map/ppermute | solution.py:764
  24.2 1.1 copy-start.24
  24.2 31.0 %collective-permute-start.8 = (bf16[48,2688]{1,0:T(8,128)(2,1)}, bf16[48,2688]{1,0:T(8,128)(2,1)S(1)}, u32[]{:S(2)}, u32[]{:S(2)}) collective-permute-start(bf16[48,2688]{1,0:T(8,128)(2,1)} %touch.5.refs_0_), channel_id=1, source_target_pairs={{0,4},{1,5},{2,6},{3,7},{4,0},{5,1},{6,2},{7,3},{8,12},{9,13},{10,... | collective-permute-start | bytes 774152 | tf_op jit(solution)/shard_map/ppermute | solution.py:764
  24.2 1.1 copy-start.26
  24.2 31.0 %collective-permute-start.7 = (bf16[48,2688]{1,0:T(8,128)(2,1)}, bf16[48,2688]{1,0:T(8,128)(2,1)S(1)}, u32[]{:S(2)}, u32[]{:S(2)}) collective-permute-start(bf16[48,2688]{1,0:T(8,128)(2,1)} %touch.5.refs_0_), channel_id=1, source_target_pairs={{0,2},{1,3},{2,0},{3,1},{4,6},{5,7},{6,4},{7,5},{8,10},{9,11},{10,... | collective-permute-start | bytes 774152 | tf_op jit(solution)/shard_map/ppermute | solution.py:764
  55.2 0.7 copy-start.7
  55.2 0.8 copy-start.8
  55.2 0.9 copy-start.9
  56.1 1.7 collective-permute-start.10
  56.1 2.1 %collective-permute-start.11 = (bf16[48,2688]{1,0:T(8,128)(2,1)}, bf16[48,2688]{1,0:T(8,128)(2,1)S(1)}, u32[]{:S(2)}, u32[]{:S(2)}) collective-permute-start(bf16[48,2688]{1,0:T(8,128)(2,1)} %get-tuple-element.95.refs_2_), channel_id=1, source_target_pairs={{0,1},{1,0},{2,3},{3,2},{4,5},{5,4},{6,7},{7,6},{8,9},{9,8},{10,11... | collective-permute-start | bytes 774152 | tf_op jit(solution)/shard_map/ppermute | solution.py:768
  56.6 2.0 collective-permute-start.12
  56.6 2.3 %collective-permute-start.13 = (bf16[48,2688]{1,0:T(8,128)(2,1)}, bf16[48,2688]{1,0:T(8,128)(2,1)S(1)}, u32[]{:S(2)}, u32[]{:S(2)}) collective-permute-start(bf16[48,2688]{1,0:T(8,128)(2,1)} %get-tuple-element.97.refs_6_), channel_id=1, source_target_pairs={{0,1},{1,0},{2,3},{3,2},{4,5},{5,4},{6,7},{7,6},{8,9},{9,8},{10,11... | collective-permute-start | bytes 774152 | tf_op jit(solution)/shard_map/ppermute | solution.py:768
  57.9 1.1 copy-start.20
  58.2 0.7 copy-start.21
  113.4 2.9 %collective-permute-start.14 = (bf16[4,48,2688]{2,1,0:T(8,128)(2,1)}, bf16[4,48,2688]{2,1,0:T(8,128)(2,1)S(1)}, u32[]{:S(2)}, u32[]{:S(2)}) collective-permute-start(bf16[4,48,2688]{2,1,0:T(8,128)(2,1)} %get-tuple-element.108), channel_id=1, source_target_pairs={{0,1},{1,0},{2,3},{3,2},{4,5},{5,4},{6,7},{7,6},{8,9},{9,8},{10,11... | collective-permute-start | bytes 3096584 | tf_op jit(solution)/shard_map/ppermute | solution.py:773
  118.2 4.5 %copy-start.11 = (bf16[48,2688]{1,0:T(8,128)(2,1)}, bf16[48,2688]{1,0:T(8,128)(2,1)S(1)}, u32[]{:S(2)}) copy-start(bf16[48,2688]{1,0:T(8,128)(2,1)S(1)} %get-tuple-element.146.refs_0_) | copy-start | bytes 774148
  118.2 4.5 %copy-start.12 = (bf16[48,2688]{1,0:T(8,128)(2,1)}, bf16[48,2688]{1,0:T(8,128)(2,1)S(1)}, u32[]{:S(2)}) copy-start(bf16[48,2688]{1,0:T(8,128)(2,1)S(1)} %get-tuple-element.145.refs_1_) | copy-start | bytes 774148
  118.2 4.5 %copy-start.13 = (bf16[48,2688]{1,0:T(8,128)(2,1)}, bf16[48,2688]{1,0:T(8,128)(2,1)S(1)}, u32[]{:S(2)}) copy-start(bf16[48,2688]{1,0:T(8,128)(2,1)S(1)} %get-tuple-element.144.refs_2_) | copy-start | bytes 774148
  118.2 47.9 %collective-permute-start.17 = (bf16[48,2688]{1,0:T(8,128)(2,1)S(1)}, bf16[48,2688]{1,0:T(8,128)(2,1)S(1)}, u32[]{:S(2)}, u32[]{:S(2)}) collective-permute-start(bf16[48,2688]{1,0:T(8,128)(2,1)S(1)} %get-tuple-element.144.refs_2_), channel_id=1, source_target_pairs={{0,6},{1,7},{2,4},{3,5},{4,2},{5,3},{6,0},{7,1},{8,14},{9,15},{10,... | collective-permute-start | bytes 774152 | tf_op jit(solution)/shard_map/ppermute | solution.py:778
  121.6 44.6 %collective-permute-start.16 = (bf16[48,2688]{1,0:T(8,128)(2,1)S(1)}, bf16[48,2688]{1,0:T(8,128)(2,1)S(1)}, u32[]{:S(2)}, u32[]{:S(2)}) collective-permute-start(bf16[48,2688]{1,0:T(8,128)(2,1)S(1)} %get-tuple-element.145.refs_1_), channel_id=1, source_target_pairs={{0,4},{1,5},{2,6},{3,7},{4,0},{5,1},{6,2},{7,3},{8,12},{9,13},{10,... | collective-permute-start | bytes 774152 | tf_op jit(solution)/shard_map/ppermute | solution.py:778
  121.6 44.6 %collective-permute-start.15 = (bf16[48,2688]{1,0:T(8,128)(2,1)S(1)}, bf16[48,2688]{1,0:T(8,128)(2,1)S(1)}, u32[]{:S(2)}, u32[]{:S(2)}) collective-permute-start(bf16[48,2688]{1,0:T(8,128)(2,1)S(1)} %get-tuple-element.146.refs_0_), channel_id=1, source_target_pairs={{0,2},{1,3},{2,0},{3,1},{4,6},{5,7},{6,4},{7,5},{8,10},{9,11},{10,... | collective-permute-start | bytes 774152 | tf_op jit(solution)/shard_map/ppermute | solution.py:778
  166.2 0.8 copy-start.2
  166.2 0.8 copy-start.4
  167.1 7.5 %copy-start.1 = (bf16[48,2688]{1,0:T(8,128)(2,1)S(1)}, bf16[48,2688]{1,0:T(8,128)(2,1)}, u32[]{:S(2)}) copy-start(bf16[48,2688]{1,0:T(8,128)(2,1)} %get-tuple-element.116) | copy-start | bytes 774148
  167.1 7.5 %copy-start.3 = (bf16[48,2688]{1,0:T(8,128)(2,1)S(1)}, bf16[48,2688]{1,0:T(8,128)(2,1)}, u32[]{:S(2)}) copy-start(bf16[48,2688]{1,0:T(8,128)(2,1)} %get-tuple-element.115) | copy-start | bytes 774148
  167.1 7.5 %copy-start.5 = (bf16[48,2688]{1,0:T(8,128)(2,1)S(1)}, bf16[48,2688]{1,0:T(8,128)(2,1)}, u32[]{:S(2)}) copy-start(bf16[48,2688]{1,0:T(8,128)(2,1)} %get-tuple-element.114) | copy-start | bytes 774148
  167.1 2.1 %collective-permute-start.18 = (bf16[4,56,1152]{2,1,0:T(8,128)(2,1)}, bf16[4,56,1152]{2,1,0:T(8,128)(2,1)S(1)}, u32[]{:S(2)}, u32[]{:S(2)}) collective-permute-start(bf16[4,56,1152]{2,1,0:T(8,128)(2,1)} %get-tuple-element.112), channel_id=1, source_target_pairs={{0,1},{1,0},{2,3},{3,2},{4,5},{5,4},{6,7},{7,6},{8,9},{9,8},{10,11... | collective-permute-start | bytes 1548296 | tf_op jit(solution)/shard_map/ppermute | solution.py:773
  170.6 7.1 %collective-permute-start.19 = (bf16[56,1152]{1,0:T(8,128)(2,1)S(1)}, bf16[56,1152]{1,0:T(8,128)(2,1)S(1)}, u32[]{:S(2)}, u32[]{:S(2)}) collective-permute-start(bf16[56,1152]{1,0:T(8,128)(2,1)S(1)} %get-tuple-element.147), channel_id=1, source_target_pairs={{0,2},{1,3},{2,0},{3,1},{4,6},{5,7},{6,4},{7,5},{8,10},{9,11},{10,... | collective-permute-start | bytes 387080 | tf_op jit(solution)/shard_map/ppermute | solution.py:778
  171.6 9.5 %collective-permute-start.21 = (bf16[56,1152]{1,0:T(8,128)(2,1)S(1)}, bf16[56,1152]{1,0:T(8,128)(2,1)S(1)}, u32[]{:S(2)}, u32[]{:S(2)}) collective-permute-start(bf16[56,1152]{1,0:T(8,128)(2,1)S(1)} %get-tuple-element.148), channel_id=1, source_target_pairs={{0,6},{1,7},{2,4},{3,5},{4,2},{5,3},{6,0},{7,1},{8,14},{9,15},{10,... | collective-permute-start | bytes 387080 | tf_op jit(solution)/shard_map/ppermute | solution.py:778
  174.0 12.3 %collective-permute-start.20 = (bf16[56,1152]{1,0:T(8,128)(2,1)S(1)}, bf16[56,1152]{1,0:T(8,128)(2,1)S(1)}, u32[]{:S(2)}, u32[]{:S(2)}) collective-permute-start(bf16[56,1152]{1,0:T(8,128)(2,1)S(1)} %get-tuple-element.149), channel_id=1, source_target_pairs={{0,4},{1,5},{2,6},{3,7},{4,0},{5,1},{6,2},{7,3},{8,12},{9,13},{10,... | collective-permute-start | bytes 387080 | tf_op jit(solution)/shard_map/ppermute | solution.py:778
  174.7 15.3 %copy-start.10 = (bf16[48,2688]{1,0:T(8,128)(2,1)}, bf16[48,2688]{1,0:T(8,128)(2,1)S(1)}, u32[]{:S(2)}) copy-start(bf16[48,2688]{1,0:T(8,128)(2,1)S(1)} %fusion.3.refs_0_) | copy-start | bytes 774148
  174.7 14.7 %collective-permute-start.27 = (bf16[48,2688]{1,0:T(8,128)(2,1)S(1)}, bf16[48,2688]{1,0:T(8,128)(2,1)S(1)}, u32[]{:S(2)}, u32[]{:S(2)}) collective-permute-start(bf16[48,2688]{1,0:T(8,128)(2,1)S(1)} %fusion.3.refs_0_), channel_id=1, source_target_pairs={{0,24},{8,16},{16,8},{24,0},{1,25},{9,17},{17,9},{25,1},{2,26},{10... | collective-permute-start | bytes 774152 | tf_op jit(solution)/shard_map/ppermute | solution.py:785
  177.2 12.7 %collective-permute-start.26 = (bf16[48,2688]{1,0:T(8,128)(2,1)S(1)}, bf16[48,2688]{1,0:T(8,128)(2,1)S(1)}, u32[]{:S(2)}, u32[]{:S(2)}) collective-permute-start(bf16[48,2688]{1,0:T(8,128)(2,1)S(1)} %fusion.3.refs_0_), channel_id=1, source_target_pairs={{0,16},{8,24},{16,0},{24,8},{1,17},{9,25},{17,1},{25,9},{2,18},{10... | collective-permute-start | bytes 774152 | tf_op jit(solution)/shard_map/ppermute | solution.py:785
  177.7 12.2 %collective-permute-start.25 = (bf16[48,2688]{1,0:T(8,128)(2,1)S(1)}, bf16[48,2688]{1,0:T(8,128)(2,1)S(1)}, u32[]{:S(2)}, u32[]{:S(2)}) collective-permute-start(bf16[48,2688]{1,0:T(8,128)(2,1)S(1)} %fusion.3.refs_0_), channel_id=1, source_target_pairs={{0,8},{8,0},{16,24},{24,16},{1,9},{9,1},{17,25},{25,17},{2,10},{10... | collective-permute-start | bytes 774152 | tf_op jit(solution)/shard_map/ppermute | solution.py:785
  186.3 8.7 %copy-start.16 = (bf16[56,1152]{1,0:T(8,128)(2,1)}, bf16[56,1152]{1,0:T(8,128)(2,1)S(1)}, u32[]{:S(2)}) copy-start(bf16[56,1152]{1,0:T(8,128)(2,1)S(1)} %fusion.7.refs_0_) | copy-start | bytes 387076
  186.4 7.7 %collective-permute-start.24 = (bf16[56,1152]{1,0:T(8,128)(2,1)S(1)}, bf16[56,1152]{1,0:T(8,128)(2,1)S(1)}, u32[]{:S(2)}, u32[]{:S(2)}) collective-permute-start(bf16[56,1152]{1,0:T(8,128)(2,1)S(1)} %fusion.7.refs_0_), channel_id=1, source_target_pairs={{0,24},{8,16},{16,8},{24,0},{1,25},{9,17},{17,9},{25,1},{2,26},{10... | collective-permute-start | bytes 387080 | tf_op jit(solution)/shard_map/ppermute | solution.py:785
  188.9 6.0 %collective-permute-start.23 = (bf16[56,1152]{1,0:T(8,128)(2,1)S(1)}, bf16[56,1152]{1,0:T(8,128)(2,1)S(1)}, u32[]{:S(2)}, u32[]{:S(2)}) collective-permute-start(bf16[56,1152]{1,0:T(8,128)(2,1)S(1)} %fusion.7.refs_0_), channel_id=1, source_target_pairs={{0,16},{8,24},{16,0},{24,8},{1,17},{9,25},{17,1},{25,9},{2,18},{10... | collective-permute-start | bytes 387080 | tf_op jit(solution)/shard_map/ppermute | solution.py:785
  189.4 0.7 copy-start.17
  189.4 5.6 %collective-permute-start.22 = (bf16[56,1152]{1,0:T(8,128)(2,1)S(1)}, bf16[56,1152]{1,0:T(8,128)(2,1)S(1)}, u32[]{:S(2)}, u32[]{:S(2)}) collective-permute-start(bf16[56,1152]{1,0:T(8,128)(2,1)S(1)} %fusion.7.refs_0_), channel_id=1, source_target_pairs={{0,8},{8,0},{16,24},{24,16},{1,9},{9,1},{17,25},{25,17},{2,10},{10... | collective-permute-start | bytes 387080 | tf_op jit(solution)/shard_map/ppermute | solution.py:785
  189.9 0.8 copy-start.19
  194.1 1.0 copy-start.25
  (11 other events, 7.4 us)

commit v6 on v5

--- a/solution.py
+++ b/solution.py
@@ -324,7 +324,7 @@
 
     @pl.when(s == 0)
     def _():
-        for ref in (tp_ref, t1_ref, t2_ref, tc1_ref, tv_ref):
+        for ref in (tp_ref, t1_ref, t2_ref, tc1_ref, tv_ref, bt_scr, dyt_scr, g_scr, du_scr):
             ref[...] = jnp.zeros_like(ref)
         if np_:
             r = pieces[0].shape[0]
@@ -427,13 +427,13 @@
     first = list(range(0, HR, RT))
     second = list(range(HR, R, RT))
     last = len(cols) - 1
+    def turn(dst, src):
+        dst[...] = src[...].T
+
     m_proj(0)
-    weave([partial(m_proj, HR)], [partial(v_norm, r) for r in first])
-    weave([partial(m_u, 0, 0), partial(m_d, 0, 0)], [partial(v_norm, r) for r in second])
-    bt_scr[...] = b_scr[...].T
-    dyt_scr[...] = dy_scr[...].T
-    m_u(0, HR)
-    m_d(0, HR)
+    weave([partial(m_proj, HR), partial(m_t1, last)], [partial(v_norm, r) for r in first])
+    weave([partial(m_t2, last), partial(m_u, 0, 0), partial(m_d, 0, 0)], [partial(v_norm, r) for r in second])
+    weave([partial(m_u, 0, HR), partial(m_d, 0, HR)], [partial(turn, bt_scr, b_scr), partial(turn, dyt_scr, dy_scr)])
     for i in range(len(cols)):
         ms = []
         if i < last:
@@ -445,14 +445,15 @@
         tc1_ref[:, c : c + w] += acc[("c1", i)]
     m_db(0, R)
     weave([partial(m_y, 0, R)], [partial(v_back, r) for r in first + second])
-    weave([partial(m_do, 0), partial(m_do, HR), m_tp, partial(m_t1, last), partial(m_t2, last)], [partial(v_out, r) for r in first + second])
+    weave([partial(m_do, 0), partial(m_do, HR), m_tp], [partial(v_out, r) for r in first + second])
     for i, k in ((2, "cp"), (3, "g2"), (4, "e2"), (5, "c2")):
         tv_ref[i * 8 : i * 8 + 8, :] += acc[k]
 
-    if np_:
-
-        @pl.when(s == pl.num_programs(0) - 1)
-        def _():
+    @pl.when(s == pl.num_programs(0) - 1)
+    def _():
+        m_t1(last)
+        m_t2(last)
+        if np_:
             r = D // np_
             for k in range(0, np_, 2):
                 for ref, flip in ((keep_ref, 0), (snd_ref, 1)):

time: 199 us -> 197 us (0.990)
  Pallas kernels: 145 us -> 143 us
    pallas_call x1, Pallas kernels: 53.7 us -> 51.7 us  [feed(): pl.pallas_call(partial(feed_body, SEQ, D, FF, T, N, np_), grid_spec=pltpu...]
  transfers between devices with their start and end apart: 28 -> 28, of which waited for: 11 -> 11; matrix products, arithmetic and copies ran while one was open for 0% -> 0% of each run, Pallas kernels for 43% -> 44%
where the time goes in v6:
time: 197 us; the launch traced here: 196 us
  Pallas kernels  143 us (73%)
  starting transfers between devices  28.1 us (14%)
  waiting for transfers between devices  15.2 us (8%)
  local copies, waits for them, and re-layouts  5.31 us (3%)
  other arithmetic  3.38 us (2%)
    pallas_call x1, Pallas kernels, feed(): pl.pallas_call(partial(feed_body, SEQ, D, FF, T, N, np_), grid_spec=pltpu...  51.7 us
    pallas_call x1, Pallas kernels, back(): pl.pallas_call(partial(back_body, SEQ, SP, TP, D, FF, np_, len(deps)), gr...  43.5 us
    pallas_call x1, Pallas kernels, attend(): pl.pallas_call(partial(attend_body, SEQ, SP, TP, D, np_), grid_spec=pltpu...  29.2 us
    ppermute x6, starting transfers between devices, fetch(): return [x] + [lax.ppermute(x, 'fsdp', pairs(n, k)) for k in range(2, n, 2)]  10.3 us
    pallas_call x1, Pallas kernels, norm(): pl.pallas_call(partial(norm_body, SEQ, D), grid=(N // GROUP, GROUP // PAI...  10.3 us
    ppermute x6, starting transfers between devices, along_z(): lax.ppermute(x, 'fsdp', pairs(n, 2 * k + 2))  8.36 us
    ppermute x6, waiting for transfers between devices, along_z(): lax.ppermute(x, 'fsdp', pairs(n, 2 * k + 2))  8.06 us
    ppermute x6, starting transfers between devices, finish(): return [b] + [lax.ppermute(b, 'dp', pairs(d, k)) for k in range(1, d)]  7.11 us
  transfers between devices with their start and end apart: 28, of which 11 were waited for; matrix products, arithmetic and copies ran while one was open for 0% of the time, Pallas kernels for 44%

profile of v6, /device:TPU:0, one launch (start us, length us, event | category | flops | bytes accessed | tf_op | source)
XLA Modules:
  0.0 196.4 jit_solution(10424769636964737457)
XLA Ops:
  0.7 2.0 %pack.1 = (bf16[56,1152]{1,0:T(8,128)(2,1)}, bf16[48,2688]{1,0:T(8,128)(2,1)}) custom-call(f32[48,1152]{1,0:T(8,128)} %refs_4_.2, f32[6,48]{1,0:T(8,128)} %refs_6_.1, f32[1,144]{1,0:T(1,128)} %bitcast.53, f32[48,1152]{1,0:T(8,128)} %refs_5_.1, f32[48,1152]{1,0:T(8,128)} %bitcast.51, f32[48,384]{1,0:T(8,128)} %refs_4_.3), custom_call_target="tpu_custom_call" | custom-call | tf_op jit(solution)/shard_map/pack/pallas_call | solution.py:116
  2.7 5.0 %collective-permute-start.2 = (bf16[56,1152]{1,0:T(8,128)(2,1)}, bf16[56,1152]{1,0:T(8,128)(2,1)S(1)}, u32[]{:S(2)}, u32[]{:S(2)}) collective-permute-start(bf16[56,1152]{1,0:T(8,128)(2,1)} %get-tuple-element.84.refs_0_), channel_id=1, source_target_pairs={{0,6},{1,7},{2,4},{3,5},{4,2},{5,3},{6,0},{7,1},{8,14},{9,15},{10,... | collective-permute-start | bytes 387080 | tf_op jit(solution)/shard_map/ppermute | solution.py:765
  7.7 0.6 collective-permute-start
  8.3 10.3 %norm.1 = (f32[24,208,384]{2,1,0:T(8,128)}, f32[24,208,128]{2,1,0:T(8,128)}) custom-call(bf16[197,24,384]{2,1,0:T(8,128)(2,1)} %bitcast.55), custom_call_target="tpu_custom_call" | custom-call | flops 8000000000 | bytes 15000000 | tf_op jit(solution)/shard_map/norm/pallas_call | solution.py:144
  18.6 0.2 collective-permute-done.1.refs_2_
  18.9 0.4 copy-done.6
  19.3 0.2 copy-done.14
  19.5 0.5 collective-permute-start.4
  20.1 0.5 collective-permute-start.6
  20.6 3.6 %collective-permute-start.9 = (bf16[48,2688]{1,0:T(8,128)(2,1)}, bf16[48,2688]{1,0:T(8,128)(2,1)S(1)}, u32[]{:S(2)}, u32[]{:S(2)}) collective-permute-start(bf16[48,2688]{1,0:T(8,128)(2,1)} %touch.5.refs_0_), channel_id=1, source_target_pairs={{0,6},{1,7},{2,4},{3,5},{4,2},{5,3},{6,0},{7,1},{8,14},{9,15},{10,... | collective-permute-start | bytes 774152 | tf_op jit(solution)/shard_map/ppermute | solution.py:765
  24.2 1.1 collective-permute-start.7
  25.3 0.6 copy-done.28
  26.0 29.2 %attend.1 = (bf16[24,208,1152]{2,1,0:T(8,128)(2,1)}, bf16[200,24,384]{2,1,0:T(8,128)(2,1)}, bf16[24,6,208,208]{3,2,1,0:T(8,128)(2,1)}, bf16[24,208,384]{2,1,0:T(...) custom-call(s32[1]{0:T(128)} %bitcast.me_ref, ...), custom_call_target="tpu_custom_call" | custom-call | flops 20000000000 | bytes 25000000 | tf_op jit(solution)/shard_map/attend/pallas_call | solution.py:295
  55.3 0.7 copy-done.7
  56.1 0.5 collective-permute-start.11
  56.6 0.5 collective-permute-start.13
  57.9 0.4 collective-permute-done.11.refs_3_
  58.2 0.4 collective-permute-done.12.refs_5_
  58.6 0.4 collective-permute-done.13.refs_7_
  59.0 0.3 copy-done.22
  59.3 0.4 copy-done.23
  59.7 51.7 %feed.1 = (bf16[197,24,384]{2,1,0:T(8,128)(2,1)}, f32[200,24,384]{2,1,0:T(8,128)}, bf16[200,24,384]{2,1,0:T(8,128)(2,1)}, f32[8,1152]{1,0:T(8,128)}, f32[64,384]...) custom-call(s32[1]{0:T(128)} %bitcast.me_ref, s32[1]{0:T(128)S(6)} %copy.76.cnt_ref, ...), custom_call_target="tpu_custom_call" | custom-call | flops 44999999488 | bytes 30000000 | tf_op jit(solution)/shard_map/feed/pallas_call | solution.py:489
  111.4 0.2 collective-permute-start.14
  111.6 2.7 %collective-permute-done.14 = bf16[4,48,2688]{2,1,0:T(8,128)(2,1)S(1)} collective-permute-done((bf16[4,48,2688]{2,1,0:T(8,128)(2,1)}, bf16[4,48,2688]{2,1,0:T(8,128)(2,1)S(1)}, u32[]{:S(2)}, u32[]{:S(2)}) %collective-permute-start.14) | collective-permute-done | bytes 1032224 | tf_op jit(solution)/shard_map/ppermute | solution.py:774
  114.3 1.8 fusion.9
  116.2 3.4 %collective-permute-start.17 = (bf16[48,2688]{1,0:T(8,128)(2,1)S(1)}, bf16[48,2688]{1,0:T(8,128)(2,1)S(1)}, u32[]{:S(2)}, u32[]{:S(2)}) collective-permute-start(bf16[48,2688]{1,0:T(8,128)(2,1)S(1)} %get-tuple-element.144.refs_2_), channel_id=1, source_target_pairs={{0,6},{1,7},{2,4},{3,5},{4,2},{5,3},{6,0},{7,1},{8,14},{9,15},{10,... | collective-permute-start | bytes 774152 | tf_op jit(solution)/shard_map/ppermute | solution.py:779
  119.6 1.1 collective-permute-start.15
  120.7 43.5 %back.1 = (bf16[197,24,384]{2,1,0:T(8,128)(2,1)}, bf16[4,56,1152]{2,1,0:T(8,128)(2,1)}, f32[4,56,1152]{2,1,0:T(8,128)}) custom-call(s32[1]{0:T(128)} %bitcast.me_ref, bf16[24,208,384]{2,1,0:T(8,128)(2,1)} %get-tuple-element.99.a_ref, f32[24,208,384]{2,1,0:T(8,128)} %get-tuple-element.83.xh_ref, f32[24,208,128]{2,1,0:T(8,128)} %get-tuple-element.85.refs_4_.r_ref, ...), custom_call_target="tpu_custom_call" | custom-call | flops 40000000000 | bytes 30000000 | tf_op jit(solution)/shard_map/back/pallas_call | solution.py:693
  164.2 0.6 copy-done
  165.1 2.1 %collective-permute-done.18 = bf16[4,56,1152]{2,1,0:T(8,128)(2,1)S(1)} collective-permute-done((bf16[4,56,1152]{2,1,0:T(8,128)(2,1)}, bf16[4,56,1152]{2,1,0:T(8,128)(2,1)S(1)}, u32[]{:S(2)}, u32[]{:S(2)}) %collective-permute-start.18) | collective-permute-done | bytes 516128 | tf_op jit(solution)/shard_map/ppermute | solution.py:774
  167.2 1.3 fusion.8
  168.6 1.0 collective-permute-start.19
  169.6 2.4 %collective-permute-start.21 = (bf16[56,1152]{1,0:T(8,128)(2,1)S(1)}, bf16[56,1152]{1,0:T(8,128)(2,1)S(1)}, u32[]{:S(2)}, u32[]{:S(2)}) collective-permute-start(bf16[56,1152]{1,0:T(8,128)(2,1)S(1)} %get-tuple-element.148), channel_id=1, source_target_pairs={{0,6},{1,7},{2,4},{3,5},{4,2},{5,3},{6,0},{7,1},{8,14},{9,15},{10,... | collective-permute-start | bytes 387080 | tf_op jit(solution)/shard_map/ppermute | solution.py:779
  172.0 0.5 collective-permute-start.20
  172.7 2.5 %collective-permute-start.27 = (bf16[48,2688]{1,0:T(8,128)(2,1)S(1)}, bf16[48,2688]{1,0:T(8,128)(2,1)S(1)}, u32[]{:S(2)}, u32[]{:S(2)}) collective-permute-start(bf16[48,2688]{1,0:T(8,128)(2,1)S(1)} %fusion.3.refs_0_), channel_id=1, source_target_pairs={{0,24},{8,16},{16,8},{24,0},{1,25},{9,17},{17,9},{25,1},{2,26},{10... | collective-permute-start | bytes 774152 | tf_op jit(solution)/shard_map/ppermute | solution.py:786
  175.2 0.5 collective-permute-start.26
  175.7 0.5 collective-permute-start.25
  176.2 2.8 %collective-permute-done.21 = bf16[56,1152]{1,0:T(8,128)(2,1)S(1)} collective-permute-done((bf16[56,1152]{1,0:T(8,128)(2,1)S(1)}, bf16[56,1152]{1,0:T(8,128)(2,1)S(1)}, u32[]{:S(2)}, u32[]{:S(2)}) %collective-permute-start.21) | collective-permute-done | bytes 129056 | tf_op jit(solution)/shard_map/ppermute | solution.py:779
  179.1 5.2 %collective-permute-done.20 = bf16[56,1152]{1,0:T(8,128)(2,1)S(1)} collective-permute-done((bf16[56,1152]{1,0:T(8,128)(2,1)S(1)}, bf16[56,1152]{1,0:T(8,128)(2,1)S(1)}, u32[]{:S(2)}, u32[]{:S(2)}) %collective-permute-start.20) | collective-permute-done | bytes 129056 | tf_op jit(solution)/shard_map/ppermute | solution.py:779
  184.3 2.5 %collective-permute-start.24 = (bf16[56,1152]{1,0:T(8,128)(2,1)S(1)}, bf16[56,1152]{1,0:T(8,128)(2,1)S(1)}, u32[]{:S(2)}, u32[]{:S(2)}) collective-permute-start(bf16[56,1152]{1,0:T(8,128)(2,1)S(1)} %fusion.7.refs_0_), channel_id=1, source_target_pairs={{0,24},{8,16},{16,8},{24,0},{1,25},{9,17},{17,9},{25,1},{2,26},{10... | collective-permute-start | bytes 387080 | tf_op jit(solution)/shard_map/ppermute | solution.py:786
  186.8 0.5 collective-permute-start.23
  187.4 0.5 collective-permute-start.22
  187.9 0.1 copy-done.17
  188.1 0.5 copy-done.18
  188.7 3.3 %adam.3 = (f32[48,384]{1,0:T(8,128)}, f32[48,1152]{1,0:T(8,128)}, f32[48,1152]{1,0:T(8,128)}, f32[48,384]{1,0:T(8,128)}, f32[48,1152]{1,0:T(8,128)}, /*index=5*/...) custom-call(s32[6]{0:T(128)} %flag_ref.3, ...), custom_call_target="tpu_custom_call" | custom-call | flops 1000000000 | bytes 5000000 | tf_op jit(solution)/shard_map/adam/pallas_call | solution.py:734
  192.1 0.8 collective-permute-done.23.refs_2_
  193.0 0.5 copy-done.27
  193.7 2.6 %adam.2 = (f32[48,1152]{1,0:T(8,128)}, f32[1,144]{1,0:T(1,128)}, f32[6,48]{1,0:T(8,128)}, f32[48,1152]{1,0:T(8,128)}, f32[1,144]{1,0:T(1,128)}, /*index=5*/f32[6...) custom-call(s32[6]{0:T(128)} %flag_ref.3, ...), custom_call_target="tpu_custom_call" | custom-call | flops 1000000000 | bytes 5000000 | tf_op jit(solution)/shard_map/adam/pallas_call | solution.py:734
  (87 shorter events, 1.3 us)
Async XLA Ops:
  2.7 15.9 %collective-permute-start.2 = (bf16[56,1152]{1,0:T(8,128)(2,1)}, bf16[56,1152]{1,0:T(8,128)(2,1)S(1)}, u32[]{:S(2)}, u32[]{:S(2)}) collective-permute-start(bf16[56,1152]{1,0:T(8,128)(2,1)} %get-tuple-element.84.refs_0_), channel_id=1, source_target_pairs={{0,6},{1,7},{2,4},{3,5},{4,2},{5,3},{6,0},{7,1},{8,14},{9,15},{10,... | collective-permute-start | bytes 387080 | tf_op jit(solution)/shard_map/ppermute | solution.py:765
  7.7 11.1 %collective-permute-start.1 = (bf16[56,1152]{1,0:T(8,128)(2,1)}, bf16[56,1152]{1,0:T(8,128)(2,1)S(1)}, u32[]{:S(2)}, u32[]{:S(2)}) collective-permute-start(bf16[56,1152]{1,0:T(8,128)(2,1)} %get-tuple-element.84.refs_0_), channel_id=1, source_target_pairs={{0,4},{1,5},{2,6},{3,7},{4,0},{5,1},{6,2},{7,3},{8,12},{9,13},{10,... | collective-permute-start | bytes 387080 | tf_op jit(solution)/shard_map/ppermute | solution.py:765
  7.7 11.1 %collective-permute-start = (bf16[56,1152]{1,0:T(8,128)(2,1)}, bf16[56,1152]{1,0:T(8,128)(2,1)S(1)}, u32[]{:S(2)}, u32[]{:S(2)}) collective-permute-start(bf16[56,1152]{1,0:T(8,128)(2,1)} %get-tuple-element.84.refs_0_), channel_id=1, source_target_pairs={{0,2},{1,3},{2,0},{3,1},{4,6},{5,7},{6,4},{7,5},{8,10},{9,11},{10,... | collective-permute-start | bytes 387080 | tf_op jit(solution)/shard_map/ppermute | solution.py:765
  19.5 4.7 %collective-permute-start.3 = (bf16[56,1152]{1,0:T(8,128)(2,1)}, bf16[56,1152]{1,0:T(8,128)(2,1)S(1)}, u32[]{:S(2)}, u32[]{:S(2)}) collective-permute-start(bf16[56,1152]{1,0:T(8,128)(2,1)} %get-tuple-element.86.refs_0_), channel_id=1, source_target_pairs={{0,1},{1,0},{2,3},{3,2},{4,5},{5,4},{6,7},{7,6},{8,9},{9,8},{10,11... | collective-permute-start | bytes 387080 | tf_op jit(solution)/shard_map/ppermute | solution.py:769
  19.5 4.7 %collective-permute-start.4 = (bf16[56,1152]{1,0:T(8,128)(2,1)}, bf16[56,1152]{1,0:T(8,128)(2,1)S(1)}, u32[]{:S(2)}, u32[]{:S(2)}) collective-permute-start(bf16[56,1152]{1,0:T(8,128)(2,1)} %get-tuple-element.87.refs_2_), channel_id=1, source_target_pairs={{0,1},{1,0},{2,3},{3,2},{4,5},{5,4},{6,7},{7,6},{8,9},{9,8},{10,11... | collective-permute-start | bytes 387080 | tf_op jit(solution)/shard_map/ppermute | solution.py:769
  20.1 5.2 %collective-permute-start.5 = (bf16[56,1152]{1,0:T(8,128)(2,1)}, bf16[56,1152]{1,0:T(8,128)(2,1)S(1)}, u32[]{:S(2)}, u32[]{:S(2)}) collective-permute-start(bf16[56,1152]{1,0:T(8,128)(2,1)} %get-tuple-element.88.refs_4_), channel_id=1, source_target_pairs={{0,1},{1,0},{2,3},{3,2},{4,5},{5,4},{6,7},{7,6},{8,9},{9,8},{10,11... | collective-permute-start | bytes 387080 | tf_op jit(solution)/shard_map/ppermute | solution.py:769
  20.1 5.2 %collective-permute-start.6 = (bf16[56,1152]{1,0:T(8,128)(2,1)}, bf16[56,1152]{1,0:T(8,128)(2,1)S(1)}, u32[]{:S(2)}, u32[]{:S(2)}) collective-permute-start(bf16[56,1152]{1,0:T(8,128)(2,1)} %get-tuple-element.89.refs_6_.refs_1_), channel_id=1, source_target_pairs={{0,1},{1,0},{2,3},{3,2},{4,5},{5,4},{6,7},{7,6},{8,9},{9,8},{10,11... | collective-permute-start | bytes 387080 | tf_op jit(solution)/shard_map/ppermute | solution.py:769
  20.6 34.6 %collective-permute-start.9 = (bf16[48,2688]{1,0:T(8,128)(2,1)}, bf16[48,2688]{1,0:T(8,128)(2,1)S(1)}, u32[]{:S(2)}, u32[]{:S(2)}) collective-permute-start(bf16[48,2688]{1,0:T(8,128)(2,1)} %touch.5.refs_0_), channel_id=1, source_target_pairs={{0,6},{1,7},{2,4},{3,5},{4,2},{5,3},{6,0},{7,1},{8,14},{9,15},{10,... | collective-permute-start | bytes 774152 | tf_op jit(solution)/shard_map/ppermute | solution.py:765
  24.2 1.1 copy-start.24
  24.2 31.0 %collective-permute-start.8 = (bf16[48,2688]{1,0:T(8,128)(2,1)}, bf16[48,2688]{1,0:T(8,128)(2,1)S(1)}, u32[]{:S(2)}, u32[]{:S(2)}) collective-permute-start(bf16[48,2688]{1,0:T(8,128)(2,1)} %touch.5.refs_0_), channel_id=1, source_target_pairs={{0,4},{1,5},{2,6},{3,7},{4,0},{5,1},{6,2},{7,3},{8,12},{9,13},{10,... | collective-permute-start | bytes 774152 | tf_op jit(solution)/shard_map/ppermute | solution.py:765
  24.2 1.1 copy-start.26
  24.2 31.0 %collective-permute-start.7 = (bf16[48,2688]{1,0:T(8,128)(2,1)}, bf16[48,2688]{1,0:T(8,128)(2,1)S(1)}, u32[]{:S(2)}, u32[]{:S(2)}) collective-permute-start(bf16[48,2688]{1,0:T(8,128)(2,1)} %touch.5.refs_0_), channel_id=1, source_target_pairs={{0,2},{1,3},{2,0},{3,1},{4,6},{5,7},{6,4},{7,5},{8,10},{9,11},{10,... | collective-permute-start | bytes 774152 | tf_op jit(solution)/shard_map/ppermute | solution.py:765
  55.2 0.7 copy-start.7
  55.2 0.8 copy-start.8
  55.2 0.9 copy-start.9
  56.1 1.7 collective-permute-start.10
  56.1 2.1 %collective-permute-start.11 = (bf16[48,2688]{1,0:T(8,128)(2,1)}, bf16[48,2688]{1,0:T(8,128)(2,1)S(1)}, u32[]{:S(2)}, u32[]{:S(2)}) collective-permute-start(bf16[48,2688]{1,0:T(8,128)(2,1)} %get-tuple-element.95.refs_2_), channel_id=1, source_target_pairs={{0,1},{1,0},{2,3},{3,2},{4,5},{5,4},{6,7},{7,6},{8,9},{9,8},{10,11... | collective-permute-start | bytes 774152 | tf_op jit(solution)/shard_map/ppermute | solution.py:769
  56.6 2.0 %collective-permute-start.12 = (bf16[48,2688]{1,0:T(8,128)(2,1)}, bf16[48,2688]{1,0:T(8,128)(2,1)S(1)}, u32[]{:S(2)}, u32[]{:S(2)}) collective-permute-start(bf16[48,2688]{1,0:T(8,128)(2,1)} %get-tuple-element.96.refs_4_), channel_id=1, source_target_pairs={{0,1},{1,0},{2,3},{3,2},{4,5},{5,4},{6,7},{7,6},{8,9},{9,8},{10,11... | collective-permute-start | bytes 774152 | tf_op jit(solution)/shard_map/ppermute | solution.py:769
  56.6 2.3 %collective-permute-start.13 = (bf16[48,2688]{1,0:T(8,128)(2,1)}, bf16[48,2688]{1,0:T(8,128)(2,1)S(1)}, u32[]{:S(2)}, u32[]{:S(2)}) collective-permute-start(bf16[48,2688]{1,0:T(8,128)(2,1)} %get-tuple-element.97.refs_6_), channel_id=1, source_target_pairs={{0,1},{1,0},{2,3},{3,2},{4,5},{5,4},{6,7},{7,6},{8,9},{9,8},{10,11... | collective-permute-start | bytes 774152 | tf_op jit(solution)/shard_map/ppermute | solution.py:769
  57.9 1.1 copy-start.20
  58.2 0.7 copy-start.21
  111.4 2.9 %collective-permute-start.14 = (bf16[4,48,2688]{2,1,0:T(8,128)(2,1)}, bf16[4,48,2688]{2,1,0:T(8,128)(2,1)S(1)}, u32[]{:S(2)}, u32[]{:S(2)}) collective-permute-start(bf16[4,48,2688]{2,1,0:T(8,128)(2,1)} %get-tuple-element.108), channel_id=1, source_target_pairs={{0,1},{1,0},{2,3},{3,2},{4,5},{5,4},{6,7},{7,6},{8,9},{9,8},{10,11... | collective-permute-start | bytes 3096584 | tf_op jit(solution)/shard_map/ppermute | solution.py:774
  116.2 4.5 %copy-start.11 = (bf16[48,2688]{1,0:T(8,128)(2,1)}, bf16[48,2688]{1,0:T(8,128)(2,1)S(1)}, u32[]{:S(2)}) copy-start(bf16[48,2688]{1,0:T(8,128)(2,1)S(1)} %get-tuple-element.146.refs_0_) | copy-start | bytes 774148
  116.2 4.5 %copy-start.12 = (bf16[48,2688]{1,0:T(8,128)(2,1)}, bf16[48,2688]{1,0:T(8,128)(2,1)S(1)}, u32[]{:S(2)}) copy-start(bf16[48,2688]{1,0:T(8,128)(2,1)S(1)} %get-tuple-element.145.refs_1_) | copy-start | bytes 774148
  116.2 4.5 %copy-start.13 = (bf16[48,2688]{1,0:T(8,128)(2,1)}, bf16[48,2688]{1,0:T(8,128)(2,1)S(1)}, u32[]{:S(2)}) copy-start(bf16[48,2688]{1,0:T(8,128)(2,1)S(1)} %get-tuple-element.144.refs_2_) | copy-start | bytes 774148
  116.2 47.9 %collective-permute-start.17 = (bf16[48,2688]{1,0:T(8,128)(2,1)S(1)}, bf16[48,2688]{1,0:T(8,128)(2,1)S(1)}, u32[]{:S(2)}, u32[]{:S(2)}) collective-permute-start(bf16[48,2688]{1,0:T(8,128)(2,1)S(1)} %get-tuple-element.144.refs_2_), channel_id=1, source_target_pairs={{0,6},{1,7},{2,4},{3,5},{4,2},{5,3},{6,0},{7,1},{8,14},{9,15},{10,... | collective-permute-start | bytes 774152 | tf_op jit(solution)/shard_map/ppermute | solution.py:779
  119.6 44.6 %collective-permute-start.16 = (bf16[48,2688]{1,0:T(8,128)(2,1)S(1)}, bf16[48,2688]{1,0:T(8,128)(2,1)S(1)}, u32[]{:S(2)}, u32[]{:S(2)}) collective-permute-start(bf16[48,2688]{1,0:T(8,128)(2,1)S(1)} %get-tuple-element.145.refs_1_), channel_id=1, source_target_pairs={{0,4},{1,5},{2,6},{3,7},{4,0},{5,1},{6,2},{7,3},{8,12},{9,13},{10,... | collective-permute-start | bytes 774152 | tf_op jit(solution)/shard_map/ppermute | solution.py:779
  119.6 44.6 %collective-permute-start.15 = (bf16[48,2688]{1,0:T(8,128)(2,1)S(1)}, bf16[48,2688]{1,0:T(8,128)(2,1)S(1)}, u32[]{:S(2)}, u32[]{:S(2)}) collective-permute-start(bf16[48,2688]{1,0:T(8,128)(2,1)S(1)} %get-tuple-element.146.refs_0_), channel_id=1, source_target_pairs={{0,2},{1,3},{2,0},{3,1},{4,6},{5,7},{6,4},{7,5},{8,10},{9,11},{10,... | collective-permute-start | bytes 774152 | tf_op jit(solution)/shard_map/ppermute | solution.py:779
  164.2 0.8 copy-start.2
  164.2 0.8 copy-start.4
  165.0 7.5 %copy-start.1 = (bf16[48,2688]{1,0:T(8,128)(2,1)S(1)}, bf16[48,2688]{1,0:T(8,128)(2,1)}, u32[]{:S(2)}) copy-start(bf16[48,2688]{1,0:T(8,128)(2,1)} %get-tuple-element.116) | copy-start | bytes 774148
  165.0 7.5 %copy-start.3 = (bf16[48,2688]{1,0:T(8,128)(2,1)S(1)}, bf16[48,2688]{1,0:T(8,128)(2,1)}, u32[]{:S(2)}) copy-start(bf16[48,2688]{1,0:T(8,128)(2,1)} %get-tuple-element.115) | copy-start | bytes 774148
  165.1 7.5 %copy-start.5 = (bf16[48,2688]{1,0:T(8,128)(2,1)S(1)}, bf16[48,2688]{1,0:T(8,128)(2,1)}, u32[]{:S(2)}) copy-start(bf16[48,2688]{1,0:T(8,128)(2,1)} %get-tuple-element.114) | copy-start | bytes 774148
  165.1 2.1 %collective-permute-start.18 = (bf16[4,56,1152]{2,1,0:T(8,128)(2,1)}, bf16[4,56,1152]{2,1,0:T(8,128)(2,1)S(1)}, u32[]{:S(2)}, u32[]{:S(2)}) collective-permute-start(bf16[4,56,1152]{2,1,0:T(8,128)(2,1)} %get-tuple-element.112), channel_id=1, source_target_pairs={{0,1},{1,0},{2,3},{3,2},{4,5},{5,4},{6,7},{7,6},{8,9},{9,8},{10,11... | collective-permute-start | bytes 1548296 | tf_op jit(solution)/shard_map/ppermute | solution.py:774
  168.6 7.1 %collective-permute-start.19 = (bf16[56,1152]{1,0:T(8,128)(2,1)S(1)}, bf16[56,1152]{1,0:T(8,128)(2,1)S(1)}, u32[]{:S(2)}, u32[]{:S(2)}) collective-permute-start(bf16[56,1152]{1,0:T(8,128)(2,1)S(1)} %get-tuple-element.147), channel_id=1, source_target_pairs={{0,2},{1,3},{2,0},{3,1},{4,6},{5,7},{6,4},{7,5},{8,10},{9,11},{10,... | collective-permute-start | bytes 387080 | tf_op jit(solution)/shard_map/ppermute | solution.py:779
  169.6 9.5 %collective-permute-start.21 = (bf16[56,1152]{1,0:T(8,128)(2,1)S(1)}, bf16[56,1152]{1,0:T(8,128)(2,1)S(1)}, u32[]{:S(2)}, u32[]{:S(2)}) collective-permute-start(bf16[56,1152]{1,0:T(8,128)(2,1)S(1)} %get-tuple-element.148), channel_id=1, source_target_pairs={{0,6},{1,7},{2,4},{3,5},{4,2},{5,3},{6,0},{7,1},{8,14},{9,15},{10,... | collective-permute-start | bytes 387080 | tf_op jit(solution)/shard_map/ppermute | solution.py:779
  172.0 12.3 %collective-permute-start.20 = (bf16[56,1152]{1,0:T(8,128)(2,1)S(1)}, bf16[56,1152]{1,0:T(8,128)(2,1)S(1)}, u32[]{:S(2)}, u32[]{:S(2)}) collective-permute-start(bf16[56,1152]{1,0:T(8,128)(2,1)S(1)} %get-tuple-element.149), channel_id=1, source_target_pairs={{0,4},{1,5},{2,6},{3,7},{4,0},{5,1},{6,2},{7,3},{8,12},{9,13},{10,... | collective-permute-start | bytes 387080 | tf_op jit(solution)/shard_map/ppermute | solution.py:779
  172.6 15.3 %copy-start.10 = (bf16[48,2688]{1,0:T(8,128)(2,1)}, bf16[48,2688]{1,0:T(8,128)(2,1)S(1)}, u32[]{:S(2)}) copy-start(bf16[48,2688]{1,0:T(8,128)(2,1)S(1)} %fusion.3.refs_0_) | copy-start | bytes 774148
  172.7 14.7 %collective-permute-start.27 = (bf16[48,2688]{1,0:T(8,128)(2,1)S(1)}, bf16[48,2688]{1,0:T(8,128)(2,1)S(1)}, u32[]{:S(2)}, u32[]{:S(2)}) collective-permute-start(bf16[48,2688]{1,0:T(8,128)(2,1)S(1)} %fusion.3.refs_0_), channel_id=1, source_target_pairs={{0,24},{8,16},{16,8},{24,0},{1,25},{9,17},{17,9},{25,1},{2,26},{10... | collective-permute-start | bytes 774152 | tf_op jit(solution)/shard_map/ppermute | solution.py:786
  175.2 12.7 %collective-permute-start.26 = (bf16[48,2688]{1,0:T(8,128)(2,1)S(1)}, bf16[48,2688]{1,0:T(8,128)(2,1)S(1)}, u32[]{:S(2)}, u32[]{:S(2)}) collective-permute-start(bf16[48,2688]{1,0:T(8,128)(2,1)S(1)} %fusion.3.refs_0_), channel_id=1, source_target_pairs={{0,16},{8,24},{16,0},{24,8},{1,17},{9,25},{17,1},{25,9},{2,18},{10... | collective-permute-start | bytes 774152 | tf_op jit(solution)/shard_map/ppermute | solution.py:786
  175.7 12.2 %collective-permute-start.25 = (bf16[48,2688]{1,0:T(8,128)(2,1)S(1)}, bf16[48,2688]{1,0:T(8,128)(2,1)S(1)}, u32[]{:S(2)}, u32[]{:S(2)}) collective-permute-start(bf16[48,2688]{1,0:T(8,128)(2,1)S(1)} %fusion.3.refs_0_), channel_id=1, source_target_pairs={{0,8},{8,0},{16,24},{24,16},{1,9},{9,1},{17,25},{25,17},{2,10},{10... | collective-permute-start | bytes 774152 | tf_op jit(solution)/shard_map/ppermute | solution.py:786
  184.3 8.7 %copy-start.16 = (bf16[56,1152]{1,0:T(8,128)(2,1)}, bf16[56,1152]{1,0:T(8,128)(2,1)S(1)}, u32[]{:S(2)}) copy-start(bf16[56,1152]{1,0:T(8,128)(2,1)S(1)} %fusion.7.refs_0_) | copy-start | bytes 387076
  184.3 7.7 %collective-permute-start.24 = (bf16[56,1152]{1,0:T(8,128)(2,1)S(1)}, bf16[56,1152]{1,0:T(8,128)(2,1)S(1)}, u32[]{:S(2)}, u32[]{:S(2)}) collective-permute-start(bf16[56,1152]{1,0:T(8,128)(2,1)S(1)} %fusion.7.refs_0_), channel_id=1, source_target_pairs={{0,24},{8,16},{16,8},{24,0},{1,25},{9,17},{17,9},{25,1},{2,26},{10... | collective-permute-start | bytes 387080 | tf_op jit(solution)/shard_map/ppermute | solution.py:786
  186.8 6.0 %collective-permute-start.23 = (bf16[56,1152]{1,0:T(8,128)(2,1)S(1)}, bf16[56,1152]{1,0:T(8,128)(2,1)S(1)}, u32[]{:S(2)}, u32[]{:S(2)}) collective-permute-start(bf16[56,1152]{1,0:T(8,128)(2,1)S(1)} %fusion.7.refs_0_), channel_id=1, source_target_pairs={{0,16},{8,24},{16,0},{24,8},{1,17},{9,25},{17,1},{25,9},{2,18},{10... | collective-permute-start | bytes 387080 | tf_op jit(solution)/shard_map/ppermute | solution.py:786
  187.4 0.7 copy-start.17
  187.4 5.6 %collective-permute-start.22 = (bf16[56,1152]{1,0:T(8,128)(2,1)S(1)}, bf16[56,1152]{1,0:T(8,128)(2,1)S(1)}, u32[]{:S(2)}, u32[]{:S(2)}) collective-permute-start(bf16[56,1152]{1,0:T(8,128)(2,1)S(1)} %fusion.7.refs_0_), channel_id=1, source_target_pairs={{0,8},{8,0},{16,24},{24,16},{1,9},{9,1},{17,25},{25,17},{2,10},{10... | collective-permute-start | bytes 387080 | tf_op jit(solution)/shard_map/ppermute | solution.py:786
  187.9 0.8 copy-start.19
  192.0 1.0 copy-start.25
  (11 other events, 7.4 us)

commit v7 on v6

--- a/solution.py
+++ b/solution.py
@@ -257,10 +257,10 @@
     score(order[0])
     for k, u in enumerate(order):
         ms = rest[k : k + 1]
+        if k >= 1:
+            ms.append(partial(mix, order[k - 1]))
         if k + 1 < nu:
             ms.append(partial(score, order[k + 1]))
-        if k >= 1:
-            ms.append(partial(mix, order[k - 1]))
         vs = [partial(f, u, t, n) for f in (vmax, vexp, vnorm) for t, n in srows]
         weave(ms, vs)
     nu = order[-1] + 1
@@ -587,12 +587,12 @@
         ms = []
         if k + 1 < nu:
             ms.append(partial(dprob, k + 1))
+        ms.append(partial(m_dv, k))
         if k >= 1:
-            ms += [partial(m_dv, k - 1), partial(m_dk, k - 1), partial(m_dq, k - 1)]
+            ms += [partial(m_dq, k - 1), partial(m_dk, k - 1)]
         vs = [partial(f, k, t, n) for f in (v_inner, v_ds) for t, n in srows]
         vs += pre[k : k + 1]
         weave(ms, vs)
-    m_dv(nu - 1)
     m_dk(nu - 1)
     m_dq(nu - 1)
     acc = {}

time: 197 us -> 195 us (0.990)
  Pallas kernels: 143 us -> 141 us
  transfers between devices with their start and end apart: 28 -> 28, of which waited for: 11 -> 11; matrix products, arithmetic and copies ran while one was open for 0% -> 0% of each run, Pallas kernels for 44% -> 43%
where the time goes in v7:
time: 195 us
  Pallas kernels  141 us (72%)
  starting transfers between devices  28.1 us (14%)
  waiting for transfers between devices  15.2 us (8%)
  local copies, waits for them, and re-layouts  5.31 us (3%)
  other arithmetic  3.38 us (2%)
    pallas_call x1, Pallas kernels, feed(): pl.pallas_call(partial(feed_body, SEQ, D, FF, T, N, np_), grid_spec=pltpu...  51.7 us
    pallas_call x1, Pallas kernels, back(): pl.pallas_call(partial(back_body, SEQ, SP, TP, D, FF, np_, len(deps)), gr...  42.5 us
    pallas_call x1, Pallas kernels, attend(): pl.pallas_call(partial(attend_body, SEQ, SP, TP, D, np_), grid_spec=pltpu...  28.4 us
    ppermute x6, starting transfers between devices, fetch(): return [x] + [lax.ppermute(x, 'fsdp', pairs(n, k)) for k in range(2, n, 2)]  10.3 us
    pallas_call x1, Pallas kernels, norm(): pl.pallas_call(partial(norm_body, SEQ, D), grid=(N // GROUP, GROUP // PAI...  10.3 us
    ppermute x6, starting transfers between devices, along_z(): lax.ppermute(x, 'fsdp', pairs(n, 2 * k + 2))  8.38 us
    ppermute x6, waiting for transfers between devices, along_z(): lax.ppermute(x, 'fsdp', pairs(n, 2 * k + 2))  8.06 us
    ppermute x6, starting transfers between devices, finish(): return [b] + [lax.ppermute(b, 'dp', pairs(d, k)) for k in range(1, d)]  7.11 us
  transfers between devices with their start and end apart: 28, of which 11 were waited for; matrix products, arithmetic and copies ran while one was open for 0% of the time, Pallas kernels for 43%

profile of v7, /device:TPU:0, one launch (start us, length us, event | category | flops | bytes accessed | tf_op | source)
XLA Modules:
  0.0 194.6 jit_solution(1724854489598997901)
XLA Ops:
  0.7 2.0 %pack.1 = (bf16[56,1152]{1,0:T(8,128)(2,1)}, bf16[48,2688]{1,0:T(8,128)(2,1)}) custom-call(f32[48,1152]{1,0:T(8,128)} %refs_4_.2, f32[6,48]{1,0:T(8,128)} %refs_6_.1, f32[1,144]{1,0:T(1,128)} %bitcast.53, f32[48,1152]{1,0:T(8,128)} %refs_5_.1, f32[48,1152]{1,0:T(8,128)} %bitcast.51, f32[48,384]{1,0:T(8,128)} %refs_4_.3), custom_call_target="tpu_custom_call" | custom-call | tf_op jit(solution)/shard_map/pack/pallas_call | solution.py:116
  2.7 5.0 %collective-permute-start.2 = (bf16[56,1152]{1,0:T(8,128)(2,1)}, bf16[56,1152]{1,0:T(8,128)(2,1)S(1)}, u32[]{:S(2)}, u32[]{:S(2)}) collective-permute-start(bf16[56,1152]{1,0:T(8,128)(2,1)} %get-tuple-element.84.refs_0_), channel_id=1, source_target_pairs={{0,6},{1,7},{2,4},{3,5},{4,2},{5,3},{6,0},{7,1},{8,14},{9,15},{10,... | collective-permute-start | bytes 387080 | tf_op jit(solution)/shard_map/ppermute | solution.py:765
  7.7 0.6 collective-permute-start
  8.3 10.3 %norm.1 = (f32[24,208,384]{2,1,0:T(8,128)}, f32[24,208,128]{2,1,0:T(8,128)}) custom-call(bf16[197,24,384]{2,1,0:T(8,128)(2,1)} %bitcast.55), custom_call_target="tpu_custom_call" | custom-call | flops 8000000000 | bytes 15000000 | tf_op jit(solution)/shard_map/norm/pallas_call | solution.py:144
  18.6 0.2 collective-permute-done.1.refs_2_
  18.9 0.4 copy-done.6
  19.3 0.2 copy-done.14
  19.5 0.5 collective-permute-start.4
  20.1 0.5 collective-permute-start.6
  20.6 3.6 %collective-permute-start.9 = (bf16[48,2688]{1,0:T(8,128)(2,1)}, bf16[48,2688]{1,0:T(8,128)(2,1)S(1)}, u32[]{:S(2)}, u32[]{:S(2)}) collective-permute-start(bf16[48,2688]{1,0:T(8,128)(2,1)} %touch.5.refs_0_), channel_id=1, source_target_pairs={{0,6},{1,7},{2,4},{3,5},{4,2},{5,3},{6,0},{7,1},{8,14},{9,15},{10,... | collective-permute-start | bytes 774152 | tf_op jit(solution)/shard_map/ppermute | solution.py:765
  24.2 1.1 collective-permute-start.7
  25.3 0.6 copy-done.28
  26.0 28.4 %attend.1 = (bf16[24,208,1152]{2,1,0:T(8,128)(2,1)}, bf16[200,24,384]{2,1,0:T(8,128)(2,1)}, bf16[24,6,208,208]{3,2,1,0:T(8,128)(2,1)}, bf16[24,208,384]{2,1,0:T(...) custom-call(s32[1]{0:T(128)} %bitcast.me_ref, ...), custom_call_target="tpu_custom_call" | custom-call | flops 20000000000 | bytes 25000000 | tf_op jit(solution)/shard_map/attend/pallas_call | solution.py:295
  54.4 0.7 copy-done.7
  55.3 0.5 collective-permute-start.11
  55.8 0.5 collective-permute-start.13
  57.0 0.4 collective-permute-done.11.refs_3_
  57.4 0.4 collective-permute-done.12.refs_5_
  57.8 0.4 collective-permute-done.13.refs_7_
  58.2 0.3 copy-done.22
  58.5 0.4 copy-done.23
  58.9 51.7 %feed.1 = (bf16[197,24,384]{2,1,0:T(8,128)(2,1)}, f32[200,24,384]{2,1,0:T(8,128)}, bf16[200,24,384]{2,1,0:T(8,128)(2,1)}, f32[8,1152]{1,0:T(8,128)}, f32[64,384]...) custom-call(s32[1]{0:T(128)} %bitcast.me_ref, s32[1]{0:T(128)S(6)} %copy.76.cnt_ref, ...), custom_call_target="tpu_custom_call" | custom-call | flops 44999999488 | bytes 30000000 | tf_op jit(solution)/shard_map/feed/pallas_call | solution.py:489
  110.6 0.2 collective-permute-start.14
  110.8 2.7 %collective-permute-done.14 = bf16[4,48,2688]{2,1,0:T(8,128)(2,1)S(1)} collective-permute-done((bf16[4,48,2688]{2,1,0:T(8,128)(2,1)}, bf16[4,48,2688]{2,1,0:T(8,128)(2,1)S(1)}, u32[]{:S(2)}, u32[]{:S(2)}) %collective-permute-start.14) | collective-permute-done | bytes 1032224 | tf_op jit(solution)/shard_map/ppermute | solution.py:774
  113.5 1.8 fusion.9
  115.4 3.4 %collective-permute-start.17 = (bf16[48,2688]{1,0:T(8,128)(2,1)S(1)}, bf16[48,2688]{1,0:T(8,128)(2,1)S(1)}, u32[]{:S(2)}, u32[]{:S(2)}) collective-permute-start(bf16[48,2688]{1,0:T(8,128)(2,1)S(1)} %get-tuple-element.144.refs_2_), channel_id=1, source_target_pairs={{0,6},{1,7},{2,4},{3,5},{4,2},{5,3},{6,0},{7,1},{8,14},{9,15},{10,... | collective-permute-start | bytes 774152 | tf_op jit(solution)/shard_map/ppermute | solution.py:779
  118.8 1.1 collective-permute-start.15
  119.9 42.5 %back.1 = (bf16[197,24,384]{2,1,0:T(8,128)(2,1)}, bf16[4,56,1152]{2,1,0:T(8,128)(2,1)}, f32[4,56,1152]{2,1,0:T(8,128)}) custom-call(s32[1]{0:T(128)} %bitcast.me_ref, bf16[24,208,384]{2,1,0:T(8,128)(2,1)} %get-tuple-element.99.a_ref, f32[24,208,384]{2,1,0:T(8,128)} %get-tuple-element.83.xh_ref, f32[24,208,128]{2,1,0:T(8,128)} %get-tuple-element.85.refs_4_.r_ref, ...), custom_call_target="tpu_custom_call" | custom-call | flops 40000000000 | bytes 30000000 | tf_op jit(solution)/shard_map/back/pallas_call | solution.py:693
  162.4 0.6 copy-done
  163.3 2.1 %collective-permute-done.18 = bf16[4,56,1152]{2,1,0:T(8,128)(2,1)S(1)} collective-permute-done((bf16[4,56,1152]{2,1,0:T(8,128)(2,1)}, bf16[4,56,1152]{2,1,0:T(8,128)(2,1)S(1)}, u32[]{:S(2)}, u32[]{:S(2)}) %collective-permute-start.18) | collective-permute-done | bytes 516128 | tf_op jit(solution)/shard_map/ppermute | solution.py:774
  165.4 1.3 fusion.8
  166.8 1.0 collective-permute-start.19
  167.8 2.4 %collective-permute-start.21 = (bf16[56,1152]{1,0:T(8,128)(2,1)S(1)}, bf16[56,1152]{1,0:T(8,128)(2,1)S(1)}, u32[]{:S(2)}, u32[]{:S(2)}) collective-permute-start(bf16[56,1152]{1,0:T(8,128)(2,1)S(1)} %get-tuple-element.148), channel_id=1, source_target_pairs={{0,6},{1,7},{2,4},{3,5},{4,2},{5,3},{6,0},{7,1},{8,14},{9,15},{10,... | collective-permute-start | bytes 387080 | tf_op jit(solution)/shard_map/ppermute | solution.py:779
  170.2 0.5 collective-permute-start.20
  170.9 2.5 %collective-permute-start.27 = (bf16[48,2688]{1,0:T(8,128)(2,1)S(1)}, bf16[48,2688]{1,0:T(8,128)(2,1)S(1)}, u32[]{:S(2)}, u32[]{:S(2)}) collective-permute-start(bf16[48,2688]{1,0:T(8,128)(2,1)S(1)} %fusion.3.refs_0_), channel_id=1, source_target_pairs={{0,24},{8,16},{16,8},{24,0},{1,25},{9,17},{17,9},{25,1},{2,26},{10... | collective-permute-start | bytes 774152 | tf_op jit(solution)/shard_map/ppermute | solution.py:786
  173.4 0.5 collective-permute-start.26
  173.9 0.5 collective-permute-start.25
  174.4 2.8 %collective-permute-done.21 = bf16[56,1152]{1,0:T(8,128)(2,1)S(1)} collective-permute-done((bf16[56,1152]{1,0:T(8,128)(2,1)S(1)}, bf16[56,1152]{1,0:T(8,128)(2,1)S(1)}, u32[]{:S(2)}, u32[]{:S(2)}) %collective-permute-start.21) | collective-permute-done | bytes 129056 | tf_op jit(solution)/shard_map/ppermute | solution.py:779
  177.3 5.2 %collective-permute-done.20 = bf16[56,1152]{1,0:T(8,128)(2,1)S(1)} collective-permute-done((bf16[56,1152]{1,0:T(8,128)(2,1)S(1)}, bf16[56,1152]{1,0:T(8,128)(2,1)S(1)}, u32[]{:S(2)}, u32[]{:S(2)}) %collective-permute-start.20) | collective-permute-done | bytes 129056 | tf_op jit(solution)/shard_map/ppermute | solution.py:779
  182.5 2.5 %collective-permute-start.24 = (bf16[56,1152]{1,0:T(8,128)(2,1)S(1)}, bf16[56,1152]{1,0:T(8,128)(2,1)S(1)}, u32[]{:S(2)}, u32[]{:S(2)}) collective-permute-start(bf16[56,1152]{1,0:T(8,128)(2,1)S(1)} %fusion.7.refs_0_), channel_id=1, source_target_pairs={{0,24},{8,16},{16,8},{24,0},{1,25},{9,17},{17,9},{25,1},{2,26},{10... | collective-permute-start | bytes 387080 | tf_op jit(solution)/shard_map/ppermute | solution.py:786
  185.1 0.5 collective-permute-start.23
  185.6 0.5 collective-permute-start.22
  186.1 0.1 copy-done.17
  186.3 0.5 copy-done.18
  186.9 3.3 %adam.3 = (f32[48,384]{1,0:T(8,128)}, f32[48,1152]{1,0:T(8,128)}, f32[48,1152]{1,0:T(8,128)}, f32[48,384]{1,0:T(8,128)}, f32[48,1152]{1,0:T(8,128)}, /*index=5*/...) custom-call(s32[6]{0:T(128)} %flag_ref.3, ...), custom_call_target="tpu_custom_call" | custom-call | flops 1000000000 | bytes 5000000 | tf_op jit(solution)/shard_map/adam/pallas_call | solution.py:734
  190.3 0.8 collective-permute-done.23.refs_2_
  191.2 0.5 copy-done.27
  191.9 2.6 %adam.2 = (f32[48,1152]{1,0:T(8,128)}, f32[1,144]{1,0:T(1,128)}, f32[6,48]{1,0:T(8,128)}, f32[48,1152]{1,0:T(8,128)}, f32[1,144]{1,0:T(1,128)}, /*index=5*/f32[6...) custom-call(s32[6]{0:T(128)} %flag_ref.3, ...), custom_call_target="tpu_custom_call" | custom-call | flops 1000000000 | bytes 5000000 | tf_op jit(solution)/shard_map/adam/pallas_call | solution.py:734
  (87 shorter events, 1.3 us)
Async XLA Ops:
  2.7 15.9 %collective-permute-start.2 = (bf16[56,1152]{1,0:T(8,128)(2,1)}, bf16[56,1152]{1,0:T(8,128)(2,1)S(1)}, u32[]{:S(2)}, u32[]{:S(2)}) collective-permute-start(bf16[56,1152]{1,0:T(8,128)(2,1)} %get-tuple-element.84.refs_0_), channel_id=1, source_target_pairs={{0,6},{1,7},{2,4},{3,5},{4,2},{5,3},{6,0},{7,1},{8,14},{9,15},{10,... | collective-permute-start | bytes 387080 | tf_op jit(solution)/shard_map/ppermute | solution.py:765
  7.7 11.1 %collective-permute-start.1 = (bf16[56,1152]{1,0:T(8,128)(2,1)}, bf16[56,1152]{1,0:T(8,128)(2,1)S(1)}, u32[]{:S(2)}, u32[]{:S(2)}) collective-permute-start(bf16[56,1152]{1,0:T(8,128)(2,1)} %get-tuple-element.84.refs_0_), channel_id=1, source_target_pairs={{0,4},{1,5},{2,6},{3,7},{4,0},{5,1},{6,2},{7,3},{8,12},{9,13},{10,... | collective-permute-start | bytes 387080 | tf_op jit(solution)/shard_map/ppermute | solution.py:765
  7.7 11.1 %collective-permute-start = (bf16[56,1152]{1,0:T(8,128)(2,1)}, bf16[56,1152]{1,0:T(8,128)(2,1)S(1)}, u32[]{:S(2)}, u32[]{:S(2)}) collective-permute-start(bf16[56,1152]{1,0:T(8,128)(2,1)} %get-tuple-element.84.refs_0_), channel_id=1, source_target_pairs={{0,2},{1,3},{2,0},{3,1},{4,6},{5,7},{6,4},{7,5},{8,10},{9,11},{10,... | collective-permute-start | bytes 387080 | tf_op jit(solution)/shard_map/ppermute | solution.py:765
  19.5 4.7 %collective-permute-start.3 = (bf16[56,1152]{1,0:T(8,128)(2,1)}, bf16[56,1152]{1,0:T(8,128)(2,1)S(1)}, u32[]{:S(2)}, u32[]{:S(2)}) collective-permute-start(bf16[56,1152]{1,0:T(8,128)(2,1)} %get-tuple-element.86.refs_0_), channel_id=1, source_target_pairs={{0,1},{1,0},{2,3},{3,2},{4,5},{5,4},{6,7},{7,6},{8,9},{9,8},{10,11... | collective-permute-start | bytes 387080 | tf_op jit(solution)/shard_map/ppermute | solution.py:769
  19.5 4.7 %collective-permute-start.4 = (bf16[56,1152]{1,0:T(8,128)(2,1)}, bf16[56,1152]{1,0:T(8,128)(2,1)S(1)}, u32[]{:S(2)}, u32[]{:S(2)}) collective-permute-start(bf16[56,1152]{1,0:T(8,128)(2,1)} %get-tuple-element.87.refs_2_), channel_id=1, source_target_pairs={{0,1},{1,0},{2,3},{3,2},{4,5},{5,4},{6,7},{7,6},{8,9},{9,8},{10,11... | collective-permute-start | bytes 387080 | tf_op jit(solution)/shard_map/ppermute | solution.py:769
  20.1 5.2 %collective-permute-start.5 = (bf16[56,1152]{1,0:T(8,128)(2,1)}, bf16[56,1152]{1,0:T(8,128)(2,1)S(1)}, u32[]{:S(2)}, u32[]{:S(2)}) collective-permute-start(bf16[56,1152]{1,0:T(8,128)(2,1)} %get-tuple-element.88.refs_4_), channel_id=1, source_target_pairs={{0,1},{1,0},{2,3},{3,2},{4,5},{5,4},{6,7},{7,6},{8,9},{9,8},{10,11... | collective-permute-start | bytes 387080 | tf_op jit(solution)/shard_map/ppermute | solution.py:769
  20.1 5.2 %collective-permute-start.6 = (bf16[56,1152]{1,0:T(8,128)(2,1)}, bf16[56,1152]{1,0:T(8,128)(2,1)S(1)}, u32[]{:S(2)}, u32[]{:S(2)}) collective-permute-start(bf16[56,1152]{1,0:T(8,128)(2,1)} %get-tuple-element.89.refs_6_.refs_1_), channel_id=1, source_target_pairs={{0,1},{1,0},{2,3},{3,2},{4,5},{5,4},{6,7},{7,6},{8,9},{9,8},{10,11... | collective-permute-start | bytes 387080 | tf_op jit(solution)/shard_map/ppermute | solution.py:769
  20.6 33.8 %collective-permute-start.9 = (bf16[48,2688]{1,0:T(8,128)(2,1)}, bf16[48,2688]{1,0:T(8,128)(2,1)S(1)}, u32[]{:S(2)}, u32[]{:S(2)}) collective-permute-start(bf16[48,2688]{1,0:T(8,128)(2,1)} %touch.5.refs_0_), channel_id=1, source_target_pairs={{0,6},{1,7},{2,4},{3,5},{4,2},{5,3},{6,0},{7,1},{8,14},{9,15},{10,... | collective-permute-start | bytes 774152 | tf_op jit(solution)/shard_map/ppermute | solution.py:765
  24.2 1.1 copy-start.24
  24.2 30.2 %collective-permute-start.8 = (bf16[48,2688]{1,0:T(8,128)(2,1)}, bf16[48,2688]{1,0:T(8,128)(2,1)S(1)}, u32[]{:S(2)}, u32[]{:S(2)}) collective-permute-start(bf16[48,2688]{1,0:T(8,128)(2,1)} %touch.5.refs_0_), channel_id=1, source_target_pairs={{0,4},{1,5},{2,6},{3,7},{4,0},{5,1},{6,2},{7,3},{8,12},{9,13},{10,... | collective-permute-start | bytes 774152 | tf_op jit(solution)/shard_map/ppermute | solution.py:765
  24.2 1.1 copy-start.26
  24.2 30.2 %collective-permute-start.7 = (bf16[48,2688]{1,0:T(8,128)(2,1)}, bf16[48,2688]{1,0:T(8,128)(2,1)S(1)}, u32[]{:S(2)}, u32[]{:S(2)}) collective-permute-start(bf16[48,2688]{1,0:T(8,128)(2,1)} %touch.5.refs_0_), channel_id=1, source_target_pairs={{0,2},{1,3},{2,0},{3,1},{4,6},{5,7},{6,4},{7,5},{8,10},{9,11},{10,... | collective-permute-start | bytes 774152 | tf_op jit(solution)/shard_map/ppermute | solution.py:765
  54.4 0.7 copy-start.7
  54.4 0.8 copy-start.8
  54.4 0.9 copy-start.9
  55.3 1.7 collective-permute-start.10
  55.3 2.1 %collective-permute-start.11 = (bf16[48,2688]{1,0:T(8,128)(2,1)}, bf16[48,2688]{1,0:T(8,128)(2,1)S(1)}, u32[]{:S(2)}, u32[]{:S(2)}) collective-permute-start(bf16[48,2688]{1,0:T(8,128)(2,1)} %get-tuple-element.95.refs_2_), channel_id=1, source_target_pairs={{0,1},{1,0},{2,3},{3,2},{4,5},{5,4},{6,7},{7,6},{8,9},{9,8},{10,11... | collective-permute-start | bytes 774152 | tf_op jit(solution)/shard_map/ppermute | solution.py:769
  55.8 2.0 %collective-permute-start.12 = (bf16[48,2688]{1,0:T(8,128)(2,1)}, bf16[48,2688]{1,0:T(8,128)(2,1)S(1)}, u32[]{:S(2)}, u32[]{:S(2)}) collective-permute-start(bf16[48,2688]{1,0:T(8,128)(2,1)} %get-tuple-element.96.refs_4_), channel_id=1, source_target_pairs={{0,1},{1,0},{2,3},{3,2},{4,5},{5,4},{6,7},{7,6},{8,9},{9,8},{10,11... | collective-permute-start | bytes 774152 | tf_op jit(solution)/shard_map/ppermute | solution.py:769
  55.8 2.3 %collective-permute-start.13 = (bf16[48,2688]{1,0:T(8,128)(2,1)}, bf16[48,2688]{1,0:T(8,128)(2,1)S(1)}, u32[]{:S(2)}, u32[]{:S(2)}) collective-permute-start(bf16[48,2688]{1,0:T(8,128)(2,1)} %get-tuple-element.97.refs_6_), channel_id=1, source_target_pairs={{0,1},{1,0},{2,3},{3,2},{4,5},{5,4},{6,7},{7,6},{8,9},{9,8},{10,11... | collective-permute-start | bytes 774152 | tf_op jit(solution)/shard_map/ppermute | solution.py:769
  57.0 1.1 copy-start.20
  57.4 0.7 copy-start.21
  110.6 2.9 %collective-permute-start.14 = (bf16[4,48,2688]{2,1,0:T(8,128)(2,1)}, bf16[4,48,2688]{2,1,0:T(8,128)(2,1)S(1)}, u32[]{:S(2)}, u32[]{:S(2)}) collective-permute-start(bf16[4,48,2688]{2,1,0:T(8,128)(2,1)} %get-tuple-element.108), channel_id=1, source_target_pairs={{0,1},{1,0},{2,3},{3,2},{4,5},{5,4},{6,7},{7,6},{8,9},{9,8},{10,11... | collective-permute-start | bytes 3096584 | tf_op jit(solution)/shard_map/ppermute | solution.py:774
  115.4 4.5 %copy-start.11 = (bf16[48,2688]{1,0:T(8,128)(2,1)}, bf16[48,2688]{1,0:T(8,128)(2,1)S(1)}, u32[]{:S(2)}) copy-start(bf16[48,2688]{1,0:T(8,128)(2,1)S(1)} %get-tuple-element.146.refs_0_) | copy-start | bytes 774148
  115.4 4.5 %copy-start.12 = (bf16[48,2688]{1,0:T(8,128)(2,1)}, bf16[48,2688]{1,0:T(8,128)(2,1)S(1)}, u32[]{:S(2)}) copy-start(bf16[48,2688]{1,0:T(8,128)(2,1)S(1)} %get-tuple-element.145.refs_1_) | copy-start | bytes 774148
  115.4 4.5 %copy-start.13 = (bf16[48,2688]{1,0:T(8,128)(2,1)}, bf16[48,2688]{1,0:T(8,128)(2,1)S(1)}, u32[]{:S(2)}) copy-start(bf16[48,2688]{1,0:T(8,128)(2,1)S(1)} %get-tuple-element.144.refs_2_) | copy-start | bytes 774148
  115.4 46.9 %collective-permute-start.17 = (bf16[48,2688]{1,0:T(8,128)(2,1)S(1)}, bf16[48,2688]{1,0:T(8,128)(2,1)S(1)}, u32[]{:S(2)}, u32[]{:S(2)}) collective-permute-start(bf16[48,2688]{1,0:T(8,128)(2,1)S(1)} %get-tuple-element.144.refs_2_), channel_id=1, source_target_pairs={{0,6},{1,7},{2,4},{3,5},{4,2},{5,3},{6,0},{7,1},{8,14},{9,15},{10,... | collective-permute-start | bytes 774152 | tf_op jit(solution)/shard_map/ppermute | solution.py:779
  118.8 43.6 %collective-permute-start.16 = (bf16[48,2688]{1,0:T(8,128)(2,1)S(1)}, bf16[48,2688]{1,0:T(8,128)(2,1)S(1)}, u32[]{:S(2)}, u32[]{:S(2)}) collective-permute-start(bf16[48,2688]{1,0:T(8,128)(2,1)S(1)} %get-tuple-element.145.refs_1_), channel_id=1, source_target_pairs={{0,4},{1,5},{2,6},{3,7},{4,0},{5,1},{6,2},{7,3},{8,12},{9,13},{10,... | collective-permute-start | bytes 774152 | tf_op jit(solution)/shard_map/ppermute | solution.py:779
  118.8 43.6 %collective-permute-start.15 = (bf16[48,2688]{1,0:T(8,128)(2,1)S(1)}, bf16[48,2688]{1,0:T(8,128)(2,1)S(1)}, u32[]{:S(2)}, u32[]{:S(2)}) collective-permute-start(bf16[48,2688]{1,0:T(8,128)(2,1)S(1)} %get-tuple-element.146.refs_0_), channel_id=1, source_target_pairs={{0,2},{1,3},{2,0},{3,1},{4,6},{5,7},{6,4},{7,5},{8,10},{9,11},{10,... | collective-permute-start | bytes 774152 | tf_op jit(solution)/shard_map/ppermute | solution.py:779
  162.4 0.8 copy-start.2
  162.4 0.8 copy-start.4
  163.2 7.5 %copy-start.1 = (bf16[48,2688]{1,0:T(8,128)(2,1)S(1)}, bf16[48,2688]{1,0:T(8,128)(2,1)}, u32[]{:S(2)}) copy-start(bf16[48,2688]{1,0:T(8,128)(2,1)} %get-tuple-element.116) | copy-start | bytes 774148
  163.2 7.5 %copy-start.3 = (bf16[48,2688]{1,0:T(8,128)(2,1)S(1)}, bf16[48,2688]{1,0:T(8,128)(2,1)}, u32[]{:S(2)}) copy-start(bf16[48,2688]{1,0:T(8,128)(2,1)} %get-tuple-element.115) | copy-start | bytes 774148
  163.2 7.5 %copy-start.5 = (bf16[48,2688]{1,0:T(8,128)(2,1)S(1)}, bf16[48,2688]{1,0:T(8,128)(2,1)}, u32[]{:S(2)}) copy-start(bf16[48,2688]{1,0:T(8,128)(2,1)} %get-tuple-element.114) | copy-start | bytes 774148
  163.3 2.1 %collective-permute-start.18 = (bf16[4,56,1152]{2,1,0:T(8,128)(2,1)}, bf16[4,56,1152]{2,1,0:T(8,128)(2,1)S(1)}, u32[]{:S(2)}, u32[]{:S(2)}) collective-permute-start(bf16[4,56,1152]{2,1,0:T(8,128)(2,1)} %get-tuple-element.112), channel_id=1, source_target_pairs={{0,1},{1,0},{2,3},{3,2},{4,5},{5,4},{6,7},{7,6},{8,9},{9,8},{10,11... | collective-permute-start | bytes 1548296 | tf_op jit(solution)/shard_map/ppermute | solution.py:774
  166.8 7.1 %collective-permute-start.19 = (bf16[56,1152]{1,0:T(8,128)(2,1)S(1)}, bf16[56,1152]{1,0:T(8,128)(2,1)S(1)}, u32[]{:S(2)}, u32[]{:S(2)}) collective-permute-start(bf16[56,1152]{1,0:T(8,128)(2,1)S(1)} %get-tuple-element.147), channel_id=1, source_target_pairs={{0,2},{1,3},{2,0},{3,1},{4,6},{5,7},{6,4},{7,5},{8,10},{9,11},{10,... | collective-permute-start | bytes 387080 | tf_op jit(solution)/shard_map/ppermute | solution.py:779
  167.8 9.5 %collective-permute-start.21 = (bf16[56,1152]{1,0:T(8,128)(2,1)S(1)}, bf16[56,1152]{1,0:T(8,128)(2,1)S(1)}, u32[]{:S(2)}, u32[]{:S(2)}) collective-permute-start(bf16[56,1152]{1,0:T(8,128)(2,1)S(1)} %get-tuple-element.148), channel_id=1, source_target_pairs={{0,6},{1,7},{2,4},{3,5},{4,2},{5,3},{6,0},{7,1},{8,14},{9,15},{10,... | collective-permute-start | bytes 387080 | tf_op jit(solution)/shard_map/ppermute | solution.py:779
  170.2 12.3 %collective-permute-start.20 = (bf16[56,1152]{1,0:T(8,128)(2,1)S(1)}, bf16[56,1152]{1,0:T(8,128)(2,1)S(1)}, u32[]{:S(2)}, u32[]{:S(2)}) collective-permute-start(bf16[56,1152]{1,0:T(8,128)(2,1)S(1)} %get-tuple-element.149), channel_id=1, source_target_pairs={{0,4},{1,5},{2,6},{3,7},{4,0},{5,1},{6,2},{7,3},{8,12},{9,13},{10,... | collective-permute-start | bytes 387080 | tf_op jit(solution)/shard_map/ppermute | solution.py:779
  170.9 15.3 %copy-start.10 = (bf16[48,2688]{1,0:T(8,128)(2,1)}, bf16[48,2688]{1,0:T(8,128)(2,1)S(1)}, u32[]{:S(2)}) copy-start(bf16[48,2688]{1,0:T(8,128)(2,1)S(1)} %fusion.3.refs_0_) | copy-start | bytes 774148
  170.9 14.7 %collective-permute-start.27 = (bf16[48,2688]{1,0:T(8,128)(2,1)S(1)}, bf16[48,2688]{1,0:T(8,128)(2,1)S(1)}, u32[]{:S(2)}, u32[]{:S(2)}) collective-permute-start(bf16[48,2688]{1,0:T(8,128)(2,1)S(1)} %fusion.3.refs_0_), channel_id=1, source_target_pairs={{0,24},{8,16},{16,8},{24,0},{1,25},{9,17},{17,9},{25,1},{2,26},{10... | collective-permute-start | bytes 774152 | tf_op jit(solution)/shard_map/ppermute | solution.py:786
  173.4 12.7 %collective-permute-start.26 = (bf16[48,2688]{1,0:T(8,128)(2,1)S(1)}, bf16[48,2688]{1,0:T(8,128)(2,1)S(1)}, u32[]{:S(2)}, u32[]{:S(2)}) collective-permute-start(bf16[48,2688]{1,0:T(8,128)(2,1)S(1)} %fusion.3.refs_0_), channel_id=1, source_target_pairs={{0,16},{8,24},{16,0},{24,8},{1,17},{9,25},{17,1},{25,9},{2,18},{10... | collective-permute-start | bytes 774152 | tf_op jit(solution)/shard_map/ppermute | solution.py:786
  173.9 12.2 %collective-permute-start.25 = (bf16[48,2688]{1,0:T(8,128)(2,1)S(1)}, bf16[48,2688]{1,0:T(8,128)(2,1)S(1)}, u32[]{:S(2)}, u32[]{:S(2)}) collective-permute-start(bf16[48,2688]{1,0:T(8,128)(2,1)S(1)} %fusion.3.refs_0_), channel_id=1, source_target_pairs={{0,8},{8,0},{16,24},{24,16},{1,9},{9,1},{17,25},{25,17},{2,10},{10... | collective-permute-start | bytes 774152 | tf_op jit(solution)/shard_map/ppermute | solution.py:786
  182.5 8.7 %copy-start.16 = (bf16[56,1152]{1,0:T(8,128)(2,1)}, bf16[56,1152]{1,0:T(8,128)(2,1)S(1)}, u32[]{:S(2)}) copy-start(bf16[56,1152]{1,0:T(8,128)(2,1)S(1)} %fusion.7.refs_0_) | copy-start | bytes 387076
  182.5 7.7 %collective-permute-start.24 = (bf16[56,1152]{1,0:T(8,128)(2,1)S(1)}, bf16[56,1152]{1,0:T(8,128)(2,1)S(1)}, u32[]{:S(2)}, u32[]{:S(2)}) collective-permute-start(bf16[56,1152]{1,0:T(8,128)(2,1)S(1)} %fusion.7.refs_0_), channel_id=1, source_target_pairs={{0,24},{8,16},{16,8},{24,0},{1,25},{9,17},{17,9},{25,1},{2,26},{10... | collective-permute-start | bytes 387080 | tf_op jit(solution)/shard_map/ppermute | solution.py:786
  185.1 6.0 %collective-permute-start.23 = (bf16[56,1152]{1,0:T(8,128)(2,1)S(1)}, bf16[56,1152]{1,0:T(8,128)(2,1)S(1)}, u32[]{:S(2)}, u32[]{:S(2)}) collective-permute-start(bf16[56,1152]{1,0:T(8,128)(2,1)S(1)} %fusion.7.refs_0_), channel_id=1, source_target_pairs={{0,16},{8,24},{16,0},{24,8},{1,17},{9,25},{17,1},{25,9},{2,18},{10... | collective-permute-start | bytes 387080 | tf_op jit(solution)/shard_map/ppermute | solution.py:786
  185.6 0.7 copy-start.17
  185.6 5.6 %collective-permute-start.22 = (bf16[56,1152]{1,0:T(8,128)(2,1)S(1)}, bf16[56,1152]{1,0:T(8,128)(2,1)S(1)}, u32[]{:S(2)}, u32[]{:S(2)}) collective-permute-start(bf16[56,1152]{1,0:T(8,128)(2,1)S(1)} %fusion.7.refs_0_), channel_id=1, source_target_pairs={{0,8},{8,0},{16,24},{24,16},{1,9},{9,1},{17,25},{25,17},{2,10},{10... | collective-permute-start | bytes 387080 | tf_op jit(solution)/shard_map/ppermute | solution.py:786
  186.1 0.8 copy-start.19
  190.3 1.0 copy-start.25
  (11 other events, 7.4 us)

commit v8 on v7

--- a/solution.py
+++ b/solution.py
@@ -479,7 +479,7 @@
     if np_:
         shape = (np_ // 2, D // np_, 2 * FF + D)
         out_specs += [whole(*shape)] * 2
-        out_shape += [s(shape, BF), s(shape, F32)]
+        out_shape += [s(shape, BF)] * 2
         scratch += [v((D, D), BF), v((D, FF), BF), v((D, FF), BF), v((D, D), F32), v((D, FF), F32), v((D, FF), F32)]
     else:
         out_specs += [whole(D, D), whole(D, FF), whole(D, FF)]
@@ -681,7 +681,7 @@
     if np_:
         shape = (np_ // 2, D // np_ + EXTRA, W3)
         out_specs += [whole(*shape)] * 2
-        out_shape += [s(shape, BF), s(shape, F32)]
+        out_shape += [s(shape, BF)] * 2
         scratch = [v((D, W3), F32), v((np_, EXTRA, up(max(FF, D) // np_, 128)), F32), v((8, D), F32)]
     else:
         out_specs += [whole(D, W3), whole(8, D)]
@@ -771,7 +771,7 @@
 
 
 def halve(snd, keep, n):
-    h = keep + lax.ppermute(snd, "fsdp", pairs(n, 1)).astype(F32)
+    h = keep.astype(F32) + lax.ppermute(snd, "fsdp", pairs(n, 1)).astype(F32)
     return h[0], [h[k].astype(BF) for k in range(1, n // 2)]
 
 

time: 195 us -> 195 us (level)
    another operation x2 -> x1, other arithmetic: 3.19 us -> 1.18 us
    unnamed x62 -> x56, local copies, waits for them, and re-layouts: 5.22 us -> 5.19 us
  transfers between devices with their start and end apart: 28 -> 28, of which waited for: 11 -> 13; matrix products, arithmetic and copies ran while one was open for 0% -> 1% of each run, Pallas kernels for 43% -> 43%
where the time goes in v8:
time: 195 us; the launch traced here: 194 us
  Pallas kernels  140 us (72%)
  starting transfers between devices  28.1 us (14%)
  waiting for transfers between devices  14.9 us (8%)
  local copies, waits for them, and re-layouts  5.28 us (3%)
  other arithmetic  4.02 us (2%)
    pallas_call x1, Pallas kernels, feed(): pl.pallas_call(partial(feed_body, SEQ, D, FF, T, N, np_), grid_spec=pltpu...  51.4 us
    pallas_call x1, Pallas kernels, back(): pl.pallas_call(partial(back_body, SEQ, SP, TP, D, FF, np_, len(deps)), gr...  42.3 us
    pallas_call x1, Pallas kernels, attend(): pl.pallas_call(partial(attend_body, SEQ, SP, TP, D, np_), grid_spec=pltpu...  28.4 us
    ppermute x6, starting transfers between devices, fetch(): return [x] + [lax.ppermute(x, 'fsdp', pairs(n, k)) for k in range(2, n, 2)]  10.3 us
    pallas_call x1, Pallas kernels, norm(): pl.pallas_call(partial(norm_body, SEQ, D), grid=(N // GROUP, GROUP // PAI...  10.3 us
    ppermute x6, starting transfers between devices, along_z(): lax.ppermute(x, 'fsdp', pairs(n, 2 * k + 2))  8.39 us
    ppermute x6, starting transfers between devices, finish(): return [b] + [lax.ppermute(b, 'dp', pairs(d, k)) for k in range(1, d)]  7.11 us
    ppermute x6, waiting for transfers between devices, along_z(): lax.ppermute(x, 'fsdp', pairs(n, 2 * k + 2))  6.89 us
  transfers between devices with their start and end apart: 28, of which 13 were waited for; matrix products, arithmetic and copies ran while one was open for 1% of the time, Pallas kernels for 43%

profile of v8, /device:TPU:0, one launch (start us, length us, event | category | flops | bytes accessed | tf_op | source)
XLA Modules:
  0.0 194.3 jit_solution(8912947131709373859)
XLA Ops:
  0.7 2.0 %pack.1 = (bf16[56,1152]{1,0:T(8,128)(2,1)}, bf16[48,2688]{1,0:T(8,128)(2,1)}) custom-call(f32[48,1152]{1,0:T(8,128)} %refs_4_.2, f32[6,48]{1,0:T(8,128)} %refs_6_.1, f32[1,144]{1,0:T(1,128)} %bitcast.53, f32[48,1152]{1,0:T(8,128)} %refs_5_.1, f32[48,1152]{1,0:T(8,128)} %bitcast.51, f32[48,384]{1,0:T(8,128)} %refs_4_.3), custom_call_target="tpu_custom_call" | custom-call | tf_op jit(solution)/shard_map/pack/pallas_call | solution.py:116
  2.7 5.0 %collective-permute-start.2 = (bf16[56,1152]{1,0:T(8,128)(2,1)}, bf16[56,1152]{1,0:T(8,128)(2,1)S(1)}, u32[]{:S(2)}, u32[]{:S(2)}) collective-permute-start(bf16[56,1152]{1,0:T(8,128)(2,1)} %get-tuple-element.84.refs_0_), channel_id=1, source_target_pairs={{0,6},{1,7},{2,4},{3,5},{4,2},{5,3},{6,0},{7,1},{8,14},{9,15},{10,... | collective-permute-start | bytes 387080 | tf_op jit(solution)/shard_map/ppermute | solution.py:765
  7.8 0.6 collective-permute-start
  8.3 10.3 %norm.1 = (f32[24,208,384]{2,1,0:T(8,128)}, f32[24,208,128]{2,1,0:T(8,128)}) custom-call(bf16[197,24,384]{2,1,0:T(8,128)(2,1)} %bitcast.55), custom_call_target="tpu_custom_call" | custom-call | flops 8000000000 | bytes 15000000 | tf_op jit(solution)/shard_map/norm/pallas_call | solution.py:144
  18.6 0.2 collective-permute-done.1.refs_2_
  18.9 0.4 copy-done.3
  19.3 0.2 copy-done.11
  19.6 0.5 collective-permute-start.4
  20.1 0.5 collective-permute-start.6
  20.6 3.6 %collective-permute-start.9 = (bf16[48,2688]{1,0:T(8,128)(2,1)}, bf16[48,2688]{1,0:T(8,128)(2,1)S(1)}, u32[]{:S(2)}, u32[]{:S(2)}) collective-permute-start(bf16[48,2688]{1,0:T(8,128)(2,1)} %touch.5.refs_0_), channel_id=1, source_target_pairs={{0,6},{1,7},{2,4},{3,5},{4,2},{5,3},{6,0},{7,1},{8,14},{9,15},{10,... | collective-permute-start | bytes 774152 | tf_op jit(solution)/shard_map/ppermute | solution.py:765
  24.2 1.1 collective-permute-start.7
  25.3 0.6 copy-done.25
  26.0 28.4 %attend.1 = (bf16[24,208,1152]{2,1,0:T(8,128)(2,1)}, bf16[200,24,384]{2,1,0:T(8,128)(2,1)}, bf16[24,6,208,208]{3,2,1,0:T(8,128)(2,1)}, bf16[24,208,384]{2,1,0:T(...) custom-call(s32[1]{0:T(128)} %bitcast.me_ref, ...), custom_call_target="tpu_custom_call" | custom-call | flops 20000000000 | bytes 25000000 | tf_op jit(solution)/shard_map/attend/pallas_call | solution.py:295
  54.5 0.7 copy-done.4
  55.3 0.5 collective-permute-start.11
  55.8 0.5 collective-permute-start.13
  57.1 0.4 collective-permute-done.11.refs_3_
  57.4 0.4 collective-permute-done.12.refs_5_
  57.8 0.4 collective-permute-done.13.refs_7_
  58.2 0.3 copy-done.19
  58.5 0.4 copy-done.20
  58.9 51.4 %feed.1 = (bf16[197,24,384]{2,1,0:T(8,128)(2,1)}, f32[200,24,384]{2,1,0:T(8,128)}, bf16[200,24,384]{2,1,0:T(8,128)(2,1)}, f32[8,1152]{1,0:T(8,128)}, f32[64,384]...) custom-call(s32[1]{0:T(128)} %bitcast.me_ref, s32[1]{0:T(128)S(6)} %copy.76.cnt_ref, ...), custom_call_target="tpu_custom_call" | custom-call | flops 44999999488 | bytes 30000000 | tf_op jit(solution)/shard_map/feed/pallas_call | solution.py:489
  110.5 2.7 %collective-permute-done.14 = bf16[4,48,2688]{2,1,0:T(8,128)(2,1)S(1)} collective-permute-done((bf16[4,48,2688]{2,1,0:T(8,128)(2,1)}, bf16[4,48,2688]{2,1,0:T(8,128)(2,1)S(1)}, u32[]{:S(2)}, u32[]{:S(2)}) %collective-permute-start.14) | collective-permute-done | bytes 1032224 | tf_op jit(solution)/shard_map/ppermute | solution.py:774
  113.2 1.5 convert_add_fusion
  114.7 3.4 %collective-permute-start.17 = (bf16[48,2688]{1,0:T(8,128)(2,1)S(1)}, bf16[48,2688]{1,0:T(8,128)(2,1)S(1)}, u32[]{:S(2)}, u32[]{:S(2)}) collective-permute-start(bf16[48,2688]{1,0:T(8,128)(2,1)S(1)} %get-tuple-element.144.refs_2_), channel_id=1, source_target_pairs={{0,6},{1,7},{2,4},{3,5},{4,2},{5,3},{6,0},{7,1},{8,14},{9,15},{10,... | collective-permute-start | bytes 774152 | tf_op jit(solution)/shard_map/ppermute | solution.py:779
  118.1 1.1 collective-permute-start.15
  119.2 42.3 %back.1 = (bf16[197,24,384]{2,1,0:T(8,128)(2,1)}, bf16[4,56,1152]{2,1,0:T(8,128)(2,1)}, bf16[4,56,1152]{2,1,0:T(8,128)(2,1)}) custom-call(s32[1]{0:T(128)} %bitcast.me_ref, bf16[24,208,384]{2,1,0:T(8,128)(2,1)} %get-tuple-element.99.a_ref, f32[24,208,384]{2,1,0:T(8,128)} %get-tuple-element.83.xh_ref, f32[24,208,128]{2,1,0:T(8,128)} %get-tuple-element.85.refs_4_.r_ref, ...), custom_call_target="tpu_custom_call" | custom-call | flops 40000000000 | bytes 30000000 | tf_op jit(solution)/shard_map/back/pallas_call | solution.py:693
  161.6 0.6 copy-done
  162.4 2.1 %collective-permute-done.18 = bf16[4,56,1152]{2,1,0:T(8,128)(2,1)S(1)} collective-permute-done((bf16[4,56,1152]{2,1,0:T(8,128)(2,1)}, bf16[4,56,1152]{2,1,0:T(8,128)(2,1)S(1)}, u32[]{:S(2)}, u32[]{:S(2)}) %collective-permute-start.18) | collective-permute-done | bytes 516128 | tf_op jit(solution)/shard_map/ppermute | solution.py:774
  164.5 1.2 fusion.8
  165.8 1.0 collective-permute-start.19
  166.8 2.4 %collective-permute-start.21 = (bf16[56,1152]{1,0:T(8,128)(2,1)S(1)}, bf16[56,1152]{1,0:T(8,128)(2,1)S(1)}, u32[]{:S(2)}, u32[]{:S(2)}) collective-permute-start(bf16[56,1152]{1,0:T(8,128)(2,1)S(1)} %get-tuple-element.148), channel_id=1, source_target_pairs={{0,6},{1,7},{2,4},{3,5},{4,2},{5,3},{6,0},{7,1},{8,14},{9,15},{10,... | collective-permute-start | bytes 387080 | tf_op jit(solution)/shard_map/ppermute | solution.py:779
  169.2 0.5 collective-permute-start.20
  169.7 1.3 fusion.3.refs_0_
  171.0 2.5 %collective-permute-start.27 = (bf16[48,2688]{1,0:T(8,128)(2,1)S(1)}, bf16[48,2688]{1,0:T(8,128)(2,1)S(1)}, u32[]{:S(2)}, u32[]{:S(2)}) collective-permute-start(bf16[48,2688]{1,0:T(8,128)(2,1)S(1)} %fusion.3.refs_0_), channel_id=1, source_target_pairs={{0,24},{8,16},{16,8},{24,0},{1,25},{9,17},{17,9},{25,1},{2,26},{10... | collective-permute-start | bytes 774152 | tf_op jit(solution)/shard_map/ppermute | solution.py:786
  173.5 0.5 collective-permute-start.26
  174.0 0.5 collective-permute-start.25
  174.6 1.7 collective-permute-done.21
  176.2 5.2 %collective-permute-done.20 = bf16[56,1152]{1,0:T(8,128)(2,1)S(1)} collective-permute-done((bf16[56,1152]{1,0:T(8,128)(2,1)S(1)}, bf16[56,1152]{1,0:T(8,128)(2,1)S(1)}, u32[]{:S(2)}, u32[]{:S(2)}) %collective-permute-start.20) | collective-permute-done | bytes 129056 | tf_op jit(solution)/shard_map/ppermute | solution.py:779
  181.5 2.5 %collective-permute-start.24 = (bf16[56,1152]{1,0:T(8,128)(2,1)S(1)}, bf16[56,1152]{1,0:T(8,128)(2,1)S(1)}, u32[]{:S(2)}, u32[]{:S(2)}) collective-permute-start(bf16[56,1152]{1,0:T(8,128)(2,1)S(1)} %fusion.7.refs_0_), channel_id=1, source_target_pairs={{0,24},{8,16},{16,8},{24,0},{1,25},{9,17},{17,9},{25,1},{2,26},{10... | collective-permute-start | bytes 387080 | tf_op jit(solution)/shard_map/ppermute | solution.py:786
  184.0 0.5 collective-permute-start.23
  184.6 0.5 collective-permute-start.22
  185.1 0.7 collective-permute-done.26.refs_2_
  185.9 0.5 copy-done.15
  186.6 3.3 %adam.3 = (f32[48,384]{1,0:T(8,128)}, f32[48,1152]{1,0:T(8,128)}, f32[48,1152]{1,0:T(8,128)}, f32[48,384]{1,0:T(8,128)}, f32[48,1152]{1,0:T(8,128)}, /*index=5*/...) custom-call(s32[6]{0:T(128)} %flag_ref.3, ...), custom_call_target="tpu_custom_call" | custom-call | flops 1000000000 | bytes 5000000 | tf_op jit(solution)/shard_map/adam/pallas_call | solution.py:734
  190.0 0.8 collective-permute-done.23.refs_2_
  190.9 0.5 copy-done.24
  191.5 2.6 %adam.2 = (f32[48,1152]{1,0:T(8,128)}, f32[1,144]{1,0:T(1,128)}, f32[6,48]{1,0:T(8,128)}, f32[48,1152]{1,0:T(8,128)}, f32[1,144]{1,0:T(1,128)}, /*index=5*/f32[6...) custom-call(s32[6]{0:T(128)} %flag_ref.3, ...), custom_call_target="tpu_custom_call" | custom-call | flops 1000000000 | bytes 5000000 | tf_op jit(solution)/shard_map/adam/pallas_call | solution.py:734
  (81 shorter events, 1.6 us)
Async XLA Ops:
  2.7 15.9 %collective-permute-start.2 = (bf16[56,1152]{1,0:T(8,128)(2,1)}, bf16[56,1152]{1,0:T(8,128)(2,1)S(1)}, u32[]{:S(2)}, u32[]{:S(2)}) collective-permute-start(bf16[56,1152]{1,0:T(8,128)(2,1)} %get-tuple-element.84.refs_0_), channel_id=1, source_target_pairs={{0,6},{1,7},{2,4},{3,5},{4,2},{5,3},{6,0},{7,1},{8,14},{9,15},{10,... | collective-permute-start | bytes 387080 | tf_op jit(solution)/shard_map/ppermute | solution.py:765
  7.7 11.1 %collective-permute-start.1 = (bf16[56,1152]{1,0:T(8,128)(2,1)}, bf16[56,1152]{1,0:T(8,128)(2,1)S(1)}, u32[]{:S(2)}, u32[]{:S(2)}) collective-permute-start(bf16[56,1152]{1,0:T(8,128)(2,1)} %get-tuple-element.84.refs_0_), channel_id=1, source_target_pairs={{0,4},{1,5},{2,6},{3,7},{4,0},{5,1},{6,2},{7,3},{8,12},{9,13},{10,... | collective-permute-start | bytes 387080 | tf_op jit(solution)/shard_map/ppermute | solution.py:765
  7.8 11.1 %collective-permute-start = (bf16[56,1152]{1,0:T(8,128)(2,1)}, bf16[56,1152]{1,0:T(8,128)(2,1)S(1)}, u32[]{:S(2)}, u32[]{:S(2)}) collective-permute-start(bf16[56,1152]{1,0:T(8,128)(2,1)} %get-tuple-element.84.refs_0_), channel_id=1, source_target_pairs={{0,2},{1,3},{2,0},{3,1},{4,6},{5,7},{6,4},{7,5},{8,10},{9,11},{10,... | collective-permute-start | bytes 387080 | tf_op jit(solution)/shard_map/ppermute | solution.py:765
  19.6 4.6 %collective-permute-start.3 = (bf16[56,1152]{1,0:T(8,128)(2,1)}, bf16[56,1152]{1,0:T(8,128)(2,1)S(1)}, u32[]{:S(2)}, u32[]{:S(2)}) collective-permute-start(bf16[56,1152]{1,0:T(8,128)(2,1)} %get-tuple-element.86.refs_0_), channel_id=1, source_target_pairs={{0,1},{1,0},{2,3},{3,2},{4,5},{5,4},{6,7},{7,6},{8,9},{9,8},{10,11... | collective-permute-start | bytes 387080 | tf_op jit(solution)/shard_map/ppermute | solution.py:769
  19.6 4.7 %collective-permute-start.4 = (bf16[56,1152]{1,0:T(8,128)(2,1)}, bf16[56,1152]{1,0:T(8,128)(2,1)S(1)}, u32[]{:S(2)}, u32[]{:S(2)}) collective-permute-start(bf16[56,1152]{1,0:T(8,128)(2,1)} %get-tuple-element.87.refs_2_), channel_id=1, source_target_pairs={{0,1},{1,0},{2,3},{3,2},{4,5},{5,4},{6,7},{7,6},{8,9},{9,8},{10,11... | collective-permute-start | bytes 387080 | tf_op jit(solution)/shard_map/ppermute | solution.py:769
  20.1 5.2 %collective-permute-start.5 = (bf16[56,1152]{1,0:T(8,128)(2,1)}, bf16[56,1152]{1,0:T(8,128)(2,1)S(1)}, u32[]{:S(2)}, u32[]{:S(2)}) collective-permute-start(bf16[56,1152]{1,0:T(8,128)(2,1)} %get-tuple-element.88.refs_4_), channel_id=1, source_target_pairs={{0,1},{1,0},{2,3},{3,2},{4,5},{5,4},{6,7},{7,6},{8,9},{9,8},{10,11... | collective-permute-start | bytes 387080 | tf_op jit(solution)/shard_map/ppermute | solution.py:769
  20.1 5.2 %collective-permute-start.6 = (bf16[56,1152]{1,0:T(8,128)(2,1)}, bf16[56,1152]{1,0:T(8,128)(2,1)S(1)}, u32[]{:S(2)}, u32[]{:S(2)}) collective-permute-start(bf16[56,1152]{1,0:T(8,128)(2,1)} %get-tuple-element.89.refs_6_.refs_1_), channel_id=1, source_target_pairs={{0,1},{1,0},{2,3},{3,2},{4,5},{5,4},{6,7},{7,6},{8,9},{9,8},{10,11... | collective-permute-start | bytes 387080 | tf_op jit(solution)/shard_map/ppermute | solution.py:769
  20.6 33.8 %collective-permute-start.9 = (bf16[48,2688]{1,0:T(8,128)(2,1)}, bf16[48,2688]{1,0:T(8,128)(2,1)S(1)}, u32[]{:S(2)}, u32[]{:S(2)}) collective-permute-start(bf16[48,2688]{1,0:T(8,128)(2,1)} %touch.5.refs_0_), channel_id=1, source_target_pairs={{0,6},{1,7},{2,4},{3,5},{4,2},{5,3},{6,0},{7,1},{8,14},{9,15},{10,... | collective-permute-start | bytes 774152 | tf_op jit(solution)/shard_map/ppermute | solution.py:765
  24.2 1.1 copy-start.21
  24.2 30.2 %collective-permute-start.8 = (bf16[48,2688]{1,0:T(8,128)(2,1)}, bf16[48,2688]{1,0:T(8,128)(2,1)S(1)}, u32[]{:S(2)}, u32[]{:S(2)}) collective-permute-start(bf16[48,2688]{1,0:T(8,128)(2,1)} %touch.5.refs_0_), channel_id=1, source_target_pairs={{0,4},{1,5},{2,6},{3,7},{4,0},{5,1},{6,2},{7,3},{8,12},{9,13},{10,... | collective-permute-start | bytes 774152 | tf_op jit(solution)/shard_map/ppermute | solution.py:765
  24.2 1.1 copy-start.23
  24.2 30.2 %collective-permute-start.7 = (bf16[48,2688]{1,0:T(8,128)(2,1)}, bf16[48,2688]{1,0:T(8,128)(2,1)S(1)}, u32[]{:S(2)}, u32[]{:S(2)}) collective-permute-start(bf16[48,2688]{1,0:T(8,128)(2,1)} %touch.5.refs_0_), channel_id=1, source_target_pairs={{0,2},{1,3},{2,0},{3,1},{4,6},{5,7},{6,4},{7,5},{8,10},{9,11},{10,... | collective-permute-start | bytes 774152 | tf_op jit(solution)/shard_map/ppermute | solution.py:765
  54.4 0.7 copy-start.4
  54.4 0.8 copy-start.5
  54.4 0.9 copy-start.6
  55.3 1.7 collective-permute-start.10
  55.3 2.1 %collective-permute-start.11 = (bf16[48,2688]{1,0:T(8,128)(2,1)}, bf16[48,2688]{1,0:T(8,128)(2,1)S(1)}, u32[]{:S(2)}, u32[]{:S(2)}) collective-permute-start(bf16[48,2688]{1,0:T(8,128)(2,1)} %get-tuple-element.95.refs_2_), channel_id=1, source_target_pairs={{0,1},{1,0},{2,3},{3,2},{4,5},{5,4},{6,7},{7,6},{8,9},{9,8},{10,11... | collective-permute-start | bytes 774152 | tf_op jit(solution)/shard_map/ppermute | solution.py:769
  55.8 2.0 %collective-permute-start.12 = (bf16[48,2688]{1,0:T(8,128)(2,1)}, bf16[48,2688]{1,0:T(8,128)(2,1)S(1)}, u32[]{:S(2)}, u32[]{:S(2)}) collective-permute-start(bf16[48,2688]{1,0:T(8,128)(2,1)} %get-tuple-element.96.refs_4_), channel_id=1, source_target_pairs={{0,1},{1,0},{2,3},{3,2},{4,5},{5,4},{6,7},{7,6},{8,9},{9,8},{10,11... | collective-permute-start | bytes 774152 | tf_op jit(solution)/shard_map/ppermute | solution.py:769
  55.8 2.3 %collective-permute-start.13 = (bf16[48,2688]{1,0:T(8,128)(2,1)}, bf16[48,2688]{1,0:T(8,128)(2,1)S(1)}, u32[]{:S(2)}, u32[]{:S(2)}) collective-permute-start(bf16[48,2688]{1,0:T(8,128)(2,1)} %get-tuple-element.97.refs_6_), channel_id=1, source_target_pairs={{0,1},{1,0},{2,3},{3,2},{4,5},{5,4},{6,7},{7,6},{8,9},{9,8},{10,11... | collective-permute-start | bytes 774152 | tf_op jit(solution)/shard_map/ppermute | solution.py:769
  57.1 1.1 copy-start.17
  57.4 0.7 copy-start.18
  57.8 0.7 copy-start.19
  58.2 0.7 copy-start.20
  110.3 2.9 %collective-permute-start.14 = (bf16[4,48,2688]{2,1,0:T(8,128)(2,1)}, bf16[4,48,2688]{2,1,0:T(8,128)(2,1)S(1)}, u32[]{:S(2)}, u32[]{:S(2)}) collective-permute-start(bf16[4,48,2688]{2,1,0:T(8,128)(2,1)} %get-tuple-element.108), channel_id=1, source_target_pairs={{0,1},{1,0},{2,3},{3,2},{4,5},{5,4},{6,7},{7,6},{8,9},{9,8},{10,11... | collective-permute-start | bytes 3096584 | tf_op jit(solution)/shard_map/ppermute | solution.py:774
  114.7 4.5 %copy-start.8 = (bf16[48,2688]{1,0:T(8,128)(2,1)}, bf16[48,2688]{1,0:T(8,128)(2,1)S(1)}, u32[]{:S(2)}) copy-start(bf16[48,2688]{1,0:T(8,128)(2,1)S(1)} %get-tuple-element.146.refs_0_) | copy-start | bytes 774148
  114.7 4.5 %copy-start.9 = (bf16[48,2688]{1,0:T(8,128)(2,1)}, bf16[48,2688]{1,0:T(8,128)(2,1)S(1)}, u32[]{:S(2)}) copy-start(bf16[48,2688]{1,0:T(8,128)(2,1)S(1)} %get-tuple-element.145.refs_1_) | copy-start | bytes 774148
  114.7 4.5 %copy-start.10 = (bf16[48,2688]{1,0:T(8,128)(2,1)}, bf16[48,2688]{1,0:T(8,128)(2,1)S(1)}, u32[]{:S(2)}) copy-start(bf16[48,2688]{1,0:T(8,128)(2,1)S(1)} %get-tuple-element.144.refs_2_) | copy-start | bytes 774148
  114.7 46.8 %collective-permute-start.17 = (bf16[48,2688]{1,0:T(8,128)(2,1)S(1)}, bf16[48,2688]{1,0:T(8,128)(2,1)S(1)}, u32[]{:S(2)}, u32[]{:S(2)}) collective-permute-start(bf16[48,2688]{1,0:T(8,128)(2,1)S(1)} %get-tuple-element.144.refs_2_), channel_id=1, source_target_pairs={{0,6},{1,7},{2,4},{3,5},{4,2},{5,3},{6,0},{7,1},{8,14},{9,15},{10,... | collective-permute-start | bytes 774152 | tf_op jit(solution)/shard_map/ppermute | solution.py:779
  118.1 43.4 %collective-permute-start.16 = (bf16[48,2688]{1,0:T(8,128)(2,1)S(1)}, bf16[48,2688]{1,0:T(8,128)(2,1)S(1)}, u32[]{:S(2)}, u32[]{:S(2)}) collective-permute-start(bf16[48,2688]{1,0:T(8,128)(2,1)S(1)} %get-tuple-element.145.refs_1_), channel_id=1, source_target_pairs={{0,4},{1,5},{2,6},{3,7},{4,0},{5,1},{6,2},{7,3},{8,12},{9,13},{10,... | collective-permute-start | bytes 774152 | tf_op jit(solution)/shard_map/ppermute | solution.py:779
  118.1 43.4 %collective-permute-start.15 = (bf16[48,2688]{1,0:T(8,128)(2,1)S(1)}, bf16[48,2688]{1,0:T(8,128)(2,1)S(1)}, u32[]{:S(2)}, u32[]{:S(2)}) collective-permute-start(bf16[48,2688]{1,0:T(8,128)(2,1)S(1)} %get-tuple-element.146.refs_0_), channel_id=1, source_target_pairs={{0,2},{1,3},{2,0},{3,1},{4,6},{5,7},{6,4},{7,5},{8,10},{9,11},{10,... | collective-permute-start | bytes 774152 | tf_op jit(solution)/shard_map/ppermute | solution.py:779
  161.5 0.7 copy-start
  161.5 0.8 copy-start.1
  161.6 0.9 copy-start.2
  162.4 2.1 %collective-permute-start.18 = (bf16[4,56,1152]{2,1,0:T(8,128)(2,1)}, bf16[4,56,1152]{2,1,0:T(8,128)(2,1)S(1)}, u32[]{:S(2)}, u32[]{:S(2)}) collective-permute-start(bf16[4,56,1152]{2,1,0:T(8,128)(2,1)} %get-tuple-element.112), channel_id=1, source_target_pairs={{0,1},{1,0},{2,3},{3,2},{4,5},{5,4},{6,7},{7,6},{8,9},{9,8},{10,11... | collective-permute-start | bytes 1548296 | tf_op jit(solution)/shard_map/ppermute | solution.py:774
  165.8 8.3 %collective-permute-start.19 = (bf16[56,1152]{1,0:T(8,128)(2,1)S(1)}, bf16[56,1152]{1,0:T(8,128)(2,1)S(1)}, u32[]{:S(2)}, u32[]{:S(2)}) collective-permute-start(bf16[56,1152]{1,0:T(8,128)(2,1)S(1)} %get-tuple-element.147), channel_id=1, source_target_pairs={{0,2},{1,3},{2,0},{3,1},{4,6},{5,7},{6,4},{7,5},{8,10},{9,11},{10,... | collective-permute-start | bytes 387080 | tf_op jit(solution)/shard_map/ppermute | solution.py:779
  166.8 9.5 %collective-permute-start.21 = (bf16[56,1152]{1,0:T(8,128)(2,1)S(1)}, bf16[56,1152]{1,0:T(8,128)(2,1)S(1)}, u32[]{:S(2)}, u32[]{:S(2)}) collective-permute-start(bf16[56,1152]{1,0:T(8,128)(2,1)S(1)} %get-tuple-element.148), channel_id=1, source_target_pairs={{0,6},{1,7},{2,4},{3,5},{4,2},{5,3},{6,0},{7,1},{8,14},{9,15},{10,... | collective-permute-start | bytes 387080 | tf_op jit(solution)/shard_map/ppermute | solution.py:779
  169.2 12.3 %collective-permute-start.20 = (bf16[56,1152]{1,0:T(8,128)(2,1)S(1)}, bf16[56,1152]{1,0:T(8,128)(2,1)S(1)}, u32[]{:S(2)}, u32[]{:S(2)}) collective-permute-start(bf16[56,1152]{1,0:T(8,128)(2,1)S(1)} %get-tuple-element.149), channel_id=1, source_target_pairs={{0,4},{1,5},{2,6},{3,7},{4,0},{5,1},{6,2},{7,3},{8,12},{9,13},{10,... | collective-permute-start | bytes 387080 | tf_op jit(solution)/shard_map/ppermute | solution.py:779
  171.0 14.9 %copy-start.7 = (bf16[48,2688]{1,0:T(8,128)(2,1)}, bf16[48,2688]{1,0:T(8,128)(2,1)S(1)}, u32[]{:S(2)}) copy-start(bf16[48,2688]{1,0:T(8,128)(2,1)S(1)} %fusion.3.refs_0_) | copy-start | bytes 774148
  171.0 13.5 %collective-permute-start.27 = (bf16[48,2688]{1,0:T(8,128)(2,1)S(1)}, bf16[48,2688]{1,0:T(8,128)(2,1)S(1)}, u32[]{:S(2)}, u32[]{:S(2)}) collective-permute-start(bf16[48,2688]{1,0:T(8,128)(2,1)S(1)} %fusion.3.refs_0_), channel_id=1, source_target_pairs={{0,24},{8,16},{16,8},{24,0},{1,25},{9,17},{17,9},{25,1},{2,26},{10... | collective-permute-start | bytes 774152 | tf_op jit(solution)/shard_map/ppermute | solution.py:786
  173.5 12.3 %collective-permute-start.26 = (bf16[48,2688]{1,0:T(8,128)(2,1)S(1)}, bf16[48,2688]{1,0:T(8,128)(2,1)S(1)}, u32[]{:S(2)}, u32[]{:S(2)}) collective-permute-start(bf16[48,2688]{1,0:T(8,128)(2,1)S(1)} %fusion.3.refs_0_), channel_id=1, source_target_pairs={{0,16},{8,24},{16,0},{24,8},{1,17},{9,25},{17,1},{25,9},{2,18},{10... | collective-permute-start | bytes 774152 | tf_op jit(solution)/shard_map/ppermute | solution.py:786
  174.0 11.9 %collective-permute-start.25 = (bf16[48,2688]{1,0:T(8,128)(2,1)S(1)}, bf16[48,2688]{1,0:T(8,128)(2,1)S(1)}, u32[]{:S(2)}, u32[]{:S(2)}) collective-permute-start(bf16[48,2688]{1,0:T(8,128)(2,1)S(1)} %fusion.3.refs_0_), channel_id=1, source_target_pairs={{0,8},{8,0},{16,24},{24,16},{1,9},{9,1},{17,25},{25,17},{2,10},{10... | collective-permute-start | bytes 774152 | tf_op jit(solution)/shard_map/ppermute | solution.py:786
  181.5 9.4 %copy-start.13 = (bf16[56,1152]{1,0:T(8,128)(2,1)}, bf16[56,1152]{1,0:T(8,128)(2,1)S(1)}, u32[]{:S(2)}) copy-start(bf16[56,1152]{1,0:T(8,128)(2,1)S(1)} %fusion.7.refs_0_) | copy-start | bytes 387076
  181.5 8.4 %collective-permute-start.24 = (bf16[56,1152]{1,0:T(8,128)(2,1)S(1)}, bf16[56,1152]{1,0:T(8,128)(2,1)S(1)}, u32[]{:S(2)}, u32[]{:S(2)}) collective-permute-start(bf16[56,1152]{1,0:T(8,128)(2,1)S(1)} %fusion.7.refs_0_), channel_id=1, source_target_pairs={{0,24},{8,16},{16,8},{24,0},{1,25},{9,17},{17,9},{25,1},{2,26},{10... | collective-permute-start | bytes 387080 | tf_op jit(solution)/shard_map/ppermute | solution.py:786
  184.0 6.7 %collective-permute-start.23 = (bf16[56,1152]{1,0:T(8,128)(2,1)S(1)}, bf16[56,1152]{1,0:T(8,128)(2,1)S(1)}, u32[]{:S(2)}, u32[]{:S(2)}) collective-permute-start(bf16[56,1152]{1,0:T(8,128)(2,1)S(1)} %fusion.7.refs_0_), channel_id=1, source_target_pairs={{0,16},{8,24},{16,0},{24,8},{1,17},{9,25},{17,1},{25,9},{2,18},{10... | collective-permute-start | bytes 387080 | tf_op jit(solution)/shard_map/ppermute | solution.py:786
  184.5 1.4 copy-start.14
  184.6 6.3 %collective-permute-start.22 = (bf16[56,1152]{1,0:T(8,128)(2,1)S(1)}, bf16[56,1152]{1,0:T(8,128)(2,1)S(1)}, u32[]{:S(2)}, u32[]{:S(2)}) collective-permute-start(bf16[56,1152]{1,0:T(8,128)(2,1)S(1)} %fusion.7.refs_0_), channel_id=1, source_target_pairs={{0,8},{8,0},{16,24},{24,16},{1,9},{9,1},{17,25},{25,17},{2,10},{10... | collective-permute-start | bytes 387080 | tf_op jit(solution)/shard_map/ppermute | solution.py:786
  185.9 0.7 copy-start.16
  190.0 0.9 copy-start.22
  (8 other events, 5.3 us)
